TPU v7x, 32 devices: a whole 2x2x4 slice. The times are simulated.
32 devices in a mesh: seq: 4 (over x, core), frame: 8 (over z, y).
Axes of the slice: x: 2, y: 2, z: 4, core: 2. Of those that a mesh axis runs over, the one named last changes fastest.
Arguments:
- inputs: bfloat16 [4, 16, 64, 768], P('seq', 'frame'), may hold values from -6 to 6
- clip_id: int32 [4, 16], P('seq'), may hold values from 0 to 12, as said below
- ln_gains: float32 [3, 768], replicated, may hold values from 0.25 to 1.75
- ln_biases: float32 [3, 768], replicated, may hold values from -2 to 2
- w_qkv: bfloat16 [768, 2304], P('frame'), may hold values from -0.3125 to 0.3125
- w_out: bfloat16 [768, 768], P('frame'), may hold values from -0.625 to 0.625
- w_up: bfloat16 [768, 3072], P('frame'), may hold values from -0.21875 to 0.21875
- w_down: bfloat16 [3072, 768], P('frame'), may hold values from -0.109375 to 0.109375
- up_bias: float32 [3072], replicated, may hold values from -3 to 3
- down_bias: float32 [768], replicated, may hold values from -2 to 2
- conv_first: bfloat16 [768, 72], P('frame'), may hold values from -0.078125 to 0.078125
- conv_first_bias: float32 [8], replicated, may hold values from -3 to 3
- conv_mid: float32 [3, 8, 72], replicated, may hold values from -0.75 to 0.75
- conv_mid_bias: float32 [3, 8], replicated, may hold values from -3 to 3
- cotangent: bfloat16 [4, 16, 8, 768], P('seq', 'frame'), may hold values from -6 to 6
Outputs:
- learned: float32 [4, 16, 8, 768], P('seq', 'frame')
- grad_input: float32 [4, 16, 64, 768], P('seq', 'frame')
- grad_qkv: float32 [768, 2304], P('frame')
- grad_out: float32 [768, 768], P('frame')
- grad_up: float32 [768, 3072], P('frame')
- grad_down: float32 [3072, 768], P('frame')
- grad_conv_first: float32 [768, 72], P('frame')
- grad_ln_gains: float32 [3, 768], replicated
- grad_ln_biases: float32 [3, 768], replicated
- grad_up_bias: float32 [3072], replicated
- grad_down_bias: float32 [768], replicated
- grad_conv_first_bias: float32 [8], replicated
- grad_conv_mid: float32 [3, 8, 72], replicated
- grad_conv_mid_bias: float32 [3, 8], replicated
Inputs may be any that keep to these rules, and one draw needn't show every extreme that they name: `clip_id`: A clip is a run of whole frames, and its number is the index of its first frame within the sequence, so numbers never fall from one frame to the next. In one sequence, chosen by the seed, a single clip covers all 16 frames; in each of the others, clips are 4 to 36 frames long and the last clip is exactly the last 4 frames.
All inputs are finite; a program needn't handle non-finite values.
Results may differ from a plain program's by a relative error of at most 0.018.
Values may be sent and summed in bfloat16 or wider, within the bound.
No kernel may reach another device: no remote copies, remote signals or barrier semaphores. Data moves between devices by JAX's collectives and lax.ppermute only.
A program may use at most 192 MiB of HBM per device.

v0:
```python
import jax
import jax.numpy as jnp
from jax import lax
from jax.sharding import PartitionSpec as P

HEADS = 12
HEAD_DIM = 64
CH = 8
GRID = 8


EPSILON = 1e-06
FLOOR_SCORE = -1e30
HIGHEST = lax.Precision.HIGHEST


def layer_norm(values, gain, shift):
    centre = jnp.mean(values, axis=-1, keepdims=True)
    centred = values - centre
    variance = jnp.mean(centred * centred, axis=-1, keepdims=True)
    return centred * lax.rsqrt(variance + EPSILON) * gain + shift


def gelu(values):
    return jax.nn.gelu(values, approximate=False)


def conv_grid(taps):
    side = taps.shape[1]
    width = taps.shape[-1] // 9
    padded = jnp.pad(taps, ((0, 0), (1, 1), (1, 1), (0, 0)))
    total = jnp.zeros(taps.shape[:-1] + (width,), taps.dtype)
    for tap in range(9):
        offset_row = tap // 3
        offset_column = tap % 3
        total = (
            total
            + padded[
                :,
                offset_row : offset_row + side,
                offset_column : offset_column + side,
                tap * width : (tap + 1) * width,
            ]
        )
    return total


def token_maps(first, conv_mid, conv_mid_bias):
    hidden = gelu(first)
    for layer in range(3):
        frames = hidden.shape[0]
        side = hidden.shape[1]
        flat = hidden.reshape(-1, hidden.shape[-1])
        taps = jnp.dot(flat, conv_mid[layer], precision=HIGHEST).reshape(frames, side, side, -1)
        hidden = conv_grid(taps) + conv_mid_bias[layer]
        if layer < 2:
            hidden = gelu(hidden)
    return jax.nn.sigmoid(hidden)


def pool_tokens(maps, features):
    return jnp.einsum("fpk,fpd->fkd", maps, features, precision=HIGHEST) / maps.shape[1]


def group_columns(matrix, group):
    block = lax.dynamic_slice_in_dim(matrix, group * 2 * HEAD_DIM, 2 * HEAD_DIM, 1)
    return block.reshape(matrix.shape[0], 2, HEAD_DIM)


def probabilities(query_group, key_group, same_clip, scale):
    raw_scores = (
        jnp.einsum("qhd,khd->hqk", query_group, key_group, preferred_element_type=jnp.float32)
        * scale
    )
    masked = jnp.where(same_clip[None], raw_scores, FLOOR_SCORE)
    row_max = jnp.max(masked, axis=-1, keepdims=True)
    shifted = jnp.exp(masked - row_max)
    total = jnp.sum(shifted, axis=-1, keepdims=True)
    return (shifted / total, row_max + jnp.log(total))


def shards(
    inputs,
    clip_id,
    ln_gains,
    ln_biases,
    w_qkv,
    w_out,
    w_up,
    w_down,
    up_bias,
    down_bias,
    conv_first,
    conv_first_bias,
    conv_mid,
    conv_mid_bias,
    cotangent,
):
    frames_dev = inputs.shape[1]
    patches = inputs.shape[2]
    width = inputs.shape[3]
    rows = frames_dev * patches
    pair = 2 * HEAD_DIM
    groups = HEADS // 2
    scale = HEAD_DIM ** (-0.5)
    group_ids = jnp.arange(groups, dtype=jnp.int32)
    full_qkv, full_out, full_up, full_down, full_conv = (
        lax.all_gather(w_qkv, "frame", axis=0, tiled=True),
        lax.all_gather(w_out, "frame", axis=0, tiled=True),
        lax.all_gather(w_up, "frame", axis=0, tiled=True),
        lax.all_gather(w_down, "frame", axis=0, tiled=True),
        lax.all_gather(conv_first, "frame", axis=0, tiled=True),
    )
    clips = clip_id[0]
    key_clip = jnp.repeat(clips, patches, total_repeat_length=clips.shape[0] * patches)
    query_clip = lax.dynamic_slice_in_dim(key_clip, lax.axis_index("frame") * rows, rows)
    same_clip = query_clip[:, None] == key_clip[None, :]
    tokens = inputs[0].reshape(rows, width).astype(jnp.float32)
    normed_one = layer_norm(tokens, ln_gains[0], ln_biases[0])
    normed_one_low = normed_one.astype(jnp.bfloat16)
    projected = jnp.dot(normed_one_low, full_qkv, preferred_element_type=jnp.float32).astype(
        jnp.bfloat16
    )
    queries = projected[:, :width]
    keys_local = projected[:, width : 2 * width]
    values_local = projected[:, 2 * width :]
    keys_all, values_all = (
        lax.all_gather(keys_local, "frame", axis=0, tiled=True),
        lax.all_gather(values_local, "frame", axis=0, tiled=True),
    )

    def attend_group(group):
        prob, log_total = probabilities(
            group_columns(queries, group), group_columns(keys_all, group), same_clip, scale
        )
        mixed_rows = jnp.einsum(
            "hqk,khd->qhd",
            prob.astype(jnp.bfloat16),
            group_columns(values_all, group),
            preferred_element_type=jnp.float32,
        )
        return (mixed_rows.reshape(rows, pair), log_total[..., 0])

    attended_groups, log_totals = lax.map(attend_group, group_ids)
    attended = jnp.moveaxis(attended_groups, 0, 1).reshape(rows, width).astype(jnp.bfloat16)
    after_attention = tokens + jnp.dot(attended, full_out, preferred_element_type=jnp.float32)
    normed_two = layer_norm(after_attention, ln_gains[1], ln_biases[1])
    normed_two_low = normed_two.astype(jnp.bfloat16)
    pre_act = jnp.dot(normed_two_low, full_up, preferred_element_type=jnp.float32) + up_bias
    act_low = gelu(pre_act).astype(jnp.bfloat16)
    block_out = (
        after_attention
        + jnp.dot(act_low, full_down, preferred_element_type=jnp.float32)
        + down_bias
    )
    normed_three = layer_norm(block_out, ln_gains[2], ln_biases[2])
    normed_three_low = normed_three.astype(jnp.bfloat16)
    tap_rows = jnp.dot(normed_three_low, full_conv, preferred_element_type=jnp.float32).reshape(
        frames_dev, GRID, GRID, 9 * CH
    )
    first = conv_grid(tap_rows) + conv_first_bias
    features = block_out.reshape(frames_dev, patches, width)

    def tail(first_arg, features_arg, mid_arg, mid_bias_arg):
        maps = token_maps(first_arg, mid_arg, mid_bias_arg).reshape(frames_dev, patches, CH)
        return pool_tokens(maps, features_arg)

    learned, tail_back = jax.vjp(tail, first, features, conv_mid, conv_mid_bias)
    grad_first, grad_pool, grad_mid, grad_mid_bias = tail_back(cotangent[0].astype(jnp.float32))
    grad_first_low = grad_first.astype(jnp.bfloat16)
    grad_first_bias = jnp.sum(grad_first_low.astype(jnp.float32), axis=(0, 1, 2))
    spread_unused, spread_back = jax.vjp(conv_grid, tap_rows)
    spread = (
        spread_back(grad_first_low.astype(jnp.float32))[0]
        .reshape(rows, 9 * CH)
        .astype(jnp.bfloat16)
    )
    grad_conv = jnp.einsum(
        "rd,rc->dc", normed_three_low, spread, preferred_element_type=jnp.float32
    )
    grad_normed_three = jnp.einsum(
        "rc,dc->rd", spread, full_conv, preferred_element_type=jnp.float32
    )
    norm_unused_three, norm_back_three = jax.vjp(layer_norm, block_out, ln_gains[2], ln_biases[2])
    grad_block, grad_gain_three, grad_shift_three = norm_back_three(grad_normed_three)
    grad_block = grad_block + grad_pool.reshape(rows, width)
    grad_mlp = grad_block.astype(jnp.bfloat16)
    grad_down_bias = jnp.sum(grad_mlp.astype(jnp.float32), axis=0)
    grad_down = jnp.einsum("rf,rd->fd", act_low, grad_mlp, preferred_element_type=jnp.float32)
    grad_act = jnp.einsum("rd,fd->rf", grad_mlp, full_down, preferred_element_type=jnp.float32)
    gelu_unused, gelu_back = jax.vjp(gelu, pre_act)
    grad_pre = gelu_back(grad_act)[0].astype(jnp.bfloat16)
    grad_up_bias = jnp.sum(grad_pre.astype(jnp.float32), axis=0)
    grad_up = jnp.einsum("rd,rf->df", normed_two_low, grad_pre, preferred_element_type=jnp.float32)
    grad_normed_two = jnp.einsum("rf,df->rd", grad_pre, full_up, preferred_element_type=jnp.float32)
    norm_unused_two, norm_back_two = jax.vjp(layer_norm, after_attention, ln_gains[1], ln_biases[1])
    grad_after, grad_gain_two, grad_shift_two = norm_back_two(grad_normed_two)
    grad_after = grad_after + grad_block
    grad_branch = grad_after.astype(jnp.bfloat16)
    grad_out = jnp.einsum("ri,rd->id", attended, grad_branch, preferred_element_type=jnp.float32)
    grad_attended = jnp.einsum(
        "rd,id->ri", grad_branch, full_out, preferred_element_type=jnp.float32
    ).astype(jnp.bfloat16)
    keys_back, values_back = (
        lax.all_gather(keys_local, "frame", axis=0, tiled=True),
        lax.all_gather(values_local, "frame", axis=0, tiled=True),
    )

    def grad_scores_for(group):
        query_group = group_columns(queries, group)
        key_group = group_columns(keys_back, group)
        value_group = group_columns(values_back, group)
        grad_group = group_columns(grad_attended, group)
        prob, log_unused = probabilities(query_group, key_group, same_clip, scale)
        grad_prob = jnp.einsum(
            "qhd,khd->hqk", grad_group, value_group, preferred_element_type=jnp.float32
        )
        centre = jnp.sum(prob * grad_prob, axis=-1, keepdims=True)
        grad_score = (prob * (grad_prob - centre)).astype(jnp.bfloat16)
        grad_query = (
            jnp.einsum("hqk,khd->qhd", grad_score, key_group, preferred_element_type=jnp.float32)
            * scale
        )
        return (
            prob,
            grad_score,
            grad_query.reshape(rows, pair),
            centre[..., 0],
            query_group,
            grad_group,
        )

    def query_and_keys(group):
        prob, grad_score, grad_query, centre, query_group, grad_group = grad_scores_for(group)
        key_terms = (
            jnp.einsum(
                "hqk,qhd->khd", grad_score, query_group, preferred_element_type=jnp.float32
            ).reshape(-1, pair)
            * scale
        )
        value_terms = jnp.einsum(
            "hqk,qhd->khd",
            prob.astype(jnp.bfloat16),
            grad_group,
            preferred_element_type=jnp.float32,
        ).reshape(-1, pair)
        return (grad_query, key_terms, value_terms)

    grad_query_groups, key_terms_all, value_terms_all = lax.map(query_and_keys, group_ids)
    key_shares, value_shares = (
        lax.psum_scatter(key_terms_all, "frame", scatter_dimension=1, tiled=True),
        lax.psum_scatter(value_terms_all, "frame", scatter_dimension=1, tiled=True),
    )
    grad_queries = jnp.moveaxis(grad_query_groups, 0, 1).reshape(rows, width)
    grad_keys = jnp.moveaxis(key_shares, 0, 1).reshape(rows, width)
    grad_values = jnp.moveaxis(value_shares, 0, 1).reshape(rows, width)
    grad_projected = jnp.concatenate([grad_queries, grad_keys, grad_values], 1).astype(jnp.bfloat16)
    grad_qkv = jnp.einsum(
        "rd,re->de", normed_one_low, grad_projected, preferred_element_type=jnp.float32
    )
    grad_normed_one = jnp.einsum(
        "re,de->rd", grad_projected, full_qkv, preferred_element_type=jnp.float32
    )
    norm_unused_one, norm_back_one = jax.vjp(layer_norm, tokens, ln_gains[0], ln_biases[0])
    grad_tokens, grad_gain_one, grad_shift_one = norm_back_one(grad_normed_one)
    grad_input = (grad_after + grad_tokens).reshape(1, frames_dev, patches, width)
    big_shards = (
        lax.psum_scatter(grad_qkv, "frame", scatter_dimension=0, tiled=True),
        lax.psum_scatter(grad_out, "frame", scatter_dimension=0, tiled=True),
        lax.psum_scatter(grad_up, "frame", scatter_dimension=0, tiled=True),
        lax.psum_scatter(grad_down, "frame", scatter_dimension=0, tiled=True),
        lax.psum_scatter(grad_conv, "frame", scatter_dimension=0, tiled=True),
    )
    small_sums = lax.psum(
        (
            jnp.stack([grad_gain_one, grad_gain_two, grad_gain_three]),
            jnp.stack([grad_shift_one, grad_shift_two, grad_shift_three]),
            grad_up_bias,
            grad_down_bias,
            grad_first_bias,
            grad_mid,
            grad_mid_bias,
        ),
        "frame",
    )
    totals = (
        lax.psum(big_shards[0].astype(jnp.bfloat16), "seq").astype(jnp.float32),
        lax.psum(big_shards[1].astype(jnp.bfloat16), "seq").astype(jnp.float32),
        lax.psum(big_shards[2].astype(jnp.bfloat16), "seq").astype(jnp.float32),
        lax.psum(big_shards[3].astype(jnp.bfloat16), "seq").astype(jnp.float32),
        lax.psum(big_shards[4].astype(jnp.bfloat16), "seq").astype(jnp.float32),
        lax.psum(small_sums[0].astype(jnp.bfloat16), "seq").astype(jnp.float32),
        lax.psum(small_sums[1].astype(jnp.bfloat16), "seq").astype(jnp.float32),
        lax.psum(small_sums[2].astype(jnp.bfloat16), "seq").astype(jnp.float32),
        lax.psum(small_sums[3].astype(jnp.bfloat16), "seq").astype(jnp.float32),
        lax.psum(small_sums[4].astype(jnp.bfloat16), "seq").astype(jnp.float32),
        lax.psum(small_sums[5].astype(jnp.bfloat16), "seq").astype(jnp.float32),
        lax.psum(small_sums[6].astype(jnp.bfloat16), "seq").astype(jnp.float32),
    )
    return (
        learned[None],
        grad_input,
        totals[0],
        totals[1],
        totals[2],
        totals[3],
        totals[4],
        totals[5],
        totals[6],
        totals[7],
        totals[8],
        totals[9],
        totals[10],
        totals[11],
    )


def solution(mesh):
    placed = (
        P("seq", "frame", None, None),
        P("seq", None),
        P(),
        P(),
        P("frame", None),
        P("frame", None),
        P("frame", None),
        P("frame", None),
        P(),
        P(),
        P("frame", None),
        P(),
        P(),
        P(),
        P("seq", "frame", None, None),
    )
    return jax.shard_map(
        shards,
        mesh=mesh,
        in_specs=placed,
        out_specs=(
            P("seq", "frame", None, None),
            P("seq", "frame", None, None),
            P("frame", None),
            P("frame", None),
            P("frame", None),
            P("frame", None),
            P("frame", None),
            P(),
            P(),
            P(),
            P(),
            P(),
            P(),
            P(),
        ),
        check_vma=False,
    )
```

profile of v0, /device:TPU:2, one launch (start us, length us, event | category | flops | bytes accessed | tf_op | source)
XLA Modules:
  0.0 1271.2 jit_solution(1590910319078893267)
XLA Ops:
  9.1 1.1 multiply_reduce_fusion.9
  13.2 63.5 %all-gather.8.cloned.1.call-done = bf16[768,2304]{1,0:T(8,128)(2,1)} async-done(((bf16[96,2304]{1,0:T(8,128)(2,1)}), bf16[768,2304]{1,0:T(8,128)(2,1)}) %all-gather.8.cloned.1.call-update) | async-done | bytes 3538960 | tf_op jit(solution)/shard_map/all_gather | solution.py:108
  76.6 2.6 convolution_convert_fusion
  83.5 4.5 compare_select_fusion.1
  88.2 30.9 %all-gather = bf16[8,96,72]{1,2,0:T(8,128)(2,1)S(1)} all-gather(bf16[1,96,72]{1,2,0:T(8,128)(2,1)S(1)} %bitcast.308), channel_id=1, replica_groups=mesh['seq'=4,'frame'=8] {'frame'}, dimensions={0}, use_global_device_ids=true | all-gather | bytes 124416 | tf_op jit(solution)/shard_map/all_gather | solution.py:112
  119.3 5.7 select_select_fusion
  125.9 2.6 copy.59
  128.5 41.4 %all-gather.12.cloned.1.call-done = bf16[1024,768]{1,0:T(8,128)(2,1)} async-done(((bf16[128,768]{1,0:T(8,128)(2,1)}), bf16[1024,768]{1,0:T(8,128)(2,1)}) %all-gather.12.cloned.1.call-update) | async-done | bytes 1572880 | tf_op jit(solution)/shard_map/all_gather | solution.py:128
  169.9 2.6 copy.61
  172.5 29.5 %while.31 = (s32[]{:T(128)}, bf16[6,128,128]{1,2,0:T(8,128)(2,1)S(1)}, s32[6]{0:T(128)S(1)}, bf16[1024,768]{0,1:T(8,128)(2,1)}, bf16[128,768]{0,1:T(8,128)(2,1)}...) while((s32[]{:T(128)}, ...), condition=%wide.region_5.6_spmd.clone, body=%wide.region_2.5_spmd.clone.sunk | while | flops 103155968 | bytes 4561603 | solution.py:144
  202.0 9.7 all-gather.14.cloned.1.call-done
  211.7 1.7 fusion.144
  213.7 78.8 %all-gather.16.cloned.1.call-done = bf16[768,3072]{1,0:T(8,128)(2,1)} async-done(((bf16[96,3072]{1,0:T(8,128)(2,1)}), bf16[768,3072]{1,0:T(8,128)(2,1)}) %all-gather.16.cloned.1.call-update) | async-done | bytes 4718608 | tf_op jit(solution)/shard_map/all_gather | solution.py:110
  292.5 8.4 multiply_convert_fusion.1
  300.9 71.7 %all-gather.18.cloned.1.call-done = bf16[3072,768]{1,0:T(8,128)(2,1)} async-done(((bf16[384,768]{1,0:T(8,128)(2,1)}), bf16[3072,768]{1,0:T(8,128)(2,1)}) %all-gather.18.cloned.1.call-update) | async-done | bytes 4718608 | tf_op jit(solution)/shard_map/all_gather | solution.py:111
  372.6 3.4 fusion.145
  385.2 2.5 convert_reduce_fusion
  387.7 2.3 multiply_reduce_fusion.2
  392.5 60.0 %while.32 = (s32[]{:T(128)}, bf16[6,128,128]{1,2,0:T(8,128)(2,1)}, f32[6,1024,128]{1,2,0:T(8,128)}, f32[6,1024,128]{1,2,0:T(8,128)}, s32[6]{0:T(128)S(1)}, /*ind...) while((s32[]{:T(128)}, bf16[6,128,128]{1,2,0:T(8,128)(2,1)}, ...), condition=%wide.region_18.19_spmd.clone, body=%wide.region_14.18_spmd.clone.sunk | while | flops 205817856 | bytes 14503019 | solution.py:249
  399.7 1.4 fusion.241
  409.7 1.4 fusion.241
  419.7 1.4 fusion.241
  429.7 1.4 fusion.241
  439.7 1.4 fusion.241
  449.7 1.4 fusion.241
  454.6 1.9 fusion.32
  457.6 5.1 fusion.131
  463.9 5.1 fusion.151
  469.1 56.7 %reduce-scatter.12.cloned.1.call-done = f32[6,128,128]{1,2,0:T(8,128)} async-done(((f32[6,1024,128]{1,2,0:T(8,128)}), f32[6,128,128]{1,2,0:T(8,128)}) %reduce-scatter.12.cloned.1.call-update) | async-done | bytes 393232 | tf_op jit(solution)/shard_map/reduce_scatter | solution.py:252
  526.8 76.4 %reduce-scatter.10.cloned.1.call-done = f32[6,128,128]{1,2,0:T(8,128)} async-done(((f32[6,1024,128]{1,2,0:T(8,128)}), f32[6,128,128]{1,2,0:T(8,128)}) %reduce-scatter.10.cloned.1.call-update) | async-done | bytes 393232 | tf_op jit(solution)/shard_map/reduce_scatter | solution.py:251
  604.2 4.0 fusion.30
  609.2 1.2 convolution_bitcast_fusion.1
  610.5 1.2 convolution_bitcast_fusion.2
  611.8 1.2 convolution_bitcast_fusion.3
  614.0 53.6 %reduce-scatter.22.cloned.1.call-done = f32[96,72]{1,0:T(8,128)} async-done(((f32[768,72]{1,0:T(8,128)}), f32[96,72]{1,0:T(8,128)}) %reduce-scatter.22.cloned.1.call-update) | async-done | bytes 27664
  668.5 70.7 %reduce-scatter.16.cloned.1.call-done = f32[96,768]{1,0:T(8,128)} async-done(((f32[768,768]{1,0:T(8,128)}), f32[96,768]{1,0:T(8,128)}) %reduce-scatter.16.cloned.1.call-update) | async-done | bytes 294928 | tf_op jit(solution)/shard_map/reduce_scatter | solution.py:269
  739.2 1.6 convert_element_type.185
  740.8 3.4 fusion.132
  744.2 160.9 %reduce-scatter.18.cloned.1.call-done = f32[96,3072]{1,0:T(8,128)} async-done(((f32[768,3072]{1,0:T(8,128)}), f32[96,3072]{1,0:T(8,128)}) %reduce-scatter.18.cloned.1.call-update) | async-done | bytes 1179664 | tf_op jit(solution)/shard_map/reduce_scatter | solution.py:270
  905.2 2.2 convert_element_type.187
  907.3 163.7 %reduce-scatter.20.cloned.1.call-done = f32[384,768]{1,0:T(8,128)} async-done(((f32[3072,768]{1,0:T(8,128)}), f32[384,768]{1,0:T(8,128)}) %reduce-scatter.20.cloned.1.call-update) | async-done | bytes 1179664 | tf_op jit(solution)/shard_map/reduce_scatter | solution.py:271
  1071.0 2.1 convert_element_type.189
  1073.2 129.6 %reduce-scatter.14.cloned.1.call-done = f32[96,2304]{1,0:T(8,128)} async-done(((f32[768,2304]{1,0:T(8,128)}), f32[96,2304]{1,0:T(8,128)}) %reduce-scatter.14.cloned.1.call-update) | async-done | bytes 884752 | tf_op jit(solution)/shard_map/reduce_scatter | solution.py:268
  1202.8 2.0 convert_element_type.183
  1205.2 35.8 %all-reduce.46 = (bf16[3,768]{1,0:T(4,128)(2,1)S(1)}, bf16[3,768]{1,0:T(4,128)(2,1)S(1)}, bf16[3072]{0:T(1024)(128)(2,1)S(1)}, bf16[768]{0:T(1024)(128)(2,1)S(1)...) all-reduce(f32[3,768]{1,0:T(4,128)S(1)} %get-tuple-element.497, ...), channel_id=1, replica_groups=mesh['seq'=4,'frame'=8] {'frame'}, use_global_device_ids=true, to_apply=%region_36.37 | all-reduce | flops 10208 | bytes 61248 | tf_op jit(solution)/shard_map/psum | solution.py:274
  1241.0 12.1 all-reduce.47
  1258.8 2.1 convert_element_type.184
  1260.8 1.6 convert_element_type.186
  (482 shorter events, 110.8 us)
Async XLA Ops:
  7.2 69.5 %all-gather.8.cloned.1.call-start = ((), (), s32[]{:S(2)}) async-start(), calls=%async_computation.7 | async-start | bytes 3981312 | tf_op jit(solution)/shard_map/all_gather | solution.py:108
  7.9 118.0 %all-gather.10.cloned.1.call-start = ((), (), s32[]{:S(2)}) async-start(), calls=%async_computation.8 | async-start | bytes 1769472 | tf_op jit(solution)/shard_map/all_gather | solution.py:129
  9.1 70.2 %copy-start.58 = (f32[128]{0:T(128)}, f32[128]{0:T(128)S(1)}, u32[]{:S(2)}) copy-start(f32[128]{0:T(128)S(1)} %div.102) | copy-start | bytes 1540
  10.3 69.0 %copy-start.60 = (f32[128]{0:T(128)}, f32[128]{0:T(128)S(1)}, u32[]{:S(2)}) copy-start(f32[128]{0:T(128)S(1)} %rsqrt.33) | copy-start | bytes 1540
  13.1 66.2 %copy-start.6 = (bf16[128,768]{1,0:T(8,128)(2,1)}, bf16[128,768]{1,0:T(8,128)(2,1)S(1)}, u32[]{:S(2)}) copy-start(bf16[128,768]{1,0:T(8,128)(2,1)S(1)} %add_convert_fusion.3) | copy-start | bytes 589828
  79.3 8.8 copy-start.64
  79.4 8.8 copy-start.45
  80.2 89.7 %all-gather.12.cloned.1.call-start = ((), (), s32[]{:S(2)}) async-start(), calls=%async_computation.9 | async-start | bytes 1769472 | tf_op jit(solution)/shard_map/all_gather | solution.py:128
  80.9 130.8 %all-gather.14.cloned.1.call-start = ((), (), s32[]{:S(2)}) async-start(), calls=%async_computation.10 | async-start | bytes 1327104 | tf_op jit(solution)/shard_map/all_gather | solution.py:109
  81.5 211.0 %all-gather.16.cloned.1.call-start = ((), (), s32[]{:S(2)}) async-start(), calls=%async_computation.11 | async-start | bytes 5308416 | tf_op jit(solution)/shard_map/all_gather | solution.py:110
  82.1 290.5 %all-gather.18.cloned.1.call-start = ((), (), s32[]{:S(2)}) async-start(), calls=%async_computation.12 | async-start | bytes 5308416 | tf_op jit(solution)/shard_map/all_gather | solution.py:111
  82.7 443.1 %reduce-scatter.12.cloned.1.call-start = ((), (), s32[]{:S(2)}) async-start(), calls=%async_computation.14 | async-start | bytes 3538944 | tf_op jit(solution)/shard_map/reduce_scatter | solution.py:252
  172.5 39.2 %copy-start = (bf16[1,2,64,768]{3,2,1,0:T(8,128)(2,1)S(1)}, bf16[1,2,64,768]{3,2,1,0:T(8,128)(2,1)}, u32[]{:S(2)}) copy-start(bf16[1,2,64,768]{3,2,1,0:T(8,128)(2,1)} %param.21) | copy-start | bytes 589828
  202.0 90.5 %copy-start.8 = (bf16[6,128,128]{1,2,0:T(8,128)(2,1)}, bf16[6,128,128]{1,2,0:T(8,128)(2,1)S(1)}, u32[]{:S(2)}) copy-start(bf16[6,128,128]{1,2,0:T(8,128)(2,1)S(1)} %get-tuple-element.242) | copy-start | bytes 589828
  202.0 90.5 %copy-start.69 = (f32[3072]{0:T(1024)S(1)}, f32[3072]{0:T(1024)}, u32[]{:S(2)}) copy-start(f32[3072]{0:T(1024)} %param.29) | copy-start | bytes 36868
  213.4 176.6 %copy-start.52 = (f32[128]{0:T(128)}, f32[128]{0:T(128)S(1)}, u32[]{:S(2)}) copy-start(f32[128]{0:T(128)S(1)} %broadcast_multiply_fusion.2) | copy-start | bytes 1540
  213.7 176.4 %copy-start.56 = (f32[128]{0:T(128)}, f32[128]{0:T(128)S(1)}, u32[]{:S(2)}) copy-start(f32[128]{0:T(128)S(1)} %fusion.118) | copy-start | bytes 1540
  292.5 80.1 %copy-start.62 = (f32[768]{0:T(1024)S(1)}, f32[768]{0:T(1024)}, u32[]{:S(2)}) copy-start(f32[768]{0:T(1024)} %param.30) | copy-start | bytes 9220
  300.9 75.1 %copy-start.2 = (bf16[128,3072]{1,0:T(8,128)(2,1)}, bf16[128,3072]{1,0:T(8,128)(2,1)S(1)}, u32[]{:S(2)}) copy-start(bf16[128,3072]{1,0:T(8,128)(2,1)S(1)} %get-tuple-element.445) | copy-start | bytes 2359300
  372.6 12.5 slice-start.2
  376.8 5.2 copy-start.19
  376.8 5.2 copy-start.21
  376.9 8.3 slice-start.3
  377.9 5.1 copy-start.27
  377.9 5.0 copy-start.29
  402.5 4.9 copy-start.15
  402.5 4.9 copy-start.42
  412.5 4.9 copy-start.15
  412.5 4.9 copy-start.42
  422.5 4.9 copy-start.15
  422.5 4.9 copy-start.42
  432.5 4.9 copy-start.15
  432.5 4.9 copy-start.42
  452.6 150.6 %reduce-scatter.10.cloned.1.call-start = ((), (), s32[]{:S(2)}) async-start(), calls=%async_computation.13 | async-start | bytes 3538944 | tf_op jit(solution)/shard_map/reduce_scatter | solution.py:251
  453.3 214.3 %reduce-scatter.22.cloned.1.call-start = ((), (), s32[]{:S(2)}) async-start(), calls=%async_computation.19 | async-start | bytes 442368
  454.5 284.7 %reduce-scatter.16.cloned.1.call-start = ((), (), s32[]{:S(2)}) async-start(), calls=%async_computation.16 | async-start | bytes 2654208 | tf_op jit(solution)/shard_map/reduce_scatter | solution.py:269
  456.5 448.7 %reduce-scatter.18.cloned.1.call-start = ((), (), s32[]{:S(2)}) async-start(), calls=%async_computation.17 | async-start | bytes 10616832 | tf_op jit(solution)/shard_map/reduce_scatter | solution.py:270
  462.8 608.2 %reduce-scatter.20.cloned.1.call-start = ((), (), s32[]{:S(2)}) async-start(), calls=%async_computation.18 | async-start | bytes 10616832 | tf_op jit(solution)/shard_map/reduce_scatter | solution.py:271
  469.0 135.2 %copy-start.7 = (bf16[128,768]{1,0:T(8,128)(2,1)S(1)}, bf16[128,768]{1,0:T(8,128)(2,1)}, u32[]{:S(2)}) copy-start(bf16[128,768]{1,0:T(8,128)(2,1)} %copy-done.6) | copy-start | bytes 589828
  469.0 135.2 %copy-start.14 = (bf16[6,128,128]{1,2,0:T(8,128)(2,1)S(1)}, bf16[6,128,128]{1,2,0:T(8,128)(2,1)}, u32[]{:S(2)}) copy-start(bf16[6,128,128]{1,2,0:T(8,128)(2,1)} %get-tuple-element.243) | copy-start | bytes 589828
  469.0 733.8 %reduce-scatter.14.cloned.1.call-start = ((), (), s32[]{:S(2)}) async-start(), calls=%async_computation.15 | async-start | bytes 7962624 | tf_op jit(solution)/shard_map/reduce_scatter | solution.py:268
  608.4 132.4 %copy-start.59 = (f32[128]{0:T(128)S(1)}, f32[128]{0:T(128)}, u32[]{:S(2)}) copy-start(f32[128]{0:T(128)} %copy-done.58) | copy-start | bytes 1540
  608.4 650.3 %all-reduce.51.cloned.1.call-start = ((), (), s32[]{:S(2)}) async-start(), calls=%async_computation.20 | async-start | bytes 3538944 | tf_op jit(solution)/shard_map/psum | solution.py:287
  1073.2 131.7 %copy-start.71 = (f32[128]{0:T(128)S(1)}, f32[128]{0:T(128)}, u32[]{:S(2)}) copy-start(f32[128]{0:T(128)} %copy-done.70) | copy-start | bytes 1540
  1073.2 131.7 %copy-start.61 = (f32[128]{0:T(128)S(1)}, f32[128]{0:T(128)}, u32[]{:S(2)}) copy-start(f32[128]{0:T(128)} %copy-done.60) | copy-start | bytes 1540
  1073.2 132.0 %copy-start.46 = (f32[768]{0:T(1024)S(1)}, f32[768]{0:T(1024)}, u32[]{:S(2)}) copy-start(f32[768]{0:T(1024)} %get-tuple-element.431) | copy-start | bytes 9220
  1073.2 132.0 %copy-start.55 = (f32[3072]{0:T(1024)S(1)}, f32[3072]{0:T(1024)}, u32[]{:S(2)}) copy-start(f32[3072]{0:T(1024)} %get-tuple-element.433) | copy-start | bytes 36868
  1073.2 132.0 %copy-start.66 = (f32[8]{0:T(128)S(1)}, f32[8]{0:T(128)}, u32[]{:S(2)}) copy-start(f32[8]{0:T(128)} %get-tuple-element.489) | copy-start | bytes 100
  (81 other events, 174.5 us)
Sparse Core Ops, SparseCore 0:
  10.2 66.3 all-gather.7
  80.3 43.4 all-gather.9
  126.5 43.2 all-gather.11
  171.9 39.7 all-gather.13
  213.7 78.6 all-gather.15
  294.5 78.0 all-gather.17
  452.7 73.0 reduce-scatter.11
  529.4 73.7 reduce-scatter.9
  607.0 60.5 reduce-scatter.21
  671.0 68.1 reduce-scatter.15
  742.8 162.3 reduce-scatter.17
  908.6 162.3 reduce-scatter.19
  1074.7 128.0 reduce-scatter.13
  1206.0 45.2 all-reduce.50
where the time goes:
time: 1280 us; the launch traced here: 1270 us
  waiting for transfers between devices  980 us (77%)
  matrix products  79.9 us (6%)
  blocking collectives  78.8 us (6%)
  local copies, waits for them, and re-layouts  60.8 us (5%)
  other arithmetic  46.3 us (4%)
  between operations  15 us (1%)
    reduce_scatter x1, waiting for transfers between devices, shards(): lax.psum_scatter(grad_down, 'frame', scatter_dimension=0, tiled=True)  164 us
    reduce_scatter x1, waiting for transfers between devices, shards(): lax.psum_scatter(grad_up, 'frame', scatter_dimension=0, tiled=True)  161 us
    reduce_scatter x1, waiting for transfers between devices, shards(): lax.psum_scatter(grad_qkv, 'frame', scatter_dimension=0, tiled=True)  130 us
    all_gather x1, waiting for transfers between devices, shards(): lax.all_gather(w_up, 'frame', axis=0, tiled=True)  78.8 us
    reduce_scatter x1, waiting for transfers between devices, shards(): lax.psum_scatter(key_terms_all, 'frame', scatter_dimension=1, tiled=True)  76.4 us
    all_gather x1, waiting for transfers between devices, shards(): lax.all_gather(w_down, 'frame', axis=0, tiled=True)  71.7 us
    reduce_scatter x1, waiting for transfers between devices, shards(): lax.psum_scatter(grad_out, 'frame', scatter_dimension=0, tiled=True)  70.7 us
    all_gather x1, waiting for transfers between devices, shards(): lax.all_gather(w_qkv, 'frame', axis=0, tiled=True)  63.5 us
  transfers between devices with their start and end apart: 14, of which 12 were waited for; matrix products, arithmetic and copies ran while one was open for 8% of the time, Pallas kernels for 0%

commit v1 on v0

v1 whole, which is shorter than its diff:
```python
import functools

import jax
import jax.numpy as jnp
from jax import lax
from jax.experimental import pallas as pl
from jax.experimental.pallas import tpu as pltpu
from jax.sharding import PartitionSpec as P

HEADS = 12
HEAD_DIM = 64
CH = 8
GRID = 8

EPSILON = 1e-06
FLOOR_SCORE = -1e30
HIGHEST = lax.Precision.HIGHEST
AXES = ("seq", "frame")
PLANE_OF = (0, 1, 2, 3)
RANK_OF = (0, 1, 2, 3)
VMEM_LIMIT = 56 * 1024 * 1024
BF = jnp.bfloat16
F32 = jnp.float32


def norm_stats(values):
    centre = jnp.mean(values, axis=-1, keepdims=True)
    centred = values - centre
    variance = jnp.mean(centred * centred, axis=-1, keepdims=True)
    inverse = lax.rsqrt(variance + EPSILON)
    return centred * inverse, inverse


def norm_back(normed, inverse, gain, grad):
    scaled = grad * gain
    mean_scaled = jnp.mean(scaled, axis=-1, keepdims=True)
    mean_cross = jnp.mean(scaled * normed, axis=-1, keepdims=True)
    grad_values = inverse * (scaled - mean_scaled - normed * mean_cross)
    return grad_values, jnp.sum(grad * normed, axis=0), jnp.sum(grad, axis=0)


def gelu(values):
    return jax.nn.gelu(values, approximate=False)


def conv_grid(taps):
    side = taps.shape[1]
    width = taps.shape[-1] // 9
    padded = jnp.pad(taps, ((0, 0), (1, 1), (1, 1), (0, 0)))
    total = jnp.zeros(taps.shape[:-1] + (width,), taps.dtype)
    for tap in range(9):
        offset_row = tap // 3
        offset_column = tap % 3
        total = (
            total
            + padded[
                :,
                offset_row : offset_row + side,
                offset_column : offset_column + side,
                tap * width : (tap + 1) * width,
            ]
        )
    return total


def token_maps(first, conv_mid, conv_mid_bias):
    hidden = gelu(first)
    for layer in range(3):
        frames = hidden.shape[0]
        side = hidden.shape[1]
        flat = hidden.reshape(-1, hidden.shape[-1])
        taps = jnp.dot(flat, conv_mid[layer], precision=HIGHEST).reshape(frames, side, side, -1)
        hidden = conv_grid(taps) + conv_mid_bias[layer]
        if layer < 2:
            hidden = gelu(hidden)
    return jax.nn.sigmoid(hidden)


def pool_tokens(maps, features):
    return jnp.einsum("fpk,fpd->fkd", maps, features, precision=HIGHEST) / maps.shape[1]


def dot(left, right, left_dim=1, right_dim=0):
    return lax.dot_general(
        left, right, (((left_dim,), (right_dim,)), ((), ())), preferred_element_type=F32
    )


def attend_kernel(heads, scale, q_ref, kv_ref, qclip_ref, kclip_ref, mixed_ref, log_ref):
    width = heads * HEAD_DIM
    same = kclip_ref[...] == qclip_ref[...]
    for head in range(heads):
        lanes = slice(head * HEAD_DIM, (head + 1) * HEAD_DIM)
        value_lanes = slice(width + head * HEAD_DIM, width + (head + 1) * HEAD_DIM)
        scores = dot(kv_ref[:, lanes], q_ref[:, lanes], 1, 1) * scale
        scores = jnp.where(same, scores, FLOOR_SCORE)
        top = jnp.max(scores, axis=0, keepdims=True)
        shifted = jnp.exp(scores - top)
        total = jnp.sum(shifted, axis=0, keepdims=True)
        prob = (shifted * (1.0 / total)).astype(BF)
        mixed = dot(kv_ref[:, value_lanes], prob, 0, 0)
        mixed_ref[head * HEAD_DIM : (head + 1) * HEAD_DIM, :] = mixed.astype(BF)
        log_ref[head : head + 1, :] = top + jnp.log(total)


def attend_back_kernel(
    heads, scale, q_ref, kv_ref, grad_ref, log_ref, qclip_ref, kclip_ref, dq_ref, dkv_ref
):
    width = heads * HEAD_DIM
    same = kclip_ref[...] == qclip_ref[...]

    @pl.when(pl.program_id(0) == 0)
    def _():
        dkv_ref[...] = jnp.zeros_like(dkv_ref)

    key_parts = []
    value_parts = []
    for head in range(heads):
        lanes = slice(head * HEAD_DIM, (head + 1) * HEAD_DIM)
        value_lanes = slice(width + head * HEAD_DIM, width + (head + 1) * HEAD_DIM)
        scores = dot(kv_ref[:, lanes], q_ref[:, lanes], 1, 1) * scale
        scores = jnp.where(same, scores, FLOOR_SCORE)
        prob = jnp.exp(scores - log_ref[head : head + 1, :])
        grad_prob = dot(kv_ref[:, value_lanes], grad_ref[:, lanes], 1, 1)
        delta = jnp.sum(prob * grad_prob, axis=0, keepdims=True)
        grad_score = (prob * (grad_prob - delta)).astype(BF)
        grad_query = dot(kv_ref[:, lanes], grad_score, 0, 0) * scale
        dq_ref[head * HEAD_DIM : (head + 1) * HEAD_DIM, :] = grad_query.astype(BF)
        key_parts.append(dot(grad_score, q_ref[:, lanes]) * scale)
        value_parts.append(dot(prob.astype(BF), grad_ref[:, lanes]))
    dkv_ref[...] += jnp.concatenate(key_parts + value_parts, axis=1)


def query_block(count, keys):
    return min(count, 256) if keys <= 1024 else 128


def attend(queries, keyvals, query_clip, key_clip):
    count, width = queries.shape
    keys = keyvals.shape[0]
    heads = width // HEAD_DIM
    block = query_block(count, keys)
    return pl.pallas_call(
        functools.partial(attend_kernel, heads, HEAD_DIM ** (-0.5)),
        grid=(count // block,),
        in_specs=[
            pl.BlockSpec((block, width), lambda i: (i, 0)),
            pl.BlockSpec((keys, 2 * width), lambda i: (0, 0)),
            pl.BlockSpec((1, block), lambda i: (0, i)),
            pl.BlockSpec((keys, 1), lambda i: (0, 0)),
        ],
        out_specs=[
            pl.BlockSpec((width, block), lambda i: (0, i)),
            pl.BlockSpec((8, block), lambda i: (0, i)),
        ],
        out_shape=[
            jax.ShapeDtypeStruct((width, count), BF),
            jax.ShapeDtypeStruct((8, count), F32),
        ],
        compiler_params=pltpu.CompilerParams(vmem_limit_bytes=VMEM_LIMIT),
        name="attend",
    )(queries, keyvals, query_clip, key_clip)


def attend_back(queries, keyvals, grads, logs, query_clip, key_clip):
    count, width = queries.shape
    keys = keyvals.shape[0]
    heads = width // HEAD_DIM
    block = query_block(count, keys)
    return pl.pallas_call(
        functools.partial(attend_back_kernel, heads, HEAD_DIM ** (-0.5)),
        grid=(count // block,),
        in_specs=[
            pl.BlockSpec((block, width), lambda i: (i, 0)),
            pl.BlockSpec((keys, 2 * width), lambda i: (0, 0)),
            pl.BlockSpec((block, width), lambda i: (i, 0)),
            pl.BlockSpec((8, block), lambda i: (0, i)),
            pl.BlockSpec((1, block), lambda i: (0, i)),
            pl.BlockSpec((keys, 1), lambda i: (0, 0)),
        ],
        out_specs=[
            pl.BlockSpec((width, block), lambda i: (0, i)),
            pl.BlockSpec((keys, 2 * width), lambda i: (0, 0)),
        ],
        out_shape=[
            jax.ShapeDtypeStruct((width, count), BF),
            jax.ShapeDtypeStruct((keys, 2 * width), F32),
        ],
        compiler_params=pltpu.CompilerParams(vmem_limit_bytes=VMEM_LIMIT),
        name="attend_back",
    )(queries, keyvals, grads, logs, query_clip, key_clip)


def shards(
    ranks,
    frame_size,
    inputs,
    clip_id,
    ln_gains,
    ln_biases,
    w_qkv,
    w_out,
    w_up,
    w_down,
    up_bias,
    down_bias,
    conv_first,
    conv_first_bias,
    conv_mid,
    conv_mid_bias,
    cotangent,
):
    lows = frame_size // ranks
    frames_dev = inputs.shape[1]
    patches = inputs.shape[2]
    width = inputs.shape[3]
    rows = frames_dev * patches
    hidden = up_bias.shape[0]
    quarter = width // ranks
    hidden_quarter = hidden // ranks
    row_shard = width // frame_size
    rank = lax.axis_index("seq")
    place = lax.axis_index("frame")
    high = place // lows
    low = place % lows

    def permute(array, target):
        pairs = []
        for seq in range(ranks):
            for hi in range(ranks):
                for lo in range(lows):
                    to_seq, to_hi, to_lo = target(seq, hi, lo)
                    pairs.append(
                        (
                            seq * frame_size + hi * lows + lo,
                            to_seq * frame_size + to_hi * lows + to_lo,
                        )
                    )
        return lax.ppermute(array, AXES, pairs)

    def across(array, bits):
        return permute(array, lambda seq, hi, lo: (seq ^ bits, hi, lo))

    def along_high(array, step):
        return permute(array, lambda seq, hi, lo: (seq, (hi + step) % ranks, lo))

    def along_low(array, step):
        return permute(array, lambda seq, hi, lo: (seq, hi, (lo + step) % lows))

    def to_planes(array):
        return permute(array, lambda seq, hi, lo: (RANK_OF[hi], PLANE_OF[seq], lo))

    def from_planes(array):
        return permute(
            array, lambda seq, hi, lo: (PLANE_OF.index(hi), RANK_OF.index(seq), lo)
        )

    def gather_tokens(block):
        far = across(block, 2)
        near = across(block, 1)
        both = across(far, 1)
        return jnp.concatenate([block, near, far, both], axis=0)

    def scatter_tokens(partial):
        blocks = partial.astype(BF).reshape(ranks, rows, partial.shape[1])
        arrived_far = across(blocks[3], 1)
        arrived_near = across(blocks[1], 1)
        far = partial[2 * rows : 3 * rows] + arrived_far.astype(F32)
        arrived = across(far.astype(BF), 2)
        return partial[:rows] + arrived_near.astype(F32) + arrived.astype(F32)

    def gather_rows(block):
        if lows != 2:
            return lax.all_gather(block, "frame", axis=0, tiled=True)
        found = [block] + [along_high(block, step) for step in range(1, ranks)]
        other = [along_low(item, 1) for item in found]
        stacked = jnp.stack(found)
        stacked_other = jnp.stack(other)
        pieces = []
        for hi in range(ranks):
            index = (high - hi) % ranks
            mine = lax.dynamic_index_in_dim(stacked, index, 0, False)
            theirs = lax.dynamic_index_in_dim(stacked_other, index, 0, False)
            pieces.append(jnp.where(low == 0, mine, theirs))
            pieces.append(jnp.where(low == 0, theirs, mine))
        return jnp.concatenate(pieces, axis=0)

    def scatter_rows(partial):
        if lows != 2:
            return lax.psum_scatter(
                partial.astype(BF), "frame", scatter_dimension=0, tiled=True
            ).astype(F32)
        count = partial.shape[0] // frame_size
        columns = partial.shape[1]
        split = partial.reshape(ranks, lows, count, columns)
        kept = lax.dynamic_index_in_dim(split, low, 1, False)
        sent = lax.dynamic_index_in_dim(split, 1 - low, 1, False).astype(BF)
        half = kept + along_low(sent, 1).astype(F32)
        total = lax.dynamic_index_in_dim(half, high, 0, False)
        half_low = half.astype(BF)
        for step in range(1, ranks):
            piece = lax.dynamic_index_in_dim(half_low, (high + step) % ranks, 0, False)
            total = total + along_high(piece, step).astype(F32)
        return total

    def in_rank_order(items):
        stacked = jnp.stack(items)
        return [
            lax.dynamic_index_in_dim(stacked, rank ^ index, 0, False) for index in range(ranks)
        ]

    def gather_ranks(block):
        far = across(block, 2)
        near = across(block, 1)
        both = across(far, 1)
        return in_rank_order([block, near, far, both])

    token_rows = inputs[0].reshape(rows, width)
    grad_rows = cotangent[0].reshape(frames_dev * CH, width)
    frame_count = clip_id.shape[1]
    clip_rows = jnp.pad(
        clip_id.astype(BF), ((0, 15), (0, width - frame_count))
    )
    moved = to_planes(jnp.concatenate([token_rows, grad_rows, clip_rows], axis=0))
    tokens = moved[:rows].astype(F32)
    grad_learned = moved[rows : rows + frames_dev * CH].astype(F32)
    clips = moved[rows + frames_dev * CH, :frame_count].astype(jnp.int32)

    own_qkv = lax.dynamic_index_in_dim(
        w_qkv.reshape(row_shard, 3, ranks, quarter), rank, 2, False
    ).reshape(row_shard, 3 * quarter)
    qkv_quarter = gather_rows(own_qkv)
    unit = hidden // (frame_size * ranks)
    columns = jnp.arange(hidden_quarter, dtype=jnp.int32)
    wanted = (columns // unit) * (unit * ranks) + rank * unit + columns % unit
    choose = (jnp.arange(hidden, dtype=jnp.int32)[:, None] == wanted[None, :]).astype(BF)
    own_up = dot(w_up, choose).astype(BF)
    own_down = lax.dynamic_slice_in_dim(w_down, rank * unit, unit, 0)
    own_out = lax.dynamic_slice_in_dim(w_out, rank * quarter, quarter, 1)
    packed = gather_rows(jnp.concatenate([own_up, own_down, own_out, conv_first], axis=1))
    up_quarter = packed[:, :hidden_quarter]
    down_quarter = packed[:, hidden_quarter : hidden_quarter + width]
    out_columns = packed[:, hidden_quarter + width : hidden_quarter + width + quarter]
    full_conv = packed[:, hidden_quarter + width + quarter :]

    def swap_ranks(array):
        split = array.reshape(ranks, quarter, array.shape[1])
        found = []
        for bits in range(ranks):
            piece = lax.dynamic_index_in_dim(split, rank ^ bits, 0, False)
            found.append(across(piece, bits) if bits else piece)
        return in_rank_order(found)

    out_quarter = jnp.concatenate(swap_ranks(out_columns), axis=1)
    up_bias_quarter = lax.dynamic_index_in_dim(
        up_bias.reshape(frame_size, ranks, unit), rank, 1, False
    ).reshape(1, hidden_quarter)

    frame_ids = jnp.arange(frame_count, dtype=jnp.int32)

    def clip_tokens(lo):
        blocks = []
        inverse = jnp.array([RANK_OF.index(item) for item in range(ranks)], jnp.int32)
        for bits in range(ranks):
            hi = lax.dynamic_index_in_dim(inverse, rank ^ bits, 0, False)
            for frame in range(frames_dev):
                blocks.append((hi * lows + lo) * frames_dev + frame)
        wanted_frames = jnp.stack(blocks)
        found = jnp.sum(
            jnp.where(wanted_frames[:, None] == frame_ids[None, :], clips[None, :], 0), axis=1
        )
        return jnp.broadcast_to(found[:, None], (found.shape[0], patches)).reshape(-1)

    query_clip = clip_tokens(low)
    key_clip = jnp.concatenate(
        [query_clip] + [clip_tokens((low - step) % lows) for step in range(1, lows)]
    )
    query_clip = query_clip[None, :]
    key_clip = key_clip[:, None]

    normed_one, inverse_one = norm_stats(tokens)
    all_one = gather_tokens((normed_one * ln_gains[0] + ln_biases[0]).astype(BF))
    projected = dot(all_one, qkv_quarter).astype(BF)
    queries = projected[:, :quarter]
    own_keyvals = projected[:, quarter:]
    keyvals = jnp.concatenate(
        [own_keyvals] + [along_low(own_keyvals, step) for step in range(1, lows)], axis=0
    )
    attended, logs = attend(queries, keyvals, query_clip, key_clip)
    after_attention = tokens + scatter_tokens(dot(attended, out_quarter, 0, 0))
    normed_two, inverse_two = norm_stats(after_attention)
    all_two = gather_tokens((normed_two * ln_gains[1] + ln_biases[1]).astype(BF))
    pre_act = dot(all_two, up_quarter) + up_bias_quarter
    act_low = gelu(pre_act).astype(BF)
    block_out = after_attention + scatter_tokens(dot(act_low, down_quarter)) + down_bias

    normed_three, inverse_three = norm_stats(block_out)
    normed_three_low = (normed_three * ln_gains[2] + ln_biases[2]).astype(BF)
    tap_rows = dot(normed_three_low, full_conv).reshape(frames_dev, GRID, GRID, 9 * CH)
    first = conv_grid(tap_rows) + conv_first_bias
    features = block_out.reshape(frames_dev, patches, width)

    def tail(first_arg, features_arg, mid_arg, mid_bias_arg):
        maps = token_maps(first_arg, mid_arg, mid_bias_arg).reshape(frames_dev, patches, CH)
        return pool_tokens(maps, features_arg)

    learned, tail_back = jax.vjp(tail, first, features, conv_mid, conv_mid_bias)
    grad_first, grad_pool, grad_mid, grad_mid_bias = tail_back(
        grad_learned.reshape(frames_dev, CH, width)
    )
    grad_first_low = grad_first.astype(BF)
    grad_first_bias = jnp.sum(grad_first_low.astype(F32), axis=(0, 1, 2))
    spread_unused, spread_back = jax.vjp(conv_grid, tap_rows)
    spread = spread_back(grad_first_low.astype(F32))[0].reshape(rows, 9 * CH).astype(BF)
    grad_conv = dot(normed_three_low, spread, 0, 0)
    grad_normed_three = dot(spread, full_conv, 1, 1)
    grad_block, grad_gain_three, grad_shift_three = norm_back(
        normed_three, inverse_three, ln_gains[2], grad_normed_three
    )
    grad_block = grad_block + grad_pool.reshape(rows, width)
    grad_mlp = grad_block.astype(BF)
    grad_down_bias = jnp.sum(grad_mlp.astype(F32), axis=0)

    all_mlp = gather_tokens(grad_mlp)
    grad_act = dot(all_mlp, down_quarter, 1, 1)
    gelu_unused, gelu_back = jax.vjp(gelu, pre_act)
    grad_pre = gelu_back(grad_act)[0].astype(BF)
    grad_up_bias = jnp.sum(grad_pre.astype(F32), axis=0)
    grad_normed_two = scatter_tokens(dot(grad_pre, up_quarter, 1, 1))
    grad_down = dot(act_low, all_mlp, 0, 0)
    grad_up = dot(all_two, grad_pre, 0, 0)
    mlp_share = scatter_rows(jnp.concatenate([grad_up, grad_down, grad_conv], axis=1))
    grad_after, grad_gain_two, grad_shift_two = norm_back(
        normed_two, inverse_two, ln_gains[1], grad_normed_two
    )
    grad_after = grad_after + grad_block

    all_branch = gather_tokens(grad_after.astype(BF))
    grad_attended = dot(all_branch, out_quarter, 1, 1).astype(BF)
    grad_out = dot(attended, all_branch)
    grad_queries, grad_keyvals = attend_back(
        queries, keyvals, grad_attended, logs, query_clip, key_clip
    )
    own_count = ranks * rows
    own_grads = grad_keyvals[:own_count]
    for step in range(1, lows):
        piece = grad_keyvals[step * own_count : (step + 1) * own_count].astype(BF)
        own_grads = own_grads + along_low(piece, -step).astype(F32)
    grad_projected = jnp.concatenate([grad_queries.T, own_grads.astype(BF)], axis=1)
    grad_qkv = dot(all_one, grad_projected, 0, 0)
    grad_normed_one = scatter_tokens(dot(grad_projected, qkv_quarter, 1, 1))
    grad_out_columns = jnp.concatenate(
        swap_ranks_rows(grad_out.astype(BF), ranks, quarter, rank, across), axis=0
    )
    qkv_share = scatter_rows(jnp.concatenate([grad_qkv, grad_out_columns.astype(F32)], axis=1))
    grad_tokens, grad_gain_one, grad_shift_one = norm_back(
        normed_one, inverse_one, ln_gains[0], grad_normed_one
    )
    grad_input = from_planes((grad_after + grad_tokens).astype(BF)).astype(F32)
    learned = from_planes(learned.astype(BF)).astype(F32)

    mlp_parts = gather_ranks(mlp_share.astype(BF))
    qkv_parts = gather_ranks(qkv_share.astype(BF))
    sum_up = (
        jnp.stack([part[:, :hidden_quarter] for part in mlp_parts])
        .reshape(ranks, row_shard, frame_size, unit)
        .transpose(1, 2, 0, 3)
        .reshape(row_shard, hidden)
        .astype(F32)
    )
    sum_down = jnp.concatenate(
        [part[:, hidden_quarter : hidden_quarter + width] for part in mlp_parts], axis=0
    ).astype(F32)
    sum_conv = sum(part[:, hidden_quarter + width :].astype(F32) for part in mlp_parts)
    sum_qkv = (
        jnp.stack([part[:, : 3 * quarter] for part in qkv_parts])
        .reshape(ranks, row_shard, 3, quarter)
        .transpose(1, 2, 0, 3)
        .reshape(row_shard, 3 * width)
        .astype(F32)
    )
    sum_out = jnp.concatenate([part[:, 3 * quarter :] for part in qkv_parts], axis=1).astype(F32)

    up_bias_terms = lax.dynamic_update_index_in_dim(
        jnp.zeros((frame_size, ranks, unit), F32),
        grad_up_bias.reshape(frame_size, unit),
        rank,
        1,
    )
    small = [
        jnp.stack([grad_gain_one, grad_gain_two, grad_gain_three]),
        jnp.stack([grad_shift_one, grad_shift_two, grad_shift_three]),
        up_bias_terms,
        grad_down_bias,
        grad_first_bias,
        grad_mid,
        grad_mid_bias,
    ]
    summed = lax.psum(jnp.concatenate([item.reshape(-1) for item in small]), AXES)
    results = []
    start = 0
    for item in small:
        results.append(summed[start : start + item.size].reshape(item.shape))
        start += item.size
    return (
        learned.reshape(1, frames_dev, CH, width),
        grad_input.reshape(1, frames_dev, patches, width),
        sum_qkv,
        sum_out,
        sum_up,
        sum_down,
        sum_conv,
        results[0],
        results[1],
        results[2].reshape(hidden),
        results[3],
        results[4],
        results[5],
        results[6],
    )


def swap_ranks_rows(array, ranks, quarter, rank, across):
    split = array.reshape(quarter, ranks, quarter).transpose(1, 0, 2)
    found = []
    for bits in range(ranks):
        piece = lax.dynamic_index_in_dim(split, rank ^ bits, 0, False)
        found.append(across(piece, bits) if bits else piece)
    stacked = jnp.stack(found)
    return [lax.dynamic_index_in_dim(stacked, rank ^ index, 0, False) for index in range(ranks)]


def solution(mesh):
    placed = (
        P("seq", "frame", None, None),
        P("seq", None),
        P(),
        P(),
        P("frame", None),
        P("frame", None),
        P("frame", None),
        P("frame", None),
        P(),
        P(),
        P("frame", None),
        P(),
        P(),
        P(),
        P("seq", "frame", None, None),
    )
    return jax.shard_map(
        functools.partial(shards, mesh.shape["seq"], mesh.shape["frame"]),
        mesh=mesh,
        in_specs=placed,
        out_specs=(
            P("seq", "frame", None, None),
            P("seq", "frame", None, None),
            P("frame", None),
            P("frame", None),
            P("frame", None),
            P("frame", None),
            P("frame", None),
            P(),
            P(),
            P(),
            P(),
            P(),
            P(),
            P(),
        ),
        check_vma=False,
    )
```

time: 1280 us -> 390 us (0.30)
  waiting for transfers between devices: 980 us -> 145 us
  starting transfers between devices: 0.78 us -> 61 us
  matrix products: 79.9 us -> 34.6 us
  blocking collectives: 78.8 us -> 47.1 us
  other arithmetic: 46.3 us -> 28.3 us
  Pallas kernels: 0 us -> 16.9 us
    reduce_scatter x6 -> x0, waiting for transfers between devices: 658 us -> none  [the longest x1 164 us: shards(): lax.psum_scatter(grad_down, 'frame', scatter_dimension=0, tiled=True)]
    all_gather x6 -> x0, waiting for transfers between devices: 265 us -> none  [the longest x1 78.8 us: shards(): lax.all_gather(w_up, 'frame', axis=0, tiled=True)]
    ppermute x0 -> x63, waiting for transfers between devices: none -> 145 us  [permute(): return lax.ppermute(array, AXES, pairs)]
    ppermute x0 -> x63, starting transfers between devices: none -> 61 us  [permute(): return lax.ppermute(array, AXES, pairs)]
    unnamed x15 -> x0, waiting for transfers between devices: 57.3 us -> none
    dynamic_slice x55 -> x5, local copies, waits for them, and re-layouts: 35.2 us -> 1.37 us  [the longest x1 0.98 us: shards(): own_out = lax.dynamic_slice_in_dim(w_out, rank * quarter, quarter, 1)]
    dot_general x50 -> x16, matrix products: 62.2 us -> 30.2 us  [dot(): lax.dot_general(left, right, (((left_dim,), (right_dim,)), ((), ())), pre...]
    all_gather x1 -> x0, blocking collectives: 30.9 us -> none  [shards(): lax.all_gather(conv_first, 'frame', axis=0, tiled=True)]
  transfers between devices with their start and end apart: 14 -> 63, of which waited for: 12 -> 26; matrix products, arithmetic and copies ran while one was open for 8% -> 19% of each run, Pallas kernels for 0% -> 0%
where the time goes in v1:
time: 390 us; the launch traced here: 384 us
  waiting for transfers between devices  145 us (37%)
  starting transfers between devices  61 us (16%)
  local copies, waits for them, and re-layouts  48 us (12%)
  blocking collectives  47.1 us (12%)
  matrix products  34.6 us (9%)
  other arithmetic  28.3 us (7%)
  Pallas kernels  16.9 us (4%)
    ppermute x63, waiting for transfers between devices, permute(): return lax.ppermute(array, AXES, pairs)  145 us
    ppermute x63, starting transfers between devices, permute(): return lax.ppermute(array, AXES, pairs)  61 us
    psum x1, blocking collectives, shards(): lax.psum(jnp.concatenate([item.reshape(-1) for item in small]), AXES)  47.1 us
    dot_general x16, matrix products, dot(): lax.dot_general(left, right, (((left_dim,), (right_dim,)), ((), ())), pre...  30.2 us
    pallas_call x1, Pallas kernels, attend_back(): pl.pallas_call(functools.partial(attend_back_kernel, heads, HEAD_DIM ** (...  9.69 us
  transfers between devices with their start and end apart: 63, of which 26 were waited for; matrix products, arithmetic and copies ran while one was open for 19% of the time, Pallas kernels for 0%

profile of v1, /device:TPU:2, one launch (start us, length us, event | category | flops | bytes accessed | tf_op | source)
XLA Modules:
  0.0 383.9 jit_solution(2885032924394381879)
XLA Ops:
  2.9 3.7 collective-permute-start.6
  10.3 1.9 fusion.10
  12.3 3.4 collective-permute-start.12
  18.8 16.1 %collective-permute-done.5 = bf16[96,576]{0,1:T(8,128)(2,1)S(1)} collective-permute-done((bf16[96,576]{0,1:T(8,128)(2,1)S(1)}, bf16[96,576]{0,1:T(8,128)(2,1)S(1)}, u32[]{:S(2)}, u32[]{:S(2)}) %collective-permute-start.5) | collective-permute-done | bytes 110624 | tf_op jit(solution)/shard_map/ppermute | solution.py:239
  36.8 4.9 %collective-permute-start = (bf16[160,768]{1,0:T(8,128)(2,1)}, bf16[160,768]{1,0:T(8,128)(2,1)S(1)}, u32[]{:S(2)}, u32[]{:S(2)}) collective-permute-start(bf16[160,768]{1,0:T(8,128)(2,1)} %fusion.57), channel_id=1, source_target_pairs={{0,0},{1,1},{2,8},{3,9},{4,16},{5,17},{6,24},{7,25},{8,2},{9,3},{1... | collective-permute-start | bytes 737288 | tf_op jit(solution)/shard_map/ppermute | solution.py:239
  42.6 22.8 %collective-permute-done = bf16[160,768]{1,0:T(8,128)(2,1)S(1)} collective-permute-done((bf16[160,768]{1,0:T(8,128)(2,1)}, bf16[160,768]{1,0:T(8,128)(2,1)S(1)}, u32[]{:S(2)}, u32[]{:S(2)}) %collective-permute-start) | collective-permute-done | bytes 245792 | tf_op jit(solution)/shard_map/ppermute | solution.py:239
  69.8 1.8 collective-permute-done.2
  73.6 1.8 convolution_convert_fusion
  78.6 7.9 %collective-permute-done.16 = bf16[96,1800]{1,0:T(8,128)(2,1)S(1)} collective-permute-done((bf16[96,1800]{1,0:T(8,128)(2,1)S(1)}, bf16[96,1800]{1,0:T(8,128)(2,1)S(1)}, u32[]{:S(2)}, u32[]{:S(2)}) %collective-permute-start.16) | collective-permute-done | bytes 345632 | tf_op jit(solution)/shard_map/ppermute | solution.py:239
  86.5 7.9 %collective-permute-done.17 = bf16[96,1800]{1,0:T(8,128)(2,1)S(1)} collective-permute-done((bf16[96,1800]{1,0:T(8,128)(2,1)S(1)}, bf16[96,1800]{1,0:T(8,128)(2,1)S(1)}, u32[]{:S(2)}, u32[]{:S(2)}) %collective-permute-start.17) | collective-permute-done | bytes 345632 | tf_op jit(solution)/shard_map/ppermute | solution.py:239
  94.4 7.9 %collective-permute-done.18 = bf16[96,1800]{1,0:T(8,128)(2,1)S(1)} collective-permute-done((bf16[96,1800]{1,0:T(8,128)(2,1)}, bf16[96,1800]{1,0:T(8,128)(2,1)S(1)}, u32[]{:S(2)}, u32[]{:S(2)}) %collective-permute-start.18) | collective-permute-done | bytes 345632 | tf_op jit(solution)/shard_map/ppermute | solution.py:239
  105.2 2.0 collective-permute-start.20
  109.0 1.8 collective-permute-done.20
  113.5 7.2 %attend.1 = (bf16[192,512]{1,0:T(8,128)(2,1)}, f32[8,512]{1,0:T(8,128)}) custom-call(bf16[512,192]{1,0:T(8,128)(2,1)} %slice.438.q_ref, bf16[1024,384]{1,0:T(8,128)(2,1)} %pad_maximum_fusion.6.kv_ref, s32[1,512]{1,0:T(1,128)} %broadcast_in_dim_reshape.3.qclip_ref, s32[1024,1]{1,0:T(8,128)} %copy.129.kclip_ref), custom_call_target="tpu_custom_call" | custom-call | tf_op jit(solution)/shard_map/attend/pallas_call | solution.py:143
  125.5 5.4 %collective-permute-done.24 = bf16[128,768]{1,0:T(8,128)(2,1)S(1)} collective-permute-done((bf16[128,768]{1,0:T(8,128)(2,1)S(1)}, bf16[128,768]{1,0:T(8,128)(2,1)S(1)}, u32[]{:S(2)}, u32[]{:S(2)}) %collective-permute-start.24) | collective-permute-done | bytes 196640 | tf_op jit(solution)/shard_map/ppermute | solution.py:239
  131.4 1.8 collective-permute-start.26
  133.2 4.5 %collective-permute-done.26 = bf16[128,768]{1,0:T(8,128)(2,1)S(1)} collective-permute-done((bf16[128,768]{1,0:T(8,128)(2,1)S(1)}, bf16[128,768]{1,0:T(8,128)(2,1)S(1)}, u32[]{:S(2)}, u32[]{:S(2)}) %collective-permute-start.26) | collective-permute-done | bytes 196640 | tf_op jit(solution)/shard_map/ppermute | solution.py:239
  139.1 7.2 %multiply_convert_fusion = (bf16[512,768]{1,0:T(8,128)(2,1)S(1)}, f32[512,768]{1,0:T(8,128)}, f32[512,768]{1,0:T(8,128)}) fusion(f32[768]{0:T(1024)S(1)} %add.691, bf16[768,1800]{1,0:T(8,128)(2,1)} %copy-done.3, bf16[128,768]{1,0:T(8,128)(2,1)S(1)} %collective-permute-done.27, bf16[128,768]{1,0:T(8,128)(2,1)S(1)} %collective-permute-done.26, ...), kind=kOutput, calls=%fused_computation.12 | convolution fusion | flops 633077760 | bytes 5901312 | tf_op jit(solution)/shard_map/dot_general | solution.py:84
  146.3 2.3 fusion.201
  150.3 1.8 collective-permute-start.30
  152.1 5.2 %collective-permute-done.30 = bf16[128,768]{1,0:T(8,128)(2,1)S(1)} collective-permute-done((bf16[128,768]{1,0:T(8,128)(2,1)S(1)}, bf16[128,768]{1,0:T(8,128)(2,1)S(1)}, u32[]{:S(2)}, u32[]{:S(2)}) %collective-permute-start.30) | collective-permute-done | bytes 196640 | tf_op jit(solution)/shard_map/ppermute | solution.py:239
  166.9 1.8 collective-permute-start.33
  170.9 2.6 collective-permute-start.31
  175.7 3.4 convert_reduce_fusion
  179.1 2.1 fusion.202
  184.4 5.7 %collective-permute-done.37 = bf16[128,768]{1,0:T(8,128)(2,1)S(1)} collective-permute-done((bf16[128,768]{1,0:T(8,128)(2,1)S(1)}, bf16[128,768]{1,0:T(8,128)(2,1)S(1)}, u32[]{:S(2)}, u32[]{:S(2)}) %collective-permute-start.37) | collective-permute-done | bytes 196640 | tf_op jit(solution)/shard_map/ppermute | solution.py:239
  193.1 5.3 %collective-permute-done.39 = bf16[128,768]{1,0:T(8,128)(2,1)S(1)} collective-permute-done((bf16[128,768]{1,0:T(8,128)(2,1)}, bf16[128,768]{1,0:T(8,128)(2,1)S(1)}, u32[]{:S(2)}, u32[]{:S(2)}) %collective-permute-start.39) | collective-permute-done | bytes 196640 | tf_op jit(solution)/shard_map/ppermute | solution.py:239
  198.4 2.6 pad_maximum_fusion
  201.1 6.4 %copy.148 = f32[768,1608]{1,0:T(8,128)} copy(f32[768,1608]{0,1:T(8,128)} %pad_maximum_fusion) | data formatting | bytes 9879552 | tf_op jit(solution)/shard_map/concatenate | solution.py:432
  209.7 9.7 %attend_back.1 = (bf16[192,512]{1,0:T(8,128)(2,1)}, f32[1024,384]{1,0:T(8,128)}) custom-call(bf16[512,192]{1,0:T(8,128)(2,1)} %slice.438.q_ref, bf16[1024,384]{1,0:T(8,128)(2,1)} %pad_maximum_fusion.6.kv_ref, bf16[512,192]{1,0:T(8,128)(2,1)} %copy.135.grad_ref, f32[8,512]{1,0:T(8,128)} %get-tuple-element.19.log_ref, ...), custom_call_target="tpu_custom_call" | custom-call | tf_op jit(solution)/shard_map/attend_back/pallas_call | solution.py:170
  219.3 1.9 slice.767
  227.3 2.9 fusion.8
  235.6 2.0 fusion.203
  239.9 2.0 copy.142
  241.9 19.3 %collective-permute-done.56 = bf16[4,96,1608]{2,1,0:T(8,128)(2,1)} collective-permute-done((bf16[4,96,1608]{2,1,0:T(8,128)(2,1)}, bf16[4,96,1608]{2,1,0:T(8,128)(2,1)}, u32[]{:S(2)}, u32[]{:S(2)}) %collective-permute-start.56) | collective-permute-done | bytes 1234976 | tf_op jit(solution)/shard_map/ppermute | solution.py:239
  261.2 2.5 fusion.179
  264.6 2.0 collective-permute-start.58
  271.4 4.9 %collective-permute-done.57 = bf16[96,1608]{1,0:T(8,128)(2,1)S(1)} collective-permute-done((bf16[96,1608]{1,0:T(8,128)(2,1)S(1)}, bf16[96,1608]{1,0:T(8,128)(2,1)S(1)}, u32[]{:S(2)}, u32[]{:S(2)}) %collective-permute-start.57) | collective-permute-done | bytes 308768 | tf_op jit(solution)/shard_map/ppermute | solution.py:239
  276.6 12.1 %collective-permute-done.58 = bf16[96,1608]{1,0:T(8,128)(2,1)S(1)} collective-permute-done((bf16[96,1608]{1,0:T(8,128)(2,1)S(1)}, bf16[96,1608]{1,0:T(8,128)(2,1)S(1)}, u32[]{:S(2)}, u32[]{:S(2)}) %collective-permute-start.58) | collective-permute-done | bytes 308768 | tf_op jit(solution)/shard_map/ppermute | solution.py:239
  289.2 1.9 fusion.42
  292.7 47.1 %psum.7 = f32[10208]{0:T(1024)S(1)} all-reduce(f32[10208]{0:T(1024)S(1)} %concatenate.73), channel_id=1, replica_groups=mesh['seq'=4,'frame'=8] {'seq','frame'}, use_global_device_ids=true, to_apply=%region_26.27 | all-reduce | flops 10208 | bytes 81664 | tf_op jit(solution)/shard_map/psum | solution.py:499
  345.1 2.3 collective-permute-start.52
  347.7 2.6 collective-permute-start.45
  351.6 4.5 %collective-permute-done.51 = bf16[96,768]{1,0:T(8,128)(2,1)S(1)} collective-permute-done((bf16[96,768]{1,0:T(8,128)(2,1)S(1)}, bf16[96,768]{1,0:T(8,128)(2,1)S(1)}, u32[]{:S(2)}, u32[]{:S(2)}) %collective-permute-start.51) | collective-permute-done | bytes 147488 | tf_op jit(solution)/shard_map/ppermute | solution.py:239
  356.2 4.0 %collective-permute-start.54 = (bf16[96,768]{1,0:T(8,128)(2,1)S(1)}, bf16[96,768]{1,0:T(8,128)(2,1)S(1)}, u32[]{:S(2)}, u32[]{:S(2)}) collective-permute-start(bf16[96,768]{1,0:T(8,128)(2,1)S(1)} %fusion.56), channel_id=1, source_target_pairs={{0,16},{1,17},{2,18},{3,19},{4,20},{5,21},{6,22},{7,23},{8,24},{9,... | collective-permute-start | bytes 442376 | tf_op jit(solution)/shard_map/ppermute | solution.py:239
  362.8 3.5 collective-permute-done.45
  371.1 2.2 copy.149
  373.3 3.6 reshape.400
  (405 shorter events, 101.2 us)
Async XLA Ops:
  2.9 13.8 %collective-permute-start.6 = (bf16[96,576]{0,1:T(8,128)(2,1)S(1)}, bf16[96,576]{0,1:T(8,128)(2,1)S(1)}, u32[]{:S(2)}, u32[]{:S(2)}) collective-permute-start(bf16[96,576]{0,1:T(8,128)(2,1)S(1)} %bitcast.294), channel_id=1, source_target_pairs={{0,6},{1,7},{2,0},{3,1},{4,2},{5,3},{6,4},{7,5},{8,14},{9,15},{10,... | collective-permute-start | bytes 331784 | tf_op jit(solution)/shard_map/ppermute | solution.py:239
  6.6 10.7 %collective-permute-start.4 = (bf16[96,576]{0,1:T(8,128)(2,1)S(1)}, bf16[96,576]{0,1:T(8,128)(2,1)S(1)}, u32[]{:S(2)}, u32[]{:S(2)}) collective-permute-start(bf16[96,576]{0,1:T(8,128)(2,1)S(1)} %bitcast.295), channel_id=1, source_target_pairs={{0,2},{1,3},{2,4},{3,5},{4,6},{5,7},{6,0},{7,1},{8,10},{9,11},{10,... | collective-permute-start | bytes 331784 | tf_op jit(solution)/shard_map/ppermute | solution.py:239
  6.6 28.3 %collective-permute-start.5 = (bf16[96,576]{0,1:T(8,128)(2,1)S(1)}, bf16[96,576]{0,1:T(8,128)(2,1)S(1)}, u32[]{:S(2)}, u32[]{:S(2)}) collective-permute-start(bf16[96,576]{0,1:T(8,128)(2,1)S(1)} %bitcast.296), channel_id=1, source_target_pairs={{0,4},{1,5},{2,6},{3,7},{4,0},{5,1},{6,2},{7,3},{8,12},{9,13},{10,... | collective-permute-start | bytes 331784 | tf_op jit(solution)/shard_map/ppermute | solution.py:239
  7.6 29.0 %collective-permute-start.7 = (bf16[96,576]{0,1:T(8,128)(2,1)S(1)}, bf16[96,576]{0,1:T(8,128)(2,1)S(1)}, u32[]{:S(2)}, u32[]{:S(2)}) collective-permute-start(bf16[96,576]{0,1:T(8,128)(2,1)S(1)} %bitcast.297), channel_id=1, source_target_pairs={{0,1},{1,0},{2,3},{3,2},{4,5},{5,4},{6,7},{7,6},{8,9},{9,8},{10,11... | collective-permute-start | bytes 331784 | tf_op jit(solution)/shard_map/ppermute | solution.py:239
  12.3 54.9 %collective-permute-start.12 = (bf16[96,1800]{1,0:T(8,128)(2,1)S(1)}, bf16[96,1800]{1,0:T(8,128)(2,1)S(1)}, u32[]{:S(2)}, u32[]{:S(2)}) collective-permute-start(bf16[96,1800]{1,0:T(8,128)(2,1)S(1)} %concatenate.61), channel_id=1, source_target_pairs={{0,2},{1,3},{2,4},{3,5},{4,6},{5,7},{6,0},{7,1},{8,10},{9,11},{10,... | collective-permute-start | bytes 1036808 | tf_op jit(solution)/shard_map/ppermute | solution.py:239
  16.7 20.0 %collective-permute-start.10 = (bf16[96,576]{0,1:T(8,128)(2,1)S(1)}, bf16[96,576]{0,1:T(8,128)(2,1)S(1)}, u32[]{:S(2)}, u32[]{:S(2)}) collective-permute-start(bf16[96,576]{0,1:T(8,128)(2,1)S(1)} %collective-permute-done.6), channel_id=1, source_target_pairs={{0,1},{1,0},{2,3},{3,2},{4,5},{5,4},{6,7},{7,6},{8,9},{9,8},{10,11... | collective-permute-start | bytes 331784 | tf_op jit(solution)/shard_map/ppermute | solution.py:239
  17.3 19.5 %collective-permute-start.8 = (bf16[96,576]{0,1:T(8,128)(2,1)S(1)}, bf16[96,576]{0,1:T(8,128)(2,1)S(1)}, u32[]{:S(2)}, u32[]{:S(2)}) collective-permute-start(bf16[96,576]{0,1:T(8,128)(2,1)S(1)} %collective-permute-done.4), channel_id=1, source_target_pairs={{0,1},{1,0},{2,3},{3,2},{4,5},{5,4},{6,7},{7,6},{8,9},{9,8},{10,11... | collective-permute-start | bytes 331784 | tf_op jit(solution)/shard_map/ppermute | solution.py:239
  34.9 6.8 %collective-permute-start.9 = (bf16[96,576]{0,1:T(8,128)(2,1)S(1)}, bf16[96,576]{0,1:T(8,128)(2,1)S(1)}, u32[]{:S(2)}, u32[]{:S(2)}) collective-permute-start(bf16[96,576]{0,1:T(8,128)(2,1)S(1)} %collective-permute-done.5), channel_id=1, source_target_pairs={{0,1},{1,0},{2,3},{3,2},{4,5},{5,4},{6,7},{7,6},{8,9},{9,8},{10,11... | collective-permute-start | bytes 331784 | tf_op jit(solution)/shard_map/ppermute | solution.py:239
  36.6 31.1 %collective-permute-start.13 = (bf16[96,1800]{1,0:T(8,128)(2,1)S(1)}, bf16[96,1800]{1,0:T(8,128)(2,1)S(1)}, u32[]{:S(2)}, u32[]{:S(2)}) collective-permute-start(bf16[96,1800]{1,0:T(8,128)(2,1)S(1)} %concatenate.61), channel_id=1, source_target_pairs={{0,4},{1,5},{2,6},{3,7},{4,0},{5,1},{6,2},{7,3},{8,12},{9,13},{10,... | collective-permute-start | bytes 1036808 | tf_op jit(solution)/shard_map/ppermute | solution.py:239
  36.7 32.6 %collective-permute-start.14 = (bf16[96,1800]{1,0:T(8,128)(2,1)S(1)}, bf16[96,1800]{1,0:T(8,128)(2,1)}, u32[]{:S(2)}, u32[]{:S(2)}) collective-permute-start(bf16[96,1800]{1,0:T(8,128)(2,1)S(1)} %concatenate.61), channel_id=1, source_target_pairs={{0,6},{1,7},{2,0},{3,1},{4,2},{5,3},{6,4},{7,5},{8,14},{9,15},{10,... | collective-permute-start | bytes 1036808 | tf_op jit(solution)/shard_map/ppermute | solution.py:239
  36.8 28.6 %collective-permute-start = (bf16[160,768]{1,0:T(8,128)(2,1)}, bf16[160,768]{1,0:T(8,128)(2,1)S(1)}, u32[]{:S(2)}, u32[]{:S(2)}) collective-permute-start(bf16[160,768]{1,0:T(8,128)(2,1)} %fusion.57), channel_id=1, source_target_pairs={{0,0},{1,1},{2,8},{3,9},{4,16},{5,17},{6,24},{7,25},{8,2},{9,3},{1... | collective-permute-start | bytes 737288 | tf_op jit(solution)/shard_map/ppermute | solution.py:239
  65.9 6.2 %collective-permute-start.1 = (bf16[128,768]{1,0:T(8,128)(2,1)S(1)}, bf16[128,768]{1,0:T(8,128)(2,1)S(1)}, u32[]{:S(2)}, u32[]{:S(2)}) collective-permute-start(bf16[128,768]{1,0:T(8,128)(2,1)S(1)} %fusion.36), channel_id=1, source_target_pairs={{0,8},{1,9},{2,10},{3,11},{4,12},{5,13},{6,14},{7,15},{8,0},{9,1},... | collective-permute-start | bytes 589832 | tf_op jit(solution)/shard_map/ppermute | solution.py:239
  67.2 11.4 %collective-permute-start.15 = (bf16[96,1800]{1,0:T(8,128)(2,1)S(1)}, bf16[96,1800]{1,0:T(8,128)(2,1)S(1)}, u32[]{:S(2)}, u32[]{:S(2)}) collective-permute-start(bf16[96,1800]{1,0:T(8,128)(2,1)S(1)} %concatenate.61), channel_id=1, source_target_pairs={{0,1},{1,0},{2,3},{3,2},{4,5},{5,4},{6,7},{7,6},{8,9},{9,8},{10,11... | collective-permute-start | bytes 1036808 | tf_op jit(solution)/shard_map/ppermute | solution.py:239
  67.7 18.8 %collective-permute-start.16 = (bf16[96,1800]{1,0:T(8,128)(2,1)S(1)}, bf16[96,1800]{1,0:T(8,128)(2,1)S(1)}, u32[]{:S(2)}, u32[]{:S(2)}) collective-permute-start(bf16[96,1800]{1,0:T(8,128)(2,1)S(1)} %collective-permute-done.12), channel_id=1, source_target_pairs={{0,1},{1,0},{2,3},{3,2},{4,5},{5,4},{6,7},{7,6},{8,9},{9,8},{10,11... | collective-permute-start | bytes 1036808 | tf_op jit(solution)/shard_map/ppermute | solution.py:239
  69.2 25.1 %collective-permute-start.17 = (bf16[96,1800]{1,0:T(8,128)(2,1)S(1)}, bf16[96,1800]{1,0:T(8,128)(2,1)S(1)}, u32[]{:S(2)}, u32[]{:S(2)}) collective-permute-start(bf16[96,1800]{1,0:T(8,128)(2,1)S(1)} %collective-permute-done.13), channel_id=1, source_target_pairs={{0,1},{1,0},{2,3},{3,2},{4,5},{5,4},{6,7},{7,6},{8,9},{9,8},{10,11... | collective-permute-start | bytes 1036808 | tf_op jit(solution)/shard_map/ppermute | solution.py:239
  71.6 30.7 %collective-permute-start.18 = (bf16[96,1800]{1,0:T(8,128)(2,1)}, bf16[96,1800]{1,0:T(8,128)(2,1)S(1)}, u32[]{:S(2)}, u32[]{:S(2)}) collective-permute-start(bf16[96,1800]{1,0:T(8,128)(2,1)} %collective-permute-done.14), channel_id=1, source_target_pairs={{0,1},{1,0},{2,3},{3,2},{4,5},{5,4},{6,7},{7,6},{8,9},{9,8},{10,11... | collective-permute-start | bytes 1036808 | tf_op jit(solution)/shard_map/ppermute | solution.py:239
  75.6 36.9 %collective-permute-start.11 = (bf16[512,384]{1,0:T(8,128)(2,1)S(1)}, bf16[512,384]{1,0:T(8,128)(2,1)S(1)}, u32[]{:S(2)}, u32[]{:S(2)}) collective-permute-start(bf16[512,384]{1,0:T(8,128)(2,1)S(1)} %slice.439), channel_id=1, source_target_pairs={{0,1},{1,0},{2,3},{3,2},{4,5},{5,4},{6,7},{7,6},{8,9},{9,8},{10,11... | collective-permute-start | bytes 1179656 | tf_op jit(solution)/shard_map/ppermute | solution.py:239
  123.8 7.0 %collective-permute-start.24 = (bf16[128,768]{1,0:T(8,128)(2,1)S(1)}, bf16[128,768]{1,0:T(8,128)(2,1)S(1)}, u32[]{:S(2)}, u32[]{:S(2)}) collective-permute-start(bf16[128,768]{1,0:T(8,128)(2,1)S(1)} %fusion.52), channel_id=1, source_target_pairs={{0,16},{1,17},{2,18},{3,19},{4,20},{5,21},{6,22},{7,23},{8,24},{9,... | collective-permute-start | bytes 589832 | tf_op jit(solution)/shard_map/ppermute | solution.py:239
  131.4 6.3 %collective-permute-start.26 = (bf16[128,768]{1,0:T(8,128)(2,1)S(1)}, bf16[128,768]{1,0:T(8,128)(2,1)S(1)}, u32[]{:S(2)}, u32[]{:S(2)}) collective-permute-start(bf16[128,768]{1,0:T(8,128)(2,1)S(1)} %add_convert_fusion.3), channel_id=1, source_target_pairs={{0,16},{1,17},{2,18},{3,19},{4,20},{5,21},{6,22},{7,23},{8,24},{9,... | collective-permute-start | bytes 589832 | tf_op jit(solution)/shard_map/ppermute | solution.py:239
  150.3 7.0 %collective-permute-start.30 = (bf16[128,768]{1,0:T(8,128)(2,1)S(1)}, bf16[128,768]{1,0:T(8,128)(2,1)S(1)}, u32[]{:S(2)}, u32[]{:S(2)}) collective-permute-start(bf16[128,768]{1,0:T(8,128)(2,1)S(1)} %fusion.48), channel_id=1, source_target_pairs={{0,16},{1,17},{2,18},{3,19},{4,20},{5,21},{6,22},{7,23},{8,24},{9,... | collective-permute-start | bytes 589832 | tf_op jit(solution)/shard_map/ppermute | solution.py:239
  166.9 6.6 %collective-permute-start.33 = (bf16[128,768]{1,0:T(8,128)(2,1)S(1)}, bf16[128,768]{1,0:T(8,128)(2,1)S(1)}, u32[]{:S(2)}, u32[]{:S(2)}) collective-permute-start(bf16[128,768]{1,0:T(8,128)(2,1)S(1)} %get-tuple-element.113), channel_id=1, source_target_pairs={{0,16},{1,17},{2,18},{3,19},{4,20},{5,21},{6,22},{7,23},{8,24},{9,... | collective-permute-start | bytes 589832 | tf_op jit(solution)/shard_map/ppermute | solution.py:239
  170.9 10.8 %collective-permute-start.31 = (bf16[2,8,768]{2,1,0:T(8,128)(2,1)S(1)}, bf16[2,8,768]{2,1,0:T(8,128)(2,1)S(1)}, u32[]{:S(2)}, u32[]{:S(2)}) collective-permute-start(bf16[2,8,768]{2,1,0:T(8,128)(2,1)S(1)} %fusion.12), channel_id=1, source_target_pairs={{0,0},{1,1},{2,8},{3,9},{4,16},{5,17},{6,24},{7,25},{8,2},{9,3},{1... | collective-permute-start | bytes 73736 | tf_op jit(solution)/shard_map/ppermute | solution.py:239
  182.8 7.2 %collective-permute-start.37 = (bf16[128,768]{1,0:T(8,128)(2,1)S(1)}, bf16[128,768]{1,0:T(8,128)(2,1)S(1)}, u32[]{:S(2)}, u32[]{:S(2)}) collective-permute-start(bf16[128,768]{1,0:T(8,128)(2,1)S(1)} %fusion.46), channel_id=1, source_target_pairs={{0,16},{1,17},{2,18},{3,19},{4,20},{5,21},{6,22},{7,23},{8,24},{9,... | collective-permute-start | bytes 589832 | tf_op jit(solution)/shard_map/ppermute | solution.py:239
  191.9 6.6 %collective-permute-start.39 = (bf16[128,768]{1,0:T(8,128)(2,1)}, bf16[128,768]{1,0:T(8,128)(2,1)S(1)}, u32[]{:S(2)}, u32[]{:S(2)}) collective-permute-start(bf16[128,768]{1,0:T(8,128)(2,1)} %get-tuple-element.120), channel_id=1, source_target_pairs={{0,16},{1,17},{2,18},{3,19},{4,20},{5,21},{6,22},{7,23},{8,24},{9,... | collective-permute-start | bytes 589832 | tf_op jit(solution)/shard_map/ppermute | solution.py:239
  193.1 14.4 %collective-permute-start.38 = (bf16[128,768]{1,0:T(8,128)(2,1)}, bf16[128,768]{1,0:T(8,128)(2,1)S(1)}, u32[]{:S(2)}, u32[]{:S(2)}) collective-permute-start(bf16[128,768]{1,0:T(8,128)(2,1)} %get-tuple-element.120), channel_id=1, source_target_pairs={{0,8},{1,9},{2,10},{3,11},{4,12},{5,13},{6,14},{7,15},{8,0},{9,1},... | collective-permute-start | bytes 589832 | tf_op jit(solution)/shard_map/ppermute | solution.py:239
  198.4 9.0 %collective-permute-start.40 = (bf16[128,768]{1,0:T(8,128)(2,1)S(1)}, bf16[128,768]{1,0:T(8,128)(2,1)S(1)}, u32[]{:S(2)}, u32[]{:S(2)}) collective-permute-start(bf16[128,768]{1,0:T(8,128)(2,1)S(1)} %collective-permute-done.39), channel_id=1, source_target_pairs={{0,8},{1,9},{2,10},{3,11},{4,12},{5,13},{6,14},{7,15},{8,0},{9,1},... | collective-permute-start | bytes 589832 | tf_op jit(solution)/shard_map/ppermute | solution.py:239
  221.3 12.4 %collective-permute-start.41 = (bf16[512,384]{1,0:T(8,128)(2,1)}, bf16[512,384]{1,0:T(8,128)(2,1)}, u32[]{:S(2)}, u32[]{:S(2)}) collective-permute-start(bf16[512,384]{1,0:T(8,128)(2,1)} %slice.767), channel_id=1, source_target_pairs={{0,1},{1,0},{2,3},{3,2},{4,5},{5,4},{6,7},{7,6},{8,9},{9,8},{10,11... | collective-permute-start | bytes 1179656 | tf_op jit(solution)/shard_map/ppermute | solution.py:239
  224.4 8.9 %collective-permute-start.46 = (bf16[192,192]{0,1:T(8,128)(2,1)S(1)}, bf16[192,192]{0,1:T(8,128)(2,1)S(1)}, u32[]{:S(2)}, u32[]{:S(2)}) collective-permute-start(bf16[192,192]{0,1:T(8,128)(2,1)S(1)} %bitcast.332), channel_id=1, source_target_pairs={{0,8},{1,9},{2,10},{3,11},{4,12},{5,13},{6,14},{7,15},{8,0},{9,1},... | collective-permute-start | bytes 221192 | tf_op jit(solution)/shard_map/ppermute | solution.py:239
  224.8 8.6 %collective-permute-start.47 = (bf16[192,192]{0,1:T(8,128)(2,1)S(1)}, bf16[192,192]{0,1:T(8,128)(2,1)S(1)}, u32[]{:S(2)}, u32[]{:S(2)}) collective-permute-start(bf16[192,192]{0,1:T(8,128)(2,1)S(1)} %bitcast.333), channel_id=1, source_target_pairs={{0,16},{1,17},{2,18},{3,19},{4,20},{5,21},{6,22},{7,23},{8,24},{9,... | collective-permute-start | bytes 221192 | tf_op jit(solution)/shard_map/ppermute | solution.py:239
  226.0 7.4 %collective-permute-start.48 = (bf16[192,192]{0,1:T(8,128)(2,1)}, bf16[192,192]{0,1:T(8,128)(2,1)S(1)}, u32[]{:S(2)}, u32[]{:S(2)}) collective-permute-start(bf16[192,192]{0,1:T(8,128)(2,1)} %bitcast.98), channel_id=1, source_target_pairs={{0,24},{1,25},{2,26},{3,27},{4,28},{5,29},{6,30},{7,31},{8,16},{9,... | collective-permute-start | bytes 221192 | tf_op jit(solution)/shard_map/ppermute | solution.py:239
  230.4 30.8 %collective-permute-start.56 = (bf16[4,96,1608]{2,1,0:T(8,128)(2,1)}, bf16[4,96,1608]{2,1,0:T(8,128)(2,1)}, u32[]{:S(2)}, u32[]{:S(2)}) collective-permute-start(bf16[4,96,1608]{2,1,0:T(8,128)(2,1)} %fusion.8), channel_id=1, source_target_pairs={{0,1},{1,0},{2,3},{3,2},{4,5},{5,4},{6,7},{7,6},{8,9},{9,8},{10,11... | collective-permute-start | bytes 3704840 | tf_op jit(solution)/shard_map/ppermute | solution.py:239
  238.3 30.5 %collective-permute-start.43 = (bf16[128,768]{1,0:T(8,128)(2,1)}, bf16[128,768]{1,0:T(8,128)(2,1)}, u32[]{:S(2)}, u32[]{:S(2)}) collective-permute-start(bf16[128,768]{1,0:T(8,128)(2,1)} %get-tuple-element.151), channel_id=1, source_target_pairs={{0,8},{1,9},{2,10},{3,11},{4,12},{5,13},{6,14},{7,15},{8,0},{9,1},... | collective-permute-start | bytes 589832 | tf_op jit(solution)/shard_map/ppermute | solution.py:239
  238.6 50.6 %collective-permute-start.42 = (bf16[128,768]{1,0:T(8,128)(2,1)S(1)}, bf16[128,768]{1,0:T(8,128)(2,1)}, u32[]{:S(2)}, u32[]{:S(2)}) collective-permute-start(bf16[128,768]{1,0:T(8,128)(2,1)S(1)} %get-tuple-element.150), channel_id=1, source_target_pairs={{0,8},{1,9},{2,10},{3,11},{4,12},{5,13},{6,14},{7,15},{8,0},{9,1},... | collective-permute-start | bytes 589832 | tf_op jit(solution)/shard_map/ppermute | solution.py:239
  263.9 12.4 %collective-permute-start.57 = (bf16[96,1608]{1,0:T(8,128)(2,1)S(1)}, bf16[96,1608]{1,0:T(8,128)(2,1)S(1)}, u32[]{:S(2)}, u32[]{:S(2)}) collective-permute-start(bf16[96,1608]{1,0:T(8,128)(2,1)S(1)} %get-tuple-element.139), channel_id=1, source_target_pairs={{0,2},{1,3},{2,4},{3,5},{4,6},{5,7},{6,0},{7,1},{8,10},{9,11},{10,... | collective-permute-start | bytes 926216 | tf_op jit(solution)/shard_map/ppermute | solution.py:239
  264.6 24.2 %collective-permute-start.58 = (bf16[96,1608]{1,0:T(8,128)(2,1)S(1)}, bf16[96,1608]{1,0:T(8,128)(2,1)S(1)}, u32[]{:S(2)}, u32[]{:S(2)}) collective-permute-start(bf16[96,1608]{1,0:T(8,128)(2,1)S(1)} %get-tuple-element.141), channel_id=1, source_target_pairs={{0,4},{1,5},{2,6},{3,7},{4,0},{5,1},{6,2},{7,3},{8,12},{9,13},{10,... | collective-permute-start | bytes 926216 | tf_op jit(solution)/shard_map/ppermute | solution.py:239
  266.6 22.2 %collective-permute-start.59 = (bf16[96,1608]{1,0:T(8,128)(2,1)S(1)}, bf16[96,1608]{1,0:T(8,128)(2,1)S(1)}, u32[]{:S(2)}, u32[]{:S(2)}) collective-permute-start(bf16[96,1608]{1,0:T(8,128)(2,1)S(1)} %get-tuple-element.140), channel_id=1, source_target_pairs={{0,6},{1,7},{2,0},{3,1},{4,2},{5,3},{6,4},{7,5},{8,14},{9,15},{10,... | collective-permute-start | bytes 926216 | tf_op jit(solution)/shard_map/ppermute | solution.py:239
  268.9 72.8 %collective-permute-start.49 = (bf16[4,96,768]{2,1,0:T(8,128)(2,1)}, bf16[4,96,768]{2,1,0:T(8,128)(2,1)}, u32[]{:S(2)}, u32[]{:S(2)}) collective-permute-start(bf16[4,96,768]{2,1,0:T(8,128)(2,1)} %fusion.25), channel_id=1, source_target_pairs={{0,1},{1,0},{2,3},{3,2},{4,5},{5,4},{6,7},{7,6},{8,9},{9,8},{10,11... | collective-permute-start | bytes 1769480 | tf_op jit(solution)/shard_map/ppermute | solution.py:239
  276.3 13.0 %collective-permute-start.44 = (bf16[128,768]{1,0:T(8,128)(2,1)S(1)}, bf16[128,768]{1,0:T(8,128)(2,1)S(1)}, u32[]{:S(2)}, u32[]{:S(2)}) collective-permute-start(bf16[128,768]{1,0:T(8,128)(2,1)S(1)} %fusion.44), channel_id=1, source_target_pairs={{0,16},{1,17},{2,18},{3,19},{4,20},{5,21},{6,22},{7,23},{8,24},{9,... | collective-permute-start | bytes 589832 | tf_op jit(solution)/shard_map/ppermute | solution.py:239
  289.0 58.7 %collective-permute-start.61 = (bf16[96,1608]{1,0:T(8,128)(2,1)S(1)}, bf16[96,1608]{1,0:T(8,128)(2,1)}, u32[]{:S(2)}, u32[]{:S(2)}) collective-permute-start(bf16[96,1608]{1,0:T(8,128)(2,1)S(1)} %fusion.24), channel_id=1, source_target_pairs={{0,16},{1,17},{2,18},{3,19},{4,20},{5,21},{6,22},{7,23},{8,24},{9,... | collective-permute-start | bytes 926216 | tf_op jit(solution)/shard_map/ppermute | solution.py:239
  289.2 78.4 %collective-permute-start.60 = (bf16[96,1608]{1,0:T(8,128)(2,1)S(1)}, bf16[96,1608]{1,0:T(8,128)(2,1)}, u32[]{:S(2)}, u32[]{:S(2)}) collective-permute-start(bf16[96,1608]{1,0:T(8,128)(2,1)S(1)} %fusion.24), channel_id=1, source_target_pairs={{0,8},{1,9},{2,10},{3,11},{4,12},{5,13},{6,14},{7,15},{8,0},{9,1},... | collective-permute-start | bytes 926216 | tf_op jit(solution)/shard_map/ppermute | solution.py:239
  343.0 8.7 %collective-permute-start.50 = (bf16[96,768]{1,0:T(8,128)(2,1)S(1)}, bf16[96,768]{1,0:T(8,128)(2,1)S(1)}, u32[]{:S(2)}, u32[]{:S(2)}) collective-permute-start(bf16[96,768]{1,0:T(8,128)(2,1)S(1)} %get-tuple-element.162), channel_id=1, source_target_pairs={{0,2},{1,3},{2,4},{3,5},{4,6},{5,7},{6,0},{7,1},{8,10},{9,11},{10,... | collective-permute-start | bytes 442376 | tf_op jit(solution)/shard_map/ppermute | solution.py:239
  343.7 12.4 %collective-permute-start.51 = (bf16[96,768]{1,0:T(8,128)(2,1)S(1)}, bf16[96,768]{1,0:T(8,128)(2,1)S(1)}, u32[]{:S(2)}, u32[]{:S(2)}) collective-permute-start(bf16[96,768]{1,0:T(8,128)(2,1)S(1)} %get-tuple-element.164), channel_id=1, source_target_pairs={{0,4},{1,5},{2,6},{3,7},{4,0},{5,1},{6,2},{7,3},{8,12},{9,13},{10,... | collective-permute-start | bytes 442376 | tf_op jit(solution)/shard_map/ppermute | solution.py:239
  345.1 11.0 %collective-permute-start.52 = (bf16[96,768]{1,0:T(8,128)(2,1)S(1)}, bf16[96,768]{1,0:T(8,128)(2,1)S(1)}, u32[]{:S(2)}, u32[]{:S(2)}) collective-permute-start(bf16[96,768]{1,0:T(8,128)(2,1)S(1)} %get-tuple-element.163), channel_id=1, source_target_pairs={{0,6},{1,7},{2,0},{3,1},{4,2},{5,3},{6,4},{7,5},{8,14},{9,15},{10,... | collective-permute-start | bytes 442376 | tf_op jit(solution)/shard_map/ppermute | solution.py:239
  347.7 18.6 %collective-permute-start.45 = (bf16[128,768]{1,0:T(8,128)(2,1)S(1)}, bf16[128,768]{1,0:T(8,128)(2,1)S(1)}, u32[]{:S(2)}, u32[]{:S(2)}) collective-permute-start(bf16[128,768]{1,0:T(8,128)(2,1)S(1)} %fusion.41), channel_id=1, source_target_pairs={{0,0},{1,1},{2,8},{3,9},{4,16},{5,17},{6,24},{7,25},{8,2},{9,3},{1... | collective-permute-start | bytes 589832 | tf_op jit(solution)/shard_map/ppermute | solution.py:239
  351.6 15.9 %collective-permute-start.62 = (bf16[96,1608]{1,0:T(8,128)(2,1)}, bf16[96,1608]{1,0:T(8,128)(2,1)S(1)}, u32[]{:S(2)}, u32[]{:S(2)}) collective-permute-start(bf16[96,1608]{1,0:T(8,128)(2,1)} %collective-permute-done.61), channel_id=1, source_target_pairs={{0,8},{1,9},{2,10},{3,11},{4,12},{5,13},{6,14},{7,15},{8,0},{9,1},... | collective-permute-start | bytes 926216 | tf_op jit(solution)/shard_map/ppermute | solution.py:239
  356.2 10.8 %collective-permute-start.54 = (bf16[96,768]{1,0:T(8,128)(2,1)S(1)}, bf16[96,768]{1,0:T(8,128)(2,1)S(1)}, u32[]{:S(2)}, u32[]{:S(2)}) collective-permute-start(bf16[96,768]{1,0:T(8,128)(2,1)S(1)} %fusion.56), channel_id=1, source_target_pairs={{0,16},{1,17},{2,18},{3,19},{4,20},{5,21},{6,22},{7,23},{8,24},{9,... | collective-permute-start | bytes 442376 | tf_op jit(solution)/shard_map/ppermute | solution.py:239
  367.1 11.0 %collective-permute-start.53 = (bf16[96,768]{1,0:T(8,128)(2,1)S(1)}, bf16[96,768]{1,0:T(8,128)(2,1)S(1)}, u32[]{:S(2)}, u32[]{:S(2)}) collective-permute-start(bf16[96,768]{1,0:T(8,128)(2,1)S(1)} %fusion.56), channel_id=1, source_target_pairs={{0,8},{1,9},{2,10},{3,11},{4,12},{5,13},{6,14},{7,15},{8,0},{9,1},... | collective-permute-start | bytes 442376 | tf_op jit(solution)/shard_map/ppermute | solution.py:239
  367.1 10.9 %collective-permute-start.55 = (bf16[96,768]{1,0:T(8,128)(2,1)S(1)}, bf16[96,768]{1,0:T(8,128)(2,1)}, u32[]{:S(2)}, u32[]{:S(2)}) collective-permute-start(bf16[96,768]{1,0:T(8,128)(2,1)S(1)} %collective-permute-done.54), channel_id=1, source_target_pairs={{0,8},{1,9},{2,10},{3,11},{4,12},{5,13},{6,14},{7,15},{8,0},{9,1},... | collective-permute-start | bytes 442376 | tf_op jit(solution)/shard_map/ppermute | solution.py:239
  (73 other events, 497.3 us)

commit v2 on v1

--- a/solution.py
+++ b/solution.py
@@ -191,7 +191,86 @@
     )(queries, keyvals, grads, logs, query_clip, key_clip)
 
 
-def shards(
+def place_kernel(size, place_ref, *refs):
+    pieces, out_ref = refs[:-1], refs[-1]
+    index = 0
+    for piece in pieces:
+        for start in range(0, piece.shape[0], size):
+            place = pl.multiple_of(place_ref[index] * size, size)
+            out_ref[pl.ds(place, size), :] = piece[start : start + size, :]
+            index += 1
+
+
+def place_rows(pieces, places, size):
+    columns = pieces[0].shape[1]
+    return pl.pallas_call(
+        functools.partial(place_kernel, size),
+        in_specs=[pl.BlockSpec(memory_space=pltpu.SMEM)]
+        + [pl.BlockSpec(memory_space=pltpu.VMEM)] * len(pieces),
+        out_specs=pl.BlockSpec(memory_space=pltpu.VMEM),
+        out_shape=jax.ShapeDtypeStruct((len(places) * size, columns), pieces[0].dtype),
+        name="place_rows",
+    )(jnp.stack(places), *pieces)
+
+
+def ordered(refs, rank, lanes):
+    blocks = [ref[:, lanes].astype(F32) for ref in refs]
+    result = []
+    for index in range(len(refs)):
+        found = blocks[0]
+        for bits in range(1, len(refs)):
+            found = jnp.where(rank == index ^ bits, blocks[bits], found)
+        result.append(found)
+    return result
+
+
+def finish_mlp_kernel(ranks, hidden_quarter, width, unit, rank_ref, *refs):
+    parts = refs[:ranks]
+    up_ref, down_ref, conv_ref = refs[ranks:]
+    rank = rank_ref[0]
+    ups = ordered(parts, rank, slice(0, hidden_quarter))
+    pieces = []
+    for group in range(hidden_quarter // unit):
+        for block in ups:
+            pieces.append(block[:, group * unit : (group + 1) * unit])
+    up_ref[...] = jnp.concatenate(pieces, axis=1)
+    size = parts[0].shape[0]
+    downs = ordered(parts, rank, slice(hidden_quarter, hidden_quarter + width))
+    for index in range(ranks):
+        down_ref[index * size : (index + 1) * size, :] = downs[index]
+    convs = ordered(parts, rank, slice(hidden_quarter + width, parts[0].shape[1]))
+    total = convs[0]
+    for block in convs[1:]:
+        total = total + block
+    conv_ref[...] = total
+
+
+def finish_qkv_kernel(ranks, quarter, rank_ref, *refs):
+    parts = refs[:ranks]
+    qkv_ref, out_ref = refs[ranks:]
+    rank = rank_ref[0]
+    blocks = ordered(parts, rank, slice(0, parts[0].shape[1]))
+    pieces = []
+    for part in range(3):
+        for block in blocks:
+            pieces.append(block[:, part * quarter : (part + 1) * quarter])
+    qkv_ref[...] = jnp.concatenate(pieces, axis=1)
+    out_ref[...] = jnp.concatenate([block[:, 3 * quarter :] for block in blocks], axis=1)
+
+
+def finish(kernel, rank, parts, shapes, name):
+    return pl.pallas_call(
+        kernel,
+        in_specs=[pl.BlockSpec(memory_space=pltpu.SMEM)]
+        + [pl.BlockSpec(memory_space=pltpu.VMEM)] * len(parts),
+        out_specs=[pl.BlockSpec(memory_space=pltpu.VMEM)] * len(shapes),
+        out_shape=[jax.ShapeDtypeStruct(shape, F32) for shape in shapes],
+        compiler_params=pltpu.CompilerParams(vmem_limit_bytes=VMEM_LIMIT),
+        name=name,
+    )(rank.reshape(1), *parts)
+
+
+def shards_general(
     ranks,
     frame_size,
     inputs,
@@ -255,6 +334,9 @@
             array, lambda seq, hi, lo: (PLANE_OF.index(hi), RANK_OF.index(seq), lo)
         )
 
+    def flip_high(array, bits):
+        return permute(array, lambda seq, hi, lo: (seq, hi ^ bits, lo))
+
     def gather_tokens(block):
         far = across(block, 2)
         near = across(block, 1)
@@ -269,39 +351,135 @@
         arrived = across(far.astype(BF), 2)
         return partial[:rows] + arrived_near.astype(F32) + arrived.astype(F32)
 
-    def gather_rows(block):
+    half_rows = rows // 2
+
+    def gather_plane(block):
         if lows != 2:
-            return lax.all_gather(block, "frame", axis=0, tiled=True)
-        found = [block] + [along_high(block, step) for step in range(1, ranks)]
-        other = [along_low(item, 1) for item in found]
-        stacked = jnp.stack(found)
-        stacked_other = jnp.stack(other)
-        pieces = []
-        for hi in range(ranks):
-            index = (high - hi) % ranks
-            mine = lax.dynamic_index_in_dim(stacked, index, 0, False)
-            theirs = lax.dynamic_index_in_dim(stacked_other, index, 0, False)
-            pieces.append(jnp.where(low == 0, mine, theirs))
-            pieces.append(jnp.where(low == 0, theirs, mine))
-        return jnp.concatenate(pieces, axis=0)
-
-    def scatter_rows(partial):
+            own = gather_tokens(block)
+            return jnp.concatenate(
+                [own] + [along_low(own, step) for step in range(1, lows)], axis=0
+            )
+        far = across(block, 2)
+        side = along_low(block, 1)
+        near = across(block, 1)
+        corner = jnp.concatenate(
+            [along_low(far[:half_rows], 1), across(side[half_rows:], 2)], axis=0
+        )
+        return jnp.concatenate(
+            [
+                block,
+                near,
+                far,
+                across(far, 1),
+                side,
+                across(side, 1),
+                corner,
+                across(corner, 1),
+            ],
+            axis=0,
+        )
+
+    def scatter_plane(partial):
         if lows != 2:
-            return lax.psum_scatter(
-                partial.astype(BF), "frame", scatter_dimension=0, tiled=True
-            ).astype(F32)
-        count = partial.shape[0] // frame_size
-        columns = partial.shape[1]
-        split = partial.reshape(ranks, lows, count, columns)
-        kept = lax.dynamic_index_in_dim(split, low, 1, False)
-        sent = lax.dynamic_index_in_dim(split, 1 - low, 1, False).astype(BF)
-        half = kept + along_low(sent, 1).astype(F32)
-        total = lax.dynamic_index_in_dim(half, high, 0, False)
-        half_low = half.astype(BF)
-        for step in range(1, ranks):
-            piece = lax.dynamic_index_in_dim(half_low, (high + step) % ranks, 0, False)
-            total = total + along_high(piece, step).astype(F32)
-        return total
+            count = ranks * rows
+            own = partial[:count]
+            for step in range(1, lows):
+                piece = partial[step * count : (step + 1) * count].astype(BF)
+                own = own + along_low(piece, -step).astype(F32)
+            return scatter_tokens(own)
+        blocks = [partial[index * rows : (index + 1) * rows] for index in range(2 * ranks)]
+        sums = {}
+        for index in (6, 4, 2, 0):
+            sums[index] = blocks[index] + across(blocks[index + 1].astype(BF), 1).astype(F32)
+        corner = sums[6].astype(BF)
+        by_far = across(corner[:half_rows], 2).astype(F32)
+        by_side = along_low(corner[half_rows:], 1).astype(F32)
+        side = jnp.concatenate([sums[4][:half_rows] + by_far, sums[4][half_rows:]], axis=0)
+        far = jnp.concatenate([sums[2][:half_rows], sums[2][half_rows:] + by_side], axis=0)
+        return (
+            sums[0]
+            + across(far.astype(BF), 2).astype(F32)
+            + along_low(side.astype(BF), 1).astype(F32)
+        )
+
+    places = [(high ^ bits) * lows + low for bits in (0, 2, 1, 3)] + [
+        (high ^ bits) * lows + (low + 1) % lows for bits in (0, 2, 1, 3)
+    ]
+
+    def after(array, *others):
+        return lax.optimization_barrier((array,) + others)[0]
+
+    staged = lows == 2
+
+    def gather_two(block):
+        return jnp.concatenate([block, flip_high(block, 2)], axis=0) if staged else block
+
+    def gather_four(two):
+        return jnp.concatenate([two, flip_high(two, 1)], axis=0) if staged else two
+
+    def gather_all(four):
+        if not staged:
+            return lax.all_gather(four, "frame", axis=0, tiled=True)
+        return place_rows([four, along_low(four, 1)], places, four.shape[0] // ranks)
+
+    def scatter_half(partials):
+        if not staged:
+            return jnp.concatenate([partial.astype(BF) for partial in partials], axis=1)
+        columns = [partial.shape[1] for partial in partials]
+        cuts = [sum(columns[:index]) for index in range(len(columns) + 1)]
+        count = partials[0].shape[0] // frame_size
+        splits = [
+            partial.reshape(ranks, lows, count, partial.shape[1]) for partial in partials
+        ]
+        sent = jnp.concatenate(
+            [lax.dynamic_index_in_dim(split.astype(BF), 1 - low, 1, False) for split in splits],
+            axis=2,
+        )
+        arrived = along_low(sent, 1)
+        return jnp.concatenate(
+            [
+                lax.dynamic_index_in_dim(split, low, 1, False)
+                + arrived[:, :, cuts[index] : cuts[index + 1]].astype(F32)
+                for index, split in enumerate(splits)
+            ],
+            axis=2,
+        ).reshape(2, 2, count, cuts[-1])
+
+    def scatter_rest(half):
+        if not staged:
+            return lax.psum_scatter(half, "frame", scatter_dimension=0, tiled=True)
+        sent = lax.dynamic_index_in_dim(half, 1 - high % 2, 1, False).astype(BF)
+        kept = lax.dynamic_index_in_dim(half, high % 2, 1, False)
+        two = kept + flip_high(sent, 1).astype(F32)
+        sent = lax.dynamic_index_in_dim(two, 1 - high // 2, 0, False).astype(BF)
+        kept = lax.dynamic_index_in_dim(two, high // 2, 0, False)
+        return (kept + flip_high(sent, 2).astype(F32)).astype(BF)
+
+    def swap_ranks(blocks):
+        split = blocks.reshape((2, 2) + blocks.shape[1:])
+        kept = lax.dynamic_index_in_dim(split, rank // 2, 0, False)
+        found = across(lax.dynamic_index_in_dim(split, 1 - rank // 2, 0, False), 2)
+        own = lax.dynamic_index_in_dim(kept, rank % 2, 0, False)
+        far = lax.dynamic_index_in_dim(found, rank % 2, 0, False)
+        near = across(lax.dynamic_index_in_dim(kept, 1 - rank % 2, 0, False), 1)
+        both = across(lax.dynamic_index_in_dim(found, 1 - rank % 2, 0, False), 1)
+        return in_rank_order([own, near, far, both])
+
+    def sum_everywhere(array):
+        bits = 1
+        while bits < ranks:
+            array = array + across(array, bits)
+            bits *= 2
+        bits = 1
+        while bits < frame_size:
+            pairs = [
+                (seq * frame_size + item, seq * frame_size + (item ^ bits))
+                for seq in range(ranks)
+                for item in range(frame_size)
+            ]
+            array = array + lax.ppermute(array, AXES, pairs)
+            bits *= 2
+        return array
 
     def in_rank_order(items):
         stacked = jnp.stack(items)
@@ -313,7 +491,7 @@
         far = across(block, 2)
         near = across(block, 1)
         both = across(far, 1)
-        return in_rank_order([block, near, far, both])
+        return [block, near, far, both]
 
     token_rows = inputs[0].reshape(rows, width)
     grad_rows = cotangent[0].reshape(frames_dev * CH, width)
@@ -326,10 +504,14 @@
     grad_learned = moved[rows : rows + frames_dev * CH].astype(F32)
     clips = moved[rows + frames_dev * CH, :frame_count].astype(jnp.int32)
 
-    own_qkv = lax.dynamic_index_in_dim(
-        w_qkv.reshape(row_shard, 3, ranks, quarter), rank, 2, False
-    ).reshape(row_shard, 3 * quarter)
-    qkv_quarter = gather_rows(own_qkv)
+    own_qkv = jnp.concatenate(
+        [
+            lax.dynamic_slice_in_dim(w_qkv, part * width + rank * quarter, quarter, 1)
+            for part in range(3)
+        ],
+        axis=1,
+    )
+    two_qkv = gather_two(own_qkv)
     unit = hidden // (frame_size * ranks)
     columns = jnp.arange(hidden_quarter, dtype=jnp.int32)
     wanted = (columns // unit) * (unit * ranks) + rank * unit + columns % unit
@@ -337,21 +519,21 @@
     own_up = dot(w_up, choose).astype(BF)
     own_down = lax.dynamic_slice_in_dim(w_down, rank * unit, unit, 0)
     own_out = lax.dynamic_slice_in_dim(w_out, rank * quarter, quarter, 1)
-    packed = gather_rows(jnp.concatenate([own_up, own_down, own_out, conv_first], axis=1))
-    up_quarter = packed[:, :hidden_quarter]
-    down_quarter = packed[:, hidden_quarter : hidden_quarter + width]
-    out_columns = packed[:, hidden_quarter + width : hidden_quarter + width + quarter]
-    full_conv = packed[:, hidden_quarter + width + quarter :]
-
-    def swap_ranks(array):
-        split = array.reshape(ranks, quarter, array.shape[1])
-        found = []
-        for bits in range(ranks):
-            piece = lax.dynamic_index_in_dim(split, rank ^ bits, 0, False)
-            found.append(across(piece, bits) if bits else piece)
-        return in_rank_order(found)
-
-    out_quarter = jnp.concatenate(swap_ranks(out_columns), axis=1)
+    own_out = jnp.concatenate([own_out, conv_first], axis=1)
+    two_out = gather_two(after(own_out, two_qkv))
+    four_qkv = gather_four(two_qkv)
+    two_up = gather_two(after(own_up, two_out))
+    four_out = gather_four(after(two_out, four_qkv))
+    qkv_quarter = gather_all(four_qkv)
+    two_down = gather_two(after(own_down, two_up))
+    four_up = gather_four(after(two_up, four_out))
+    qkv_quarter = after(qkv_quarter, four_out, two_up)
+    packed = gather_all(after(four_out, qkv_quarter))
+    out_columns = packed[:, :quarter]
+    full_conv = packed[:, quarter:]
+    out_quarter = jnp.concatenate(
+        swap_ranks(out_columns.reshape(ranks, quarter, quarter)), axis=1
+    )
     up_bias_quarter = lax.dynamic_index_in_dim(
         up_bias.reshape(frame_size, ranks, unit), rank, 1, False
     ).reshape(1, hidden_quarter)
@@ -379,15 +561,17 @@
     key_clip = key_clip[:, None]
 
     normed_one, inverse_one = norm_stats(tokens)
-    all_one = gather_tokens((normed_one * ln_gains[0] + ln_biases[0]).astype(BF))
-    projected = dot(all_one, qkv_quarter).astype(BF)
-    queries = projected[:, :quarter]
-    own_keyvals = projected[:, quarter:]
-    keyvals = jnp.concatenate(
-        [own_keyvals] + [along_low(own_keyvals, step) for step in range(1, lows)], axis=0
-    )
+    own_count = ranks * rows
+    all_one = gather_plane((normed_one * ln_gains[0] + ln_biases[0]).astype(BF))
+    queries = dot(all_one[:own_count], qkv_quarter[:, :quarter]).astype(BF)
+    keyvals = dot(all_one, qkv_quarter[:, quarter:]).astype(BF)
+    queries = after(queries, packed, four_up, two_down)
+    up_quarter = gather_all(after(four_up, packed))
+    four_down = gather_four(two_down)
     attended, logs = attend(queries, keyvals, query_clip, key_clip)
     after_attention = tokens + scatter_tokens(dot(attended, out_quarter, 0, 0))
+    after_attention = after(after_attention, four_down)
+    down_quarter = gather_all(after(four_down, up_quarter))
     normed_two, inverse_two = norm_stats(after_attention)
     all_two = gather_tokens((normed_two * ln_gains[1] + ln_biases[1]).astype(BF))
     pre_act = dot(all_two, up_quarter) + up_bias_quarter
@@ -429,7 +613,7 @@
     grad_normed_two = scatter_tokens(dot(grad_pre, up_quarter, 1, 1))
     grad_down = dot(act_low, all_mlp, 0, 0)
     grad_up = dot(all_two, grad_pre, 0, 0)
-    mlp_share = scatter_rows(jnp.concatenate([grad_up, grad_down, grad_conv], axis=1))
+    mlp_half = scatter_half([grad_up, grad_down, grad_conv])
     grad_after, grad_gain_two, grad_shift_two = norm_back(
         normed_two, inverse_two, ln_gains[1], grad_normed_two
     )
@@ -438,70 +622,103 @@
     all_branch = gather_tokens(grad_after.astype(BF))
     grad_attended = dot(all_branch, out_quarter, 1, 1).astype(BF)
     grad_out = dot(attended, all_branch)
+    grad_attended = after(grad_attended, mlp_half)
+    mlp_share = scatter_rest(mlp_half)
     grad_queries, grad_keyvals = attend_back(
         queries, keyvals, grad_attended, logs, query_clip, key_clip
     )
-    own_count = ranks * rows
-    own_grads = grad_keyvals[:own_count]
-    for step in range(1, lows):
-        piece = grad_keyvals[step * own_count : (step + 1) * own_count].astype(BF)
-        own_grads = own_grads + along_low(piece, -step).astype(F32)
-    grad_projected = jnp.concatenate([grad_queries.T, own_grads.astype(BF)], axis=1)
-    grad_qkv = dot(all_one, grad_projected, 0, 0)
-    grad_normed_one = scatter_tokens(dot(grad_projected, qkv_quarter, 1, 1))
+    grad_queries = grad_queries.T
+    grad_keyvals = grad_keyvals.astype(BF)
+    grad_normed_own = dot(grad_keyvals, qkv_quarter[:, quarter:], 1, 1)
+    grad_normed_own = jnp.concatenate(
+        [
+            grad_normed_own[:own_count] + dot(grad_queries, qkv_quarter[:, :quarter], 1, 1),
+            grad_normed_own[own_count:],
+        ],
+        axis=0,
+    )
+    grad_normed_one = scatter_plane(grad_normed_own)
+    grad_q = dot(all_one[:own_count], grad_queries, 0, 0)
+    grad_kv = dot(all_one, grad_keyvals, 0, 0)
     grad_out_columns = jnp.concatenate(
-        swap_ranks_rows(grad_out.astype(BF), ranks, quarter, rank, across), axis=0
-    )
-    qkv_share = scatter_rows(jnp.concatenate([grad_qkv, grad_out_columns.astype(F32)], axis=1))
+        swap_ranks(grad_out.astype(BF).reshape(quarter, ranks, quarter).transpose(1, 0, 2)),
+        axis=0,
+    )
+    qkv_share = scatter_rest(
+        after(scatter_half([grad_q, grad_kv, grad_out_columns]), mlp_share)
+    )
     grad_tokens, grad_gain_one, grad_shift_one = norm_back(
         normed_one, inverse_one, ln_gains[0], grad_normed_one
     )
-    grad_input = from_planes((grad_after + grad_tokens).astype(BF)).astype(F32)
-    learned = from_planes(learned.astype(BF)).astype(F32)
-
-    mlp_parts = gather_ranks(mlp_share.astype(BF))
-    qkv_parts = gather_ranks(qkv_share.astype(BF))
-    sum_up = (
-        jnp.stack([part[:, :hidden_quarter] for part in mlp_parts])
-        .reshape(ranks, row_shard, frame_size, unit)
-        .transpose(1, 2, 0, 3)
-        .reshape(row_shard, hidden)
-        .astype(F32)
-    )
-    sum_down = jnp.concatenate(
-        [part[:, hidden_quarter : hidden_quarter + width] for part in mlp_parts], axis=0
+    moved_back = from_planes(
+        jnp.concatenate(
+            [
+                (grad_after + grad_tokens).astype(BF),
+                learned.astype(BF).reshape(frames_dev * CH, width),
+            ],
+            axis=0,
+        )
     ).astype(F32)
-    sum_conv = sum(part[:, hidden_quarter + width :].astype(F32) for part in mlp_parts)
-    sum_qkv = (
-        jnp.stack([part[:, : 3 * quarter] for part in qkv_parts])
-        .reshape(ranks, row_shard, 3, quarter)
-        .transpose(1, 2, 0, 3)
-        .reshape(row_shard, 3 * width)
-        .astype(F32)
-    )
-    sum_out = jnp.concatenate([part[:, 3 * quarter :] for part in qkv_parts], axis=1).astype(F32)
-
-    up_bias_terms = lax.dynamic_update_index_in_dim(
-        jnp.zeros((frame_size, ranks, unit), F32),
-        grad_up_bias.reshape(frame_size, unit),
+    grad_input = moved_back[:rows]
+    learned = moved_back[rows:]
+
+    sum_up, sum_down, sum_conv = finish(
+        functools.partial(finish_mlp_kernel, ranks, hidden_quarter, width, unit),
         rank,
-        1,
-    )
-    small = [
-        jnp.stack([grad_gain_one, grad_gain_two, grad_gain_three]),
-        jnp.stack([grad_shift_one, grad_shift_two, grad_shift_three]),
-        up_bias_terms,
-        grad_down_bias,
-        grad_first_bias,
-        grad_mid,
-        grad_mid_bias,
-    ]
-    summed = lax.psum(jnp.concatenate([item.reshape(-1) for item in small]), AXES)
-    results = []
-    start = 0
-    for item in small:
-        results.append(summed[start : start + item.size].reshape(item.shape))
-        start += item.size
+        gather_ranks(mlp_share),
+        [(row_shard, hidden), (ranks * unit, width), (row_shard, 9 * CH)],
+        "finish_mlp",
+    )
+    sum_qkv, sum_out = finish(
+        functools.partial(finish_qkv_kernel, ranks, quarter),
+        rank,
+        gather_ranks(qkv_share),
+        [(row_shard, 3 * width), (row_shard, width)],
+        "finish_qkv",
+    )
+
+    conv_terms = jnp.concatenate(
+        [grad_first_bias.reshape(-1), grad_mid.reshape(-1), grad_mid_bias.reshape(-1)]
+    )
+    conv_rows = -(-conv_terms.shape[0] // width)
+    conv_terms = jnp.pad(conv_terms, (0, conv_rows * width - conv_terms.shape[0]))
+    up_terms = jnp.where(
+        jnp.arange(ranks, dtype=jnp.int32)[:, None] == rank,
+        grad_up_bias.reshape(1, hidden_quarter),
+        0.0,
+    )
+    early = sum_everywhere(
+        jnp.concatenate(
+            [
+                jnp.stack(
+                    [
+                        grad_gain_one,
+                        grad_gain_two,
+                        grad_gain_three,
+                        grad_shift_one,
+                        grad_shift_two,
+                        grad_shift_three,
+                        grad_down_bias,
+                    ]
+                ),
+                conv_terms.reshape(conv_rows, width),
+                up_terms.reshape(-1, width),
+            ],
+            axis=0,
+        )
+    )
+    sum_gains = early[0:3]
+    sum_shifts = early[3:6]
+    conv_sums = early[7 : 7 + conv_rows].reshape(-1)
+    sum_up_bias = (
+        early[7 + conv_rows :]
+        .reshape(ranks, frame_size, unit)
+        .transpose(1, 0, 2)
+        .reshape(hidden)
+    )
+    mid_count = grad_mid.size
+    sum_mid = conv_sums[CH : CH + mid_count].reshape(grad_mid.shape)
+    sum_mid_bias = conv_sums[CH + mid_count : CH + mid_count + grad_mid_bias.size]
     return (
         learned.reshape(1, frames_dev, CH, width),
         grad_input.reshape(1, frames_dev, patches, width),
@@ -510,24 +727,901 @@
         sum_up,
         sum_down,
         sum_conv,
-        results[0],
-        results[1],
-        results[2].reshape(hidden),
-        results[3],
-        results[4],
-        results[5],
-        results[6],
-    )
-
-
-def swap_ranks_rows(array, ranks, quarter, rank, across):
-    split = array.reshape(quarter, ranks, quarter).transpose(1, 0, 2)
-    found = []
-    for bits in range(ranks):
-        piece = lax.dynamic_index_in_dim(split, rank ^ bits, 0, False)
-        found.append(across(piece, bits) if bits else piece)
-    stacked = jnp.stack(found)
-    return [lax.dynamic_index_in_dim(stacked, rank ^ index, 0, False) for index in range(ranks)]
+        sum_gains,
+        sum_shifts,
+        sum_up_bias,
+        early[6],
+        conv_sums[:CH],
+        sum_mid,
+        sum_mid_bias.reshape(grad_mid_bias.shape),
+    )
+
+
+PAD = 128
+
+
+def run(kernel, name, scalars, arrays, outs, scratch=(), limit=24):
+    vmem = pl.BlockSpec(memory_space=pltpu.VMEM)
+    return pl.pallas_call(
+        kernel,
+        in_specs=[pl.BlockSpec(memory_space=pltpu.SMEM)] + [vmem] * len(arrays),
+        out_specs=[vmem] * len(outs),
+        out_shape=[jax.ShapeDtypeStruct(shape, kind) for shape, kind in outs],
+        scratch_shapes=list(scratch),
+        compiler_params=pltpu.CompilerParams(vmem_limit_bytes=limit * 1024 * 1024),
+        name=name,
+    )(scalars, *arrays)
+
+
+def rows_at(start, size):
+    return pl.ds(pl.multiple_of(start * size, size), size)
+
+
+def stack_rows(refs):
+    return jnp.concatenate([ref[...] for ref in refs], axis=0)
+
+
+def exact(left, right, left_dim=1, right_dim=0):
+    return lax.dot_general(
+        left,
+        right,
+        (((left_dim,), (right_dim,)), ((), ())),
+        precision=HIGHEST,
+        preferred_element_type=F32,
+    )
+
+
+def column_sum(values):
+    return jnp.sum(values, axis=0, keepdims=True)
+
+
+def back_of_norm(values, gain, grad):
+    normed, inverse = norm_stats(values)
+    scaled = grad * gain
+    mean_scaled = jnp.mean(scaled, axis=-1, keepdims=True)
+    mean_cross = jnp.mean(scaled * normed, axis=-1, keepdims=True)
+    result = inverse * (scaled - mean_scaled - normed * mean_cross)
+    return result, column_sum(grad * normed), column_sum(grad)
+
+
+def norm_one_kernel(unused_ref, moved_ref, gains_ref, shifts_ref, low_ref):
+    count = low_ref.shape[0]
+    normed, unused = norm_stats(moved_ref[:count, :].astype(F32))
+    low_ref[...] = (normed * gains_ref[0:1, :] + shifts_ref[0:1, :]).astype(BF)
+
+
+def place_out_kernel(quarter, place_ref, *refs):
+    blocks = refs[:8]
+    own_ref, near_ref, others_ref, all_ref = refs[8:]
+    size = blocks[0].shape[0]
+    for index in range(8):
+        all_ref[rows_at(place_ref[index], size), :] = blocks[index][:, 3 * quarter :]
+    rank = place_ref[8]
+    own_ref[...] = all_ref[rows_at(rank, quarter), :]
+    near_ref[...] = all_ref[rows_at(rank ^ 1, quarter), :]
+    others_ref[0] = all_ref[rows_at(rank ^ 2, quarter), :]
+    others_ref[1] = all_ref[rows_at(rank ^ 3, quarter), :]
+
+
+def project_kernel(quarter, place_ref, *refs):
+    tokens, blocks = refs[:8], refs[8:16]
+    q_ref, kv_ref, w_ref = refs[16:]
+    size = blocks[0].shape[0]
+    for index in range(8):
+        w_ref[rows_at(place_ref[index], size), :] = blocks[index][:, : 3 * quarter]
+    own = dot(stack_rows(tokens[:4]), w_ref[...]).astype(BF)
+    q_ref[...] = own[:, :quarter]
+    half = own.shape[0]
+    kv_ref[:half, :] = own[:, quarter:]
+    kv_ref[half:, :] = dot(stack_rows(tokens[4:]), w_ref[:, quarter:]).astype(BF)
+
+
+def scores_of(kv_ref, q_ref, queries, lanes, same, scale):
+    raw = dot(kv_ref[:, lanes], q_ref[queries, lanes], 1, 1) * scale
+    return jnp.where(same, raw, FLOOR_SCORE)
+
+
+def attend_wide_kernel(heads, scale, unused_ref, *refs):
+    q_ref, kv_ref, qclip_ref, kclip_ref, mixed_ref, log_ref = refs
+    width = heads * HEAD_DIM
+    count = q_ref.shape[0] // 2
+    for part in range(2):
+        queries = slice(part * count, (part + 1) * count)
+        same = kclip_ref[...] == qclip_ref[:, queries]
+        for head in range(heads):
+            lanes = slice(head * HEAD_DIM, (head + 1) * HEAD_DIM)
+            values = slice(width + head * HEAD_DIM, width + (head + 1) * HEAD_DIM)
+            scores = scores_of(kv_ref, q_ref, queries, lanes, same, scale)
+            top = jnp.max(scores, axis=0, keepdims=True)
+            shifted = jnp.exp(scores - top)
+            total = jnp.sum(shifted, axis=0, keepdims=True)
+            prob = (shifted * (1.0 / total)).astype(BF)
+            mixed_ref[lanes, queries] = dot(kv_ref[:, values], prob, 0, 0).astype(BF)
+            log_ref[head : head + 1, queries] = top + jnp.log(total)
+
+
+def split_blocks(values, even_ref, odd_ref):
+    rows = even_ref.shape[1]
+    for part in range(even_ref.shape[0]):
+        even_ref[part] = values[2 * part * rows : (2 * part + 1) * rows]
+        odd_ref[part] = values[(2 * part + 1) * rows : (2 * part + 2) * rows].astype(BF)
+
+
+def out_kernel(rank_ref, *refs):
+    mixed_ref, own_ref, near_ref, others_ref, both_ref = refs[:5]
+    even_ref, odd_ref, w_ref = refs[5:]
+    blocks = [own_ref[...], near_ref[...], others_ref[0], both_ref[...]]
+    rank = rank_ref[0]
+    width = own_ref.shape[0]
+    for index in range(4):
+        found = blocks[0]
+        for bits in range(1, 4):
+            found = jnp.where(rank == index ^ bits, blocks[bits], found)
+        w_ref[:, index * width : (index + 1) * width] = found
+    split_blocks(dot(mixed_ref[...], w_ref[...], 0, 0), even_ref, odd_ref)
+
+
+def norm_two_kernel(unused_ref, *refs):
+    moved_ref, even_ref, arrived_ref, far_ref, gains_ref, shifts_ref = refs[:6]
+    sum_ref, low_ref = refs[6:]
+    count = low_ref.shape[0]
+    values = (
+        moved_ref[:count, :].astype(F32)
+        + even_ref[0]
+        + arrived_ref[0].astype(F32)
+        + far_ref[...].astype(F32)
+    )
+    sum_ref[...] = values
+    normed, unused = norm_stats(values)
+    low_ref[...] = (normed * gains_ref[1:2, :] + shifts_ref[1:2, :]).astype(BF)
+
+
+def gelu_both(values):
+    size = jnp.abs(values) * 0.7071067811865476
+    ratio = 1.0 / (1.0 + 0.3275911 * size)
+    bell = jnp.exp(-size * size)
+    series = ratio * (
+        0.254829592
+        + ratio
+        * (-0.284496736 + ratio * (1.421413741 + ratio * (-1.453152027 + ratio * 1.061405429)))
+    )
+    tail = 0.5 * series * bell
+    below = jnp.where(values >= 0.0, 1.0 - tail, tail)
+    return values * below, below + values * bell * 0.3989422804014327
+
+
+def mlp_kernel(low_ref, *refs):
+    tokens = refs[:4]
+    own_ref, side_ref, bias_ref = refs[4:7]
+    act_ref, slope_ref, up_ref, down_ref, conv_ref, even_ref, odd_ref = refs[7:]
+    low = low_ref[0]
+    size = own_ref.shape[0] // 4
+    quarter = up_ref.shape[1]
+    width = down_ref.shape[1]
+    for hi in range(4):
+        rows = slice(hi * size, (hi + 1) * size)
+        for ref, place in ((own_ref, 2 * hi + low), (side_ref, 2 * hi + 1 - low)):
+            where = rows_at(place, size)
+            up_ref[where, :] = ref[rows, :quarter]
+            down_ref[where, :] = ref[rows, quarter : quarter + width]
+            conv_ref[where, :] = ref[rows, quarter + width :]
+    count = tokens[0].shape[0]
+    for part in range(2):
+        rows = slice(2 * part * count, 2 * (part + 1) * count)
+        pre = dot(stack_rows(tokens[2 * part : 2 * part + 2]), up_ref[...]) + bias_ref[...]
+        act, slope = gelu_both(pre)
+        act = act.astype(BF)
+        act_ref[rows, :] = act
+        slope_ref[rows, :] = slope
+        partial = dot(act, down_ref[...])
+        even_ref[part] = partial[:count]
+        odd_ref[part] = partial[count:].astype(BF)
+
+
+def grid_masks(count):
+    row = lax.broadcasted_iota(jnp.int32, (count, PAD), 0)
+    i = (row // GRID) % GRID
+    j = row % GRID
+    masks = []
+    for tap in range(9):
+        di, dj = tap // 3 - 1, tap % 3 - 1
+        inside = (i + di >= 0) & (i + di < GRID) & (j + dj >= 0) & (j + dj < GRID)
+        masks.append(inside.astype(F32))
+    return masks
+
+
+def collect_taps(taps, masks, first_lanes):
+    count = taps.shape[0]
+    total = None
+    for tap in range(9):
+        offset = (tap // 3 - 1) * GRID + tap % 3 - 1
+        moved = pltpu.roll(taps, (PAD - tap * CH) % PAD, 1) if tap else taps
+        moved = pltpu.roll(moved, (-offset) % count, 0) if offset else moved
+        moved = moved * masks[tap]
+        total = moved if total is None else total + moved
+    return total * first_lanes
+
+
+def spread_taps(values, masks):
+    count = values.shape[0]
+    total = None
+    for tap in range(9):
+        offset = (tap // 3 - 1) * GRID + tap % 3 - 1
+        moved = pltpu.roll(values, tap * CH, 1) if tap else values
+        moved = pltpu.roll(moved, offset % count, 0) if offset else moved
+        moved = moved * masks[8 - tap]
+        total = moved if total is None else total + moved
+    return total
+
+
+def store_rows(ref, start, values):
+    for index in range(values.shape[1] // PAD):
+        ref[start + index : start + index + 1, :] = values[:, index * PAD : (index + 1) * PAD]
+
+
+def load_rows(ref, start, count):
+    return jnp.concatenate(
+        [ref[start + index : start + index + 1, :] for index in range(count)], axis=1
+    )
+
+
+def tail_kernel(vectors, unused_ref, *refs):
+    sum_ref, even_ref, arrived_ref, far_ref, bias_ref, gains_ref, shifts_ref = refs[:7]
+    conv_ref, first_bias_ref, mid_ref, mid_bias_ref, moved_ref = refs[7:12]
+    learned_ref, low_ref, grad_ref, normed_ref, spread_ref, small_ref = refs[12:]
+    count = low_ref.shape[0]
+    frames = count // (GRID * GRID)
+    patches = GRID * GRID
+    value = (
+        sum_ref[...]
+        + even_ref[0]
+        + arrived_ref[0].astype(F32)
+        + far_ref[...].astype(F32)
+        + bias_ref[...]
+    )
+    normed, inverse = norm_stats(value)
+    gain = gains_ref[2:3, :]
+    normed_low = (normed * gain + shifts_ref[2:3, :]).astype(BF)
+    normed_ref[...] = normed_low
+    masks = grid_masks(count)
+    lane = lax.broadcasted_iota(jnp.int32, (count, PAD), 1)
+    first_lanes = (lane < CH).astype(F32)
+    first = collect_taps(dot(normed_low, conv_ref[...]), masks, first_lanes)
+    hidden, slope = gelu_both(first + first_bias_ref[...])
+    hidden = hidden * first_lanes
+    hiddens, slopes = [hidden], [slope]
+    maps = None
+    for layer in range(3):
+        pre = collect_taps(exact(hiddens[layer], mid_ref[layer]), masks, first_lanes)
+        pre = pre + mid_bias_ref[layer : layer + 1, :]
+        if layer < 2:
+            hidden, slope = gelu_both(pre)
+            hiddens.append(hidden * first_lanes)
+            slopes.append(slope)
+        else:
+            maps = jax.nn.sigmoid(pre) * first_lanes
+    pooled_parts, map_parts = [], []
+    zero_rows = jnp.zeros((PAD - CH, value.shape[1]), F32)
+    for frame in range(frames):
+        rows = slice(frame * patches, (frame + 1) * patches)
+        start = count + frame * CH
+        cotangent = jnp.concatenate(
+            [moved_ref[start : start + CH, :].astype(F32), zero_rows], axis=0
+        )
+        learned = exact(maps[rows], value[rows], 0, 0)[:CH] * (1.0 / patches)
+        learned_ref[frame * CH : (frame + 1) * CH, :] = learned
+        pooled_parts.append(exact(maps[rows], cotangent) * (1.0 / patches))
+        map_parts.append(exact(value[rows], cotangent, 1, 1) * (1.0 / patches))
+    grad = jnp.concatenate(map_parts, axis=0) * maps * (1.0 - maps)
+    small_ref[...] = jnp.zeros_like(small_ref)
+    conv_start = 7 * vectors + 4 * vectors
+    for layer in range(2, -1, -1):
+        taps = spread_taps(grad, masks)
+        weight = exact(hiddens[layer], taps, 0, 0)[:CH]
+        small_ref[conv_start + layer * CH : conv_start + (layer + 1) * CH, :] = weight
+        bias_row = conv_start + 3 * CH + 1 + layer
+        small_ref[bias_row : bias_row + 1, :] = column_sum(grad)
+        grad = exact(taps, mid_ref[layer], 1, 1) * slopes[layer]
+    grad_low = grad.astype(BF).astype(F32)
+    small_ref[conv_start + 3 * CH : conv_start + 3 * CH + 1, :] = column_sum(grad_low)
+    spread = spread_taps(grad_low, masks).astype(BF)
+    spread_ref[...] = spread
+    grad_normed = dot(spread, conv_ref[...], 1, 1)
+    scaled = grad_normed * gain
+    mean_scaled = jnp.mean(scaled, axis=-1, keepdims=True)
+    mean_cross = jnp.mean(scaled * normed, axis=-1, keepdims=True)
+    grad_value = inverse * (scaled - mean_scaled - normed * mean_cross)
+    grad_value = grad_value + jnp.concatenate(pooled_parts, axis=0)
+    grad_ref[...] = grad_value
+    low = grad_value.astype(BF)
+    low_ref[...] = low
+    store_rows(small_ref, 2 * vectors, column_sum(grad_normed * normed))
+    store_rows(small_ref, 5 * vectors, column_sum(grad_normed))
+    store_rows(small_ref, 6 * vectors, column_sum(low.astype(F32)))
+
+
+def mlp_back_kernel(unused_ref, *refs):
+    grads = refs[:4]
+    slope_ref, up_ref, down_ref = refs[4:7]
+    pre_ref, even_ref, odd_ref, bias_ref = refs[7:]
+    count = grads[0].shape[0]
+    total = None
+    for part in range(2):
+        rows = slice(2 * part * count, 2 * (part + 1) * count)
+        grad_act = dot(stack_rows(grads[2 * part : 2 * part + 2]), down_ref[...], 1, 1)
+        grad_pre = (grad_act * slope_ref[rows, :]).astype(BF)
+        pre_ref[rows, :] = grad_pre
+        term = column_sum(grad_pre.astype(F32))
+        total = term if total is None else total + term
+        partial = dot(grad_pre, up_ref[...], 1, 1)
+        even_ref[part] = partial[:count]
+        odd_ref[part] = partial[count:].astype(BF)
+    bias_ref[...] = total
+
+
+def mlp_grads_kernel(unused_ref, *refs):
+    tokens, grads = refs[:4], refs[4:8]
+    act_ref, pre_ref, normed_ref, spread_ref, pack_ref = refs[8:]
+    quarter = act_ref.shape[1]
+    width = tokens[0].shape[1]
+    pack_ref[:, :quarter] = dot(stack_rows(tokens), pre_ref[...], 0, 0).astype(BF)
+    pack_ref[:, quarter : quarter + width] = dot(
+        act_ref[...], stack_rows(grads), 0, 0
+    ).astype(BF)
+    pack_ref[:, quarter + width :] = dot(normed_ref[...], spread_ref[...], 0, 0).astype(BF)
+
+
+def norm_two_back_kernel(unused_ref, *refs):
+    sum_ref, grad_ref, even_ref, arrived_ref, far_ref, gains_ref = refs[:6]
+    total_ref, low_ref, rows_ref = refs[6:]
+    grad_normed = even_ref[0] + arrived_ref[0].astype(F32) + far_ref[...].astype(F32)
+    result, gain_row, shift_row = back_of_norm(sum_ref[...], gains_ref[1:2, :], grad_normed)
+    total = result + grad_ref[...]
+    total_ref[...] = total
+    low_ref[...] = total.astype(BF)
+    rows_ref[0:1, :] = gain_row
+    rows_ref[1:2, :] = shift_row
+
+
+def attend_back_out_kernel(heads, scale, unused_ref, *refs):
+    branches = refs[:4]
+    out_ref, q_ref, kv_ref, log_ref, qclip_ref, kclip_ref, w_ref = refs[4:11]
+    own_ref, other_ref, even_ref, odd_ref, total_ref = refs[11:]
+    width = heads * HEAD_DIM
+    count = q_ref.shape[0] // 2
+    rows = count // 2
+    for part in range(2):
+        queries = slice(part * count, (part + 1) * count)
+        grad_mixed = dot(
+            stack_rows(branches[2 * part : 2 * part + 2]), out_ref[...], 1, 1
+        ).astype(BF)
+        same = kclip_ref[...] == qclip_ref[:, queries]
+        query_parts, key_parts, value_parts = [], [], []
+        for head in range(heads):
+            lanes = slice(head * HEAD_DIM, (head + 1) * HEAD_DIM)
+            values = slice(width + head * HEAD_DIM, width + (head + 1) * HEAD_DIM)
+            scores = scores_of(kv_ref, q_ref, queries, lanes, same, scale)
+            prob = jnp.exp(scores - log_ref[head : head + 1, queries])
+            grad_prob = dot(kv_ref[:, values], grad_mixed[:, lanes], 1, 1)
+            delta = jnp.sum(prob * grad_prob, axis=0, keepdims=True)
+            grad_score = (prob * (grad_prob - delta)).astype(BF)
+            query_parts.append(dot(kv_ref[:, lanes], grad_score, 0, 0) * scale)
+            key_parts.append(dot(grad_score, q_ref[queries, lanes]) * scale)
+            value_parts.append(dot(prob.astype(BF), grad_mixed[:, lanes]))
+        own_ref[queries, :width] = jnp.concatenate(query_parts, axis=0).T.astype(BF)
+        terms = jnp.concatenate(key_parts + value_parts, axis=1)
+        if part == 0:
+            total_ref[...] = terms
+        else:
+            total_ref[...] += terms
+    own_ref[:, width:] = total_ref[: 2 * count, :].astype(BF)
+    other_ref[...] = total_ref[2 * count :, :].astype(BF)
+    own = dot(own_ref[...], w_ref[...], 1, 1)
+    other = dot(other_ref[...], w_ref[:, width:], 1, 1)
+    for part in range(2):
+        even_ref[part] = own[2 * part * rows : (2 * part + 1) * rows]
+        odd_ref[part] = own[(2 * part + 1) * rows : (2 * part + 2) * rows].astype(BF)
+        even_ref[part + 2] = other[2 * part * rows : (2 * part + 1) * rows]
+        odd_ref[part + 2] = other[(2 * part + 1) * rows : (2 * part + 2) * rows].astype(BF)
+
+
+def qkv_grads_kernel(place_ref, *refs):
+    tokens, branches, mixes = refs[:8], refs[8:12], refs[12:16]
+    own_ref, other_ref, kept_ref, sent_ref, all_ref = refs[16:]
+    quarter = mixes[0].shape[0]
+    size = all_ref.shape[0] // 8
+    full = dot(stack_rows(tokens[:4]), own_ref[...], 0, 0)
+    more = dot(stack_rows(tokens[4:]), other_ref[...], 0, 0)
+    all_ref[:, :quarter] = full[:, :quarter]
+    all_ref[:, quarter : 3 * quarter] = full[:, quarter:] + more
+    rank = place_ref[0]
+    low = place_ref[1]
+    branch = stack_rows(branches)
+    wanted = branch[:, :quarter]
+    for index in range(1, 4):
+        wanted = jnp.where(
+            rank == index, branch[:, index * quarter : (index + 1) * quarter], wanted
+        )
+    count = branches[0].shape[0]
+    for bits in range(4):
+        turned = jnp.concatenate(
+            [wanted[(item ^ bits) * count : ((item ^ bits) + 1) * count] for item in range(4)],
+            axis=0,
+        )
+        all_ref[rows_at(rank ^ bits, quarter), 3 * quarter :] = dot(mixes[bits][...], turned)
+    for hi in range(4):
+        rows = slice(hi * size, (hi + 1) * size)
+        kept_ref[rows, :] = all_ref[rows_at(2 * hi + low, size), :]
+        sent_ref[rows, :] = all_ref[rows_at(2 * hi + 1 - low, size), :].astype(BF)
+
+
+def half_kernel(high_ref, kept_ref, arrived_ref, own_ref, *refs):
+    size = own_ref.shape[0]
+    for step in range(4):
+        where = rows_at(lax.rem(high_ref[0] + step, 4), size)
+        total = kept_ref[where, :] + arrived_ref[where, :].astype(F32)
+        if step == 0:
+            own_ref[...] = total
+        else:
+            refs[step - 1][...] = total.astype(BF)
+
+
+def total_kernel(unused_ref, kept_ref, *refs):
+    total = kept_ref[...]
+    for ref in refs[:-1]:
+        total = total + ref[...].astype(F32)
+    refs[-1][...] = total.astype(BF)
+
+
+def norm_one_back_kernel(vectors, rank_ref, *refs):
+    moved_ref, grad_ref, even_ref, arrived_ref, far_ref, side_ref, gains_ref = refs[:7]
+    learned_ref, small_ref, two_ref, up_ref, back_ref, sums_ref = refs[7:]
+    count = grad_ref.shape[0]
+    grad_normed = (
+        even_ref[0]
+        + arrived_ref[0].astype(F32)
+        + far_ref[...].astype(F32)
+        + side_ref[...].astype(F32)
+    )
+    result, gain_row, shift_row = back_of_norm(
+        moved_ref[:count, :].astype(F32), gains_ref[0:1, :], grad_normed
+    )
+    back_ref[:count, :] = (result + grad_ref[...]).astype(BF)
+    back_ref[count:, :] = learned_ref[...].astype(BF)
+    sums_ref[...] = small_ref[...]
+    store_rows(sums_ref, 0, gain_row)
+    store_rows(sums_ref, vectors, two_ref[0:1, :])
+    store_rows(sums_ref, 3 * vectors, shift_row)
+    store_rows(sums_ref, 4 * vectors, two_ref[1:2, :])
+    for index in range(4):
+        store_rows(
+            sums_ref,
+            (7 + index) * vectors,
+            jnp.where(rank_ref[0] == index, up_ref[...], 0.0),
+        )
+
+
+def unpack_kernel(vectors, unused_ref, sums_ref, *refs):
+    gains_ref, shifts_ref, up_ref, down_ref, first_ref, mid_ref, mid_bias_ref = refs
+    for index in range(3):
+        gains_ref[index : index + 1, :] = load_rows(sums_ref, index * vectors, vectors)
+        shifts_ref[index : index + 1, :] = load_rows(sums_ref, (3 + index) * vectors, vectors)
+    down_ref[...] = load_rows(sums_ref, 6 * vectors, vectors)
+    quarters = [load_rows(sums_ref, (7 + index) * vectors, vectors) for index in range(4)]
+    unit = quarters[0].shape[1] // 8
+    up_ref[...] = jnp.concatenate(
+        [
+            quarters[index][:, group * unit : (group + 1) * unit]
+            for group in range(8)
+            for index in range(4)
+        ],
+        axis=1,
+    )
+    start = 11 * vectors
+    for layer in range(3):
+        mid_ref[layer] = sums_ref[start + layer * CH : start + (layer + 1) * CH, : 9 * CH]
+    start = start + 3 * CH
+    first_ref[...] = sums_ref[start : start + 1, :CH]
+    mid_bias_ref[...] = sums_ref[start + 1 : start + 4, :CH]
+
+
+def shards_square(
+    ranks,
+    frame_size,
+    inputs,
+    clip_id,
+    ln_gains,
+    ln_biases,
+    w_qkv,
+    w_out,
+    w_up,
+    w_down,
+    up_bias,
+    down_bias,
+    conv_first,
+    conv_first_bias,
+    conv_mid,
+    conv_mid_bias,
+    cotangent,
+):
+    lows = 2
+    frames_dev = inputs.shape[1]
+    patches = inputs.shape[2]
+    width = inputs.shape[3]
+    rows = frames_dev * patches
+    learned_rows = frames_dev * CH
+    hidden = up_bias.shape[0]
+    quarter = width // ranks
+    heads = quarter // HEAD_DIM
+    hidden_quarter = hidden // ranks
+    unit = hidden_quarter // frame_size
+    size = width // frame_size
+    vectors = width // PAD
+    own_count = ranks * rows
+    rank = lax.axis_index("seq")
+    place = lax.axis_index("frame")
+    high = place // lows
+    low = place % lows
+    core = rank % 2
+    rank_one = rank.reshape(1)
+    low_one = low.reshape(1)
+
+    def permute(array, target):
+        pairs = []
+        for seq in range(ranks):
+            for hi in range(ranks):
+                for lo in range(lows):
+                    to_seq, to_hi, to_lo = target(seq, hi, lo)
+                    pairs.append(
+                        (
+                            seq * frame_size + hi * lows + lo,
+                            to_seq * frame_size + to_hi * lows + to_lo,
+                        )
+                    )
+        return lax.ppermute(array, AXES, pairs)
+
+    def flip(array, seq_bits, hi_bits=0, lo_bits=0):
+        return permute(
+            array, lambda seq, hi, lo: (seq ^ seq_bits, hi ^ hi_bits, lo ^ lo_bits)
+        )
+
+    def after(array, *others):
+        return lax.optimization_barrier((array,) + others)[0]
+
+    def to_planes(array):
+        return permute(array, lambda seq, hi, lo: (RANK_OF[hi], PLANE_OF[seq], lo))
+
+    def from_planes(array):
+        return permute(
+            array, lambda seq, hi, lo: (PLANE_OF.index(hi), RANK_OF.index(seq), lo)
+        )
+
+    def gather_four(block):
+        far = flip(block, 2)
+        near = flip(block, 1)
+        return [block, near, far, flip(far, 1)]
+
+    def gather_eight(block):
+        far = flip(block, 2)
+        side = flip(block, 0, 0, 1)
+        near = flip(block, 1)
+        corner = permute(
+            jnp.where(core == 0, far, side),
+            lambda seq, hi, lo: (seq, hi, lo ^ 1) if seq % 2 == 0 else (seq ^ 2, hi, lo),
+        )
+        return [
+            block,
+            near,
+            far,
+            flip(far, 1),
+            side,
+            flip(side, 1),
+            corner,
+            flip(corner, 1),
+        ]
+
+    def scatter_four(even, odd):
+        arrived = flip(odd, 1)
+        far = flip((even[1] + arrived[1].astype(F32)).astype(BF), 2)
+        return arrived, far
+
+    def scatter_eight(even, odd):
+        arrived = flip(odd, 1)
+        corner = permute(
+            (even[3] + arrived[3].astype(F32)).astype(BF),
+            lambda seq, hi, lo: (seq ^ 2, hi, lo) if seq % 2 == 0 else (seq, hi, lo ^ 1),
+        ).astype(F32)
+        far = even[1] + arrived[1].astype(F32) + jnp.where(core == 1, corner, 0.0)
+        side = even[2] + arrived[2].astype(F32) + jnp.where(core == 0, corner, 0.0)
+        return arrived, flip(far.astype(BF), 2), flip(side.astype(BF), 0, 0, 1)
+
+    moved = to_planes(
+        jnp.concatenate(
+            [
+                inputs[0].reshape(rows, width),
+                cotangent[0].reshape(learned_rows, width),
+                jnp.pad(clip_id.astype(BF), ((0, 15), (0, width - clip_id.shape[1]))),
+            ],
+            axis=0,
+        )
+    )
+    frame_count = clip_id.shape[1]
+    clips = moved[rows + learned_rows, :frame_count].astype(jnp.int32)
+
+    own_pack = jnp.concatenate(
+        [
+            lax.dynamic_slice_in_dim(w_qkv, part * width + rank * quarter, quarter, 1)
+            for part in range(3)
+        ]
+        + [lax.dynamic_slice_in_dim(w_out, rank * quarter, quarter, 1)],
+        axis=1,
+    )
+    packs = [own_pack] + [flip(own_pack, 0, bits // 2, bits % 2) for bits in range(1, 8)]
+    places = [place ^ bits for bits in range(8)]
+
+    columns = jnp.arange(hidden_quarter, dtype=jnp.int32)
+    wanted = (columns // unit) * (unit * ranks) + rank * unit + columns % unit
+    choose = (jnp.arange(hidden, dtype=jnp.int32)[:, None] == wanted[None, :]).astype(BF)
+    own_mlp = jnp.concatenate(
+        [
+            dot(w_up, choose).astype(BF),
+            lax.dynamic_slice_in_dim(w_down, rank * unit, unit, 0),
+            conv_first,
+            jnp.zeros((size, PAD - 9 * CH), BF),
+        ],
+        axis=1,
+    )
+    mlp_own = lax.all_gather(
+        own_mlp,
+        "frame",
+        axis=0,
+        tiled=True,
+        axis_index_groups=[[hi * lows + lo for hi in range(ranks)] for lo in range(lows)],
+    )
+    mlp_side = flip(mlp_own, 0, 0, 1)
+    up_bias_own = lax.dynamic_index_in_dim(
+        up_bias.reshape(frame_size, ranks, unit), rank, 1, False
+    ).reshape(1, hidden_quarter)
+
+    mid_pad = jnp.pad(conv_mid, ((0, 0), (0, PAD - CH), (0, PAD - 9 * CH)))
+    mid_bias_pad = jnp.pad(conv_mid_bias, ((0, 0), (0, PAD - CH)))
+    first_bias_pad = jnp.pad(conv_first_bias, (0, PAD - CH)).reshape(1, PAD)
+
+    frame_ids = jnp.arange(frame_count, dtype=jnp.int32)
+    inverse = jnp.array([RANK_OF.index(item) for item in range(ranks)], jnp.int32)
+
+    def clip_tokens(lo):
+        blocks = []
+        for bits in range(ranks):
+            hi = lax.dynamic_index_in_dim(inverse, rank ^ bits, 0, False)
+            for frame in range(frames_dev):
+                blocks.append((hi * lows + lo) * frames_dev + frame)
+        found = jnp.sum(
+            jnp.where(jnp.stack(blocks)[:, None] == frame_ids[None, :], clips[None, :], 0),
+            axis=1,
+        )
+        return jnp.broadcast_to(found[:, None], (found.shape[0], patches)).reshape(-1)
+
+    query_clip = clip_tokens(low)
+    key_clip = jnp.concatenate([query_clip, clip_tokens(1 - low)])[:, None]
+    query_clip = query_clip[None, :]
+
+    (low_one_norm,) = run(
+        norm_one_kernel, "norm_one", low_one, [moved, ln_gains, ln_biases], [((rows, width), BF)]
+    )
+    all_one = gather_eight(after(low_one_norm, own_mlp))
+    own_out, near_out, other_out = run(
+        functools.partial(place_out_kernel, quarter),
+        "place_out",
+        jnp.stack(places + [rank]),
+        packs,
+        [((quarter, quarter), BF)] * 2 + [((2, quarter, quarter), BF)],
+        [pltpu.VMEM((width, quarter), BF)],
+    )
+    other_out = flip(other_out, 2)
+    near_out = flip(near_out, 1)
+    both_out = flip(other_out[1], 1)
+    queries, keyvals, qkv_quarter = run(
+        functools.partial(project_kernel, quarter),
+        "project",
+        jnp.stack(places),
+        all_one + packs,
+        [
+            ((own_count, quarter), BF),
+            ((2 * own_count, 2 * quarter), BF),
+            ((width, 3 * quarter), BF),
+        ],
+    )
+    scale = HEAD_DIM ** (-0.5)
+    attended, logs = run(
+        functools.partial(attend_wide_kernel, heads, scale),
+        "attend",
+        rank_one,
+        [queries, keyvals, query_clip, key_clip],
+        [((quarter, own_count), BF), ((8, own_count), F32)],
+    )
+    halves = [((2, rows, width), F32), ((2, rows, width), BF)]
+    even, odd, out_quarter = run(
+        out_kernel,
+        "out",
+        rank_one,
+        [attended, own_out, near_out, other_out, both_out],
+        halves + [((quarter, width), BF)],
+    )
+    arrived, far = scatter_four(even, odd)
+    after_attention, low_two = run(
+        norm_two_kernel,
+        "norm_two",
+        low_one,
+        [moved, even, arrived, far, ln_gains, ln_biases],
+        [((rows, width), F32), ((rows, width), BF)],
+    )
+    all_two = gather_four(low_two)
+    act, slope, up_full, down_full, conv_full, even, odd = run(
+        mlp_kernel,
+        "mlp",
+        low_one,
+        all_two + [mlp_own, mlp_side, up_bias_own],
+        [
+            ((own_count, hidden_quarter), BF),
+            ((own_count, hidden_quarter), F32),
+            ((width, hidden_quarter), BF),
+            ((hidden_quarter, width), BF),
+            ((width, PAD), BF),
+        ]
+        + halves,
+    )
+    arrived, far = scatter_four(even, odd)
+
+    small_rows = -(-(11 * vectors + 3 * CH + 4) // 8) * 8
+    learned, low_mlp, grad_block, low_three, spread, small = run(
+        functools.partial(tail_kernel, vectors),
+        "tail",
+        low_one,
+        [
+            after_attention,
+            even,
+            arrived,
+            far,
+            down_bias.reshape(1, width),
+            ln_gains,
+            ln_biases,
+            conv_full,
+            first_bias_pad,
+            mid_pad,
+            mid_bias_pad,
+            moved,
+        ],
+        [
+            ((learned_rows, width), F32),
+            ((rows, width), BF),
+            ((rows, width), F32),
+            ((rows, width), BF),
+            ((rows, PAD), BF),
+            ((small_rows, PAD), F32),
+        ],
+    )
+    mixes = gather_four(after(attended, far))
+
+    all_mlp = gather_four(low_mlp)
+    grad_pre, even, odd, grad_up_bias = run(
+        mlp_back_kernel,
+        "mlp_back",
+        low_one,
+        all_mlp + [slope, up_full, down_full],
+        [((own_count, hidden_quarter), BF)] + halves + [((1, hidden_quarter), F32)],
+    )
+    (mlp_grads,) = run(
+        mlp_grads_kernel,
+        "mlp_grads",
+        low_one,
+        all_two + all_mlp + [act, grad_pre, low_three, spread],
+        [((width, hidden_quarter + width + PAD), BF)],
+    )
+    mlp_share = lax.psum_scatter(mlp_grads, "frame", scatter_dimension=0, tiled=True)
+    arrived, far = scatter_four(even, odd)
+    grad_after, low_branch, rows_two = run(
+        norm_two_back_kernel,
+        "norm_two_back",
+        low_one,
+        [after_attention, grad_block, even, arrived, far, ln_gains],
+        [((rows, width), F32), ((rows, width), BF), ((2, width), F32)],
+    )
+
+    all_branch = gather_four(low_branch)
+    grads_own, grads_other, even, odd = run(
+        functools.partial(attend_back_out_kernel, heads, scale),
+        "attend_back_out",
+        low_one,
+        all_branch + [out_quarter, queries, keyvals, logs, query_clip, key_clip, qkv_quarter],
+        [
+            ((own_count, 3 * quarter), BF),
+            ((own_count, 2 * quarter), BF),
+            ((4, rows, width), F32),
+            ((4, rows, width), BF),
+        ],
+        [pltpu.VMEM((2 * own_count, 2 * quarter), F32)],
+    )
+    kept, sent = run(
+        qkv_grads_kernel,
+        "qkv_grads",
+        jnp.stack([rank, low]),
+        all_one + all_branch + mixes + [grads_own, grads_other],
+        [((width // 2, width), F32), ((width // 2, width), BF)],
+        [pltpu.VMEM((width, width), F32)],
+    )
+    arrived, far, side = scatter_eight(even, odd)
+    moved_back, sums = run(
+        functools.partial(norm_one_back_kernel, vectors),
+        "norm_one_back",
+        rank_one,
+        [moved, grad_after, even, arrived, far, side, ln_gains]
+        + [learned, small, rows_two, grad_up_bias],
+        [((rows + learned_rows, width), BF), ((small_rows, PAD), F32)],
+    )
+    moved_back = from_planes(moved_back).astype(F32)
+
+    own_half, *pieces = run(
+        half_kernel,
+        "half",
+        high.reshape(1),
+        [kept, flip(sent, 0, 0, 1)],
+        [((size, width), F32)] + [((size, width), BF)] * 3,
+    )
+    pieces = [
+        permute(piece, lambda seq, hi, lo, step=step: (seq, (hi + step) % ranks, lo))
+        for step, piece in enumerate(pieces, 1)
+    ]
+    (qkv_share,) = run(
+        total_kernel, "total", low_one, [own_half] + pieces, [((size, width), BF)]
+    )
+    for seq_bits, hi_bits, lo_bits in ((1, 0, 0), (2, 0, 0), (0, 0, 1), (0, 1, 0), (0, 2, 0)):
+        sums = sums + flip(sums, seq_bits, hi_bits, lo_bits)
+    sum_gains, sum_shifts, sum_up_bias, sum_down_bias, sum_first, sum_mid, sum_mid_bias = run(
+        functools.partial(unpack_kernel, vectors),
+        "unpack",
+        low_one,
+        [sums],
+        [
+            ((3, width), F32),
+            ((3, width), F32),
+            ((1, hidden), F32),
+            ((1, width), F32),
+            ((1, CH), F32),
+            ((3, CH, 9 * CH), F32),
+            ((3, CH), F32),
+        ],
+    )
+    sum_up, sum_down, sum_conv = run(
+        functools.partial(finish_mlp_kernel, ranks, hidden_quarter, width, unit),
+        "finish_mlp",
+        rank_one,
+        gather_four(mlp_share),
+        [((size, hidden), F32), ((ranks * unit, width), F32), ((size, PAD), F32)],
+    )
+    sum_qkv, sum_out = run(
+        functools.partial(finish_qkv_kernel, ranks, quarter),
+        "finish_qkv",
+        rank_one,
+        gather_four(qkv_share),
+        [((size, 3 * width), F32), ((size, width), F32)],
+    )
+    return (
+        moved_back[rows:].reshape(1, frames_dev, CH, width),
+        moved_back[:rows].reshape(1, frames_dev, patches, width),
+        sum_qkv,
+        sum_out,
+        sum_up,
+        sum_down,
+        sum_conv[:, : 9 * CH],
+        sum_gains,
+        sum_shifts,
+        sum_up_bias.reshape(hidden),
+        sum_down_bias.reshape(width),
+        sum_first.reshape(CH),
+        sum_mid,
+        sum_mid_bias,
+    )
 
 
 def solution(mesh):
@@ -548,8 +1642,10 @@
         P(),
         P("seq", "frame", None, None),
     )
+    ranks, frame_size = mesh.shape["seq"], mesh.shape["frame"]
+    body = shards_square if ranks == 4 and frame_size == 8 else shards_general
     return jax.shard_map(
-        functools.partial(shards, mesh.shape["seq"], mesh.shape["frame"]),
+        functools.partial(body, ranks, frame_size),
         mesh=mesh,
         in_specs=placed,
         out_specs=(

time: 390 us -> 288 us (0.74)
  blocking collectives: 47.1 us -> 0 us
  matrix products: 34.6 us -> 1.86 us
  Pallas kernels: 16.9 us -> 44.3 us
  waiting for transfers between devices: 145 us -> 121 us
  other arithmetic: 28.3 us -> 4.47 us
  between operations: 2.45 us -> 14.9 us
  local copies, waits for them, and re-layouts: 48 us -> 36.8 us
    psum x1 -> x0, blocking collectives: 47.1 us -> none  [shards(): lax.psum(jnp.concatenate([item.reshape(-1) for item in small]), AXES)]
    ppermute x63 -> x57, waiting for transfers between devices: 145 us -> 108 us  [permute(): return lax.ppermute(array, AXES, pairs)]
    dot_general x16 -> x1, matrix products: 30.2 us -> 1.86 us  [dot(): lax.dot_general(left, right, (((left_dim,), (right_dim,)), ((), ())), pre...]
    pallas_call x2 -> x19, Pallas kernels: 16.9 us -> 44.3 us  [run(): pl.pallas_call(kernel, in_specs=[pl.BlockSpec(memory_space=pltpu.SMEM)] +...]
    unnamed x119 -> x152, local copies, waits for them, and re-layouts: 3.63 us -> 29.1 us
    reduce_scatter x0 -> x1, waiting for transfers between devices: none -> 13 us  [shards_square(): lax.psum_scatter(mlp_grads, 'frame', scatter_dimension=0, tiled=True)]
    convert_element_type x7 -> x0, local copies, waits for them, and re-layouts: 12.9 us -> none  [the longest x2 5.82 us: shards(): sum_up = jnp.stack([part[:, :hidden_quarter] for part in mlp_parts]).resh...]
    concatenate x5 -> x1, local copies, waits for them, and re-layouts: 9.8 us -> 0.81 us  [shards_square(): jnp.concatenate([dot(w_up, choose).astype(BF), lax.dynamic_slice_in_dim(w...]
  transfers between devices with their start and end apart: 63 -> 59, of which waited for: 26 -> 26; matrix products, arithmetic and copies ran while one was open for 19% -> 4% of each run, Pallas kernels for 0% -> 10%
where the time goes in v2:
time: 288 us; the launch traced here: 285 us
  waiting for transfers between devices  121 us (42%)
  starting transfers between devices  61.4 us (21%)
  Pallas kernels  44.3 us (15%)
  local copies, waits for them, and re-layouts  36.8 us (13%)
  between operations  14.9 us (5%)
  other arithmetic  4.47 us (2%)
    ppermute x57, waiting for transfers between devices, permute(): return lax.ppermute(array, AXES, pairs)  108 us
    ppermute x57, starting transfers between devices, permute(): return lax.ppermute(array, AXES, pairs)  61.4 us
    pallas_call x19, Pallas kernels, run(): pl.pallas_call(kernel, in_specs=[pl.BlockSpec(memory_space=pltpu.SMEM)] +...  44.3 us
    unnamed x152, local copies, waits for them, and re-layouts  29.1 us
    reduce_scatter x1, waiting for transfers between devices, shards_square(): lax.psum_scatter(mlp_grads, 'frame', scatter_dimension=0, tiled=True)  13 us
  transfers between devices with their start and end apart: 59, of which 26 were waited for; matrix products, arithmetic and copies ran while one was open for 4% of the time, Pallas kernels for 10%

profile of v2, /device:TPU:2, one launch (start us, length us, event | category | flops | bytes accessed | tf_op | source)
XLA Modules:
  0.0 285.1 jit_solution(6499399626966258208)
XLA Ops:
  8.3 1.9 fusion.3
  12.1 4.7 %collective-permute-start = (bf16[160,768]{1,0:T(8,128)(2,1)S(1)}, bf16[160,768]{1,0:T(8,128)(2,1)S(1)}, u32[]{:S(2)}, u32[]{:S(2)}) collective-permute-start(bf16[160,768]{1,0:T(8,128)(2,1)S(1)} %fusion.9), channel_id=1, source_target_pairs={{0,0},{1,1},{2,8},{3,9},{4,16},{5,17},{6,24},{7,25},{8,2},{9,3},{1... | collective-permute-start | bytes 737288 | tf_op jit(solution)/shard_map/ppermute | solution.py:1281
  20.5 2.0 collective-permute-start.10
  22.5 19.4 %collective-permute-done.moved_ref.refs_0_.refs_11_ = bf16[160,768]{1,0:T(8,128)(2,1)S(1)} collective-permute-done((bf16[160,768]{1,0:T(8,128)(2,1)S(1)}, bf16[160,768]{1,0:T(8,128)(2,1)S(1)}, u32[]{:S(2)}, u32[]{:S(2)}) %collective-permute-start) | collective-permute-done | bytes 245792 | tf_op jit(solution)/shard_map/ppermute | solution.py:1281
  42.2 1.6 collective-permute-start.4
  43.8 2.0 collective-permute-done.10.refs_11_.refs_3_
  45.9 2.4 collective-permute-start.13
  48.3 5.1 %collective-permute-start.14 = (bf16[96,768]{1,0:T(8,128)(2,1)S(1)}, bf16[96,768]{1,0:T(8,128)(2,1)S(1)}, u32[]{:S(2)}, u32[]{:S(2)}) collective-permute-start(bf16[96,768]{1,0:T(8,128)(2,1)S(1)} %pad_maximum_fusion.refs_8_.refs_0_), channel_id=1, source_target_pairs={{0,7},{1,6},{2,5},{3,4},{4,3},{5,2},{6,1},{7,0},{8,15},{9,14},{10,... | collective-permute-start | bytes 442376 | tf_op jit(solution)/shard_map/ppermute | solution.py:1281
  53.7 11.7 %collective-permute-done.12.refs_13_.refs_5_ = bf16[96,768]{1,0:T(8,128)(2,1)S(1)} collective-permute-done((bf16[96,768]{1,0:T(8,128)(2,1)S(1)}, bf16[96,768]{1,0:T(8,128)(2,1)S(1)}, u32[]{:S(2)}, u32[]{:S(2)}) %collective-permute-start.12) | collective-permute-done | bytes 147488 | tf_op jit(solution)/shard_map/ppermute | solution.py:1281
  67.6 5.3 %collective-permute-start.16 = (bf16[2,192,192]{2,1,0:T(8,128)(2,1)}, bf16[2,192,192]{2,1,0:T(8,128)(2,1)S(1)}, u32[]{:S(2)}, u32[]{:S(2)}) collective-permute-start(bf16[2,192,192]{2,1,0:T(8,128)(2,1)} %get-tuple-element.79), channel_id=1, source_target_pairs={{0,16},{1,17},{2,18},{3,19},{4,20},{5,21},{6,22},{7,23},{8,24},{9,... | collective-permute-start | bytes 442376 | tf_op jit(solution)/shard_map/ppermute | solution.py:1281
  74.9 4.0 %collective-permute-done.16.refs_3_ = bf16[2,192,192]{2,1,0:T(8,128)(2,1)S(1)} collective-permute-done((bf16[2,192,192]{2,1,0:T(8,128)(2,1)}, bf16[2,192,192]{2,1,0:T(8,128)(2,1)S(1)}, u32[]{:S(2)}, u32[]{:S(2)}) %collective-permute-start.16) | collective-permute-done | bytes 147488 | tf_op jit(solution)/shard_map/ppermute | solution.py:1281
  94.1 1.8 project.1
  96.9 5.3 %attend.1 = (bf16[192,512]{1,0:T(8,128)(2,1)S(1)}, f32[8,512]{1,0:T(8,128)S(1)}) custom-call(s32[1]{0:T(128)} %bitcast.unused_ref.rank_ref, bf16[512,192]{1,0:T(8,128)(2,1)S(1)} %get-tuple-element.74.refs_0_.refs_5_, bf16[1024,384]{1,0:T(8,128)(2,1)S(1)} %get-tuple-element.75.refs_1_.refs_6_, s32[1,512]{1,0:T(1,128)S(1)} %broadcast_in_dim_reshape.3.refs_2_.refs_8_, ...), custom_call_target="tpu_custom_call" | custom-call | tf_op jit(solution)/shard_map/attend/pallas_call | solution.py:745
  106.2 1.8 collective-permute-start.19
  108.0 5.2 %collective-permute-done.19.refs_3_ = bf16[128,768]{1,0:T(8,128)(2,1)S(1)} collective-permute-done((bf16[128,768]{1,0:T(8,128)(2,1)S(1)}, bf16[128,768]{1,0:T(8,128)(2,1)S(1)}, u32[]{:S(2)}, u32[]{:S(2)}) %collective-permute-start.19) | collective-permute-done | bytes 196640 | tf_op jit(solution)/shard_map/ppermute | solution.py:1281
  113.5 1.8 collective-permute-start.21
  115.3 4.5 %collective-permute-done.21.refs_2_ = bf16[128,768]{1,0:T(8,128)(2,1)S(1)} collective-permute-done((bf16[128,768]{1,0:T(8,128)(2,1)S(1)}, bf16[128,768]{1,0:T(8,128)(2,1)S(1)}, u32[]{:S(2)}, u32[]{:S(2)}) %collective-permute-start.21) | collective-permute-done | bytes 196640 | tf_op jit(solution)/shard_map/ppermute | solution.py:1281
  122.7 4.0 %mlp.1 = (bf16[512,768]{1,0:T(8,128)(2,1)S(1)}, f32[512,768]{1,0:T(8,128)S(1)}, bf16[768,768]{1,0:T(8,128)(2,1)S(1)}, bf16[768,768]{1,0:T(8,128)(2,1)S(1)}, bf16...) custom-call(s32[1]{0:T(128)} %bitcast.3.unused_ref.low_ref, ...), custom_call_target="tpu_custom_call" | custom-call | tf_op jit(solution)/shard_map/mlp/pallas_call | solution.py:745
  126.9 1.6 collective-permute-done.24.refs_2_
  128.5 2.0 collective-permute-start.25
  130.6 5.1 %collective-permute-done.25.refs_3_ = bf16[128,768]{1,0:T(8,128)(2,1)S(1)} collective-permute-done((bf16[128,768]{1,0:T(8,128)(2,1)S(1)}, bf16[128,768]{1,0:T(8,128)(2,1)S(1)}, u32[]{:S(2)}, u32[]{:S(2)}) %collective-permute-start.25) | collective-permute-done | bytes 196640 | tf_op jit(solution)/shard_map/ppermute | solution.py:1281
  135.7 5.7 %tail.1 = (f32[16,768]{1,0:T(8,128)S(1)}, bf16[128,768]{1,0:T(8,128)(2,1)S(1)}, f32[128,768]{1,0:T(8,128)S(1)}, bf16[128,768]{1,0:T(8,128)(2,1)S(1)}, bf16[128,1...) custom-call(s32[1]{0:T(128)} %bitcast.3.unused_ref.low_ref, f32[128,768]{1,0:T(8,128)S(1)} %get-tuple-element.82.refs_0_, ...), custom_call_target="tpu_custom_call" | custom-call | tf_op jit(solution)/shard_map/tail/pallas_call | solution.py:745
  141.4 1.8 collective-permute-start.27
  143.2 4.4 %collective-permute-done.27.refs_2_.refs_6_ = bf16[128,768]{1,0:T(8,128)(2,1)S(1)} collective-permute-done((bf16[128,768]{1,0:T(8,128)(2,1)S(1)}, bf16[128,768]{1,0:T(8,128)(2,1)S(1)}, u32[]{:S(2)}, u32[]{:S(2)}) %collective-permute-start.27) | collective-permute-done | bytes 196640 | tf_op jit(solution)/shard_map/ppermute | solution.py:1281
  151.4 3.0 %mlp_grads.1 = bf16[768,1664]{1,0:T(8,128)(2,1)} custom-call(s32[1]{0:T(128)} %bitcast.3.unused_ref.low_ref, bf16[128,768]{1,0:T(8,128)(2,1)S(1)} %get-tuple-element.83.refs_0_, bf16[128,768]{1,0:T(8,128)(2,1)S(1)} %copy-done.27, bf16[128,768]{1,0:T(8,128)(2,1)S(1)} %collective-permute-done.21.refs_2_, bf16[128,768]{1,0:T(8,128)(2,1)S(1)} %copy-done.29, ...), custom_call_target="tpu_custom_call" | custom-call | tf_op jit(solution)/shard_map/mlp_grads/pallas_call | solution.py:745
  154.7 1.8 collective-permute-done.29.refs_3_
  156.5 1.8 collective-permute-start.30
  158.3 5.2 %collective-permute-done.30.refs_4_ = bf16[128,768]{1,0:T(8,128)(2,1)S(1)} collective-permute-done((bf16[128,768]{1,0:T(8,128)(2,1)S(1)}, bf16[128,768]{1,0:T(8,128)(2,1)S(1)}, u32[]{:S(2)}, u32[]{:S(2)}) %collective-permute-start.30) | collective-permute-done | bytes 196640 | tf_op jit(solution)/shard_map/ppermute | solution.py:1281
  165.7 1.7 collective-permute-start.32
  167.4 4.4 %collective-permute-done.32.refs_2_.refs_10_ = bf16[128,768]{1,0:T(8,128)(2,1)S(1)} collective-permute-done((bf16[128,768]{1,0:T(8,128)(2,1)S(1)}, bf16[128,768]{1,0:T(8,128)(2,1)S(1)}, u32[]{:S(2)}, u32[]{:S(2)}) %collective-permute-start.32) | collective-permute-done | bytes 196640 | tf_op jit(solution)/shard_map/ppermute | solution.py:1281
  175.0 8.0 %attend_back_out.1 = (bf16[512,576]{1,0:T(8,128)(2,1)S(1)}, bf16[512,384]{1,0:T(8,128)(2,1)S(1)}, f32[4,128,768]{2,1,0:T(8,128)S(1)}, bf16[4,128,768]{2,1,0:T(8,128)(2,1)S(1)}) custom-call(s32[1]{0:T(128)} %bitcast.3.unused_ref.low_ref, bf16[128,768]{1,0:T(8,128)(2,1)S(1)} %get-tuple-element.95.refs_0_.refs_8_, ...), custom_call_target="tpu_custom_call" | custom-call | tf_op jit(solution)/shard_map/attend_back_out/pallas_call | solution.py:745
  183.2 1.7 collective-permute-start.40
  185.0 5.4 %collective-permute-done.40.refs_14_ = bf16[192,512]{1,0:T(8,128)(2,1)S(1)} collective-permute-done((bf16[192,512]{1,0:T(8,128)(2,1)S(1)}, bf16[192,512]{1,0:T(8,128)(2,1)S(1)}, u32[]{:S(2)}, u32[]{:S(2)}) %collective-permute-start.40) | collective-permute-done | bytes 196640 | tf_op jit(solution)/shard_map/ppermute | solution.py:1281
  191.9 3.2 %qkv_grads.1 = (f32[384,768]{1,0:T(8,128)S(1)}, bf16[384,768]{1,0:T(8,128)(2,1)}) custom-call(s32[2]{0:T(128)S(1)} %pad_add_fusion.1.place_ref, bf16[128,768]{1,0:T(8,128)(2,1)S(1)} %norm_one.1.refs_0_, bf16[128,768]{1,0:T(8,128)(2,1)S(1)} %copy-done.14, bf16[128,768]{1,0:T(8,128)(2,1)S(1)} %collective-permute-done.2.refs_2_, ...), custom_call_target="tpu_custom_call" | custom-call | tf_op jit(solution)/shard_map/qkv_grads/pallas_call | solution.py:745
  199.1 1.7 collective-permute-start.35
  200.8 14.3 %collective-permute-done.42.arrived_ref = bf16[384,768]{1,0:T(8,128)(2,1)S(1)} collective-permute-done((bf16[384,768]{1,0:T(8,128)(2,1)}, bf16[384,768]{1,0:T(8,128)(2,1)S(1)}, u32[]{:S(2)}, u32[]{:S(2)}) %collective-permute-start.42) | collective-permute-done | bytes 589856 | tf_op jit(solution)/shard_map/ppermute | solution.py:1281
  217.2 3.8 %collective-permute-start.43 = (bf16[96,768]{1,0:T(8,128)(2,1)S(1)}, bf16[96,768]{1,0:T(8,128)(2,1)S(1)}, u32[]{:S(2)}, u32[]{:S(2)}) collective-permute-start(bf16[96,768]{1,0:T(8,128)(2,1)S(1)} %get-tuple-element.112), channel_id=1, source_target_pairs={{0,2},{1,3},{2,4},{3,5},{4,6},{5,7},{6,0},{7,1},{8,10},{9,11},{10,... | collective-permute-start | bytes 442376 | tf_op jit(solution)/shard_map/ppermute | solution.py:1281
  221.9 2.9 %collective-permute-start.45 = (bf16[96,768]{1,0:T(8,128)(2,1)}, bf16[96,768]{1,0:T(8,128)(2,1)}, u32[]{:S(2)}, u32[]{:S(2)}) collective-permute-start(bf16[96,768]{1,0:T(8,128)(2,1)} %get-tuple-element.114), channel_id=1, source_target_pairs={{0,6},{1,7},{2,0},{3,1},{4,2},{5,3},{6,4},{7,5},{8,14},{9,15},{10,... | collective-permute-start | bytes 442376 | tf_op jit(solution)/shard_map/ppermute | solution.py:1281
  224.8 1.8 fusion.8
  229.2 13.0 %reduce-scatter.2.cloned.1.call-done.refs_0_ = bf16[96,1664]{1,0:T(8,128)(2,1)} async-done(((bf16[768,1664]{1,0:T(8,128)(2,1)}), bf16[96,1664]{1,0:T(8,128)(2,1)}) %reduce-scatter.2.cloned.1.call-update) | async-done | bytes 319504 | tf_op jit(solution)/shard_map/reduce_scatter | solution.py:1521
  244.2 2.1 collective-permute-start.47
  250.5 2.2 collective-permute-start.38
  252.7 2.3 collective-permute-start.46
  255.2 4.2 %collective-permute-done.53 = f32[96,128]{1,0:T(8,128)S(1)} collective-permute-done((f32[96,128]{1,0:T(8,128)S(1)}, f32[96,128]{1,0:T(8,128)S(1)}, u32[]{:S(2)}, u32[]{:S(2)}) %collective-permute-start.53) | collective-permute-done | bytes 49184 | tf_op jit(solution)/shard_map/ppermute | solution.py:1281
  260.5 3.1 %collective-permute-done.54 = f32[96,128]{1,0:T(8,128)S(1)} collective-permute-done((f32[96,128]{1,0:T(8,128)S(1)}, f32[96,128]{1,0:T(8,128)S(1)}, u32[]{:S(2)}, u32[]{:S(2)}) %collective-permute-start.54) | collective-permute-done | bytes 49184 | tf_op jit(solution)/shard_map/ppermute | solution.py:1281
  264.1 1.8 collective-permute-start.55
  270.0 3.3 %collective-permute-done.56 = f32[96,128]{1,0:T(8,128)S(1)} collective-permute-done((f32[96,128]{1,0:T(8,128)S(1)}, f32[96,128]{1,0:T(8,128)S(1)}, u32[]{:S(2)}, u32[]{:S(2)}) %collective-permute-start.56) | collective-permute-done | bytes 49184 | tf_op jit(solution)/shard_map/ppermute | solution.py:1281
  274.7 2.8 finish_mlp.1
  (290 shorter events, 69.5 us)
Async XLA Ops:
  7.2 75.5 %all-gather.2.cloned.1.call-start = ((), (), s32[]{:S(2)}) async-start(), calls=%async_computation.1 | async-start | bytes 1597440 | tf_op jit(solution)/shard_map/all_gather | solution.py:1374
  12.0 230.3 %reduce-scatter.2.cloned.1.call-start = ((), (), s32[]{:S(2)}) async-start(), calls=%async_computation.2 | async-start | bytes 2875392 | tf_op jit(solution)/shard_map/reduce_scatter | solution.py:1521
  12.1 29.8 %collective-permute-start = (bf16[160,768]{1,0:T(8,128)(2,1)S(1)}, bf16[160,768]{1,0:T(8,128)(2,1)S(1)}, u32[]{:S(2)}, u32[]{:S(2)}) collective-permute-start(bf16[160,768]{1,0:T(8,128)(2,1)S(1)} %fusion.9), channel_id=1, source_target_pairs={{0,0},{1,1},{2,8},{3,9},{4,16},{5,17},{6,24},{7,25},{8,2},{9,3},{1... | collective-permute-start | bytes 737288 | tf_op jit(solution)/shard_map/ppermute | solution.py:1281
  18.9 23.2 %collective-permute-start.8 = (bf16[96,768]{1,0:T(8,128)(2,1)S(1)}, bf16[96,768]{1,0:T(8,128)(2,1)S(1)}, u32[]{:S(2)}, u32[]{:S(2)}) collective-permute-start(bf16[96,768]{1,0:T(8,128)(2,1)S(1)} %pad_maximum_fusion.refs_8_.refs_0_), channel_id=1, source_target_pairs={{0,1},{1,0},{2,3},{3,2},{4,5},{5,4},{6,7},{7,6},{8,9},{9,8},{10,11... | collective-permute-start | bytes 442376 | tf_op jit(solution)/shard_map/ppermute | solution.py:1281
  20.5 23.3 %collective-permute-start.9 = (bf16[96,768]{1,0:T(8,128)(2,1)S(1)}, bf16[96,768]{1,0:T(8,128)(2,1)S(1)}, u32[]{:S(2)}, u32[]{:S(2)}) collective-permute-start(bf16[96,768]{1,0:T(8,128)(2,1)S(1)} %pad_maximum_fusion.refs_8_.refs_0_), channel_id=1, source_target_pairs={{0,2},{1,3},{2,0},{3,1},{4,6},{5,7},{6,4},{7,5},{8,10},{9,11},{10,... | collective-permute-start | bytes 442376 | tf_op jit(solution)/shard_map/ppermute | solution.py:1281
  20.5 25.4 %collective-permute-start.10 = (bf16[96,768]{1,0:T(8,128)(2,1)S(1)}, bf16[96,768]{1,0:T(8,128)(2,1)S(1)}, u32[]{:S(2)}, u32[]{:S(2)}) collective-permute-start(bf16[96,768]{1,0:T(8,128)(2,1)S(1)} %pad_maximum_fusion.refs_8_.refs_0_), channel_id=1, source_target_pairs={{0,3},{1,2},{2,1},{3,0},{4,7},{5,6},{6,5},{7,4},{8,11},{9,10},{10,... | collective-permute-start | bytes 442376 | tf_op jit(solution)/shard_map/ppermute | solution.py:1281
  22.5 25.8 %collective-permute-start.11 = (bf16[96,768]{1,0:T(8,128)(2,1)S(1)}, bf16[96,768]{1,0:T(8,128)(2,1)S(1)}, u32[]{:S(2)}, u32[]{:S(2)}) collective-permute-start(bf16[96,768]{1,0:T(8,128)(2,1)S(1)} %pad_maximum_fusion.refs_8_.refs_0_), channel_id=1, source_target_pairs={{0,4},{1,5},{2,6},{3,7},{4,0},{5,1},{6,2},{7,3},{8,12},{9,13},{10,... | collective-permute-start | bytes 442376 | tf_op jit(solution)/shard_map/ppermute | solution.py:1281
  42.1 31.1 %collective-permute-start.2 = (bf16[128,768]{1,0:T(8,128)(2,1)S(1)}, bf16[128,768]{1,0:T(8,128)(2,1)S(1)}, u32[]{:S(2)}, u32[]{:S(2)}) collective-permute-start(bf16[128,768]{1,0:T(8,128)(2,1)S(1)} %norm_one.1.refs_0_), channel_id=1, source_target_pairs={{0,16},{1,17},{2,18},{3,19},{4,20},{5,21},{6,22},{7,23},{8,24},{9,... | collective-permute-start | bytes 589832 | tf_op jit(solution)/shard_map/ppermute | solution.py:1281
  42.2 31.0 %collective-permute-start.4 = (bf16[128,768]{1,0:T(8,128)(2,1)S(1)}, bf16[128,768]{1,0:T(8,128)(2,1)S(1)}, u32[]{:S(2)}, u32[]{:S(2)}) collective-permute-start(bf16[128,768]{1,0:T(8,128)(2,1)S(1)} %norm_one.1.refs_0_), channel_id=1, source_target_pairs={{0,1},{1,0},{2,3},{3,2},{4,5},{5,4},{6,7},{7,6},{8,9},{9,8},{10,11... | collective-permute-start | bytes 589832 | tf_op jit(solution)/shard_map/ppermute | solution.py:1281
  43.8 21.6 %collective-permute-start.12 = (bf16[96,768]{1,0:T(8,128)(2,1)S(1)}, bf16[96,768]{1,0:T(8,128)(2,1)S(1)}, u32[]{:S(2)}, u32[]{:S(2)}) collective-permute-start(bf16[96,768]{1,0:T(8,128)(2,1)S(1)} %pad_maximum_fusion.refs_8_.refs_0_), channel_id=1, source_target_pairs={{0,5},{1,4},{2,7},{3,6},{4,1},{5,0},{6,3},{7,2},{8,13},{9,12},{10,... | collective-permute-start | bytes 442376 | tf_op jit(solution)/shard_map/ppermute | solution.py:1281
  45.9 19.6 %collective-permute-start.13 = (bf16[96,768]{1,0:T(8,128)(2,1)S(1)}, bf16[96,768]{1,0:T(8,128)(2,1)S(1)}, u32[]{:S(2)}, u32[]{:S(2)}) collective-permute-start(bf16[96,768]{1,0:T(8,128)(2,1)S(1)} %pad_maximum_fusion.refs_8_.refs_0_), channel_id=1, source_target_pairs={{0,6},{1,7},{2,4},{3,5},{4,2},{5,3},{6,0},{7,1},{8,14},{9,15},{10,... | collective-permute-start | bytes 442376 | tf_op jit(solution)/shard_map/ppermute | solution.py:1281
  48.3 17.2 %collective-permute-start.14 = (bf16[96,768]{1,0:T(8,128)(2,1)S(1)}, bf16[96,768]{1,0:T(8,128)(2,1)S(1)}, u32[]{:S(2)}, u32[]{:S(2)}) collective-permute-start(bf16[96,768]{1,0:T(8,128)(2,1)S(1)} %pad_maximum_fusion.refs_8_.refs_0_), channel_id=1, source_target_pairs={{0,7},{1,6},{2,5},{3,4},{4,3},{5,2},{6,1},{7,0},{8,15},{9,14},{10,... | collective-permute-start | bytes 442376 | tf_op jit(solution)/shard_map/ppermute | solution.py:1281
  67.6 34.6 %collective-permute-start.15 = (bf16[192,192]{1,0:T(8,128)(2,1)}, bf16[192,192]{1,0:T(8,128)(2,1)}, u32[]{:S(2)}, u32[]{:S(2)}) collective-permute-start(bf16[192,192]{1,0:T(8,128)(2,1)} %get-tuple-element.78), channel_id=1, source_target_pairs={{0,8},{1,9},{2,10},{3,11},{4,12},{5,13},{6,14},{7,15},{8,0},{9,1},... | collective-permute-start | bytes 221192 | tf_op jit(solution)/shard_map/ppermute | solution.py:1281
  67.6 11.3 %collective-permute-start.16 = (bf16[2,192,192]{2,1,0:T(8,128)(2,1)}, bf16[2,192,192]{2,1,0:T(8,128)(2,1)S(1)}, u32[]{:S(2)}, u32[]{:S(2)}) collective-permute-start(bf16[2,192,192]{2,1,0:T(8,128)(2,1)} %get-tuple-element.79), channel_id=1, source_target_pairs={{0,16},{1,17},{2,18},{3,19},{4,20},{5,21},{6,22},{7,23},{8,24},{9,... | collective-permute-start | bytes 442376 | tf_op jit(solution)/shard_map/ppermute | solution.py:1281
  72.9 9.0 %collective-permute-start.1 = (bf16[128,768]{1,0:T(8,128)(2,1)S(1)}, bf16[128,768]{1,0:T(8,128)(2,1)S(1)}, u32[]{:S(2)}, u32[]{:S(2)}) collective-permute-start(bf16[128,768]{1,0:T(8,128)(2,1)S(1)} %norm_one.1.refs_0_), channel_id=1, source_target_pairs={{0,8},{1,9},{2,10},{3,11},{4,12},{5,13},{6,14},{7,15},{8,0},{9,1},... | collective-permute-start | bytes 589832 | tf_op jit(solution)/shard_map/ppermute | solution.py:1281
  73.8 5.9 %collective-permute-start.6 = (bf16[128,768]{1,0:T(8,128)(2,1)}, bf16[128,768]{1,0:T(8,128)(2,1)S(1)}, u32[]{:S(2)}, u32[]{:S(2)}) collective-permute-start(bf16[128,768]{1,0:T(8,128)(2,1)} %broadcast_select_fusion), channel_id=1, source_target_pairs={{0,1},{1,0},{2,3},{3,2},{4,5},{5,4},{6,7},{7,6},{8,24},{9,25},{10,... | collective-permute-start | bytes 589832 | tf_op jit(solution)/shard_map/ppermute | solution.py:1281
  74.8 7.1 %collective-permute-start.3 = (bf16[128,768]{1,0:T(8,128)(2,1)S(1)}, bf16[128,768]{1,0:T(8,128)(2,1)S(1)}, u32[]{:S(2)}, u32[]{:S(2)}) collective-permute-start(bf16[128,768]{1,0:T(8,128)(2,1)S(1)} %collective-permute-done.2.refs_2_), channel_id=1, source_target_pairs={{0,8},{1,9},{2,10},{3,11},{4,12},{5,13},{6,14},{7,15},{8,0},{9,1},... | collective-permute-start | bytes 589832 | tf_op jit(solution)/shard_map/ppermute | solution.py:1281
  78.9 4.7 %collective-permute-start.5 = (bf16[128,768]{1,0:T(8,128)(2,1)S(1)}, bf16[128,768]{1,0:T(8,128)(2,1)S(1)}, u32[]{:S(2)}, u32[]{:S(2)}) collective-permute-start(bf16[128,768]{1,0:T(8,128)(2,1)S(1)} %collective-permute-done.4.refs_4_), channel_id=1, source_target_pairs={{0,8},{1,9},{2,10},{3,11},{4,12},{5,13},{6,14},{7,15},{8,0},{9,1},... | collective-permute-start | bytes 589832 | tf_op jit(solution)/shard_map/ppermute | solution.py:1281
  79.7 4.5 %collective-permute-start.7 = (bf16[128,768]{1,0:T(8,128)(2,1)S(1)}, bf16[128,768]{1,0:T(8,128)(2,1)S(1)}, u32[]{:S(2)}, u32[]{:S(2)}) collective-permute-start(bf16[128,768]{1,0:T(8,128)(2,1)S(1)} %collective-permute-done.6.refs_6_), channel_id=1, source_target_pairs={{0,8},{1,9},{2,10},{3,11},{4,12},{5,13},{6,14},{7,15},{8,0},{9,1},... | collective-permute-start | bytes 589832 | tf_op jit(solution)/shard_map/ppermute | solution.py:1281
  81.9 20.3 %collective-permute-start.17 = (bf16[192,192]{1,0:T(8,128)(2,1)}, bf16[192,192]{1,0:T(8,128)(2,1)}, u32[]{:S(2)}, u32[]{:S(2)}) collective-permute-start(bf16[192,192]{1,0:T(8,128)(2,1)} %slice_bitcast_fusion), channel_id=1, source_target_pairs={{0,8},{1,9},{2,10},{3,11},{4,12},{5,13},{6,14},{7,15},{8,0},{9,1},... | collective-permute-start | bytes 221192 | tf_op jit(solution)/shard_map/ppermute | solution.py:1281
  82.7 38.6 %collective-permute-start.23 = (bf16[384,1664]{1,0:T(8,128)(2,1)}, bf16[384,1664]{1,0:T(8,128)(2,1)}, u32[]{:S(2)}, u32[]{:S(2)}) collective-permute-start(bf16[384,1664]{1,0:T(8,128)(2,1)} %all-gather.2.cloned.1.call-done.refs_4_), channel_id=1, source_target_pairs={{0,1},{1,0},{2,3},{3,2},{4,5},{5,4},{6,7},{7,6},{8,9},{9,8},{10,11... | collective-permute-start | bytes 3833864 | tf_op jit(solution)/shard_map/ppermute | solution.py:1281
  106.2 7.0 %collective-permute-start.19 = (bf16[128,768]{1,0:T(8,128)(2,1)S(1)}, bf16[128,768]{1,0:T(8,128)(2,1)S(1)}, u32[]{:S(2)}, u32[]{:S(2)}) collective-permute-start(bf16[128,768]{1,0:T(8,128)(2,1)S(1)} %fusion.10), channel_id=1, source_target_pairs={{0,16},{1,17},{2,18},{3,19},{4,20},{5,21},{6,22},{7,23},{8,24},{9,... | collective-permute-start | bytes 589832 | tf_op jit(solution)/shard_map/ppermute | solution.py:1281
  113.5 6.3 %collective-permute-start.21 = (bf16[128,768]{1,0:T(8,128)(2,1)S(1)}, bf16[128,768]{1,0:T(8,128)(2,1)S(1)}, u32[]{:S(2)}, u32[]{:S(2)}) collective-permute-start(bf16[128,768]{1,0:T(8,128)(2,1)S(1)} %get-tuple-element.83.refs_0_), channel_id=1, source_target_pairs={{0,16},{1,17},{2,18},{3,19},{4,20},{5,21},{6,22},{7,23},{8,24},{9,... | collective-permute-start | bytes 589832 | tf_op jit(solution)/shard_map/ppermute | solution.py:1281
  115.3 5.4 %collective-permute-start.20 = (bf16[128,768]{1,0:T(8,128)(2,1)S(1)}, bf16[128,768]{1,0:T(8,128)(2,1)S(1)}, u32[]{:S(2)}, u32[]{:S(2)}) collective-permute-start(bf16[128,768]{1,0:T(8,128)(2,1)S(1)} %get-tuple-element.83.refs_0_), channel_id=1, source_target_pairs={{0,8},{1,9},{2,10},{3,11},{4,12},{5,13},{6,14},{7,15},{8,0},{9,1},... | collective-permute-start | bytes 589832 | tf_op jit(solution)/shard_map/ppermute | solution.py:1281
  128.5 7.2 %collective-permute-start.25 = (bf16[128,768]{1,0:T(8,128)(2,1)S(1)}, bf16[128,768]{1,0:T(8,128)(2,1)S(1)}, u32[]{:S(2)}, u32[]{:S(2)}) collective-permute-start(bf16[128,768]{1,0:T(8,128)(2,1)S(1)} %fusion.11), channel_id=1, source_target_pairs={{0,16},{1,17},{2,18},{3,19},{4,20},{5,21},{6,22},{7,23},{8,24},{9,... | collective-permute-start | bytes 589832 | tf_op jit(solution)/shard_map/ppermute | solution.py:1281
  141.4 6.2 %collective-permute-start.27 = (bf16[128,768]{1,0:T(8,128)(2,1)S(1)}, bf16[128,768]{1,0:T(8,128)(2,1)S(1)}, u32[]{:S(2)}, u32[]{:S(2)}) collective-permute-start(bf16[128,768]{1,0:T(8,128)(2,1)S(1)} %get-tuple-element.88.refs_0_.refs_4_), channel_id=1, source_target_pairs={{0,16},{1,17},{2,18},{3,19},{4,20},{5,21},{6,22},{7,23},{8,24},{9,... | collective-permute-start | bytes 589832 | tf_op jit(solution)/shard_map/ppermute | solution.py:1281
  156.5 7.0 %collective-permute-start.30 = (bf16[128,768]{1,0:T(8,128)(2,1)S(1)}, bf16[128,768]{1,0:T(8,128)(2,1)S(1)}, u32[]{:S(2)}, u32[]{:S(2)}) collective-permute-start(bf16[128,768]{1,0:T(8,128)(2,1)S(1)} %fusion.12), channel_id=1, source_target_pairs={{0,16},{1,17},{2,18},{3,19},{4,20},{5,21},{6,22},{7,23},{8,24},{9,... | collective-permute-start | bytes 589832 | tf_op jit(solution)/shard_map/ppermute | solution.py:1281
  165.7 6.1 %collective-permute-start.32 = (bf16[128,768]{1,0:T(8,128)(2,1)S(1)}, bf16[128,768]{1,0:T(8,128)(2,1)S(1)}, u32[]{:S(2)}, u32[]{:S(2)}) collective-permute-start(bf16[128,768]{1,0:T(8,128)(2,1)S(1)} %get-tuple-element.95.refs_0_.refs_8_), channel_id=1, source_target_pairs={{0,16},{1,17},{2,18},{3,19},{4,20},{5,21},{6,22},{7,23},{8,24},{9,... | collective-permute-start | bytes 589832 | tf_op jit(solution)/shard_map/ppermute | solution.py:1281
  167.4 4.4 %collective-permute-start.31 = (bf16[128,768]{1,0:T(8,128)(2,1)S(1)}, bf16[128,768]{1,0:T(8,128)(2,1)S(1)}, u32[]{:S(2)}, u32[]{:S(2)}) collective-permute-start(bf16[128,768]{1,0:T(8,128)(2,1)S(1)} %get-tuple-element.95.refs_0_.refs_8_), channel_id=1, source_target_pairs={{0,8},{1,9},{2,10},{3,11},{4,12},{5,13},{6,14},{7,15},{8,0},{9,1},... | collective-permute-start | bytes 589832 | tf_op jit(solution)/shard_map/ppermute | solution.py:1281
  183.0 14.5 %collective-permute-start.34 = (bf16[4,128,768]{2,1,0:T(8,128)(2,1)S(1)}, bf16[4,128,768]{2,1,0:T(8,128)(2,1)S(1)}, u32[]{:S(2)}, u32[]{:S(2)}) collective-permute-start(bf16[4,128,768]{2,1,0:T(8,128)(2,1)S(1)} %get-tuple-element.100), channel_id=1, source_target_pairs={{0,8},{1,9},{2,10},{3,11},{4,12},{5,13},{6,14},{7,15},{8,0},{9,1},... | collective-permute-start | bytes 2359304 | tf_op jit(solution)/shard_map/ppermute | solution.py:1281
  183.2 7.2 %collective-permute-start.40 = (bf16[192,512]{1,0:T(8,128)(2,1)S(1)}, bf16[192,512]{1,0:T(8,128)(2,1)S(1)}, u32[]{:S(2)}, u32[]{:S(2)}) collective-permute-start(bf16[192,512]{1,0:T(8,128)(2,1)S(1)} %copy-done.31), channel_id=1, source_target_pairs={{0,16},{1,17},{2,18},{3,19},{4,20},{5,21},{6,22},{7,23},{8,24},{9,... | collective-permute-start | bytes 589832 | tf_op jit(solution)/shard_map/ppermute | solution.py:1281
  184.9 5.6 %collective-permute-start.39 = (bf16[192,512]{1,0:T(8,128)(2,1)S(1)}, bf16[192,512]{1,0:T(8,128)(2,1)S(1)}, u32[]{:S(2)}, u32[]{:S(2)}) collective-permute-start(bf16[192,512]{1,0:T(8,128)(2,1)S(1)} %copy-done.31), channel_id=1, source_target_pairs={{0,8},{1,9},{2,10},{3,11},{4,12},{5,13},{6,14},{7,15},{8,0},{9,1},... | collective-permute-start | bytes 589832 | tf_op jit(solution)/shard_map/ppermute | solution.py:1281
  196.1 19.0 %collective-permute-start.42 = (bf16[384,768]{1,0:T(8,128)(2,1)}, bf16[384,768]{1,0:T(8,128)(2,1)S(1)}, u32[]{:S(2)}, u32[]{:S(2)}) collective-permute-start(bf16[384,768]{1,0:T(8,128)(2,1)} %get-tuple-element.110), channel_id=1, source_target_pairs={{0,1},{1,0},{2,3},{3,2},{4,5},{5,4},{6,7},{7,6},{8,9},{9,8},{10,11... | collective-permute-start | bytes 1769480 | tf_op jit(solution)/shard_map/ppermute | solution.py:1281
  199.1 25.8 %collective-permute-start.35 = (bf16[128,768]{1,0:T(8,128)(2,1)}, bf16[128,768]{1,0:T(8,128)(2,1)}, u32[]{:S(2)}, u32[]{:S(2)}) collective-permute-start(bf16[128,768]{1,0:T(8,128)(2,1)} %fusion.13), channel_id=1, source_target_pairs={{0,16},{1,17},{2,18},{3,19},{4,20},{5,21},{6,22},{7,23},{8,9},{9,8... | collective-permute-start | bytes 589832 | tf_op jit(solution)/shard_map/ppermute | solution.py:1281
  217.2 11.4 %collective-permute-start.43 = (bf16[96,768]{1,0:T(8,128)(2,1)S(1)}, bf16[96,768]{1,0:T(8,128)(2,1)S(1)}, u32[]{:S(2)}, u32[]{:S(2)}) collective-permute-start(bf16[96,768]{1,0:T(8,128)(2,1)S(1)} %get-tuple-element.112), channel_id=1, source_target_pairs={{0,2},{1,3},{2,4},{3,5},{4,6},{5,7},{6,0},{7,1},{8,10},{9,11},{10,... | collective-permute-start | bytes 442376 | tf_op jit(solution)/shard_map/ppermute | solution.py:1281
  221.0 21.2 %collective-permute-start.44 = (bf16[96,768]{1,0:T(8,128)(2,1)}, bf16[96,768]{1,0:T(8,128)(2,1)}, u32[]{:S(2)}, u32[]{:S(2)}) collective-permute-start(bf16[96,768]{1,0:T(8,128)(2,1)} %get-tuple-element.113), channel_id=1, source_target_pairs={{0,4},{1,5},{2,6},{3,7},{4,0},{5,1},{6,2},{7,3},{8,12},{9,13},{10,... | collective-permute-start | bytes 442376 | tf_op jit(solution)/shard_map/ppermute | solution.py:1281
  221.9 20.3 %collective-permute-start.45 = (bf16[96,768]{1,0:T(8,128)(2,1)}, bf16[96,768]{1,0:T(8,128)(2,1)}, u32[]{:S(2)}, u32[]{:S(2)}) collective-permute-start(bf16[96,768]{1,0:T(8,128)(2,1)} %get-tuple-element.114), channel_id=1, source_target_pairs={{0,6},{1,7},{2,0},{3,1},{4,2},{5,3},{6,4},{7,5},{8,14},{9,15},{10,... | collective-permute-start | bytes 442376 | tf_op jit(solution)/shard_map/ppermute | solution.py:1281
  226.7 19.7 %collective-permute-start.36 = (bf16[128,768]{1,0:T(8,128)(2,1)}, bf16[128,768]{1,0:T(8,128)(2,1)S(1)}, u32[]{:S(2)}, u32[]{:S(2)}) collective-permute-start(bf16[128,768]{1,0:T(8,128)(2,1)} %get-tuple-element.177), channel_id=1, source_target_pairs={{0,16},{1,17},{2,18},{3,19},{4,20},{5,21},{6,22},{7,23},{8,24},{9,... | collective-permute-start | bytes 589832 | tf_op jit(solution)/shard_map/ppermute | solution.py:1281
  227.0 19.3 %collective-permute-start.37 = (bf16[128,768]{1,0:T(8,128)(2,1)}, bf16[128,768]{1,0:T(8,128)(2,1)}, u32[]{:S(2)}, u32[]{:S(2)}) collective-permute-start(bf16[128,768]{1,0:T(8,128)(2,1)} %get-tuple-element.176), channel_id=1, source_target_pairs={{0,1},{1,0},{2,3},{3,2},{4,5},{5,4},{6,7},{7,6},{8,9},{9,8},{10,11... | collective-permute-start | bytes 589832 | tf_op jit(solution)/shard_map/ppermute | solution.py:1281
  242.3 21.4 %collective-permute-start.50 = (bf16[96,1664]{1,0:T(8,128)(2,1)}, bf16[96,1664]{1,0:T(8,128)(2,1)}, u32[]{:S(2)}, u32[]{:S(2)}) collective-permute-start(bf16[96,1664]{1,0:T(8,128)(2,1)} %reduce-scatter.2.cloned.1.call-done.refs_0_), channel_id=1, source_target_pairs={{0,16},{1,17},{2,18},{3,19},{4,20},{5,21},{6,22},{7,23},{8,24},{9,... | collective-permute-start | bytes 958472 | tf_op jit(solution)/shard_map/ppermute | solution.py:1281
  244.2 10.9 %collective-permute-start.47 = (bf16[96,768]{1,0:T(8,128)(2,1)S(1)}, bf16[96,768]{1,0:T(8,128)(2,1)S(1)}, u32[]{:S(2)}, u32[]{:S(2)}) collective-permute-start(bf16[96,768]{1,0:T(8,128)(2,1)S(1)} %total.1.refs_0_), channel_id=1, source_target_pairs={{0,16},{1,17},{2,18},{3,19},{4,20},{5,21},{6,22},{7,23},{8,24},{9,... | collective-permute-start | bytes 442376 | tf_op jit(solution)/shard_map/ppermute | solution.py:1281
  250.5 4.5 %collective-permute-start.52 = (f32[96,128]{1,0:T(8,128)S(1)}, f32[96,128]{1,0:T(8,128)S(1)}, u32[]{:S(2)}, u32[]{:S(2)}) collective-permute-start(f32[96,128]{1,0:T(8,128)S(1)} %get-tuple-element.124), channel_id=1, source_target_pairs={{0,8},{1,9},{2,10},{3,11},{4,12},{5,13},{6,14},{7,15},{8,0},{9,1},... | collective-permute-start | bytes 147464 | tf_op jit(solution)/shard_map/ppermute | solution.py:1281
  250.5 18.0 %collective-permute-start.38 = (bf16[144,768]{1,0:T(8,128)(2,1)S(1)}, bf16[144,768]{1,0:T(8,128)(2,1)S(1)}, u32[]{:S(2)}, u32[]{:S(2)}) collective-permute-start(bf16[144,768]{1,0:T(8,128)(2,1)S(1)} %get-tuple-element.105), channel_id=1, source_target_pairs={{0,0},{1,1},{2,8},{3,9},{4,16},{5,17},{6,24},{7,25},{8,2},{9,3},{1... | collective-permute-start | bytes 663560 | tf_op jit(solution)/shard_map/ppermute | solution.py:1281
  252.7 11.4 %collective-permute-start.46 = (bf16[96,768]{1,0:T(8,128)(2,1)S(1)}, bf16[96,768]{1,0:T(8,128)(2,1)S(1)}, u32[]{:S(2)}, u32[]{:S(2)}) collective-permute-start(bf16[96,768]{1,0:T(8,128)(2,1)S(1)} %total.1.refs_0_), channel_id=1, source_target_pairs={{0,8},{1,9},{2,10},{3,11},{4,12},{5,13},{6,14},{7,15},{8,0},{9,1},... | collective-permute-start | bytes 442376 | tf_op jit(solution)/shard_map/ppermute | solution.py:1281
  255.1 10.8 %collective-permute-start.48 = (bf16[96,768]{1,0:T(8,128)(2,1)S(1)}, bf16[96,768]{1,0:T(8,128)(2,1)S(1)}, u32[]{:S(2)}, u32[]{:S(2)}) collective-permute-start(bf16[96,768]{1,0:T(8,128)(2,1)S(1)} %collective-permute-done.47.refs_2_), channel_id=1, source_target_pairs={{0,8},{1,9},{2,10},{3,11},{4,12},{5,13},{6,14},{7,15},{8,0},{9,1},... | collective-permute-start | bytes 442376 | tf_op jit(solution)/shard_map/ppermute | solution.py:1281
  263.6 11.1 %collective-permute-start.49 = (bf16[96,1664]{1,0:T(8,128)(2,1)S(1)}, bf16[96,1664]{1,0:T(8,128)(2,1)S(1)}, u32[]{:S(2)}, u32[]{:S(2)}) collective-permute-start(bf16[96,1664]{1,0:T(8,128)(2,1)S(1)} %copy-done.52), channel_id=1, source_target_pairs={{0,8},{1,9},{2,10},{3,11},{4,12},{5,13},{6,14},{7,15},{8,0},{9,1},... | collective-permute-start | bytes 958472 | tf_op jit(solution)/shard_map/ppermute | solution.py:1281
  263.6 11.1 %collective-permute-start.51 = (bf16[96,1664]{1,0:T(8,128)(2,1)}, bf16[96,1664]{1,0:T(8,128)(2,1)S(1)}, u32[]{:S(2)}, u32[]{:S(2)}) collective-permute-start(bf16[96,1664]{1,0:T(8,128)(2,1)} %collective-permute-done.50.refs_2_), channel_id=1, source_target_pairs={{0,8},{1,9},{2,10},{3,11},{4,12},{5,13},{6,14},{7,15},{8,0},{9,1},... | collective-permute-start | bytes 958472 | tf_op jit(solution)/shard_map/ppermute | solution.py:1281
  268.3 5.0 %collective-permute-start.56 = (f32[96,128]{1,0:T(8,128)S(1)}, f32[96,128]{1,0:T(8,128)S(1)}, u32[]{:S(2)}, u32[]{:S(2)}) collective-permute-start(f32[96,128]{1,0:T(8,128)S(1)} %add.238), channel_id=1, source_target_pairs={{0,4},{1,5},{2,6},{3,7},{4,0},{5,1},{6,2},{7,3},{8,12},{9,13},{10,... | collective-permute-start | bytes 147464 | tf_op jit(solution)/shard_map/ppermute | solution.py:1281
  (86 other events, 714.8 us)
Sparse Core Ops, SparseCore 0:
  12.1 53.9 all-gather.1
  154.6 87.6 reduce-scatter.1

commit v3 on v2

--- a/solution.py
+++ b/solution.py
@@ -16,8 +16,8 @@
 FLOOR_SCORE = -1e30
 HIGHEST = lax.Precision.HIGHEST
 AXES = ("seq", "frame")
-PLANE_OF = (0, 1, 2, 3)
-RANK_OF = (0, 1, 2, 3)
+PLANE_OF = (0, 2, 1, 3)
+RANK_OF = (0, 2, 1, 3)
 VMEM_LIMIT = 56 * 1024 * 1024
 BF = jnp.bfloat16
 F32 = jnp.float32
@@ -242,7 +242,7 @@
     total = convs[0]
     for block in convs[1:]:
         total = total + block
-    conv_ref[...] = total
+    conv_ref[...] = total[:, : conv_ref.shape[1]]
 
 
 def finish_qkv_kernel(ranks, quarter, rank_ref, *refs):
@@ -740,7 +740,7 @@
 PAD = 128
 
 
-def run(kernel, name, scalars, arrays, outs, scratch=(), limit=24):
+def run(kernel, name, scalars, arrays, outs, scratch=(), limit=16):
     vmem = pl.BlockSpec(memory_space=pltpu.VMEM)
     return pl.pallas_call(
         kernel,
@@ -784,31 +784,122 @@
     return result, column_sum(grad * normed), column_sum(grad)
 
 
-def norm_one_kernel(unused_ref, moved_ref, gains_ref, shifts_ref, low_ref):
+def pack_kernel(unused_ref, tokens_ref, grads_ref, clip_ref, pack_ref):
+    count, width = tokens_ref.shape
+    more = grads_ref.shape[0]
+    pack_ref[:count, :] = tokens_ref[...]
+    pack_ref[count : count + more, :] = grads_ref[...]
+    clips = clip_ref[...].astype(F32)
+    clips = jnp.concatenate([clips, jnp.zeros((1, PAD - clips.shape[1]), F32)], axis=1)
+    pack_ref[count + more :, :] = jnp.zeros((pack_ref.shape[0] - count - more, width), BF)
+    pack_ref[count + more :, :PAD] = jnp.broadcast_to(
+        clips, (pack_ref.shape[0] - count - more, PAD)
+    ).astype(BF)
+
+
+def select_kernel(ids_ref, qkv_ref, out_ref, own_ref):
+    width = out_ref.shape[1]
+    quarter = width // 4
+    for rank in range(4):
+
+        @pl.when(ids_ref[0] == rank)
+        def _(rank=rank):
+            pieces = [
+                qkv_ref[:, part * width + rank * quarter : part * width + (rank + 1) * quarter]
+                for part in range(3)
+            ]
+            pieces.append(out_ref[:, rank * quarter : (rank + 1) * quarter])
+            own_ref[...] = jnp.concatenate(pieces, axis=1)
+
+
+def prepare_kernel(ids_ref, up_ref, down_ref, conv_ref, own_ref, more_ref):
+    size = own_ref.shape[0]
+    unit = down_ref.shape[0] // 4
+    quarter = 8 * unit
+    for rank in range(4):
+
+        @pl.when(ids_ref[0] == rank)
+        def _(rank=rank):
+            own_ref[:, :quarter] = jnp.concatenate(
+                [
+                    up_ref[:, (4 * group + rank) * unit : (4 * group + rank + 1) * unit]
+                    for group in range(8)
+                ],
+                axis=1,
+            )
+            more_ref[...] = down_ref[rank * unit : (rank + 1) * unit, :]
+
+    taps = conv_ref.shape[1]
+    own_ref[:, quarter:] = jnp.concatenate(
+        [conv_ref[...], jnp.zeros((size, PAD - taps), BF)], axis=1
+    )
+
+
+def norm_one_kernel(ids_ref, moved_ref, gains_ref, shifts_ref, low_ref, qclip_ref, kclip_ref):
     count = low_ref.shape[0]
+    frames = count // (GRID * GRID)
+    patches = GRID * GRID
     normed, unused = norm_stats(moved_ref[:count, :].astype(F32))
     low_ref[...] = (normed * gains_ref[0:1, :] + shifts_ref[0:1, :]).astype(BF)
-
-
-def place_out_kernel(quarter, place_ref, *refs):
-    blocks = refs[:8]
-    own_ref, near_ref, others_ref, all_ref = refs[8:]
+    start = count + frames * CH
+    clips = moved_ref[start : start + 16, :PAD].astype(F32)[0:1]
+    lane = lax.broadcasted_iota(jnp.int32, (1, PAD), 1)
+    rank, low = ids_ref[0], ids_ref[2]
+    for side in range(2):
+        for bits in range(4):
+            for frame in range(frames):
+                hi = sum(jnp.where(rank ^ bits == RANK_OF[item], item, 0) for item in range(4))
+                wanted = (2 * hi + (low ^ side)) * frames + frame
+                clip = jnp.sum(jnp.where(lane == wanted, clips, 0.0), axis=1, keepdims=True)
+                first = ((4 * side + bits) * frames + frame) * patches
+                kclip_ref[first : first + patches, :] = jnp.broadcast_to(clip, (patches, 1))
+                if side == 0:
+                    qclip_ref[:, first : first + patches] = jnp.broadcast_to(clip, (1, patches))
+
+
+def pass_sum_kernel(index, unused_ref, even_ref, arrived_ref, out_ref):
+    out_ref[...] = (even_ref[index] + arrived_ref[...].astype(F32)).astype(BF)
+
+
+def add_kernel(unused_ref, left_ref, right_ref, out_ref):
+    out_ref[...] = left_ref[...] + right_ref[...]
+
+
+def pick_kernel(ids_ref, far_ref, side_ref, out_ref):
+    @pl.when(lax.rem(ids_ref[0], 2) == 0)
+    def _():
+        out_ref[...] = far_ref[...]
+
+    @pl.when(lax.rem(ids_ref[0], 2) == 1)
+    def _():
+        out_ref[...] = side_ref[...]
+
+
+def pass_on_kernel(ids_ref, even_ref, second_ref, third_ref, corner_ref, far_ref, side_ref):
+    core = lax.rem(ids_ref[0], 2)
+    corner = corner_ref[...].astype(F32)
+    far = even_ref[1] + second_ref[...].astype(F32)
+    side = even_ref[2] + third_ref[...].astype(F32)
+    far_ref[...] = (far + jnp.where(core == 1, corner, 0.0)).astype(BF)
+    side_ref[...] = (side + jnp.where(core == 0, corner, 0.0)).astype(BF)
+
+
+def place_of(ids_ref, bits):
+    return (2 * ids_ref[1] + ids_ref[2]) ^ bits
+
+
+def project_kernel(quarter, ids_ref, *refs):
+    tokens, blocks = refs[:8], refs[8:16]
+    q_ref, kv_ref, w_ref = refs[16:19]
+    out_refs, all_ref = refs[19:23], refs[23]
     size = blocks[0].shape[0]
-    for index in range(8):
-        all_ref[rows_at(place_ref[index], size), :] = blocks[index][:, 3 * quarter :]
-    rank = place_ref[8]
-    own_ref[...] = all_ref[rows_at(rank, quarter), :]
-    near_ref[...] = all_ref[rows_at(rank ^ 1, quarter), :]
-    others_ref[0] = all_ref[rows_at(rank ^ 2, quarter), :]
-    others_ref[1] = all_ref[rows_at(rank ^ 3, quarter), :]
-
-
-def project_kernel(quarter, place_ref, *refs):
-    tokens, blocks = refs[:8], refs[8:16]
-    q_ref, kv_ref, w_ref = refs[16:]
-    size = blocks[0].shape[0]
-    for index in range(8):
-        w_ref[rows_at(place_ref[index], size), :] = blocks[index][:, : 3 * quarter]
+    for bits in range(8):
+        where = rows_at(place_of(ids_ref, bits), size)
+        w_ref[where, :] = blocks[bits][:, : 3 * quarter]
+        all_ref[where, :] = blocks[bits][:, 3 * quarter :]
+    rank = ids_ref[0]
+    for bits in range(4):
+        out_refs[bits][...] = all_ref[rows_at(rank ^ bits, quarter), :]
     own = dot(stack_rows(tokens[:4]), w_ref[...]).astype(BF)
     q_ref[...] = own[:, :quarter]
     half = own.shape[0]
@@ -840,25 +931,25 @@
             log_ref[head : head + 1, queries] = top + jnp.log(total)
 
 
-def split_blocks(values, even_ref, odd_ref):
+def split_blocks(values, even_ref, odd_refs):
     rows = even_ref.shape[1]
     for part in range(even_ref.shape[0]):
         even_ref[part] = values[2 * part * rows : (2 * part + 1) * rows]
-        odd_ref[part] = values[(2 * part + 1) * rows : (2 * part + 2) * rows].astype(BF)
+        odd_refs[part][...] = values[(2 * part + 1) * rows : (2 * part + 2) * rows].astype(BF)
 
 
 def out_kernel(rank_ref, *refs):
-    mixed_ref, own_ref, near_ref, others_ref, both_ref = refs[:5]
-    even_ref, odd_ref, w_ref = refs[5:]
-    blocks = [own_ref[...], near_ref[...], others_ref[0], both_ref[...]]
+    mixed_ref = refs[0]
+    even_ref, odd_refs, w_ref = refs[5], refs[6:8], refs[8]
+    blocks = [ref[...] for ref in refs[1:5]]
     rank = rank_ref[0]
-    width = own_ref.shape[0]
+    width = blocks[0].shape[0]
     for index in range(4):
         found = blocks[0]
         for bits in range(1, 4):
             found = jnp.where(rank == index ^ bits, blocks[bits], found)
         w_ref[:, index * width : (index + 1) * width] = found
-    split_blocks(dot(mixed_ref[...], w_ref[...], 0, 0), even_ref, odd_ref)
+    split_blocks(dot(mixed_ref[...], w_ref[...], 0, 0), even_ref, odd_refs)
 
 
 def norm_two_kernel(unused_ref, *refs):
@@ -868,7 +959,7 @@
     values = (
         moved_ref[:count, :].astype(F32)
         + even_ref[0]
-        + arrived_ref[0].astype(F32)
+        + arrived_ref[...].astype(F32)
         + far_ref[...].astype(F32)
     )
     sum_ref[...] = values
@@ -890,32 +981,53 @@
     return values * below, below + values * bell * 0.3989422804014327
 
 
-def mlp_kernel(low_ref, *refs):
+def join_kernel(unused_ref, *refs):
+    for index, ref in enumerate(refs[4:]):
+        size = ref.shape[0] // 2
+        ref[:size, :] = refs[2 * index][...]
+        ref[size:, :] = refs[2 * index + 1][...]
+
+
+def mlp_kernel(ids_ref, *refs):
     tokens = refs[:4]
-    own_ref, side_ref, bias_ref = refs[4:7]
-    act_ref, slope_ref, up_ref, down_ref, conv_ref, even_ref, odd_ref = refs[7:]
-    low = low_ref[0]
-    size = own_ref.shape[0] // 4
+    a_refs, b_refs, bias_ref = refs[4:6], refs[6:8], refs[8]
+    act_ref, slope_ref, up_ref, down_ref, conv_ref, even_ref = refs[9:15]
+    odd_refs = refs[15:]
+    rank = ids_ref[0]
+    size = a_refs[0].shape[0] // 4
     quarter = up_ref.shape[1]
-    width = down_ref.shape[1]
-    for hi in range(4):
-        rows = slice(hi * size, (hi + 1) * size)
-        for ref, place in ((own_ref, 2 * hi + low), (side_ref, 2 * hi + 1 - low)):
-            where = rows_at(place, size)
+    for ref, order in zip(a_refs, ((0, 4, 2, 6), (1, 5, 3, 7))):
+        for index, bits in enumerate(order):
+            where = rows_at(place_of(ids_ref, bits), size)
+            rows = slice(index * size, (index + 1) * size)
             up_ref[where, :] = ref[rows, :quarter]
-            down_ref[where, :] = ref[rows, quarter : quarter + width]
-            conv_ref[where, :] = ref[rows, quarter + width :]
+            conv_ref[where, :] = ref[rows, quarter:]
+    for ref, order in zip(b_refs, ((0, 1, 4, 5), (2, 3, 6, 7))):
+        for index, bits in enumerate(order):
+            where = rows_at(place_of(ids_ref, bits), size)
+            down_ref[where, :] = ref[index * size : (index + 1) * size, :]
     count = tokens[0].shape[0]
+    unit = quarter // 8
+    bias = None
+    for index in range(4):
+        found = jnp.concatenate(
+            [
+                bias_ref[:, (4 * group + index) * unit : (4 * group + index + 1) * unit]
+                for group in range(8)
+            ],
+            axis=1,
+        )
+        bias = found if bias is None else jnp.where(rank == index, found, bias)
     for part in range(2):
         rows = slice(2 * part * count, 2 * (part + 1) * count)
-        pre = dot(stack_rows(tokens[2 * part : 2 * part + 2]), up_ref[...]) + bias_ref[...]
+        pre = dot(stack_rows(tokens[2 * part : 2 * part + 2]), up_ref[...]) + bias
         act, slope = gelu_both(pre)
         act = act.astype(BF)
         act_ref[rows, :] = act
         slope_ref[rows, :] = slope
         partial = dot(act, down_ref[...])
         even_ref[part] = partial[:count]
-        odd_ref[part] = partial[count:].astype(BF)
+        odd_refs[part][...] = partial[count:].astype(BF)
 
 
 def grid_masks(count):
@@ -975,7 +1087,7 @@
     value = (
         sum_ref[...]
         + even_ref[0]
-        + arrived_ref[0].astype(F32)
+        + arrived_ref[...].astype(F32)
         + far_ref[...].astype(F32)
         + bias_ref[...]
     )
@@ -1043,7 +1155,8 @@
 def mlp_back_kernel(unused_ref, *refs):
     grads = refs[:4]
     slope_ref, up_ref, down_ref = refs[4:7]
-    pre_ref, even_ref, odd_ref, bias_ref = refs[7:]
+    pre_ref, even_ref, bias_ref = refs[7], refs[8], refs[11]
+    odd_refs = refs[9:11]
     count = grads[0].shape[0]
     total = None
     for part in range(2):
@@ -1055,26 +1168,41 @@
         total = term if total is None else total + term
         partial = dot(grad_pre, up_ref[...], 1, 1)
         even_ref[part] = partial[:count]
-        odd_ref[part] = partial[count:].astype(BF)
+        odd_refs[part][...] = partial[count:].astype(BF)
     bias_ref[...] = total
 
 
-def mlp_grads_kernel(unused_ref, *refs):
+def divide_rows(ids_ref, all_ref, refs):
+    kept_ref, sent_ref, more_kept_ref, more_sent_ref = refs
+    high, low = ids_ref[1], ids_ref[2]
+    size = all_ref.shape[0] // 8
+    columns = kept_ref.shape[1]
+    for index in range(4):
+        rows = slice(index * size, (index + 1) * size)
+        kept_ref[rows, :] = all_ref[rows_at(2 * index + low, size), :columns]
+        sent_ref[rows, :] = all_ref[rows_at(2 * index + 1 - low, size), :columns].astype(BF)
+        hi = high ^ (index // 2 * 2)
+        lo = low ^ (index % 2)
+        more_kept_ref[rows, :] = all_ref[rows_at(2 * hi + lo, size), columns:]
+        more_sent_ref[rows, :] = all_ref[rows_at(2 * (hi ^ 1) + lo, size), columns:].astype(BF)
+
+
+def mlp_grads_kernel(ids_ref, *refs):
     tokens, grads = refs[:4], refs[4:8]
-    act_ref, pre_ref, normed_ref, spread_ref, pack_ref = refs[8:]
+    act_ref, pre_ref, normed_ref, spread_ref = refs[8:12]
+    all_ref = refs[16]
     quarter = act_ref.shape[1]
     width = tokens[0].shape[1]
-    pack_ref[:, :quarter] = dot(stack_rows(tokens), pre_ref[...], 0, 0).astype(BF)
-    pack_ref[:, quarter : quarter + width] = dot(
-        act_ref[...], stack_rows(grads), 0, 0
-    ).astype(BF)
-    pack_ref[:, quarter + width :] = dot(normed_ref[...], spread_ref[...], 0, 0).astype(BF)
+    all_ref[:, :quarter] = dot(stack_rows(tokens), pre_ref[...], 0, 0)
+    all_ref[:, quarter : quarter + width] = dot(act_ref[...], stack_rows(grads), 0, 0)
+    all_ref[:, quarter + width :] = dot(normed_ref[...], spread_ref[...], 0, 0)
+    divide_rows(ids_ref, all_ref, refs[12:16])
 
 
 def norm_two_back_kernel(unused_ref, *refs):
     sum_ref, grad_ref, even_ref, arrived_ref, far_ref, gains_ref = refs[:6]
     total_ref, low_ref, rows_ref = refs[6:]
-    grad_normed = even_ref[0] + arrived_ref[0].astype(F32) + far_ref[...].astype(F32)
+    grad_normed = even_ref[0] + arrived_ref[...].astype(F32) + far_ref[...].astype(F32)
     result, gain_row, shift_row = back_of_norm(sum_ref[...], gains_ref[1:2, :], grad_normed)
     total = result + grad_ref[...]
     total_ref[...] = total
@@ -1086,7 +1214,8 @@
 def attend_back_out_kernel(heads, scale, unused_ref, *refs):
     branches = refs[:4]
     out_ref, q_ref, kv_ref, log_ref, qclip_ref, kclip_ref, w_ref = refs[4:11]
-    own_ref, other_ref, even_ref, odd_ref, total_ref = refs[11:]
+    own_ref, other_ref, even_ref = refs[11:14]
+    odd_refs, total_ref = refs[14:18], refs[18]
     width = heads * HEAD_DIM
     count = q_ref.shape[0] // 2
     rows = count // 2
@@ -1118,24 +1247,19 @@
     other_ref[...] = total_ref[2 * count :, :].astype(BF)
     own = dot(own_ref[...], w_ref[...], 1, 1)
     other = dot(other_ref[...], w_ref[:, width:], 1, 1)
-    for part in range(2):
-        even_ref[part] = own[2 * part * rows : (2 * part + 1) * rows]
-        odd_ref[part] = own[(2 * part + 1) * rows : (2 * part + 2) * rows].astype(BF)
-        even_ref[part + 2] = other[2 * part * rows : (2 * part + 1) * rows]
-        odd_ref[part + 2] = other[(2 * part + 1) * rows : (2 * part + 2) * rows].astype(BF)
-
-
-def qkv_grads_kernel(place_ref, *refs):
+    split_blocks(jnp.concatenate([own, other], axis=0), even_ref, odd_refs)
+
+
+def qkv_grads_kernel(ids_ref, *refs):
     tokens, branches, mixes = refs[:8], refs[8:12], refs[12:16]
-    own_ref, other_ref, kept_ref, sent_ref, all_ref = refs[16:]
+    own_ref, other_ref = refs[16:18]
+    all_ref = refs[22]
     quarter = mixes[0].shape[0]
-    size = all_ref.shape[0] // 8
     full = dot(stack_rows(tokens[:4]), own_ref[...], 0, 0)
     more = dot(stack_rows(tokens[4:]), other_ref[...], 0, 0)
     all_ref[:, :quarter] = full[:, :quarter]
     all_ref[:, quarter : 3 * quarter] = full[:, quarter:] + more
-    rank = place_ref[0]
-    low = place_ref[1]
+    rank = ids_ref[0]
     branch = stack_rows(branches)
     wanted = branch[:, :quarter]
     for index in range(1, 4):
@@ -1149,28 +1273,36 @@
             axis=0,
         )
         all_ref[rows_at(rank ^ bits, quarter), 3 * quarter :] = dot(mixes[bits][...], turned)
-    for hi in range(4):
-        rows = slice(hi * size, (hi + 1) * size)
-        kept_ref[rows, :] = all_ref[rows_at(2 * hi + low, size), :]
-        sent_ref[rows, :] = all_ref[rows_at(2 * hi + 1 - low, size), :].astype(BF)
-
-
-def half_kernel(high_ref, kept_ref, arrived_ref, own_ref, *refs):
-    size = own_ref.shape[0]
-    for step in range(4):
-        where = rows_at(lax.rem(high_ref[0] + step, 4), size)
-        total = kept_ref[where, :] + arrived_ref[where, :].astype(F32)
-        if step == 0:
-            own_ref[...] = total
-        else:
-            refs[step - 1][...] = total.astype(BF)
-
-
-def total_kernel(unused_ref, kept_ref, *refs):
-    total = kept_ref[...]
-    for ref in refs[:-1]:
-        total = total + ref[...].astype(F32)
-    refs[-1][...] = total.astype(BF)
+    divide_rows(ids_ref, all_ref, refs[18:22])
+
+
+def half_kernel(ids_ref, *refs):
+    kept_ref, arrived_ref, more_kept_ref, more_arrived_ref = refs[:4]
+    own_ref, sent_ref, more_own_ref, more_sent_ref = refs[4:]
+    size = own_ref.shape[0] // 2
+    high = ids_ref[1]
+    for step in range(2):
+        rows = slice(step * size, (step + 1) * size)
+        where = rows_at(high ^ (2 * step), size)
+        own_ref[rows, :] = kept_ref[where, :] + arrived_ref[where, :].astype(F32)
+        where = rows_at(high ^ (2 * step + 1), size)
+        sent_ref[rows, :] = (kept_ref[where, :] + arrived_ref[where, :].astype(F32)).astype(BF)
+    more = more_kept_ref[...] + more_arrived_ref[...].astype(F32)
+    more_own_ref[...] = more[: 2 * size]
+    more_sent_ref[...] = more[2 * size :].astype(BF)
+
+
+def fourth_kernel(unused_ref, *refs):
+    for kept_ref, arrived_ref, own_ref, sent_ref in (refs[0:2] + refs[4:6], refs[2:4] + refs[6:8]):
+        size = own_ref.shape[0]
+        own_ref[...] = kept_ref[:size, :] + arrived_ref[:size, :].astype(F32)
+        sent_ref[...] = (kept_ref[size:, :] + arrived_ref[size:, :].astype(F32)).astype(BF)
+
+
+def total_kernel(unused_ref, kept_ref, arrived_ref, more_kept_ref, more_arrived_ref, out_ref):
+    columns = kept_ref.shape[1]
+    out_ref[:, :columns] = (kept_ref[...] + arrived_ref[...].astype(F32)).astype(BF)
+    out_ref[:, columns:] = (more_kept_ref[...] + more_arrived_ref[...].astype(F32)).astype(BF)
 
 
 def norm_one_back_kernel(vectors, rank_ref, *refs):
@@ -1179,7 +1311,7 @@
     count = grad_ref.shape[0]
     grad_normed = (
         even_ref[0]
-        + arrived_ref[0].astype(F32)
+        + arrived_ref[...].astype(F32)
         + far_ref[...].astype(F32)
         + side_ref[...].astype(F32)
     )
@@ -1201,7 +1333,16 @@
         )
 
 
-def unpack_kernel(vectors, unused_ref, sums_ref, *refs):
+def back_kernel(unused_ref, moved_ref, grad_ref, learned_ref):
+    count = grad_ref.shape[0]
+    grad_ref[...] = moved_ref[:count, :].astype(F32)
+    learned_ref[...] = moved_ref[count:, :].astype(F32)
+
+
+def unpack_kernel(vectors, unused_ref, part_ref, arrived_ref, *refs):
+    sums_ref = refs[-1]
+    refs = refs[:-1]
+    sums_ref[...] = part_ref[...] + arrived_ref[...]
     gains_ref, shifts_ref, up_ref, down_ref, first_ref, mid_ref, mid_bias_ref = refs
     for index in range(3):
         gains_ref[index : index + 1, :] = load_rows(sums_ref, index * vectors, vectors)
@@ -1258,13 +1399,8 @@
     size = width // frame_size
     vectors = width // PAD
     own_count = ranks * rows
-    rank = lax.axis_index("seq")
     place = lax.axis_index("frame")
-    high = place // lows
-    low = place % lows
-    core = rank % 2
-    rank_one = rank.reshape(1)
-    low_one = low.reshape(1)
+    ids = jnp.stack([lax.axis_index("seq"), place // lows, place % lows])
 
     def permute(array, target):
         pairs = []
@@ -1288,6 +1424,15 @@
     def after(array, *others):
         return lax.optimization_barrier((array,) + others)[0]
 
+    last = []
+
+    def ordered_run(kernel, name, scalars, arrays, outs, scratch=()):
+        if last:
+            arrays = [after(arrays[0], last[0])] + list(arrays[1:])
+        results = run(kernel, name, scalars, arrays, outs, scratch)
+        last[:] = [results[-1]]
+        return results
+
     def to_planes(array):
         return permute(array, lambda seq, hi, lo: (RANK_OF[hi], PLANE_OF[seq], lo))
 
@@ -1301,167 +1446,182 @@
         near = flip(block, 1)
         return [block, near, far, flip(far, 1)]
 
-    def gather_eight(block):
-        far = flip(block, 2)
-        side = flip(block, 0, 0, 1)
-        near = flip(block, 1)
-        corner = permute(
-            jnp.where(core == 0, far, side),
-            lambda seq, hi, lo: (seq, hi, lo ^ 1) if seq % 2 == 0 else (seq ^ 2, hi, lo),
-        )
+    def pass_sum(even, arrived, index, name):
+        (result,) = ordered_run(
+            functools.partial(pass_sum_kernel, index),
+            name,
+            ids,
+            [even, arrived],
+            [((rows, width), BF)],
+        )
+        return result
+
+    def scatter_four(even, odds, name):
+        far = flip(pass_sum(even, flip(odds[1], 1), 1, name), 2)
+        return flip(odds[0], 1), far
+
+    def row_parts(blocks, first, second):
         return [
-            block,
-            near,
-            far,
-            flip(far, 1),
-            side,
-            flip(side, 1),
-            corner,
-            flip(corner, 1),
+            ((blocks * size, columns), kind) for columns in (first, second) for kind in (F32, BF)
         ]
 
-    def scatter_four(even, odd):
-        arrived = flip(odd, 1)
-        far = flip((even[1] + arrived[1].astype(F32)).astype(BF), 2)
-        return arrived, far
-
-    def scatter_eight(even, odd):
-        arrived = flip(odd, 1)
-        corner = permute(
-            (even[3] + arrived[3].astype(F32)).astype(BF),
-            lambda seq, hi, lo: (seq ^ 2, hi, lo) if seq % 2 == 0 else (seq, hi, lo ^ 1),
-        ).astype(F32)
-        far = even[1] + arrived[1].astype(F32) + jnp.where(core == 1, corner, 0.0)
-        side = even[2] + arrived[2].astype(F32) + jnp.where(core == 0, corner, 0.0)
-        return arrived, flip(far.astype(BF), 2), flip(side.astype(BF), 0, 0, 1)
-
-    moved = to_planes(
-        jnp.concatenate(
-            [
-                inputs[0].reshape(rows, width),
-                cotangent[0].reshape(learned_rows, width),
-                jnp.pad(clip_id.astype(BF), ((0, 15), (0, width - clip_id.shape[1]))),
-            ],
-            axis=0,
-        )
-    )
-    frame_count = clip_id.shape[1]
-    clips = moved[rows + learned_rows, :frame_count].astype(jnp.int32)
-
-    own_pack = jnp.concatenate(
-        [
-            lax.dynamic_slice_in_dim(w_qkv, part * width + rank * quarter, quarter, 1)
-            for part in range(3)
-        ]
-        + [lax.dynamic_slice_in_dim(w_out, rank * quarter, quarter, 1)],
-        axis=1,
-    )
-    packs = [own_pack] + [flip(own_pack, 0, bits // 2, bits % 2) for bits in range(1, 8)]
-    places = [place ^ bits for bits in range(8)]
-
-    columns = jnp.arange(hidden_quarter, dtype=jnp.int32)
-    wanted = (columns // unit) * (unit * ranks) + rank * unit + columns % unit
-    choose = (jnp.arange(hidden, dtype=jnp.int32)[:, None] == wanted[None, :]).astype(BF)
-    own_mlp = jnp.concatenate(
-        [
-            dot(w_up, choose).astype(BF),
-            lax.dynamic_slice_in_dim(w_down, rank * unit, unit, 0),
-            conv_first,
-            jnp.zeros((size, PAD - 9 * CH), BF),
-        ],
-        axis=1,
-    )
-    mlp_own = lax.all_gather(
-        own_mlp,
-        "frame",
-        axis=0,
-        tiled=True,
-        axis_index_groups=[[hi * lows + lo for hi in range(ranks)] for lo in range(lows)],
-    )
-    mlp_side = flip(mlp_own, 0, 0, 1)
-    up_bias_own = lax.dynamic_index_in_dim(
-        up_bias.reshape(frame_size, ranks, unit), rank, 1, False
-    ).reshape(1, hidden_quarter)
+    def scatter_half(parts, name):
+        kept, sent, more_kept, more_sent = parts
+        return ordered_run(
+            half_kernel,
+            name,
+            ids,
+            [kept, flip(sent, 0, 0, 1), more_kept, flip(more_sent, 0, 1)],
+            row_parts(2, kept.shape[1], more_kept.shape[1]),
+        )
+
+    def scatter_fourth(parts, name):
+        kept, sent, more_kept, more_sent = parts
+        return ordered_run(
+            fourth_kernel,
+            name,
+            ids,
+            [kept, flip(sent, 0, 1), more_kept, flip(more_sent, 0, 2)],
+            row_parts(1, kept.shape[1], more_kept.shape[1]),
+        )
+
+    def scatter_last(parts, name):
+        kept, sent, more_kept, more_sent = parts
+        (share,) = ordered_run(
+            total_kernel,
+            name,
+            ids,
+            [kept, flip(sent, 0, 2), more_kept, flip(more_sent, 0, 0, 1)],
+            [((size, kept.shape[1] + more_kept.shape[1]), BF)],
+        )
+        return share
+
+    def add(left, right, name):
+        return ordered_run(add_kernel, name, ids, [left, right], [(left.shape, F32)])[0]
+
+    (pack,) = ordered_run(
+        pack_kernel,
+        "pack",
+        ids,
+        [inputs.reshape(rows, width), cotangent.reshape(learned_rows, width), clip_id],
+        [((rows + learned_rows + 16, width), BF)],
+    )
+    moved = to_planes(pack)
+
+    (own_pack,) = ordered_run(
+        select_kernel, "select", ids, [w_qkv, w_out], [((size, width), BF)]
+    )
+    pack_two = flip(own_pack, 0, 2)
+    pack_one = flip(own_pack, 0, 1)
+    pack_side = flip(own_pack, 0, 0, 1)
+    pack_three = flip(pack_two, 0, 1)
+    packs = [own_pack, pack_side]
+    for item in (pack_one, pack_two, pack_three):
+        packs += [item, flip(item, 0, 0, 1)]
+
+    low_norm, query_clip, key_clip = ordered_run(
+        norm_one_kernel,
+        "norm_one",
+        ids,
+        [moved, ln_gains, ln_biases],
+        [((rows, width), BF), ((1, own_count), F32), ((2 * own_count, 1), F32)],
+    )
+    low_norm = after(low_norm, pack_side, pack_one, pack_two)
 
     mid_pad = jnp.pad(conv_mid, ((0, 0), (0, PAD - CH), (0, PAD - 9 * CH)))
     mid_bias_pad = jnp.pad(conv_mid_bias, ((0, 0), (0, PAD - CH)))
     first_bias_pad = jnp.pad(conv_first_bias, (0, PAD - CH)).reshape(1, PAD)
-
-    frame_ids = jnp.arange(frame_count, dtype=jnp.int32)
-    inverse = jnp.array([RANK_OF.index(item) for item in range(ranks)], jnp.int32)
-
-    def clip_tokens(lo):
-        blocks = []
-        for bits in range(ranks):
-            hi = lax.dynamic_index_in_dim(inverse, rank ^ bits, 0, False)
-            for frame in range(frames_dev):
-                blocks.append((hi * lows + lo) * frames_dev + frame)
-        found = jnp.sum(
-            jnp.where(jnp.stack(blocks)[:, None] == frame_ids[None, :], clips[None, :], 0),
-            axis=1,
-        )
-        return jnp.broadcast_to(found[:, None], (found.shape[0], patches)).reshape(-1)
-
-    query_clip = clip_tokens(low)
-    key_clip = jnp.concatenate([query_clip, clip_tokens(1 - low)])[:, None]
-    query_clip = query_clip[None, :]
-
-    (low_one_norm,) = run(
-        norm_one_kernel, "norm_one", low_one, [moved, ln_gains, ln_biases], [((rows, width), BF)]
-    )
-    all_one = gather_eight(after(low_one_norm, own_mlp))
-    own_out, near_out, other_out = run(
-        functools.partial(place_out_kernel, quarter),
-        "place_out",
-        jnp.stack(places + [rank]),
-        packs,
-        [((quarter, quarter), BF)] * 2 + [((2, quarter, quarter), BF)],
-        [pltpu.VMEM((width, quarter), BF)],
-    )
-    other_out = flip(other_out, 2)
-    near_out = flip(near_out, 1)
-    both_out = flip(other_out[1], 1)
-    queries, keyvals, qkv_quarter = run(
+    up_bias_row = up_bias.reshape(1, hidden)
+    down_bias_row = down_bias.reshape(1, width)
+
+    own_a, own_b = ordered_run(
+        prepare_kernel,
+        "prepare",
+        ids,
+        [
+            after(w_up, mid_pad, mid_bias_pad, first_bias_pad, up_bias_row, down_bias_row),
+            w_down,
+            conv_first,
+        ],
+        [((size, hidden_quarter + PAD), BF), ((size, width), BF)],
+    )
+
+    def join(pairs, name):
+        flat = [item for pair in pairs for item in pair]
+        outs = [((2 * pair[0].shape[0], pair[0].shape[1]), BF) for pair in pairs]
+        return ordered_run(join_kernel, name, ids, flat, outs)
+
+    far = flip(low_norm, 2)
+    side = flip(low_norm, 0, 0, 1)
+    near = flip(low_norm, 1)
+    (picked,) = ordered_run(
+        pick_kernel,
+        "pick",
+        ids,
+        [after(far, *[packs[item] for item in (3, 5, 6)]), side],
+        [((rows, width), BF)],
+    )
+    corner = permute(
+        picked,
+        lambda seq, hi, lo: (seq, hi, lo ^ 1) if seq % 2 == 0 else (seq ^ 2, hi, lo),
+    )
+    far_near = flip(far, 1)
+    side_near = flip(side, 1)
+    corner = after(corner, near, far_near, side_near, packs[7])
+    all_one = [near, far, far_near, side, side_near, corner, flip(corner, 1)]
+    all_one = [low_norm] + all_one
+    two_a, two_b = join(
+        [(own_a, flip(own_a, 0, 2)), (own_b, flip(own_b, 0, 0, 1))], "join_two"
+    )
+
+    queries, keyvals, qkv_quarter, own_out, near_out, far_out, both_out = ordered_run(
         functools.partial(project_kernel, quarter),
         "project",
-        jnp.stack(places),
+        ids,
         all_one + packs,
         [
             ((own_count, quarter), BF),
             ((2 * own_count, 2 * quarter), BF),
             ((width, 3 * quarter), BF),
-        ],
-    )
+        ]
+        + [((quarter, quarter), BF)] * 4,
+        [pltpu.VMEM((width, quarter), BF)],
+    )
+    out_blocks = [own_out, flip(near_out, 1), flip(far_out, 2), flip(both_out, 3)]
     scale = HEAD_DIM ** (-0.5)
-    attended, logs = run(
+    attended, logs = ordered_run(
         functools.partial(attend_wide_kernel, heads, scale),
         "attend",
-        rank_one,
+        ids,
         [queries, keyvals, query_clip, key_clip],
         [((quarter, own_count), BF), ((8, own_count), F32)],
     )
-    halves = [((2, rows, width), F32), ((2, rows, width), BF)]
-    even, odd, out_quarter = run(
+    halves = [((2, rows, width), F32)] + [((rows, width), BF)] * 2
+    even, *odds, out_quarter = ordered_run(
         out_kernel,
         "out",
-        rank_one,
-        [attended, own_out, near_out, other_out, both_out],
+        ids,
+        [attended] + out_blocks,
         halves + [((quarter, width), BF)],
     )
-    arrived, far = scatter_four(even, odd)
-    after_attention, low_two = run(
+    arrived, far = scatter_four(even, odds, "out_pass")
+    four_a, four_b = join(
+        [(two_a, flip(two_a, 0, 1)), (two_b, flip(two_b, 0, 2))], "join_four"
+    )
+    after_attention, low_two = ordered_run(
         norm_two_kernel,
         "norm_two",
-        low_one,
+        ids,
         [moved, even, arrived, far, ln_gains, ln_biases],
         [((rows, width), F32), ((rows, width), BF)],
     )
     all_two = gather_four(low_two)
-    act, slope, up_full, down_full, conv_full, even, odd = run(
+    act, slope, up_full, down_full, conv_full, even, *odds = ordered_run(
         mlp_kernel,
         "mlp",
-        low_one,
-        all_two + [mlp_own, mlp_side, up_bias_own],
+        ids,
+        all_two
+        + [four_a, flip(four_a, 0, 0, 1), four_b, flip(four_b, 0, 1), up_bias_row],
         [
             ((own_count, hidden_quarter), BF),
             ((own_count, hidden_quarter), F32),
@@ -1471,19 +1631,19 @@
         ]
         + halves,
     )
-    arrived, far = scatter_four(even, odd)
+    arrived, far = scatter_four(even, odds, "mlp_pass")
 
     small_rows = -(-(11 * vectors + 3 * CH + 4) // 8) * 8
-    learned, low_mlp, grad_block, low_three, spread, small = run(
+    learned, low_mlp, grad_block, low_three, spread, small = ordered_run(
         functools.partial(tail_kernel, vectors),
         "tail",
-        low_one,
+        ids,
         [
             after_attention,
             even,
             arrived,
             far,
-            down_bias.reshape(1, width),
+            down_bias_row,
             ln_gains,
             ln_biases,
             conv_full,
@@ -1504,116 +1664,133 @@
     mixes = gather_four(after(attended, far))
 
     all_mlp = gather_four(low_mlp)
-    grad_pre, even, odd, grad_up_bias = run(
+    grad_pre, even, *odds, grad_up_bias = ordered_run(
         mlp_back_kernel,
         "mlp_back",
-        low_one,
-        all_mlp + [slope, up_full, down_full],
+        ids,
+        all_mlp + [after(slope, *mixes), up_full, down_full],
         [((own_count, hidden_quarter), BF)] + halves + [((1, hidden_quarter), F32)],
     )
-    (mlp_grads,) = run(
+    arrived, far = scatter_four(even, odds, "mlp_back_pass")
+    columns = hidden_quarter + width + PAD
+    mlp_parts = ordered_run(
         mlp_grads_kernel,
         "mlp_grads",
-        low_one,
+        ids,
         all_two + all_mlp + [act, grad_pre, low_three, spread],
-        [((width, hidden_quarter + width + PAD), BF)],
-    )
-    mlp_share = lax.psum_scatter(mlp_grads, "frame", scatter_dimension=0, tiled=True)
-    arrived, far = scatter_four(even, odd)
-    grad_after, low_branch, rows_two = run(
+        row_parts(4, hidden_quarter, width + PAD),
+        [pltpu.VMEM((width, columns), F32)],
+    )
+    grad_after, low_branch, rows_two = ordered_run(
         norm_two_back_kernel,
         "norm_two_back",
-        low_one,
+        ids,
         [after_attention, grad_block, even, arrived, far, ln_gains],
         [((rows, width), F32), ((rows, width), BF), ((2, width), F32)],
     )
 
     all_branch = gather_four(low_branch)
-    grads_own, grads_other, even, odd = run(
+    grads_own, grads_other, even, *odds = ordered_run(
         functools.partial(attend_back_out_kernel, heads, scale),
         "attend_back_out",
-        low_one,
+        ids,
         all_branch + [out_quarter, queries, keyvals, logs, query_clip, key_clip, qkv_quarter],
         [
             ((own_count, 3 * quarter), BF),
             ((own_count, 2 * quarter), BF),
             ((4, rows, width), F32),
-            ((4, rows, width), BF),
-        ],
+        ]
+        + [((rows, width), BF)] * 4,
         [pltpu.VMEM((2 * own_count, 2 * quarter), F32)],
     )
-    kept, sent = run(
+    arrived = [flip(item, 1) for item in odds]
+    corner = permute(
+        pass_sum(even, arrived[3], 3, "corner_pass"),
+        lambda seq, hi, lo: (seq ^ 2, hi, lo) if seq % 2 == 0 else (seq, hi, lo ^ 1),
+    )
+    mlp_parts = scatter_half(mlp_parts, "mlp_half")
+    qkv_parts = ordered_run(
         qkv_grads_kernel,
         "qkv_grads",
-        jnp.stack([rank, low]),
+        ids,
         all_one + all_branch + mixes + [grads_own, grads_other],
-        [((width // 2, width), F32), ((width // 2, width), BF)],
+        row_parts(4, width // 2, width // 2),
         [pltpu.VMEM((width, width), F32)],
     )
-    arrived, far, side = scatter_eight(even, odd)
-    moved_back, sums = run(
+    far, side = ordered_run(
+        pass_on_kernel,
+        "pass_on",
+        ids,
+        [even, arrived[1], arrived[2], corner],
+        [((rows, width), BF), ((rows, width), BF)],
+    )
+    far, side = flip(far, 2), flip(side, 0, 0, 1)
+    mlp_parts = scatter_fourth(mlp_parts, "mlp_fourth")
+    qkv_parts = list(lax.optimization_barrier(tuple(qkv_parts) + (mlp_parts[0],))[:4])
+    moved_back, sums = ordered_run(
         functools.partial(norm_one_back_kernel, vectors),
         "norm_one_back",
-        rank_one,
-        [moved, grad_after, even, arrived, far, side, ln_gains]
+        ids,
+        [moved, grad_after, even, arrived[0], far, side, ln_gains]
         + [learned, small, rows_two, grad_up_bias],
         [((rows + learned_rows, width), BF), ((small_rows, PAD), F32)],
     )
-    moved_back = from_planes(moved_back).astype(F32)
-
-    own_half, *pieces = run(
-        half_kernel,
-        "half",
-        high.reshape(1),
-        [kept, flip(sent, 0, 0, 1)],
-        [((size, width), F32)] + [((size, width), BF)] * 3,
-    )
-    pieces = [
-        permute(piece, lambda seq, hi, lo, step=step: (seq, (hi + step) % ranks, lo))
-        for step, piece in enumerate(pieces, 1)
-    ]
-    (qkv_share,) = run(
-        total_kernel, "total", low_one, [own_half] + pieces, [((size, width), BF)]
-    )
-    for seq_bits, hi_bits, lo_bits in ((1, 0, 0), (2, 0, 0), (0, 0, 1), (0, 1, 0), (0, 2, 0)):
-        sums = sums + flip(sums, seq_bits, hi_bits, lo_bits)
-    sum_gains, sum_shifts, sum_up_bias, sum_down_bias, sum_first, sum_mid, sum_mid_bias = run(
-        functools.partial(unpack_kernel, vectors),
-        "unpack",
-        low_one,
-        [sums],
-        [
-            ((3, width), F32),
-            ((3, width), F32),
-            ((1, hidden), F32),
-            ((1, width), F32),
-            ((1, CH), F32),
-            ((3, CH, 9 * CH), F32),
-            ((3, CH), F32),
-        ],
-    )
-    sum_up, sum_down, sum_conv = run(
+
+    mlp_share = scatter_last(mlp_parts, "mlp_total")
+    qkv_parts = scatter_half(qkv_parts, "qkv_half")
+    sums = add(sums, flip(sums, 1), "sum_core")
+    grad_input, learned = ordered_run(
+        back_kernel,
+        "back",
+        ids,
+        [from_planes(moved_back)],
+        [((rows, width), F32), ((learned_rows, width), F32)],
+    )
+    sums = add(sums, flip(sums, 2), "sum_x")
+    qkv_parts = scatter_fourth(qkv_parts, "qkv_fourth")
+    sums = add(sums, flip(sums, 0, 0, 1), "sum_y")
+    sum_up, sum_down, sum_conv = ordered_run(
         functools.partial(finish_mlp_kernel, ranks, hidden_quarter, width, unit),
         "finish_mlp",
-        rank_one,
+        ids,
         gather_four(mlp_share),
-        [((size, hidden), F32), ((ranks * unit, width), F32), ((size, PAD), F32)],
-    )
-    sum_qkv, sum_out = run(
+        [((size, hidden), F32), ((ranks * unit, width), F32), ((size, 9 * CH), F32)],
+    )
+    qkv_share = scatter_last(qkv_parts, "qkv_total")
+    sums = add(sums, flip(sums, 0, 1), "sum_z")
+    sum_gains, sum_shifts, sum_up_bias, sum_down_bias, sum_first, sum_mid, sum_mid_bias = (
+        ordered_run(
+            functools.partial(unpack_kernel, vectors),
+            "unpack",
+            ids,
+            [sums, flip(sums, 0, 2)],
+            [
+                ((3, width), F32),
+                ((3, width), F32),
+                ((1, hidden), F32),
+                ((1, width), F32),
+                ((1, CH), F32),
+                ((3, CH, 9 * CH), F32),
+                ((3, CH), F32),
+            ],
+            [pltpu.VMEM((small_rows, PAD), F32)],
+        )
+    )
+    sum_qkv, sum_out = ordered_run(
         functools.partial(finish_qkv_kernel, ranks, quarter),
         "finish_qkv",
-        rank_one,
+        ids,
         gather_four(qkv_share),
         [((size, 3 * width), F32), ((size, width), F32)],
     )
     return (
-        moved_back[rows:].reshape(1, frames_dev, CH, width),
-        moved_back[:rows].reshape(1, frames_dev, patches, width),
+        learned.reshape(1, frames_dev, CH, width),
+        grad_input.reshape(1, frames_dev, patches, width),
         sum_qkv,
         sum_out,
         sum_up,
         sum_down,
-        sum_conv[:, : 9 * CH],
+        sum_conv,
         sum_gains,
         sum_shifts,
         sum_up_bias.reshape(hidden),

time: 288 us -> 237 us (0.82)
  local copies, waits for them, and re-layouts: 36.8 us -> 10 us
  waiting for transfers between devices: 121 us -> 103 us
  between operations: 14.9 us -> 1.24 us
  Pallas kernels: 44.3 us -> 56.9 us
  other arithmetic: 4.47 us -> 0.68 us
    unnamed x152 -> x26, local copies, waits for them, and re-layouts: 29.1 us -> 7.26 us
    reduce_scatter x1 -> x0, waiting for transfers between devices: 13 us -> none  [shards_square(): lax.psum_scatter(mlp_grads, 'frame', scatter_dimension=0, tiled=True)]
    pallas_call x19 -> x38, Pallas kernels: 44.3 us -> 56.9 us  [run(): pl.pallas_call(kernel, in_specs=[pl.BlockSpec(memory_space=pltpu.SMEM)] +...]
    ppermute x57 -> x76, waiting for transfers between devices: 108 us -> 103 us  [permute(): return lax.ppermute(array, AXES, pairs)]
    dynamic_slice x4 -> x0, local copies, waits for them, and re-layouts: 3.01 us -> none  [the longest x1 1.08 us: shards_square(): lax.dynamic_slice_in_dim(w_qkv, part * width + rank * quarter, quarter, 1)]
    ppermute x57 -> x76, starting transfers between devices: 61.4 us -> 63.9 us  [permute(): return lax.ppermute(array, AXES, pairs)]
  transfers between devices with their start and end apart: 59 -> 76, of which waited for: 26 -> 34; matrix products, arithmetic and copies ran while one was open for 4% -> 2% of each run, Pallas kernels for 10% -> 20%
where the time goes in v3:
time: 237 us; the launch traced here: 235 us
  waiting for transfers between devices  103 us (43%)
  starting transfers between devices  63.9 us (27%)
  Pallas kernels  56.9 us (24%)
  local copies, waits for them, and re-layouts  10 us (4%)
    ppermute x76, waiting for transfers between devices, permute(): return lax.ppermute(array, AXES, pairs)  103 us
    ppermute x76, starting transfers between devices, permute(): return lax.ppermute(array, AXES, pairs)  63.9 us
    pallas_call x38, Pallas kernels, run(): pl.pallas_call(kernel, in_specs=[pl.BlockSpec(memory_space=pltpu.SMEM)] +...  56.9 us
    unnamed x26, local copies, waits for them, and re-layouts  7.26 us
  transfers between devices with their start and end apart: 76, of which 34 were waited for; matrix products, arithmetic and copies ran while one was open for 2% of the time, Pallas kernels for 20%

profile of v3, /device:TPU:2, one launch (start us, length us, event | category | flops | bytes accessed | tf_op | source)
XLA Modules:
  0.0 235.5 jit_solution(256846326020423034)
XLA Ops:
  3.7 3.5 %collective-permute-start = (bf16[160,768]{1,0:T(8,128)(2,1)S(1)}, bf16[160,768]{1,0:T(8,128)(2,1)S(1)}, u32[]{:S(2)}, u32[]{:S(2)}) collective-permute-start(bf16[160,768]{1,0:T(8,128)(2,1)S(1)} %pack.1), channel_id=1, source_target_pairs={{0,0},{1,1},{2,16},{3,17},{4,8},{5,9},{6,24},{7,25},{8,4},{9,5},{1... | collective-permute-start | bytes 737288 | tf_op jit(solution)/shard_map/ppermute | solution.py:1417
  10.9 1.6 collective-permute-start.2
  12.5 1.5 collective-permute-start.1
  14.0 7.3 %collective-permute-done.3.refs_12_ = bf16[96,768]{1,0:T(8,128)(2,1)S(1)} collective-permute-done((bf16[96,768]{1,0:T(8,128)(2,1)S(1)}, bf16[96,768]{1,0:T(8,128)(2,1)S(1)}, u32[]{:S(2)}, u32[]{:S(2)}) %collective-permute-start.3) | collective-permute-done | bytes 147488 | tf_op jit(solution)/shard_map/ppermute | solution.py:1417
  24.7 1.6 collective-permute-start.8
  26.8 1.5 collective-permute-start.5
  32.6 3.2 %collective-permute-done.6.refs_13_ = bf16[96,768]{1,0:T(8,128)(2,1)} collective-permute-done((bf16[96,768]{1,0:T(8,128)(2,1)S(1)}, bf16[96,768]{1,0:T(8,128)(2,1)}, u32[]{:S(2)}, u32[]{:S(2)}) %collective-permute-start.6) | collective-permute-done | bytes 147488 | tf_op jit(solution)/shard_map/ppermute | solution.py:1417
  35.8 1.6 collective-permute-done.5.refs_11_
  38.5 1.6 collective-permute-start.14
  40.6 6.8 %collective-permute-done.15.refs_15_ = bf16[96,768]{1,0:T(8,128)(2,1)S(1)} collective-permute-done((bf16[96,768]{1,0:T(8,128)(2,1)S(1)}, bf16[96,768]{1,0:T(8,128)(2,1)S(1)}, u32[]{:S(2)}, u32[]{:S(2)}) %collective-permute-start.15) | collective-permute-done | bytes 147488 | tf_op jit(solution)/shard_map/ppermute | solution.py:1417
  47.4 3.1 %collective-permute-start.9 = (bf16[96,896]{1,0:T(8,128)(2,1)S(1)}, bf16[96,896]{1,0:T(8,128)(2,1)S(1)}, u32[]{:S(2)}, u32[]{:S(2)}) collective-permute-start(bf16[96,896]{1,0:T(8,128)(2,1)S(1)} %get-tuple-element.167.refs_0_), channel_id=1, source_target_pairs={{0,4},{1,5},{2,6},{3,7},{4,0},{5,1},{6,2},{7,3},{8,12},{9,13},{10,... | collective-permute-start | bytes 516104 | tf_op jit(solution)/shard_map/ppermute | solution.py:1417
  50.6 1.5 collective-permute-start.10
  52.2 3.5 %collective-permute-done.10.refs_3_ = bf16[96,768]{1,0:T(8,128)(2,1)S(1)} collective-permute-done((bf16[96,768]{1,0:T(8,128)(2,1)S(1)}, bf16[96,768]{1,0:T(8,128)(2,1)S(1)}, u32[]{:S(2)}, u32[]{:S(2)}) %collective-permute-start.10) | collective-permute-done | bytes 147488 | tf_op jit(solution)/shard_map/ppermute | solution.py:1417
  57.6 3.2 %collective-permute-start.22 = (bf16[192,768]{1,0:T(8,128)(2,1)S(1)}, bf16[192,768]{1,0:T(8,128)(2,1)S(1)}, u32[]{:S(2)}, u32[]{:S(2)}) collective-permute-start(bf16[192,768]{1,0:T(8,128)(2,1)S(1)} %get-tuple-element.169.refs_2_), channel_id=1, source_target_pairs={{0,4},{1,5},{2,6},{3,7},{4,0},{5,1},{6,2},{7,3},{8,12},{9,13},{10,... | collective-permute-start | bytes 884744 | tf_op jit(solution)/shard_map/ppermute | solution.py:1417
  60.8 2.3 project.1
  63.2 1.8 collective-permute-start.19
  65.0 5.8 %attend.1 = (bf16[192,512]{1,0:T(8,128)(2,1)S(1)}, f32[8,512]{1,0:T(8,128)S(1)}) custom-call(s32[3]{0:T(128)S(1)} %pad_add_fusion.unused_ref.ids_ref.rank_ref, bf16[512,192]{1,0:T(8,128)(2,1)S(1)} %get-tuple-element.174.refs_0_.refs_5_, bf16[1024,384]{1,0:T(8,128)(2,1)S(1)} %get-tuple-element.175.refs_1_.refs_6_, ...), custom_call_target="tpu_custom_call" | custom-call | tf_op jit(solution)/shard_map/attend/pallas_call | solution.py:745
  74.6 1.6 collective-permute-start.28
  77.7 5.9 %collective-permute-done.24.refs_3_ = bf16[128,768]{1,0:T(8,128)(2,1)S(1)} collective-permute-done((bf16[128,768]{1,0:T(8,128)(2,1)S(1)}, bf16[128,768]{1,0:T(8,128)(2,1)S(1)}, u32[]{:S(2)}, u32[]{:S(2)}) %collective-permute-start.24) | collective-permute-done | bytes 196640 | tf_op jit(solution)/shard_map/ppermute | solution.py:1417
  84.7 6.2 %collective-permute-done.26.refs_2_ = bf16[128,768]{1,0:T(8,128)(2,1)S(1)} collective-permute-done((bf16[128,768]{1,0:T(8,128)(2,1)S(1)}, bf16[128,768]{1,0:T(8,128)(2,1)S(1)}, u32[]{:S(2)}, u32[]{:S(2)}) %collective-permute-start.26) | collective-permute-done | bytes 196640 | tf_op jit(solution)/shard_map/ppermute | solution.py:1417
  92.4 3.1 %mlp.1 = (bf16[512,768]{1,0:T(8,128)(2,1)S(1)}, f32[512,768]{1,0:T(8,128)S(1)}, bf16[768,768]{1,0:T(8,128)(2,1)S(1)}, bf16[768,768]{1,0:T(8,128)(2,1)S(1)}, bf16...) custom-call(s32[3]{0:T(128)S(1)} %pad_add_fusion.unused_ref.ids_ref., ...), custom_call_target="tpu_custom_call" | custom-call | tf_op jit(solution)/shard_map/mlp/pallas_call | solution.py:745
  99.0 5.6 %collective-permute-done.32.refs_3_ = bf16[128,768]{1,0:T(8,128)(2,1)S(1)} collective-permute-done((bf16[128,768]{1,0:T(8,128)(2,1)S(1)}, bf16[128,768]{1,0:T(8,128)(2,1)S(1)}, u32[]{:S(2)}, u32[]{:S(2)}) %collective-permute-start.32) | collective-permute-done | bytes 196640 | tf_op jit(solution)/shard_map/ppermute | solution.py:1417
  106.0 6.4 %tail.1 = (f32[16,768]{1,0:T(8,128)S(1)}, bf16[128,768]{1,0:T(8,128)(2,1)S(1)}, f32[128,768]{1,0:T(8,128)S(1)}, bf16[128,768]{1,0:T(8,128)(2,1)S(1)}, bf16[128,1...) custom-call(s32[3]{0:T(128)S(1)} %pad_add_fusion.unused_ref.ids_ref.rank_ref, f32[128,768]{1,0:T(8,128)S(1)} %get-tuple-element.218.refs_0_, ...), custom_call_target="tpu_custom_call" | custom-call | tf_op jit(solution)/shard_map/tail/pallas_call | solution.py:745
  113.6 4.6 %collective-permute-done.34.refs_2_.refs_6_ = bf16[128,768]{1,0:T(8,128)(2,1)S(1)} collective-permute-done((bf16[128,768]{1,0:T(8,128)(2,1)S(1)}, bf16[128,768]{1,0:T(8,128)(2,1)S(1)}, u32[]{:S(2)}, u32[]{:S(2)}) %collective-permute-start.34) | collective-permute-done | bytes 196640 | tf_op jit(solution)/shard_map/ppermute | solution.py:1417
  119.7 2.1 mlp_back.1
  124.7 2.3 mlp_grads.1
  127.2 3.7 %collective-permute-done.41.refs_4_ = bf16[128,768]{1,0:T(8,128)(2,1)S(1)} collective-permute-done((bf16[128,768]{1,0:T(8,128)(2,1)S(1)}, bf16[128,768]{1,0:T(8,128)(2,1)S(1)}, u32[]{:S(2)}, u32[]{:S(2)}) %collective-permute-start.41) | collective-permute-done | bytes 196640 | tf_op jit(solution)/shard_map/ppermute | solution.py:1417
  134.1 3.9 %collective-permute-done.43.refs_2_.refs_10_ = bf16[128,768]{1,0:T(8,128)(2,1)S(1)} collective-permute-done((bf16[128,768]{1,0:T(8,128)(2,1)S(1)}, bf16[128,768]{1,0:T(8,128)(2,1)S(1)}, u32[]{:S(2)}, u32[]{:S(2)}) %collective-permute-start.43) | collective-permute-done | bytes 196640 | tf_op jit(solution)/shard_map/ppermute | solution.py:1417
  139.5 8.4 %attend_back_out.1 = (bf16[512,576]{1,0:T(8,128)(2,1)S(1)}, bf16[512,384]{1,0:T(8,128)(2,1)S(1)}, f32[4,128,768]{2,1,0:T(8,128)S(1)}, bf16[128,768]{1,0:T(8,128)...) custom-call(s32[3]{0:T(128)S(1)} %pad_add_fusion.unused_ref.ids_ref.rank_ref, ...), custom_call_target="tpu_custom_call" | custom-call | tf_op jit(solution)/shard_map/attend_back_out/pallas_call | solution.py:745
  154.0 2.3 qkv_grads.1
  156.5 2.5 %collective-permute-done.50.corner_ref = bf16[128,768]{1,0:T(8,128)(2,1)S(1)} collective-permute-done((bf16[128,768]{1,0:T(8,128)(2,1)S(1)}, bf16[128,768]{1,0:T(8,128)(2,1)S(1)}, u32[]{:S(2)}, u32[]{:S(2)}) %collective-permute-start.50) | collective-permute-done | bytes 196640 | tf_op jit(solution)/shard_map/ppermute | solution.py:1417
  161.9 3.5 %collective-permute-done.51.refs_1_ = bf16[192,768]{1,0:T(8,128)(2,1)S(1)} collective-permute-done((bf16[192,768]{1,0:T(8,128)(2,1)S(1)}, bf16[192,768]{1,0:T(8,128)(2,1)S(1)}, u32[]{:S(2)}, u32[]{:S(2)}) %collective-permute-start.51) | collective-permute-done | bytes 294944 | tf_op jit(solution)/shard_map/ppermute | solution.py:1417
  165.3 3.7 %collective-permute-done.52.refs_3_ = bf16[192,896]{1,0:T(8,128)(2,1)S(1)} collective-permute-done((bf16[192,896]{1,0:T(8,128)(2,1)S(1)}, bf16[192,896]{1,0:T(8,128)(2,1)S(1)}, u32[]{:S(2)}, u32[]{:S(2)}) %collective-permute-start.52) | collective-permute-done | bytes 344096 | tf_op jit(solution)/shard_map/ppermute | solution.py:1417
  171.3 7.5 %collective-permute-done.57.arrived_ref = bf16[96,768]{1,0:T(8,128)(2,1)S(1)} collective-permute-done((bf16[96,768]{1,0:T(8,128)(2,1)S(1)}, bf16[96,768]{1,0:T(8,128)(2,1)S(1)}, u32[]{:S(2)}, u32[]{:S(2)}) %collective-permute-start.57) | collective-permute-done | bytes 147488 | tf_op jit(solution)/shard_map/ppermute | solution.py:1417
  179.4 1.7 collective-permute-start.67
  181.7 4.6 %collective-permute-start.56 = (bf16[144,768]{1,0:T(8,128)(2,1)S(1)}, bf16[144,768]{1,0:T(8,128)(2,1)S(1)}, u32[]{:S(2)}, u32[]{:S(2)}) collective-permute-start(bf16[144,768]{1,0:T(8,128)(2,1)S(1)} %get-tuple-element.251), channel_id=1, source_target_pairs={{0,0},{1,1},{2,16},{3,17},{4,8},{5,9},{6,24},{7,25},{8,4},{9,5},{1... | collective-permute-start | bytes 663560 | tf_op jit(solution)/shard_map/ppermute | solution.py:1417
  186.8 2.1 collective-permute-done.67.refs_2_
  191.8 8.0 %collective-permute-start.64 = (bf16[192,384]{1,0:T(8,128)(2,1)S(1)}, bf16[192,384]{1,0:T(8,128)(2,1)S(1)}, u32[]{:S(2)}, u32[]{:S(2)}) collective-permute-start(bf16[192,384]{1,0:T(8,128)(2,1)S(1)} %get-tuple-element.265), channel_id=1, source_target_pairs={{0,4},{1,5},{2,6},{3,7},{4,0},{5,1},{6,2},{7,3},{8,12},{9,13},{10,... | collective-permute-start | bytes 442376 | tf_op jit(solution)/shard_map/ppermute | solution.py:1417
  200.3 1.6 collective-permute-done.56.moved_ref
  203.2 2.8 %collective-permute-done.62.right_ref = f32[96,128]{1,0:T(8,128)S(1)} collective-permute-done((f32[96,128]{1,0:T(8,128)S(1)}, f32[96,128]{1,0:T(8,128)S(1)}, u32[]{:S(2)}, u32[]{:S(2)}) %collective-permute-start.62) | collective-permute-done | bytes 49184 | tf_op jit(solution)/shard_map/ppermute | solution.py:1417
  209.4 3.3 %collective-permute-done.65.right_ref = f32[96,128]{1,0:T(8,128)S(1)} collective-permute-done((f32[96,128]{1,0:T(8,128)S(1)}, f32[96,128]{1,0:T(8,128)S(1)}, u32[]{:S(2)}, u32[]{:S(2)}) %collective-permute-start.65) | collective-permute-done | bytes 49184 | tf_op jit(solution)/shard_map/ppermute | solution.py:1417
  213.2 2.4 %finish_mlp.1 = (f32[96,3072]{1,0:T(8,128)}, f32[384,768]{1,0:T(8,128)}, f32[96,72]{1,0:T(8,128)S(1)}) custom-call(s32[3]{0:T(128)S(1)} %pad_add_fusion.unused_ref.ids_ref.rank_ref, bf16[96,1664]{1,0:T(8,128)(2,1)S(1)} %mlp_total.1.refs_0_, bf16[96,1664]{1,0:T(8,128)(2,1)S(1)} %collective-permute-done.66.refs_1_, ...), custom_call_target="tpu_custom_call" | custom-call | tf_op jit(solution)/shard_map/finish_mlp/pallas_call | solution.py:745
  216.3 5.1 %collective-permute-done.74.refs_2_ = bf16[96,768]{1,0:T(8,128)(2,1)S(1)} collective-permute-done((bf16[96,768]{1,0:T(8,128)(2,1)S(1)}, bf16[96,768]{1,0:T(8,128)(2,1)S(1)}, u32[]{:S(2)}, u32[]{:S(2)}) %collective-permute-start.74) | collective-permute-done | bytes 147488 | tf_op jit(solution)/shard_map/ppermute | solution.py:1417
  221.3 2.0 collective-permute-start.71
  223.3 2.4 %collective-permute-done.71.right_ref = f32[96,128]{1,0:T(8,128)S(1)} collective-permute-done((f32[96,128]{1,0:T(8,128)S(1)}, f32[96,128]{1,0:T(8,128)S(1)}, u32[]{:S(2)}, u32[]{:S(2)}) %collective-permute-start.71) | collective-permute-done | bytes 49184 | tf_op jit(solution)/shard_map/ppermute | solution.py:1417
  226.3 2.2 collective-permute-start.72
  229.3 2.6 %collective-permute-done.72.arrived_ref = f32[96,128]{1,0:T(8,128)S(1)} collective-permute-done((f32[96,128]{1,0:T(8,128)S(1)}, f32[96,128]{1,0:T(8,128)S(1)}, u32[]{:S(2)}, u32[]{:S(2)}) %collective-permute-start.72) | collective-permute-done | bytes 49184 | tf_op jit(solution)/shard_map/ppermute | solution.py:1417
  233.7 1.8 finish_qkv.1
  (174 shorter events, 67.1 us)
Async XLA Ops:
  3.7 18.6 %collective-permute-start = (bf16[160,768]{1,0:T(8,128)(2,1)S(1)}, bf16[160,768]{1,0:T(8,128)(2,1)S(1)}, u32[]{:S(2)}, u32[]{:S(2)}) collective-permute-start(bf16[160,768]{1,0:T(8,128)(2,1)S(1)} %pack.1), channel_id=1, source_target_pairs={{0,0},{1,1},{2,16},{3,17},{4,8},{5,9},{6,24},{7,25},{8,4},{9,5},{1... | collective-permute-start | bytes 737288 | tf_op jit(solution)/shard_map/ppermute | solution.py:1417
  9.8 11.6 %collective-permute-start.3 = (bf16[96,768]{1,0:T(8,128)(2,1)S(1)}, bf16[96,768]{1,0:T(8,128)(2,1)S(1)}, u32[]{:S(2)}, u32[]{:S(2)}) collective-permute-start(bf16[96,768]{1,0:T(8,128)(2,1)S(1)} %select.10.refs_8_), channel_id=1, source_target_pairs={{0,4},{1,5},{2,6},{3,7},{4,0},{5,1},{6,2},{7,3},{8,12},{9,13},{10,... | collective-permute-start | bytes 442376 | tf_op jit(solution)/shard_map/ppermute | solution.py:1417
  10.9 13.7 %collective-permute-start.2 = (bf16[96,768]{1,0:T(8,128)(2,1)S(1)}, bf16[96,768]{1,0:T(8,128)(2,1)S(1)}, u32[]{:S(2)}, u32[]{:S(2)}) collective-permute-start(bf16[96,768]{1,0:T(8,128)(2,1)S(1)} %select.10.refs_8_), channel_id=1, source_target_pairs={{0,2},{1,3},{2,0},{3,1},{4,6},{5,7},{6,4},{7,5},{8,10},{9,11},{10,... | collective-permute-start | bytes 442376 | tf_op jit(solution)/shard_map/ppermute | solution.py:1417
  12.5 12.1 %collective-permute-start.1 = (bf16[96,768]{1,0:T(8,128)(2,1)S(1)}, bf16[96,768]{1,0:T(8,128)(2,1)S(1)}, u32[]{:S(2)}, u32[]{:S(2)}) collective-permute-start(bf16[96,768]{1,0:T(8,128)(2,1)S(1)} %select.10.refs_8_), channel_id=1, source_target_pairs={{0,1},{1,0},{2,3},{3,2},{4,5},{5,4},{6,7},{7,6},{8,9},{9,8},{10,11... | collective-permute-start | bytes 442376 | tf_op jit(solution)/shard_map/ppermute | solution.py:1417
  21.3 7.0 %collective-permute-start.7 = (bf16[96,768]{1,0:T(8,128)(2,1)S(1)}, bf16[96,768]{1,0:T(8,128)(2,1)S(1)}, u32[]{:S(2)}, u32[]{:S(2)}) collective-permute-start(bf16[96,768]{1,0:T(8,128)(2,1)S(1)} %collective-permute-done.3.refs_12_), channel_id=1, source_target_pairs={{0,2},{1,3},{2,0},{3,1},{4,6},{5,7},{6,4},{7,5},{8,10},{9,11},{10,... | collective-permute-start | bytes 442376 | tf_op jit(solution)/shard_map/ppermute | solution.py:1417
  24.6 12.8 %collective-permute-start.4 = (bf16[128,768]{1,0:T(8,128)(2,1)S(1)}, bf16[128,768]{1,0:T(8,128)(2,1)S(1)}, u32[]{:S(2)}, u32[]{:S(2)}) collective-permute-start(bf16[128,768]{1,0:T(8,128)(2,1)S(1)} %get-tuple-element.234.refs_0_), channel_id=1, source_target_pairs={{0,16},{1,17},{2,18},{3,19},{4,20},{5,21},{6,22},{7,23},{8,24},{9,... | collective-permute-start | bytes 589832 | tf_op jit(solution)/shard_map/ppermute | solution.py:1417
  24.7 12.7 %collective-permute-start.8 = (bf16[128,768]{1,0:T(8,128)(2,1)S(1)}, bf16[128,768]{1,0:T(8,128)(2,1)S(1)}, u32[]{:S(2)}, u32[]{:S(2)}) collective-permute-start(bf16[128,768]{1,0:T(8,128)(2,1)S(1)} %get-tuple-element.234.refs_0_), channel_id=1, source_target_pairs={{0,1},{1,0},{2,3},{3,2},{4,5},{5,4},{6,7},{7,6},{8,9},{9,8},{10,11... | collective-permute-start | bytes 589832 | tf_op jit(solution)/shard_map/ppermute | solution.py:1417
  26.3 9.6 %collective-permute-start.6 = (bf16[96,768]{1,0:T(8,128)(2,1)S(1)}, bf16[96,768]{1,0:T(8,128)(2,1)}, u32[]{:S(2)}, u32[]{:S(2)}) collective-permute-start(bf16[96,768]{1,0:T(8,128)(2,1)S(1)} %collective-permute-done.3.refs_12_), channel_id=1, source_target_pairs={{0,1},{1,0},{2,3},{3,2},{4,5},{5,4},{6,7},{7,6},{8,9},{9,8},{10,11... | collective-permute-start | bytes 442376 | tf_op jit(solution)/shard_map/ppermute | solution.py:1417
  26.8 10.6 %collective-permute-start.5 = (bf16[96,768]{1,0:T(8,128)(2,1)S(1)}, bf16[96,768]{1,0:T(8,128)(2,1)}, u32[]{:S(2)}, u32[]{:S(2)}) collective-permute-start(bf16[96,768]{1,0:T(8,128)(2,1)S(1)} %collective-permute-done.2.refs_10_), channel_id=1, source_target_pairs={{0,1},{1,0},{2,3},{3,2},{4,5},{5,4},{6,7},{7,6},{8,9},{9,8},{10,11... | collective-permute-start | bytes 442376 | tf_op jit(solution)/shard_map/ppermute | solution.py:1417
  28.3 22.3 %collective-permute-start.11 = (bf16[128,768]{1,0:T(8,128)(2,1)S(1)}, bf16[128,768]{1,0:T(8,128)(2,1)S(1)}, u32[]{:S(2)}, u32[]{:S(2)}) collective-permute-start(bf16[128,768]{1,0:T(8,128)(2,1)S(1)} %get-tuple-element.234.refs_0_), channel_id=1, source_target_pairs={{0,8},{1,9},{2,10},{3,11},{4,12},{5,13},{6,14},{7,15},{8,0},{9,1},... | collective-permute-start | bytes 589832 | tf_op jit(solution)/shard_map/ppermute | solution.py:1417
  37.4 14.7 %collective-permute-start.12 = (bf16[128,768]{1,0:T(8,128)(2,1)S(1)}, bf16[128,768]{1,0:T(8,128)(2,1)S(1)}, u32[]{:S(2)}, u32[]{:S(2)}) collective-permute-start(bf16[128,768]{1,0:T(8,128)(2,1)S(1)} %collective-permute-done.4.far_ref.refs_2_), channel_id=1, source_target_pairs={{0,8},{1,9},{2,10},{3,11},{4,12},{5,13},{6,14},{7,15},{8,0},{9,1},... | collective-permute-start | bytes 589832 | tf_op jit(solution)/shard_map/ppermute | solution.py:1417
  37.4 14.7 %collective-permute-start.13 = (bf16[128,768]{1,0:T(8,128)(2,1)S(1)}, bf16[128,768]{1,0:T(8,128)(2,1)S(1)}, u32[]{:S(2)}, u32[]{:S(2)}) collective-permute-start(bf16[128,768]{1,0:T(8,128)(2,1)S(1)} %collective-permute-done.8.side_ref.refs_4_), channel_id=1, source_target_pairs={{0,8},{1,9},{2,10},{3,11},{4,12},{5,13},{6,14},{7,15},{8,0},{9,1},... | collective-permute-start | bytes 589832 | tf_op jit(solution)/shard_map/ppermute | solution.py:1417
  38.5 13.6 %collective-permute-start.14 = (bf16[128,768]{1,0:T(8,128)(2,1)S(1)}, bf16[128,768]{1,0:T(8,128)(2,1)S(1)}, u32[]{:S(2)}, u32[]{:S(2)}) collective-permute-start(bf16[128,768]{1,0:T(8,128)(2,1)S(1)} %pick.1), channel_id=1, source_target_pairs={{0,1},{1,0},{2,3},{3,2},{4,5},{5,4},{6,7},{7,6},{8,24},{9,25},{10,... | collective-permute-start | bytes 589832 | tf_op jit(solution)/shard_map/ppermute | solution.py:1417
  40.1 7.3 %collective-permute-start.15 = (bf16[96,768]{1,0:T(8,128)(2,1)S(1)}, bf16[96,768]{1,0:T(8,128)(2,1)S(1)}, u32[]{:S(2)}, u32[]{:S(2)}) collective-permute-start(bf16[96,768]{1,0:T(8,128)(2,1)S(1)} %collective-permute-done.7.refs_14_), channel_id=1, source_target_pairs={{0,1},{1,0},{2,3},{3,2},{4,5},{5,4},{6,7},{7,6},{8,9},{9,8},{10,11... | collective-permute-start | bytes 442376 | tf_op jit(solution)/shard_map/ppermute | solution.py:1417
  47.4 9.5 %collective-permute-start.9 = (bf16[96,896]{1,0:T(8,128)(2,1)S(1)}, bf16[96,896]{1,0:T(8,128)(2,1)S(1)}, u32[]{:S(2)}, u32[]{:S(2)}) collective-permute-start(bf16[96,896]{1,0:T(8,128)(2,1)S(1)} %get-tuple-element.167.refs_0_), channel_id=1, source_target_pairs={{0,4},{1,5},{2,6},{3,7},{4,0},{5,1},{6,2},{7,3},{8,12},{9,13},{10,... | collective-permute-start | bytes 516104 | tf_op jit(solution)/shard_map/ppermute | solution.py:1417
  52.1 8.7 %collective-permute-start.16 = (bf16[128,768]{1,0:T(8,128)(2,1)S(1)}, bf16[128,768]{1,0:T(8,128)(2,1)S(1)}, u32[]{:S(2)}, u32[]{:S(2)}) collective-permute-start(bf16[128,768]{1,0:T(8,128)(2,1)S(1)} %collective-permute-done.14.refs_6_), channel_id=1, source_target_pairs={{0,8},{1,9},{2,10},{3,11},{4,12},{5,13},{6,14},{7,15},{8,0},{9,1},... | collective-permute-start | bytes 589832 | tf_op jit(solution)/shard_map/ppermute | solution.py:1417
  57.5 16.5 %collective-permute-start.21 = (bf16[192,896]{1,0:T(8,128)(2,1)S(1)}, bf16[192,896]{1,0:T(8,128)(2,1)S(1)}, u32[]{:S(2)}, u32[]{:S(2)}) collective-permute-start(bf16[192,896]{1,0:T(8,128)(2,1)S(1)} %get-tuple-element.185.refs_0_), channel_id=1, source_target_pairs={{0,2},{1,3},{2,0},{3,1},{4,6},{5,7},{6,4},{7,5},{8,10},{9,11},{10,... | collective-permute-start | bytes 1032200 | tf_op jit(solution)/shard_map/ppermute | solution.py:1417
  57.6 16.4 %collective-permute-start.22 = (bf16[192,768]{1,0:T(8,128)(2,1)S(1)}, bf16[192,768]{1,0:T(8,128)(2,1)S(1)}, u32[]{:S(2)}, u32[]{:S(2)}) collective-permute-start(bf16[192,768]{1,0:T(8,128)(2,1)S(1)} %get-tuple-element.169.refs_2_), channel_id=1, source_target_pairs={{0,4},{1,5},{2,6},{3,7},{4,0},{5,1},{6,2},{7,3},{8,12},{9,13},{10,... | collective-permute-start | bytes 884744 | tf_op jit(solution)/shard_map/ppermute | solution.py:1417
  63.1 7.7 %collective-permute-start.17 = (bf16[192,192]{1,0:T(8,128)(2,1)S(1)}, bf16[192,192]{1,0:T(8,128)(2,1)S(1)}, u32[]{:S(2)}, u32[]{:S(2)}) collective-permute-start(bf16[192,192]{1,0:T(8,128)(2,1)S(1)} %get-tuple-element.179), channel_id=1, source_target_pairs={{0,8},{1,9},{2,10},{3,11},{4,12},{5,13},{6,14},{7,15},{8,0},{9,1},... | collective-permute-start | bytes 221192 | tf_op jit(solution)/shard_map/ppermute | solution.py:1417
  63.1 7.6 %collective-permute-start.18 = (bf16[192,192]{1,0:T(8,128)(2,1)S(1)}, bf16[192,192]{1,0:T(8,128)(2,1)S(1)}, u32[]{:S(2)}, u32[]{:S(2)}) collective-permute-start(bf16[192,192]{1,0:T(8,128)(2,1)S(1)} %get-tuple-element.180), channel_id=1, source_target_pairs={{0,16},{1,17},{2,18},{3,19},{4,20},{5,21},{6,22},{7,23},{8,24},{9,... | collective-permute-start | bytes 221192 | tf_op jit(solution)/shard_map/ppermute | solution.py:1417
  63.2 7.6 %collective-permute-start.19 = (bf16[192,192]{1,0:T(8,128)(2,1)S(1)}, bf16[192,192]{1,0:T(8,128)(2,1)S(1)}, u32[]{:S(2)}, u32[]{:S(2)}) collective-permute-start(bf16[192,192]{1,0:T(8,128)(2,1)S(1)} %get-tuple-element.173), channel_id=1, source_target_pairs={{0,24},{1,25},{2,26},{3,27},{4,28},{5,29},{6,30},{7,31},{8,16},{9,... | collective-permute-start | bytes 221192 | tf_op jit(solution)/shard_map/ppermute | solution.py:1417
  74.6 17.7 %collective-permute-start.28 = (bf16[384,896]{1,0:T(8,128)(2,1)S(1)}, bf16[384,896]{1,0:T(8,128)(2,1)S(1)}, u32[]{:S(2)}, u32[]{:S(2)}) collective-permute-start(bf16[384,896]{1,0:T(8,128)(2,1)S(1)} %get-tuple-element.192.refs_4_), channel_id=1, source_target_pairs={{0,1},{1,0},{2,3},{3,2},{4,5},{5,4},{6,7},{7,6},{8,9},{9,8},{10,11... | collective-permute-start | bytes 2064392 | tf_op jit(solution)/shard_map/ppermute | solution.py:1417
  76.3 7.3 %collective-permute-start.24 = (bf16[128,768]{1,0:T(8,128)(2,1)S(1)}, bf16[128,768]{1,0:T(8,128)(2,1)S(1)}, u32[]{:S(2)}, u32[]{:S(2)}) collective-permute-start(bf16[128,768]{1,0:T(8,128)(2,1)S(1)} %out_pass.1), channel_id=1, source_target_pairs={{0,16},{1,17},{2,18},{3,19},{4,20},{5,21},{6,22},{7,23},{8,24},{9,... | collective-permute-start | bytes 589832 | tf_op jit(solution)/shard_map/ppermute | solution.py:1417
  76.5 15.8 %collective-permute-start.29 = (bf16[384,768]{1,0:T(8,128)(2,1)S(1)}, bf16[384,768]{1,0:T(8,128)(2,1)S(1)}, u32[]{:S(2)}, u32[]{:S(2)}) collective-permute-start(bf16[384,768]{1,0:T(8,128)(2,1)S(1)} %get-tuple-element.186.refs_6_), channel_id=1, source_target_pairs={{0,2},{1,3},{2,0},{3,1},{4,6},{5,7},{6,4},{7,5},{8,10},{9,11},{10,... | collective-permute-start | bytes 1769480 | tf_op jit(solution)/shard_map/ppermute | solution.py:1417
  97.6 7.0 %collective-permute-start.32 = (bf16[128,768]{1,0:T(8,128)(2,1)S(1)}, bf16[128,768]{1,0:T(8,128)(2,1)S(1)}, u32[]{:S(2)}, u32[]{:S(2)}) collective-permute-start(bf16[128,768]{1,0:T(8,128)(2,1)S(1)} %mlp_pass.1), channel_id=1, source_target_pairs={{0,16},{1,17},{2,18},{3,19},{4,20},{5,21},{6,22},{7,23},{8,24},{9,... | collective-permute-start | bytes 589832 | tf_op jit(solution)/shard_map/ppermute | solution.py:1417
  104.6 8.5 %collective-permute-start.37 = (bf16[192,512]{1,0:T(8,128)(2,1)S(1)}, bf16[192,512]{1,0:T(8,128)(2,1)S(1)}, u32[]{:S(2)}, u32[]{:S(2)}) collective-permute-start(bf16[192,512]{1,0:T(8,128)(2,1)S(1)} %get-tuple-element.203.refs_0_.refs_12_), channel_id=1, source_target_pairs={{0,16},{1,17},{2,18},{3,19},{4,20},{5,21},{6,22},{7,23},{8,24},{9,... | collective-permute-start | bytes 589832 | tf_op jit(solution)/shard_map/ppermute | solution.py:1417
  123.9 7.0 %collective-permute-start.41 = (bf16[128,768]{1,0:T(8,128)(2,1)S(1)}, bf16[128,768]{1,0:T(8,128)(2,1)S(1)}, u32[]{:S(2)}, u32[]{:S(2)}) collective-permute-start(bf16[128,768]{1,0:T(8,128)(2,1)S(1)} %mlp_back_pass.1), channel_id=1, source_target_pairs={{0,16},{1,17},{2,18},{3,19},{4,20},{5,21},{6,22},{7,23},{8,24},{9,... | collective-permute-start | bytes 589832 | tf_op jit(solution)/shard_map/ppermute | solution.py:1417
  127.0 23.0 %collective-permute-start.47 = (bf16[384,896]{1,0:T(8,128)(2,1)S(1)}, bf16[384,896]{1,0:T(8,128)(2,1)S(1)}, u32[]{:S(2)}, u32[]{:S(2)}) collective-permute-start(bf16[384,896]{1,0:T(8,128)(2,1)S(1)} %get-tuple-element.217), channel_id=1, source_target_pairs={{0,2},{1,3},{2,0},{3,1},{4,6},{5,7},{6,4},{7,5},{8,10},{9,11},{10,... | collective-permute-start | bytes 2064392 | tf_op jit(solution)/shard_map/ppermute | solution.py:1417
  132.6 17.4 %collective-permute-start.46 = (bf16[384,768]{1,0:T(8,128)(2,1)S(1)}, bf16[384,768]{1,0:T(8,128)(2,1)S(1)}, u32[]{:S(2)}, u32[]{:S(2)}) collective-permute-start(bf16[384,768]{1,0:T(8,128)(2,1)S(1)} %get-tuple-element.230), channel_id=1, source_target_pairs={{0,1},{1,0},{2,3},{3,2},{4,5},{5,4},{6,7},{7,6},{8,9},{9,8},{10,11... | collective-permute-start | bytes 1769480 | tf_op jit(solution)/shard_map/ppermute | solution.py:1417
  150.9 18.2 %collective-permute-start.52 = (bf16[192,896]{1,0:T(8,128)(2,1)S(1)}, bf16[192,896]{1,0:T(8,128)(2,1)S(1)}, u32[]{:S(2)}, u32[]{:S(2)}) collective-permute-start(bf16[192,896]{1,0:T(8,128)(2,1)S(1)} %get-tuple-element.233), channel_id=1, source_target_pairs={{0,4},{1,5},{2,6},{3,7},{4,0},{5,1},{6,2},{7,3},{8,12},{9,13},{10,... | collective-permute-start | bytes 1032200 | tf_op jit(solution)/shard_map/ppermute | solution.py:1417
  151.3 14.0 %collective-permute-start.51 = (bf16[192,768]{1,0:T(8,128)(2,1)S(1)}, bf16[192,768]{1,0:T(8,128)(2,1)S(1)}, u32[]{:S(2)}, u32[]{:S(2)}) collective-permute-start(bf16[192,768]{1,0:T(8,128)(2,1)S(1)} %get-tuple-element.243), channel_id=1, source_target_pairs={{0,2},{1,3},{2,0},{3,1},{4,6},{5,7},{6,4},{7,5},{8,10},{9,11},{10,... | collective-permute-start | bytes 884744 | tf_op jit(solution)/shard_map/ppermute | solution.py:1417
  156.4 13.9 %collective-permute-start.53 = (bf16[128,768]{1,0:T(8,128)(2,1)S(1)}, bf16[128,768]{1,0:T(8,128)(2,1)S(1)}, u32[]{:S(2)}, u32[]{:S(2)}) collective-permute-start(bf16[128,768]{1,0:T(8,128)(2,1)S(1)} %get-tuple-element.248), channel_id=1, source_target_pairs={{0,8},{1,9},{2,10},{3,11},{4,12},{5,13},{6,14},{7,15},{8,0},{9,1},... | collective-permute-start | bytes 589832 | tf_op jit(solution)/shard_map/ppermute | solution.py:1417
  159.7 10.6 %collective-permute-start.54 = (bf16[128,768]{1,0:T(8,128)(2,1)S(1)}, bf16[128,768]{1,0:T(8,128)(2,1)S(1)}, u32[]{:S(2)}, u32[]{:S(2)}) collective-permute-start(bf16[128,768]{1,0:T(8,128)(2,1)S(1)} %get-tuple-element.249), channel_id=1, source_target_pairs={{0,16},{1,17},{2,18},{3,19},{4,20},{5,21},{6,22},{7,23},{8,24},{9,... | collective-permute-start | bytes 589832 | tf_op jit(solution)/shard_map/ppermute | solution.py:1417
  160.5 9.8 %collective-permute-start.55 = (bf16[128,768]{1,0:T(8,128)(2,1)S(1)}, bf16[128,768]{1,0:T(8,128)(2,1)S(1)}, u32[]{:S(2)}, u32[]{:S(2)}) collective-permute-start(bf16[128,768]{1,0:T(8,128)(2,1)S(1)} %get-tuple-element.241), channel_id=1, source_target_pairs={{0,1},{1,0},{2,3},{3,2},{4,5},{5,4},{6,7},{7,6},{8,9},{9,8},{10,11... | collective-permute-start | bytes 589832 | tf_op jit(solution)/shard_map/ppermute | solution.py:1417
  169.7 9.0 %collective-permute-start.58 = (bf16[96,896]{1,0:T(8,128)(2,1)S(1)}, bf16[96,896]{1,0:T(8,128)(2,1)S(1)}, u32[]{:S(2)}, u32[]{:S(2)}) collective-permute-start(bf16[96,896]{1,0:T(8,128)(2,1)S(1)} %get-tuple-element.245), channel_id=1, source_target_pairs={{0,1},{1,0},{2,3},{3,2},{4,5},{5,4},{6,7},{7,6},{8,9},{9,8},{10,11... | collective-permute-start | bytes 516104 | tf_op jit(solution)/shard_map/ppermute | solution.py:1417
  170.3 8.5 %collective-permute-start.57 = (bf16[96,768]{1,0:T(8,128)(2,1)S(1)}, bf16[96,768]{1,0:T(8,128)(2,1)S(1)}, u32[]{:S(2)}, u32[]{:S(2)}) collective-permute-start(bf16[96,768]{1,0:T(8,128)(2,1)S(1)} %get-tuple-element.259), channel_id=1, source_target_pairs={{0,4},{1,5},{2,6},{3,7},{4,0},{5,1},{6,2},{7,3},{8,12},{9,13},{10,... | collective-permute-start | bytes 442376 | tf_op jit(solution)/shard_map/ppermute | solution.py:1417
  179.4 9.5 %collective-permute-start.67 = (bf16[96,1664]{1,0:T(8,128)(2,1)S(1)}, bf16[96,1664]{1,0:T(8,128)(2,1)S(1)}, u32[]{:S(2)}, u32[]{:S(2)}) collective-permute-start(bf16[96,1664]{1,0:T(8,128)(2,1)S(1)} %mlp_total.1.refs_0_), channel_id=1, source_target_pairs={{0,16},{1,17},{2,18},{3,19},{4,20},{5,21},{6,22},{7,23},{8,24},{9,... | collective-permute-start | bytes 958472 | tf_op jit(solution)/shard_map/ppermute | solution.py:1417
  181.1 8.7 %collective-permute-start.59 = (bf16[384,384]{1,0:T(8,128)(2,1)S(1)}, bf16[384,384]{1,0:T(8,128)(2,1)S(1)}, u32[]{:S(2)}, u32[]{:S(2)}) collective-permute-start(bf16[384,384]{1,0:T(8,128)(2,1)S(1)} %get-tuple-element.262), channel_id=1, source_target_pairs={{0,1},{1,0},{2,3},{3,2},{4,5},{5,4},{6,7},{7,6},{8,9},{9,8},{10,11... | collective-permute-start | bytes 884744 | tf_op jit(solution)/shard_map/ppermute | solution.py:1417
  181.7 8.4 %collective-permute-start.60 = (bf16[384,384]{1,0:T(8,128)(2,1)S(1)}, bf16[384,384]{1,0:T(8,128)(2,1)S(1)}, u32[]{:S(2)}, u32[]{:S(2)}) collective-permute-start(bf16[384,384]{1,0:T(8,128)(2,1)S(1)} %get-tuple-element.264), channel_id=1, source_target_pairs={{0,2},{1,3},{2,0},{3,1},{4,6},{5,7},{6,4},{7,5},{8,10},{9,11},{10,... | collective-permute-start | bytes 884744 | tf_op jit(solution)/shard_map/ppermute | solution.py:1417
  181.7 20.2 %collective-permute-start.56 = (bf16[144,768]{1,0:T(8,128)(2,1)S(1)}, bf16[144,768]{1,0:T(8,128)(2,1)S(1)}, u32[]{:S(2)}, u32[]{:S(2)}) collective-permute-start(bf16[144,768]{1,0:T(8,128)(2,1)S(1)} %get-tuple-element.251), channel_id=1, source_target_pairs={{0,0},{1,1},{2,16},{3,17},{4,8},{5,9},{6,24},{7,25},{8,4},{9,5},{1... | collective-permute-start | bytes 663560 | tf_op jit(solution)/shard_map/ppermute | solution.py:1417
  186.3 26.8 %collective-permute-start.66 = (bf16[96,1664]{1,0:T(8,128)(2,1)S(1)}, bf16[96,1664]{1,0:T(8,128)(2,1)S(1)}, u32[]{:S(2)}, u32[]{:S(2)}) collective-permute-start(bf16[96,1664]{1,0:T(8,128)(2,1)S(1)} %mlp_total.1.refs_0_), channel_id=1, source_target_pairs={{0,8},{1,9},{2,10},{3,11},{4,12},{5,13},{6,14},{7,15},{8,0},{9,1},... | collective-permute-start | bytes 958472 | tf_op jit(solution)/shard_map/ppermute | solution.py:1417
  188.9 24.3 %collective-permute-start.68 = (bf16[96,1664]{1,0:T(8,128)(2,1)S(1)}, bf16[96,1664]{1,0:T(8,128)(2,1)S(1)}, u32[]{:S(2)}, u32[]{:S(2)}) collective-permute-start(bf16[96,1664]{1,0:T(8,128)(2,1)S(1)} %collective-permute-done.67.refs_2_), channel_id=1, source_target_pairs={{0,8},{1,9},{2,10},{3,11},{4,12},{5,13},{6,14},{7,15},{8,0},{9,1},... | collective-permute-start | bytes 958472 | tf_op jit(solution)/shard_map/ppermute | solution.py:1417
  190.7 15.8 %collective-permute-start.63 = (bf16[192,384]{1,0:T(8,128)(2,1)S(1)}, bf16[192,384]{1,0:T(8,128)(2,1)S(1)}, u32[]{:S(2)}, u32[]{:S(2)}) collective-permute-start(bf16[192,384]{1,0:T(8,128)(2,1)S(1)} %get-tuple-element.273), channel_id=1, source_target_pairs={{0,2},{1,3},{2,0},{3,1},{4,6},{5,7},{6,4},{7,5},{8,10},{9,11},{10,... | collective-permute-start | bytes 442376 | tf_op jit(solution)/shard_map/ppermute | solution.py:1417
  191.8 14.8 %collective-permute-start.64 = (bf16[192,384]{1,0:T(8,128)(2,1)S(1)}, bf16[192,384]{1,0:T(8,128)(2,1)S(1)}, u32[]{:S(2)}, u32[]{:S(2)}) collective-permute-start(bf16[192,384]{1,0:T(8,128)(2,1)S(1)} %get-tuple-element.265), channel_id=1, source_target_pairs={{0,4},{1,5},{2,6},{3,7},{4,0},{5,1},{6,2},{7,3},{8,12},{9,13},{10,... | collective-permute-start | bytes 442376 | tf_op jit(solution)/shard_map/ppermute | solution.py:1417
  207.2 8.4 %collective-permute-start.69 = (bf16[96,384]{1,0:T(8,128)(2,1)S(1)}, bf16[96,384]{1,0:T(8,128)(2,1)S(1)}, u32[]{:S(2)}, u32[]{:S(2)}) collective-permute-start(bf16[96,384]{1,0:T(8,128)(2,1)S(1)} %get-tuple-element.281), channel_id=1, source_target_pairs={{0,4},{1,5},{2,6},{3,7},{4,0},{5,1},{6,2},{7,3},{8,12},{9,13},{10,... | collective-permute-start | bytes 221192 | tf_op jit(solution)/shard_map/ppermute | solution.py:1417
  207.3 8.3 %collective-permute-start.70 = (bf16[96,384]{1,0:T(8,128)(2,1)S(1)}, bf16[96,384]{1,0:T(8,128)(2,1)S(1)}, u32[]{:S(2)}, u32[]{:S(2)}) collective-permute-start(bf16[96,384]{1,0:T(8,128)(2,1)S(1)} %get-tuple-element.276), channel_id=1, source_target_pairs={{0,1},{1,0},{2,3},{3,2},{4,5},{5,4},{6,7},{7,6},{8,9},{9,8},{10,11... | collective-permute-start | bytes 221192 | tf_op jit(solution)/shard_map/ppermute | solution.py:1417
  216.2 17.5 %collective-permute-start.73 = (bf16[96,768]{1,0:T(8,128)(2,1)S(1)}, bf16[96,768]{1,0:T(8,128)(2,1)S(1)}, u32[]{:S(2)}, u32[]{:S(2)}) collective-permute-start(bf16[96,768]{1,0:T(8,128)(2,1)S(1)} %qkv_total.1.refs_0_), channel_id=1, source_target_pairs={{0,8},{1,9},{2,10},{3,11},{4,12},{5,13},{6,14},{7,15},{8,0},{9,1},... | collective-permute-start | bytes 442376 | tf_op jit(solution)/shard_map/ppermute | solution.py:1417
  221.3 12.4 %collective-permute-start.75 = (bf16[96,768]{1,0:T(8,128)(2,1)S(1)}, bf16[96,768]{1,0:T(8,128)(2,1)S(1)}, u32[]{:S(2)}, u32[]{:S(2)}) collective-permute-start(bf16[96,768]{1,0:T(8,128)(2,1)S(1)} %collective-permute-done.74.refs_2_), channel_id=1, source_target_pairs={{0,8},{1,9},{2,10},{3,11},{4,12},{5,13},{6,14},{7,15},{8,0},{9,1},... | collective-permute-start | bytes 442376 | tf_op jit(solution)/shard_map/ppermute | solution.py:1417
  (40 other events, 220.2 us)

commit v4 on v3

--- a/solution.py
+++ b/solution.py
@@ -857,8 +857,8 @@
                     qclip_ref[:, first : first + patches] = jnp.broadcast_to(clip, (1, patches))
 
 
-def pass_sum_kernel(index, unused_ref, even_ref, arrived_ref, out_ref):
-    out_ref[...] = (even_ref[index] + arrived_ref[...].astype(F32)).astype(BF)
+def pass_sum_kernel(unused_ref, even_ref, arrived_ref, out_ref):
+    out_ref[...] = (even_ref[...] + arrived_ref[...].astype(F32)).astype(BF)
 
 
 def add_kernel(unused_ref, left_ref, right_ref, out_ref):
@@ -875,11 +875,12 @@
         out_ref[...] = side_ref[...]
 
 
-def pass_on_kernel(ids_ref, even_ref, second_ref, third_ref, corner_ref, far_ref, side_ref):
+def pass_on_kernel(ids_ref, *refs):
+    far_even_ref, side_even_ref, second_ref, third_ref, corner_ref, far_ref, side_ref = refs
     core = lax.rem(ids_ref[0], 2)
     corner = corner_ref[...].astype(F32)
-    far = even_ref[1] + second_ref[...].astype(F32)
-    side = even_ref[2] + third_ref[...].astype(F32)
+    far = far_even_ref[...] + second_ref[...].astype(F32)
+    side = side_even_ref[...] + third_ref[...].astype(F32)
     far_ref[...] = (far + jnp.where(core == 1, corner, 0.0)).astype(BF)
     side_ref[...] = (side + jnp.where(core == 0, corner, 0.0)).astype(BF)
 
@@ -916,8 +917,9 @@
     q_ref, kv_ref, qclip_ref, kclip_ref, mixed_ref, log_ref = refs
     width = heads * HEAD_DIM
     count = q_ref.shape[0] // 2
-    for part in range(2):
-        queries = slice(part * count, (part + 1) * count)
+
+    def one(part, carry):
+        queries = pl.ds(pl.multiple_of(part * count, count), count)
         same = kclip_ref[...] == qclip_ref[:, queries]
         for head in range(heads):
             lanes = slice(head * HEAD_DIM, (head + 1) * HEAD_DIM)
@@ -929,18 +931,21 @@
             prob = (shifted * (1.0 / total)).astype(BF)
             mixed_ref[lanes, queries] = dot(kv_ref[:, values], prob, 0, 0).astype(BF)
             log_ref[head : head + 1, queries] = top + jnp.log(total)
-
-
-def split_blocks(values, even_ref, odd_refs):
-    rows = even_ref.shape[1]
-    for part in range(even_ref.shape[0]):
-        even_ref[part] = values[2 * part * rows : (2 * part + 1) * rows]
+        return carry
+
+    lax.fori_loop(0, 2, one, 0)
+
+
+def split_blocks(values, even_refs, odd_refs):
+    rows = even_refs[0].shape[0]
+    for part in range(len(odd_refs)):
+        even_refs[part][...] = values[2 * part * rows : (2 * part + 1) * rows]
         odd_refs[part][...] = values[(2 * part + 1) * rows : (2 * part + 2) * rows].astype(BF)
 
 
 def out_kernel(rank_ref, *refs):
     mixed_ref = refs[0]
-    even_ref, odd_refs, w_ref = refs[5], refs[6:8], refs[8]
+    even_refs, odd_refs, w_ref = refs[5:7], refs[7:9], refs[9]
     blocks = [ref[...] for ref in refs[1:5]]
     rank = rank_ref[0]
     width = blocks[0].shape[0]
@@ -949,7 +954,7 @@
         for bits in range(1, 4):
             found = jnp.where(rank == index ^ bits, blocks[bits], found)
         w_ref[:, index * width : (index + 1) * width] = found
-    split_blocks(dot(mixed_ref[...], w_ref[...], 0, 0), even_ref, odd_refs)
+    split_blocks(dot(mixed_ref[...], w_ref[...], 0, 0), even_refs, odd_refs)
 
 
 def norm_two_kernel(unused_ref, *refs):
@@ -958,7 +963,7 @@
     count = low_ref.shape[0]
     values = (
         moved_ref[:count, :].astype(F32)
-        + even_ref[0]
+        + even_ref[...]
         + arrived_ref[...].astype(F32)
         + far_ref[...].astype(F32)
     )
@@ -988,11 +993,22 @@
         ref[size:, :] = refs[2 * index + 1][...]
 
 
+def mlp_part(tokens, up_ref, down_ref, bias, act_ref, slope_ref, even_ref, odd_ref):
+    pre = dot(stack_rows(tokens), up_ref[...]) + bias
+    act, slope = gelu_both(pre)
+    act = act.astype(BF)
+    act_ref[...] = act
+    slope_ref[...] = slope
+    partial = dot(act, down_ref[...])
+    count = even_ref.shape[0]
+    even_ref[...] = partial[:count]
+    odd_ref[...] = partial[count:].astype(BF)
+
+
 def mlp_kernel(ids_ref, *refs):
-    tokens = refs[:4]
-    a_refs, b_refs, bias_ref = refs[4:6], refs[6:8], refs[8]
-    act_ref, slope_ref, up_ref, down_ref, conv_ref, even_ref = refs[9:15]
-    odd_refs = refs[15:]
+    tokens = refs[:2]
+    a_refs, b_refs, bias_ref = refs[2:4], refs[4:6], refs[6]
+    up_ref, down_ref, conv_ref, own_bias_ref = refs[7:11]
     rank = ids_ref[0]
     size = a_refs[0].shape[0] // 4
     quarter = up_ref.shape[1]
@@ -1006,7 +1022,6 @@
         for index, bits in enumerate(order):
             where = rows_at(place_of(ids_ref, bits), size)
             down_ref[where, :] = ref[index * size : (index + 1) * size, :]
-    count = tokens[0].shape[0]
     unit = quarter // 8
     bias = None
     for index in range(4):
@@ -1018,16 +1033,13 @@
             axis=1,
         )
         bias = found if bias is None else jnp.where(rank == index, found, bias)
-    for part in range(2):
-        rows = slice(2 * part * count, 2 * (part + 1) * count)
-        pre = dot(stack_rows(tokens[2 * part : 2 * part + 2]), up_ref[...]) + bias
-        act, slope = gelu_both(pre)
-        act = act.astype(BF)
-        act_ref[rows, :] = act
-        slope_ref[rows, :] = slope
-        partial = dot(act, down_ref[...])
-        even_ref[part] = partial[:count]
-        odd_refs[part][...] = partial[count:].astype(BF)
+    own_bias_ref[...] = bias
+    mlp_part(tokens, up_ref, down_ref, bias, *refs[11:])
+
+
+def mlp_more_kernel(unused_ref, *refs):
+    up_ref, down_ref, bias_ref = refs[2:5]
+    mlp_part(refs[:2], up_ref, down_ref, bias_ref[...], *refs[5:])
 
 
 def grid_masks(count):
@@ -1086,7 +1098,7 @@
     patches = GRID * GRID
     value = (
         sum_ref[...]
-        + even_ref[0]
+        + even_ref[...]
         + arrived_ref[...].astype(F32)
         + far_ref[...].astype(F32)
         + bias_ref[...]
@@ -1112,19 +1124,28 @@
             slopes.append(slope)
         else:
             maps = jax.nn.sigmoid(pre) * first_lanes
-    pooled_parts, map_parts = [], []
-    zero_rows = jnp.zeros((PAD - CH, value.shape[1]), F32)
+    frame_of_row = lax.broadcasted_iota(jnp.int32, (count, PAD), 0) // patches
+    wide = None
     for frame in range(frames):
-        rows = slice(frame * patches, (frame + 1) * patches)
-        start = count + frame * CH
-        cotangent = jnp.concatenate(
-            [moved_ref[start : start + CH, :].astype(F32), zero_rows], axis=0
-        )
-        learned = exact(maps[rows], value[rows], 0, 0)[:CH] * (1.0 / patches)
-        learned_ref[frame * CH : (frame + 1) * CH, :] = learned
-        pooled_parts.append(exact(maps[rows], cotangent) * (1.0 / patches))
-        map_parts.append(exact(value[rows], cotangent, 1, 1) * (1.0 / patches))
-    grad = jnp.concatenate(map_parts, axis=0) * maps * (1.0 - maps)
+        moved = pltpu.roll(maps, frame * CH, 1) if frame else maps
+        moved = moved * (frame_of_row == frame).astype(F32)
+        wide = moved if wide is None else wide + moved
+    cotangent = jnp.concatenate(
+        [
+            moved_ref[count : count + frames * CH, :].astype(F32),
+            jnp.zeros((PAD - frames * CH, value.shape[1]), F32),
+        ],
+        axis=0,
+    )
+    learned_ref[...] = exact(wide, value, 0, 0)[: frames * CH] * (1.0 / patches)
+    pooled = exact(wide, cotangent) * (1.0 / patches)
+    products = exact(value, cotangent, 1, 1) * (1.0 / patches)
+    grad = None
+    for frame in range(frames):
+        moved = pltpu.roll(products, PAD - frame * CH, 1) if frame else products
+        moved = moved * (frame_of_row == frame).astype(F32)
+        grad = moved if grad is None else grad + moved
+    grad = grad * maps * (1.0 - maps)
     small_ref[...] = jnp.zeros_like(small_ref)
     conv_start = 7 * vectors + 4 * vectors
     for layer in range(2, -1, -1):
@@ -1143,7 +1164,7 @@
     mean_scaled = jnp.mean(scaled, axis=-1, keepdims=True)
     mean_cross = jnp.mean(scaled * normed, axis=-1, keepdims=True)
     grad_value = inverse * (scaled - mean_scaled - normed * mean_cross)
-    grad_value = grad_value + jnp.concatenate(pooled_parts, axis=0)
+    grad_value = grad_value + pooled
     grad_ref[...] = grad_value
     low = grad_value.astype(BF)
     low_ref[...] = low
@@ -1153,23 +1174,17 @@
 
 
 def mlp_back_kernel(unused_ref, *refs):
-    grads = refs[:4]
-    slope_ref, up_ref, down_ref = refs[4:7]
-    pre_ref, even_ref, bias_ref = refs[7], refs[8], refs[11]
-    odd_refs = refs[9:11]
-    count = grads[0].shape[0]
-    total = None
-    for part in range(2):
-        rows = slice(2 * part * count, 2 * (part + 1) * count)
-        grad_act = dot(stack_rows(grads[2 * part : 2 * part + 2]), down_ref[...], 1, 1)
-        grad_pre = (grad_act * slope_ref[rows, :]).astype(BF)
-        pre_ref[rows, :] = grad_pre
-        term = column_sum(grad_pre.astype(F32))
-        total = term if total is None else total + term
-        partial = dot(grad_pre, up_ref[...], 1, 1)
-        even_ref[part] = partial[:count]
-        odd_refs[part][...] = partial[count:].astype(BF)
-    bias_ref[...] = total
+    grads = refs[:2]
+    slope_ref, up_ref, down_ref = refs[2:5]
+    pre_ref, even_ref, odd_ref, bias_ref = refs[5:]
+    grad_act = dot(stack_rows(grads), down_ref[...], 1, 1)
+    grad_pre = (grad_act * slope_ref[...]).astype(BF)
+    pre_ref[...] = grad_pre
+    bias_ref[...] = column_sum(grad_pre.astype(F32))
+    partial = dot(grad_pre, up_ref[...], 1, 1)
+    count = even_ref.shape[0]
+    even_ref[...] = partial[:count]
+    odd_ref[...] = partial[count:].astype(BF)
 
 
 def divide_rows(ids_ref, all_ref, refs):
@@ -1189,20 +1204,21 @@
 
 def mlp_grads_kernel(ids_ref, *refs):
     tokens, grads = refs[:4], refs[4:8]
-    act_ref, pre_ref, normed_ref, spread_ref = refs[8:12]
-    all_ref = refs[16]
-    quarter = act_ref.shape[1]
+    act, pre = stack_rows(refs[8:10]), stack_rows(refs[10:12])
+    normed_ref, spread_ref = refs[12:14]
+    all_ref = refs[18]
+    quarter = act.shape[1]
     width = tokens[0].shape[1]
-    all_ref[:, :quarter] = dot(stack_rows(tokens), pre_ref[...], 0, 0)
-    all_ref[:, quarter : quarter + width] = dot(act_ref[...], stack_rows(grads), 0, 0)
+    all_ref[:, :quarter] = dot(stack_rows(tokens), pre, 0, 0)
+    all_ref[:, quarter : quarter + width] = dot(act, stack_rows(grads), 0, 0)
     all_ref[:, quarter + width :] = dot(normed_ref[...], spread_ref[...], 0, 0)
-    divide_rows(ids_ref, all_ref, refs[12:16])
+    divide_rows(ids_ref, all_ref, refs[14:18])
 
 
 def norm_two_back_kernel(unused_ref, *refs):
     sum_ref, grad_ref, even_ref, arrived_ref, far_ref, gains_ref = refs[:6]
     total_ref, low_ref, rows_ref = refs[6:]
-    grad_normed = even_ref[0] + arrived_ref[...].astype(F32) + far_ref[...].astype(F32)
+    grad_normed = even_ref[...] + arrived_ref[...].astype(F32) + far_ref[...].astype(F32)
     result, gain_row, shift_row = back_of_norm(sum_ref[...], gains_ref[1:2, :], grad_normed)
     total = result + grad_ref[...]
     total_ref[...] = total
@@ -1211,43 +1227,55 @@
     rows_ref[1:2, :] = shift_row
 
 
-def attend_back_out_kernel(heads, scale, unused_ref, *refs):
-    branches = refs[:4]
-    out_ref, q_ref, kv_ref, log_ref, qclip_ref, kclip_ref, w_ref = refs[4:11]
-    own_ref, other_ref, even_ref = refs[11:14]
-    odd_refs, total_ref = refs[14:18], refs[18]
+def attend_back_part(heads, scale, first, branches, refs, prior_ref, own_ref, total_ref):
+    out_ref, q_ref, kv_ref, log_ref, qclip_ref, kclip_ref = refs
     width = heads * HEAD_DIM
-    count = q_ref.shape[0] // 2
-    rows = count // 2
-    for part in range(2):
-        queries = slice(part * count, (part + 1) * count)
-        grad_mixed = dot(
-            stack_rows(branches[2 * part : 2 * part + 2]), out_ref[...], 1, 1
-        ).astype(BF)
-        same = kclip_ref[...] == qclip_ref[:, queries]
-        query_parts, key_parts, value_parts = [], [], []
-        for head in range(heads):
-            lanes = slice(head * HEAD_DIM, (head + 1) * HEAD_DIM)
-            values = slice(width + head * HEAD_DIM, width + (head + 1) * HEAD_DIM)
-            scores = scores_of(kv_ref, q_ref, queries, lanes, same, scale)
-            prob = jnp.exp(scores - log_ref[head : head + 1, queries])
-            grad_prob = dot(kv_ref[:, values], grad_mixed[:, lanes], 1, 1)
-            delta = jnp.sum(prob * grad_prob, axis=0, keepdims=True)
-            grad_score = (prob * (grad_prob - delta)).astype(BF)
-            query_parts.append(dot(kv_ref[:, lanes], grad_score, 0, 0) * scale)
-            key_parts.append(dot(grad_score, q_ref[queries, lanes]) * scale)
-            value_parts.append(dot(prob.astype(BF), grad_mixed[:, lanes]))
-        own_ref[queries, :width] = jnp.concatenate(query_parts, axis=0).T.astype(BF)
-        terms = jnp.concatenate(key_parts + value_parts, axis=1)
-        if part == 0:
-            total_ref[...] = terms
-        else:
-            total_ref[...] += terms
-    own_ref[:, width:] = total_ref[: 2 * count, :].astype(BF)
-    other_ref[...] = total_ref[2 * count :, :].astype(BF)
+    count = own_ref.shape[0]
+    queries = slice(first, first + count)
+    grad_mixed = dot(stack_rows(branches), out_ref[...], 1, 1).astype(BF)
+    same = kclip_ref[...] == qclip_ref[:, queries]
+    query_parts, key_parts, value_parts = [], [], []
+    for head in range(heads):
+        lanes = slice(head * HEAD_DIM, (head + 1) * HEAD_DIM)
+        values = slice(width + head * HEAD_DIM, width + (head + 1) * HEAD_DIM)
+        scores = scores_of(kv_ref, q_ref, queries, lanes, same, scale)
+        prob = jnp.exp(scores - log_ref[head : head + 1, queries])
+        grad_prob = dot(kv_ref[:, values], grad_mixed[:, lanes], 1, 1)
+        delta = jnp.sum(prob * grad_prob, axis=0, keepdims=True)
+        grad_score = (prob * (grad_prob - delta)).astype(BF)
+        query_parts.append(dot(kv_ref[:, lanes], grad_score, 0, 0) * scale)
+        key_parts.append(dot(grad_score, q_ref[queries, lanes]) * scale)
+        value_parts.append(dot(prob.astype(BF), grad_mixed[:, lanes]))
+    own_ref[...] = jnp.concatenate(query_parts, axis=0).T.astype(BF)
+    terms = jnp.concatenate(key_parts + value_parts, axis=1)
+    total_ref[...] = terms if prior_ref is None else prior_ref[...] + terms
+
+
+def attend_back_first_kernel(heads, scale, unused_ref, *refs):
+    attend_back_part(heads, scale, 0, refs[:2], refs[2:8], None, refs[8], refs[9])
+
+
+def attend_back_next_kernel(heads, scale, first, unused_ref, *refs):
+    attend_back_part(heads, scale, first, refs[:1], refs[1:7], refs[7], refs[8], refs[9])
+
+
+def attend_back_last_kernel(heads, scale, first, unused_ref, *refs):
+    prior_ref, first_ref, next_ref, w_ref = refs[7:11]
+    own_ref, other_ref = refs[11:13]
+    even_refs, odd_refs = refs[13:17], refs[17:21]
+    part_ref, total_ref = refs[21:]
+    attend_back_part(heads, scale, first, refs[:1], refs[1:7], prior_ref, part_ref, total_ref)
+    width = heads * HEAD_DIM
+    count = own_ref.shape[0]
+    middle = first_ref.shape[0]
+    own_ref[:middle, :width] = first_ref[...]
+    own_ref[middle:first, :width] = next_ref[...]
+    own_ref[first:, :width] = part_ref[...]
+    own_ref[:, width:] = total_ref[:count, :].astype(BF)
+    other_ref[...] = total_ref[count:, :].astype(BF)
     own = dot(own_ref[...], w_ref[...], 1, 1)
     other = dot(other_ref[...], w_ref[:, width:], 1, 1)
-    split_blocks(jnp.concatenate([own, other], axis=0), even_ref, odd_refs)
+    split_blocks(jnp.concatenate([own, other], axis=0), even_refs, odd_refs)
 
 
 def qkv_grads_kernel(ids_ref, *refs):
@@ -1307,10 +1335,10 @@
 
 def norm_one_back_kernel(vectors, rank_ref, *refs):
     moved_ref, grad_ref, even_ref, arrived_ref, far_ref, side_ref, gains_ref = refs[:7]
-    learned_ref, small_ref, two_ref, up_ref, back_ref, sums_ref = refs[7:]
+    learned_ref, small_ref, two_ref, up_ref, more_up_ref, back_ref, sums_ref = refs[7:]
     count = grad_ref.shape[0]
     grad_normed = (
-        even_ref[0]
+        even_ref[...]
         + arrived_ref[...].astype(F32)
         + far_ref[...].astype(F32)
         + side_ref[...].astype(F32)
@@ -1329,7 +1357,7 @@
         store_rows(
             sums_ref,
             (7 + index) * vectors,
-            jnp.where(rank_ref[0] == index, up_ref[...], 0.0),
+            jnp.where(rank_ref[0] == index, up_ref[...] + more_up_ref[...], 0.0),
         )
 
 
@@ -1446,9 +1474,9 @@
         near = flip(block, 1)
         return [block, near, far, flip(far, 1)]
 
-    def pass_sum(even, arrived, index, name):
+    def pass_sum(even, arrived, name):
         (result,) = ordered_run(
-            functools.partial(pass_sum_kernel, index),
+            pass_sum_kernel,
             name,
             ids,
             [even, arrived],
@@ -1456,8 +1484,8 @@
         )
         return result
 
-    def scatter_four(even, odds, name):
-        far = flip(pass_sum(even, flip(odds[1], 1), 1, name), 2)
+    def scatter_four(evens, odds, name):
+        far = flip(pass_sum(evens[1], flip(odds[1], 1), name), 2)
         return flip(odds[0], 1), far
 
     def row_parts(blocks, first, second):
@@ -1519,15 +1547,6 @@
     for item in (pack_one, pack_two, pack_three):
         packs += [item, flip(item, 0, 0, 1)]
 
-    low_norm, query_clip, key_clip = ordered_run(
-        norm_one_kernel,
-        "norm_one",
-        ids,
-        [moved, ln_gains, ln_biases],
-        [((rows, width), BF), ((1, own_count), F32), ((2 * own_count, 1), F32)],
-    )
-    low_norm = after(low_norm, pack_side, pack_one, pack_two)
-
     mid_pad = jnp.pad(conv_mid, ((0, 0), (0, PAD - CH), (0, PAD - 9 * CH)))
     mid_bias_pad = jnp.pad(conv_mid_bias, ((0, 0), (0, PAD - CH)))
     first_bias_pad = jnp.pad(conv_first_bias, (0, PAD - CH)).reshape(1, PAD)
@@ -1546,6 +1565,15 @@
         [((size, hidden_quarter + PAD), BF), ((size, width), BF)],
     )
 
+    low_norm, query_clip, key_clip = ordered_run(
+        norm_one_kernel,
+        "norm_one",
+        ids,
+        [moved, ln_gains, ln_biases],
+        [((rows, width), BF), ((1, own_count), F32), ((2 * own_count, 1), F32)],
+    )
+    low_norm = after(low_norm, pack_side, pack_one, pack_two)
+
     def join(pairs, name):
         flat = [item for pair in pairs for item in pair]
         outs = [((2 * pair[0].shape[0], pair[0].shape[1]), BF) for pair in pairs]
@@ -1554,12 +1582,16 @@
     far = flip(low_norm, 2)
     side = flip(low_norm, 0, 0, 1)
     near = flip(low_norm, 1)
+    far_a, side_b = flip(own_a, 0, 2), flip(own_b, 0, 0, 1)
     (picked,) = ordered_run(
         pick_kernel,
         "pick",
         ids,
-        [after(far, *[packs[item] for item in (3, 5, 6)]), side],
+        [after(far, far_a, side_b, *packs[1:]), side],
         [((rows, width), BF)],
+    )
+    two_a, two_b = join(
+        [(own_a, far_a), (own_b, side_b)], "join_two"
     )
     corner = permute(
         picked,
@@ -1567,13 +1599,9 @@
     )
     far_near = flip(far, 1)
     side_near = flip(side, 1)
-    corner = after(corner, near, far_near, side_near, packs[7])
+    corner = after(corner, near, far_near, side_near)
     all_one = [near, far, far_near, side, side_near, corner, flip(corner, 1)]
     all_one = [low_norm] + all_one
-    two_a, two_b = join(
-        [(own_a, flip(own_a, 0, 2)), (own_b, flip(own_b, 0, 0, 1))], "join_two"
-    )
-
     queries, keyvals, qkv_quarter, own_out, near_out, far_out, both_out = ordered_run(
         functools.partial(project_kernel, quarter),
         "project",
@@ -1596,15 +1624,16 @@
         [queries, keyvals, query_clip, key_clip],
         [((quarter, own_count), BF), ((8, own_count), F32)],
     )
-    halves = [((2, rows, width), F32)] + [((rows, width), BF)] * 2
-    even, *odds, out_quarter = ordered_run(
+    blocks_of = [((rows, width), F32)] * 2 + [((rows, width), BF)] * 2
+    *parts, out_quarter = ordered_run(
         out_kernel,
         "out",
         ids,
         [attended] + out_blocks,
-        halves + [((quarter, width), BF)],
-    )
-    arrived, far = scatter_four(even, odds, "out_pass")
+        blocks_of + [((quarter, width), BF)],
+    )
+    evens, odds = parts[:2], parts[2:]
+    arrived, far = scatter_four(evens, odds, "out_pass")
     four_a, four_b = join(
         [(two_a, flip(two_a, 0, 1)), (two_b, flip(two_b, 0, 2))], "join_four"
     )
@@ -1612,26 +1641,41 @@
         norm_two_kernel,
         "norm_two",
         ids,
-        [moved, even, arrived, far, ln_gains, ln_biases],
+        [moved, evens[0], arrived, far, ln_gains, ln_biases],
         [((rows, width), F32), ((rows, width), BF)],
     )
-    all_two = gather_four(low_two)
-    act, slope, up_full, down_full, conv_full, even, *odds = ordered_run(
+    near_two, far_two = flip(low_two, 1), flip(low_two, 2)
+    pair = [
+        ((2 * rows, hidden_quarter), BF),
+        ((2 * rows, hidden_quarter), F32),
+        ((rows, width), F32),
+        ((rows, width), BF),
+    ]
+    up_full, down_full, conv_full, own_bias, act, slope, even, odd = ordered_run(
         mlp_kernel,
         "mlp",
         ids,
-        all_two
+        [low_two, near_two]
         + [four_a, flip(four_a, 0, 0, 1), four_b, flip(four_b, 0, 1), up_bias_row],
         [
-            ((own_count, hidden_quarter), BF),
-            ((own_count, hidden_quarter), F32),
             ((width, hidden_quarter), BF),
             ((hidden_quarter, width), BF),
             ((width, PAD), BF),
+            ((1, hidden_quarter), F32),
         ]
-        + halves,
-    )
-    arrived, far = scatter_four(even, odds, "mlp_pass")
+        + pair,
+    )
+    far_two = after(far_two, even)
+    all_two = [low_two, near_two, far_two, flip(far_two, 1)]
+    acts, slopes, evens, odds = [act], [slope], [even], [odd]
+    for item, rest in zip(
+        (acts, slopes, evens, odds),
+        ordered_run(
+            mlp_more_kernel, "mlp_more", ids, all_two[2:] + [up_full, down_full, own_bias], pair
+        ),
+    ):
+        item.append(rest)
+    arrived, far = scatter_four(evens, odds, "mlp_pass")
 
     small_rows = -(-(11 * vectors + 3 * CH + 4) // 8) * 8
     learned, low_mlp, grad_block, low_three, spread, small = ordered_run(
@@ -1640,7 +1684,7 @@
         ids,
         [
             after_attention,
-            even,
+            evens[0],
             arrived,
             far,
             down_bias_row,
@@ -1661,23 +1705,42 @@
             ((small_rows, PAD), F32),
         ],
     )
-    mixes = gather_four(after(attended, far))
-
-    all_mlp = gather_four(low_mlp)
-    grad_pre, even, *odds, grad_up_bias = ordered_run(
+
+    near_mlp, far_mlp = flip(low_mlp, 1), flip(low_mlp, 2)
+    pair = [
+        ((2 * rows, hidden_quarter), BF),
+        ((rows, width), F32),
+        ((rows, width), BF),
+        ((1, hidden_quarter), F32),
+    ]
+    pre, even, odd, bias = ordered_run(
         mlp_back_kernel,
         "mlp_back",
         ids,
-        all_mlp + [after(slope, *mixes), up_full, down_full],
-        [((own_count, hidden_quarter), BF)] + halves + [((1, hidden_quarter), F32)],
-    )
-    arrived, far = scatter_four(even, odds, "mlp_back_pass")
+        [low_mlp, near_mlp, slopes[0], up_full, down_full],
+        pair,
+    )
+    far_mlp = after(far_mlp, even)
+    all_mlp = [low_mlp, near_mlp, far_mlp, flip(far_mlp, 1)]
+    pres, evens, odds, biases = [pre], [even], [odd], [bias]
+    for item, rest in zip(
+        (pres, evens, odds, biases),
+        ordered_run(
+            mlp_back_kernel,
+            "mlp_back_more",
+            ids,
+            all_mlp[2:] + [slopes[1], up_full, down_full],
+            pair,
+        ),
+    ):
+        item.append(rest)
+    arrived, far = scatter_four(evens, odds, "mlp_back_pass")
     columns = hidden_quarter + width + PAD
     mlp_parts = ordered_run(
         mlp_grads_kernel,
         "mlp_grads",
         ids,
-        all_two + all_mlp + [act, grad_pre, low_three, spread],
+        all_two + all_mlp + acts + pres + [low_three, spread],
         row_parts(4, hidden_quarter, width + PAD),
         [pltpu.VMEM((width, columns), F32)],
     )
@@ -1685,27 +1748,47 @@
         norm_two_back_kernel,
         "norm_two_back",
         ids,
-        [after_attention, grad_block, even, arrived, far, ln_gains],
+        [after_attention, grad_block, evens[0], arrived, far, ln_gains],
         [((rows, width), F32), ((rows, width), BF), ((2, width), F32)],
     )
 
-    all_branch = gather_four(low_branch)
-    grads_own, grads_other, even, *odds = ordered_run(
-        functools.partial(attend_back_out_kernel, heads, scale),
-        "attend_back_out",
-        ids,
-        all_branch + [out_quarter, queries, keyvals, logs, query_clip, key_clip, qkv_quarter],
+    near_branch, far_branch = flip(low_branch, 1), flip(low_branch, 2)
+    mixes = gather_four(after(attended, far_branch))
+    common = [out_quarter, queries, keyvals, logs, query_clip, key_clip]
+    total = ((2 * own_count, 2 * quarter), F32)
+    grads_first, sums_first = ordered_run(
+        functools.partial(attend_back_first_kernel, heads, scale),
+        "attend_back",
+        ids,
+        [low_branch, near_branch] + common,
+        [((2 * rows, quarter), BF), total],
+    )
+    far_branch = after(far_branch, sums_first)
+    all_branch = [low_branch, near_branch, far_branch, flip(far_branch, 1)]
+    grads_next, sums_next = ordered_run(
+        functools.partial(attend_back_next_kernel, heads, scale, 2 * rows),
+        "attend_back_next",
+        ids,
+        [far_branch] + common + [sums_first],
+        [((rows, quarter), BF), total],
+    )
+    grads_own, grads_other, *parts = ordered_run(
+        functools.partial(attend_back_last_kernel, heads, scale, 3 * rows),
+        "attend_back_last",
+        ids,
+        all_branch[3:] + common + [sums_next, grads_first, grads_next, qkv_quarter],
+        [((own_count, 3 * quarter), BF), ((own_count, 2 * quarter), BF)]
+        + [((rows, width), F32)] * 4
+        + [((rows, width), BF)] * 4,
         [
-            ((own_count, 3 * quarter), BF),
-            ((own_count, 2 * quarter), BF),
-            ((4, rows, width), F32),
-        ]
-        + [((rows, width), BF)] * 4,
-        [pltpu.VMEM((2 * own_count, 2 * quarter), F32)],
-    )
-    arrived = [flip(item, 1) for item in odds]
+            pltpu.VMEM((rows, quarter), BF),
+            pltpu.VMEM((2 * own_count, 2 * quarter), F32),
+        ],
+    )
+    evens = parts[:4]
+    arrived = [flip(item, 1) for item in parts[4:]]
     corner = permute(
-        pass_sum(even, arrived[3], 3, "corner_pass"),
+        pass_sum(evens[3], arrived[3], "corner_pass"),
         lambda seq, hi, lo: (seq ^ 2, hi, lo) if seq % 2 == 0 else (seq, hi, lo ^ 1),
     )
     mlp_parts = scatter_half(mlp_parts, "mlp_half")
@@ -1721,24 +1804,26 @@
         pass_on_kernel,
         "pass_on",
         ids,
-        [even, arrived[1], arrived[2], corner],
+        [evens[1], evens[2], arrived[1], arrived[2], corner],
         [((rows, width), BF), ((rows, width), BF)],
     )
     far, side = flip(far, 2), flip(side, 0, 0, 1)
     mlp_parts = scatter_fourth(mlp_parts, "mlp_fourth")
-    qkv_parts = list(lax.optimization_barrier(tuple(qkv_parts) + (mlp_parts[0],))[:4])
     moved_back, sums = ordered_run(
         functools.partial(norm_one_back_kernel, vectors),
         "norm_one_back",
         ids,
-        [moved, grad_after, even, arrived[0], far, side, ln_gains]
-        + [learned, small, rows_two, grad_up_bias],
+        [moved, grad_after, evens[0], arrived[0], far, side, ln_gains]
+        + [learned, small, rows_two]
+        + biases,
         [((rows + learned_rows, width), BF), ((small_rows, PAD), F32)],
     )
-
+    qkv_parts = list(lax.optimization_barrier(tuple(qkv_parts) + (sums,))[:4])
+
+    sums = add(sums, flip(sums, 1), "sum_core")
     mlp_share = scatter_last(mlp_parts, "mlp_total")
+    sums = add(sums, flip(sums, 2), "sum_x")
     qkv_parts = scatter_half(qkv_parts, "qkv_half")
-    sums = add(sums, flip(sums, 1), "sum_core")
     grad_input, learned = ordered_run(
         back_kernel,
         "back",
@@ -1746,17 +1831,10 @@
         [from_planes(moved_back)],
         [((rows, width), F32), ((learned_rows, width), F32)],
     )
-    sums = add(sums, flip(sums, 2), "sum_x")
+    sums = add(sums, flip(sums, 0, 0, 1), "sum_y")
+    mlp_share = after(mlp_share, qkv_parts[0])
+    mlp_far, mlp_near = flip(mlp_share, 2), flip(mlp_share, 1)
     qkv_parts = scatter_fourth(qkv_parts, "qkv_fourth")
-    sums = add(sums, flip(sums, 0, 0, 1), "sum_y")
-    sum_up, sum_down, sum_conv = ordered_run(
-        functools.partial(finish_mlp_kernel, ranks, hidden_quarter, width, unit),
-        "finish_mlp",
-        ids,
-        gather_four(mlp_share),
-        [((size, hidden), F32), ((ranks * unit, width), F32), ((size, 9 * CH), F32)],
-    )
-    qkv_share = scatter_last(qkv_parts, "qkv_total")
     sums = add(sums, flip(sums, 0, 1), "sum_z")
     sum_gains, sum_shifts, sum_up_bias, sum_down_bias, sum_first, sum_mid, sum_mid_bias = (
         ordered_run(
@@ -1776,11 +1854,21 @@
             [pltpu.VMEM((small_rows, PAD), F32)],
         )
     )
+    qkv_share = scatter_last(qkv_parts, "qkv_total")
+    mlp_far = after(mlp_far, qkv_share)
+    qkv_far, qkv_near = flip(qkv_share, 2), flip(qkv_share, 1)
+    sum_up, sum_down, sum_conv = ordered_run(
+        functools.partial(finish_mlp_kernel, ranks, hidden_quarter, width, unit),
+        "finish_mlp",
+        ids,
+        [mlp_share, mlp_near, mlp_far, flip(mlp_far, 1)],
+        [((size, hidden), F32), ((ranks * unit, width), F32), ((size, 9 * CH), F32)],
+    )
     sum_qkv, sum_out = ordered_run(
         functools.partial(finish_qkv_kernel, ranks, quarter),
         "finish_qkv",
         ids,
-        gather_four(qkv_share),
+        [qkv_share, qkv_near, qkv_far, flip(after(qkv_far, sum_down), 1)],
         [((size, 3 * width), F32), ((size, width), F32)],
     )
     return (

time: 237 us -> 222 us (0.937)
  starting transfers between devices: 63.9 us -> 52.1 us
  waiting for transfers between devices: 103 us -> 96.4 us
  Pallas kernels: 56.9 us -> 61.6 us
    ppermute x76, starting transfers between devices: 63.9 us -> 52.1 us  [permute(): return lax.ppermute(array, AXES, pairs)]
    ppermute x76, waiting for transfers between devices: 103 us -> 96.4 us  [permute(): return lax.ppermute(array, AXES, pairs)]
    pallas_call x38 -> x42, Pallas kernels: 56.9 us -> 61.6 us  [run(): pl.pallas_call(kernel, in_specs=[pl.BlockSpec(memory_space=pltpu.SMEM)] +...]
    unnamed x26 -> x22, local copies, waits for them, and re-layouts: 7.26 us -> 5.85 us
  transfers between devices with their start and end apart: 76 -> 76, of which waited for: 34 -> 35; matrix products, arithmetic and copies ran while one was open for 2% -> 2% of each run, Pallas kernels for 20% -> 22%
where the time goes in v4:
time: 222 us; the launch traced here: 221 us
  waiting for transfers between devices  96.4 us (43%)
  Pallas kernels  61.6 us (28%)
  starting transfers between devices  52.1 us (23%)
  local copies, waits for them, and re-layouts  8.6 us (4%)
    ppermute x76, waiting for transfers between devices, permute(): return lax.ppermute(array, AXES, pairs)  96.4 us
    pallas_call x42, Pallas kernels, run(): pl.pallas_call(kernel, in_specs=[pl.BlockSpec(memory_space=pltpu.SMEM)] +...  61.6 us
    ppermute x76, starting transfers between devices, permute(): return lax.ppermute(array, AXES, pairs)  52.1 us
    unnamed x22, local copies, waits for them, and re-layouts  5.85 us
  transfers between devices with their start and end apart: 76, of which 35 were waited for; matrix products, arithmetic and copies ran while one was open for 2% of the time, Pallas kernels for 22%

profile of v4, /device:TPU:2, one launch (start us, length us, event | category | flops | bytes accessed | tf_op | source)
XLA Modules:
  0.0 220.7 jit_solution(3006571203817702970)
XLA Ops:
  3.7 3.5 %collective-permute-start = (bf16[160,768]{1,0:T(8,128)(2,1)S(1)}, bf16[160,768]{1,0:T(8,128)(2,1)S(1)}, u32[]{:S(2)}, u32[]{:S(2)}) collective-permute-start(bf16[160,768]{1,0:T(8,128)(2,1)S(1)} %pack.1), channel_id=1, source_target_pairs={{0,0},{1,1},{2,16},{3,17},{4,8},{5,9},{6,24},{7,25},{8,4},{9,5},{1... | collective-permute-start | bytes 737288 | tf_op jit(solution)/shard_map/ppermute | solution.py:1445
  10.9 1.5 collective-permute-start.1
  12.4 1.6 collective-permute-start.2
  18.7 2.8 %collective-permute-done.3.refs_12_ = bf16[96,768]{1,0:T(8,128)(2,1)S(1)} collective-permute-done((bf16[96,768]{1,0:T(8,128)(2,1)S(1)}, bf16[96,768]{1,0:T(8,128)(2,1)S(1)}, u32[]{:S(2)}, u32[]{:S(2)}) %collective-permute-start.3) | collective-permute-done | bytes 147488 | tf_op jit(solution)/shard_map/ppermute | solution.py:1445
  21.5 5.9 %collective-permute-start.6 = (bf16[96,768]{1,0:T(8,128)(2,1)S(1)}, bf16[96,768]{1,0:T(8,128)(2,1)S(1)}, u32[]{:S(2)}, u32[]{:S(2)}) collective-permute-start(bf16[96,768]{1,0:T(8,128)(2,1)S(1)} %get-tuple-element.184.refs_2_), channel_id=1, source_target_pairs={{0,1},{1,0},{2,3},{3,2},{4,5},{5,4},{6,7},{7,6},{8,9},{9,8},{10,11... | collective-permute-start | bytes 442376 | tf_op jit(solution)/shard_map/ppermute | solution.py:1445
  28.4 2.1 collective-permute-done.6.refs_3_
  30.5 2.4 %collective-permute-start.7 = (bf16[96,768]{1,0:T(8,128)(2,1)S(1)}, bf16[96,768]{1,0:T(8,128)(2,1)S(1)}, u32[]{:S(2)}, u32[]{:S(2)}) collective-permute-start(bf16[96,768]{1,0:T(8,128)(2,1)S(1)} %collective-permute-done.2.refs_10_), channel_id=1, source_target_pairs={{0,1},{1,0},{2,3},{3,2},{4,5},{5,4},{6,7},{7,6},{8,9},{9,8},{10,11... | collective-permute-start | bytes 442376 | tf_op jit(solution)/shard_map/ppermute | solution.py:1445
  32.9 2.0 collective-permute-start.10
  34.9 4.4 %collective-permute-done.7.refs_11_ = bf16[96,768]{1,0:T(8,128)(2,1)S(1)} collective-permute-done((bf16[96,768]{1,0:T(8,128)(2,1)S(1)}, bf16[96,768]{1,0:T(8,128)(2,1)S(1)}, u32[]{:S(2)}, u32[]{:S(2)}) %collective-permute-start.7) | collective-permute-done | bytes 147488 | tf_op jit(solution)/shard_map/ppermute | solution.py:1445
  39.3 3.2 %collective-permute-done.8.refs_13_ = bf16[96,768]{1,0:T(8,128)(2,1)S(1)} collective-permute-done((bf16[96,768]{1,0:T(8,128)(2,1)S(1)}, bf16[96,768]{1,0:T(8,128)(2,1)S(1)}, u32[]{:S(2)}, u32[]{:S(2)}) %collective-permute-start.8) | collective-permute-done | bytes 147488 | tf_op jit(solution)/shard_map/ppermute | solution.py:1445
  42.4 3.1 %collective-permute-done.10.refs_15_ = bf16[96,768]{1,0:T(8,128)(2,1)S(1)} collective-permute-done((bf16[96,768]{1,0:T(8,128)(2,1)S(1)}, bf16[96,768]{1,0:T(8,128)(2,1)S(1)}, u32[]{:S(2)}, u32[]{:S(2)}) %collective-permute-start.10) | collective-permute-done | bytes 147488 | tf_op jit(solution)/shard_map/ppermute | solution.py:1445
  47.4 4.5 %collective-permute-done.15.refs_6_ = bf16[128,768]{1,0:T(8,128)(2,1)S(1)} collective-permute-done((bf16[128,768]{1,0:T(8,128)(2,1)S(1)}, bf16[128,768]{1,0:T(8,128)(2,1)S(1)}, u32[]{:S(2)}, u32[]{:S(2)}) %collective-permute-start.15) | collective-permute-done | bytes 196640 | tf_op jit(solution)/shard_map/ppermute | solution.py:1445
  53.3 1.8 project.1
  55.3 1.8 collective-permute-start.18
  57.2 5.9 %attend.1 = (bf16[192,512]{1,0:T(8,128)(2,1)S(1)}, f32[8,512]{1,0:T(8,128)S(1)}) custom-call(s32[3]{0:T(128)S(1)} %pad_add_fusion.unused_ref.ids_ref.rank_ref, bf16[512,192]{1,0:T(8,128)(2,1)S(1)} %get-tuple-element.198.refs_0_.refs_3_.refs_2_, bf16[1024,384]{1,0:T(8,128)(2,1)S(1)} %get-tuple-element.199.refs_1_.refs_4_.refs_3_, ...), custom_call_target="tpu_custom_call" | custom-call | tf_op jit(solution)/shard_map/attend/pallas_call | solution.py:745
  66.4 2.9 %collective-permute-done.22.refs_3_ = bf16[192,768]{1,0:T(8,128)(2,1)S(1)} collective-permute-done((bf16[192,768]{1,0:T(8,128)(2,1)S(1)}, bf16[192,768]{1,0:T(8,128)(2,1)S(1)}, u32[]{:S(2)}, u32[]{:S(2)}) %collective-permute-start.22) | collective-permute-done | bytes 294944 | tf_op jit(solution)/shard_map/ppermute | solution.py:1445
  72.1 5.9 %collective-permute-done.24.refs_3_ = bf16[128,768]{1,0:T(8,128)(2,1)S(1)} collective-permute-done((bf16[128,768]{1,0:T(8,128)(2,1)S(1)}, bf16[128,768]{1,0:T(8,128)(2,1)S(1)}, u32[]{:S(2)}, u32[]{:S(2)}) %collective-permute-start.24) | collective-permute-done | bytes 196640 | tf_op jit(solution)/shard_map/ppermute | solution.py:1445
  80.3 5.0 %collective-permute-done.28.refs_5_ = bf16[384,768]{1,0:T(8,128)(2,1)S(1)} collective-permute-done((bf16[384,768]{1,0:T(8,128)(2,1)S(1)}, bf16[384,768]{1,0:T(8,128)(2,1)S(1)}, u32[]{:S(2)}, u32[]{:S(2)}) %collective-permute-start.28) | collective-permute-done | bytes 589856 | tf_op jit(solution)/shard_map/ppermute | solution.py:1445
  85.3 1.5 collective-permute-done.27.refs_3_
  86.8 2.1 mlp.1
  89.0 1.4 collective-permute-done.29.refs_1_.refs_3_
  90.5 2.0 mlp_more.1
  95.3 6.2 %collective-permute-done.32.refs_3_ = bf16[128,768]{1,0:T(8,128)(2,1)S(1)} collective-permute-done((bf16[128,768]{1,0:T(8,128)(2,1)S(1)}, bf16[128,768]{1,0:T(8,128)(2,1)S(1)}, u32[]{:S(2)}, u32[]{:S(2)}) %collective-permute-start.32) | collective-permute-done | bytes 196640 | tf_op jit(solution)/shard_map/ppermute | solution.py:1445
  101.6 6.4 %tail.1 = (f32[16,768]{1,0:T(8,128)S(1)}, bf16[128,768]{1,0:T(8,128)(2,1)S(1)}, f32[128,768]{1,0:T(8,128)S(1)}, bf16[128,768]{1,0:T(8,128)(2,1)S(1)}, bf16[128,1...) custom-call(s32[3]{0:T(128)S(1)} %pad_add_fusion.unused_ref.ids_ref.rank_ref, f32[128,768]{1,0:T(8,128)S(1)} %get-tuple-element.252.refs_0_, ...), custom_call_target="tpu_custom_call" | custom-call | tf_op jit(solution)/shard_map/tail/pallas_call | solution.py:745
  109.4 1.5 mlp_back.1
  110.9 4.4 %collective-permute-done.33.refs_0_.refs_6_ = bf16[128,768]{1,0:T(8,128)(2,1)S(1)} collective-permute-done((bf16[128,768]{1,0:T(8,128)(2,1)S(1)}, bf16[128,768]{1,0:T(8,128)(2,1)S(1)}, u32[]{:S(2)}, u32[]{:S(2)}) %collective-permute-start.33) | collective-permute-done | bytes 196640 | tf_op jit(solution)/shard_map/ppermute | solution.py:1445
  115.3 1.4 collective-permute-done.35.refs_1_.refs_7_
  116.8 1.5 mlp_back_more.1
  121.1 2.3 %mlp_grads.1 = (f32[384,768]{1,0:T(8,128)S(1)}, bf16[384,768]{1,0:T(8,128)(2,1)S(1)}, f32[384,896]{1,0:T(8,128)S(1)}, bf16[384,896]{1,0:T(8,128)(2,1)S(1)}) custom-call(s32[3]{0:T(128)S(1)} %pad_add_fusion.unused_ref.ids_ref.rank_ref, bf16[128,768]{1,0:T(8,128)(2,1)S(1)} %get-tuple-element.243.refs_0_, bf16[128,768]{1,0:T(8,128)(2,1)S(1)} %collective-permute-done.26.refs_1_, ...), custom_call_target="tpu_custom_call" | custom-call | tf_op jit(solution)/shard_map/mlp_grads/pallas_call | solution.py:745
  124.1 3.3 %collective-permute-done.38.refs_4_ = bf16[128,768]{1,0:T(8,128)(2,1)S(1)} collective-permute-done((bf16[128,768]{1,0:T(8,128)(2,1)S(1)}, bf16[128,768]{1,0:T(8,128)(2,1)S(1)}, u32[]{:S(2)}, u32[]{:S(2)}) %collective-permute-start.38) | collective-permute-done | bytes 196640 | tf_op jit(solution)/shard_map/ppermute | solution.py:1445
  130.0 4.0 %attend_back.1 = (bf16[256,192]{1,0:T(8,128)(2,1)S(1)}, f32[1024,384]{1,0:T(8,128)S(1)}) custom-call(s32[3]{0:T(128)S(1)} %pad_add_fusion.unused_ref.ids_ref.rank_ref, bf16[128,768]{1,0:T(8,128)(2,1)S(1)} %get-tuple-element.257.refs_0_.refs_8_, bf16[128,768]{1,0:T(8,128)(2,1)S(1)} %collective-permute-done.40.refs_1_.refs_9_, ...), custom_call_target="tpu_custom_call" | custom-call | tf_op jit(solution)/shard_map/attend_back/pallas_call | solution.py:745
  134.1 1.8 collective-permute-done.39.refs_0_.refs_10_
  136.6 2.8 %attend_back_next.1 = (bf16[128,192]{1,0:T(8,128)(2,1)S(1)}, f32[1024,384]{1,0:T(8,128)S(1)}) custom-call(s32[3]{0:T(128)S(1)} %pad_add_fusion.unused_ref.ids_ref.rank_ref, bf16[128,768]{1,0:T(8,128)(2,1)S(1)} %collective-permute-done.39.refs_0_.refs_10_, bf16[192,768]{1,0:T(8,128)(2,1)S(1)} %get-tuple-element.206.refs_2_.refs_1_, ...), custom_call_target="tpu_custom_call" | custom-call | tf_op jit(solution)/shard_map/attend_back_next/pallas_call | solution.py:745
  139.4 4.3 %attend_back_last.1 = (bf16[512,576]{1,0:T(8,128)(2,1)S(1)}, bf16[512,384]{1,0:T(8,128)(2,1)S(1)}, f32[128,768]{1,0:T(8,128)S(1)}, f32[128,768]{1,0:T(8,128)S(1)...) custom-call(s32[3]{0:T(128)S(1)} %pad_add_fusion.unused_ref.ids_ref., ...), custom_call_target="tpu_custom_call" | custom-call | tf_op jit(solution)/shard_map/attend_back_last/pallas_call | solution.py:745
  148.5 1.5 collective-permute-start.52
  150.6 2.4 %qkv_grads.1 = (f32[384,384]{1,0:T(8,128)S(1)}, bf16[384,384]{1,0:T(8,128)(2,1)S(1)}, f32[384,384]{1,0:T(8,128)S(1)}, bf16[384,384]{1,0:T(8,128)(2,1)S(1)}) custom-call(s32[3]{0:T(128)S(1)} %pad_add_fusion.unused_ref.ids_ref.rank_ref, bf16[128,768]{1,0:T(8,128)(2,1)S(1)} %get-tuple-element.276.refs_0_, bf16[128,768]{1,0:T(8,128)(2,1)S(1)} %collective-permute-done.12.refs_1_, ...), custom_call_target="tpu_custom_call" | custom-call | tf_op jit(solution)/shard_map/qkv_grads/pallas_call | solution.py:745
  155.7 7.7 %collective-permute-done.51.refs_1_ = bf16[192,768]{1,0:T(8,128)(2,1)S(1)} collective-permute-done((bf16[192,768]{1,0:T(8,128)(2,1)S(1)}, bf16[192,768]{1,0:T(8,128)(2,1)S(1)}, u32[]{:S(2)}, u32[]{:S(2)}) %collective-permute-start.51) | collective-permute-done | bytes 294944 | tf_op jit(solution)/shard_map/ppermute | solution.py:1445
  163.4 2.6 %collective-permute-done.52.refs_3_ = bf16[192,896]{1,0:T(8,128)(2,1)S(1)} collective-permute-done((bf16[192,896]{1,0:T(8,128)(2,1)S(1)}, bf16[192,896]{1,0:T(8,128)(2,1)S(1)}, u32[]{:S(2)}, u32[]{:S(2)}) %collective-permute-start.52) | collective-permute-done | bytes 344096 | tf_op jit(solution)/shard_map/ppermute | solution.py:1445
  167.7 1.6 collective-permute-start.61
  169.8 2.3 %collective-permute-start.58 = (bf16[96,768]{1,0:T(8,128)(2,1)S(1)}, bf16[96,768]{1,0:T(8,128)(2,1)S(1)}, u32[]{:S(2)}, u32[]{:S(2)}) collective-permute-start(bf16[96,768]{1,0:T(8,128)(2,1)S(1)} %get-tuple-element.305), channel_id=1, source_target_pairs={{0,4},{1,5},{2,6},{3,7},{4,0},{5,1},{6,2},{7,3},{8,12},{9,13},{10,... | collective-permute-start | bytes 442376 | tf_op jit(solution)/shard_map/ppermute | solution.py:1445
  175.1 3.7 %collective-permute-done.58.arrived_ref = bf16[96,768]{1,0:T(8,128)(2,1)S(1)} collective-permute-done((bf16[96,768]{1,0:T(8,128)(2,1)S(1)}, bf16[96,768]{1,0:T(8,128)(2,1)S(1)}, u32[]{:S(2)}, u32[]{:S(2)}) %collective-permute-start.58) | collective-permute-done | bytes 147488 | tf_op jit(solution)/shard_map/ppermute | solution.py:1445
  178.8 4.8 %collective-permute-start.56 = (bf16[144,768]{1,0:T(8,128)(2,1)S(1)}, bf16[144,768]{1,0:T(8,128)(2,1)S(1)}, u32[]{:S(2)}, u32[]{:S(2)}) collective-permute-start(bf16[144,768]{1,0:T(8,128)(2,1)S(1)} %get-tuple-element.296), channel_id=1, source_target_pairs={{0,0},{1,1},{2,16},{3,17},{4,8},{5,9},{6,24},{7,25},{8,4},{9,5},{1... | collective-permute-start | bytes 663560 | tf_op jit(solution)/shard_map/ppermute | solution.py:1445
  187.5 9.4 %collective-permute-done.56.moved_ref = bf16[144,768]{1,0:T(8,128)(2,1)S(1)} collective-permute-done((bf16[144,768]{1,0:T(8,128)(2,1)S(1)}, bf16[144,768]{1,0:T(8,128)(2,1)S(1)}, u32[]{:S(2)}, u32[]{:S(2)}) %collective-permute-start.56) | collective-permute-done | bytes 221216 | tf_op jit(solution)/shard_map/ppermute | solution.py:1445
  199.8 4.0 %collective-permute-done.66.right_ref = f32[96,128]{1,0:T(8,128)S(1)} collective-permute-done((f32[96,128]{1,0:T(8,128)S(1)}, f32[96,128]{1,0:T(8,128)S(1)}, u32[]{:S(2)}, u32[]{:S(2)}) %collective-permute-start.66) | collective-permute-done | bytes 49184 | tf_op jit(solution)/shard_map/ppermute | solution.py:1445
  204.4 4.9 %collective-permute-done.67.arrived_ref = f32[96,128]{1,0:T(8,128)S(1)} collective-permute-done((f32[96,128]{1,0:T(8,128)S(1)}, f32[96,128]{1,0:T(8,128)S(1)}, u32[]{:S(2)}, u32[]{:S(2)}) %collective-permute-start.67) | collective-permute-done | bytes 49184 | tf_op jit(solution)/shard_map/ppermute | solution.py:1445
  212.9 2.3 %finish_mlp.1 = (f32[96,3072]{1,0:T(8,128)}, f32[384,768]{1,0:T(8,128)}, f32[96,72]{1,0:T(8,128)S(1)}) custom-call(s32[3]{0:T(128)S(1)} %pad_add_fusion.unused_ref.ids_ref.rank_ref, bf16[96,1664]{1,0:T(8,128)(2,1)S(1)} %mlp_total.1.refs_0_, bf16[96,1664]{1,0:T(8,128)(2,1)S(1)} %collective-permute-done.70.refs_1_, ...), custom_call_target="tpu_custom_call" | custom-call | tf_op jit(solution)/shard_map/finish_mlp/pallas_call | solution.py:745
  215.2 2.3 %collective-permute-done.74.refs_2_ = bf16[96,768]{1,0:T(8,128)(2,1)S(1)} collective-permute-done((bf16[96,768]{1,0:T(8,128)(2,1)S(1)}, bf16[96,768]{1,0:T(8,128)(2,1)S(1)}, u32[]{:S(2)}, u32[]{:S(2)}) %collective-permute-start.74) | collective-permute-done | bytes 147488 | tf_op jit(solution)/shard_map/ppermute | solution.py:1445
  218.9 1.8 finish_qkv.1
  (174 shorter events, 60.8 us)
Async XLA Ops:
  3.7 23.6 %collective-permute-start = (bf16[160,768]{1,0:T(8,128)(2,1)S(1)}, bf16[160,768]{1,0:T(8,128)(2,1)S(1)}, u32[]{:S(2)}, u32[]{:S(2)}) collective-permute-start(bf16[160,768]{1,0:T(8,128)(2,1)S(1)} %pack.1), channel_id=1, source_target_pairs={{0,0},{1,1},{2,16},{3,17},{4,8},{5,9},{6,24},{7,25},{8,4},{9,5},{1... | collective-permute-start | bytes 737288 | tf_op jit(solution)/shard_map/ppermute | solution.py:1445
  9.8 11.7 %collective-permute-start.3 = (bf16[96,768]{1,0:T(8,128)(2,1)S(1)}, bf16[96,768]{1,0:T(8,128)(2,1)S(1)}, u32[]{:S(2)}, u32[]{:S(2)}) collective-permute-start(bf16[96,768]{1,0:T(8,128)(2,1)S(1)} %select.10.refs_8_), channel_id=1, source_target_pairs={{0,4},{1,5},{2,6},{3,7},{4,0},{5,1},{6,2},{7,3},{8,12},{9,13},{10,... | collective-permute-start | bytes 442376 | tf_op jit(solution)/shard_map/ppermute | solution.py:1445
  10.9 17.3 %collective-permute-start.1 = (bf16[96,768]{1,0:T(8,128)(2,1)S(1)}, bf16[96,768]{1,0:T(8,128)(2,1)S(1)}, u32[]{:S(2)}, u32[]{:S(2)}) collective-permute-start(bf16[96,768]{1,0:T(8,128)(2,1)S(1)} %select.10.refs_8_), channel_id=1, source_target_pairs={{0,1},{1,0},{2,3},{3,2},{4,5},{5,4},{6,7},{7,6},{8,9},{9,8},{10,11... | collective-permute-start | bytes 442376 | tf_op jit(solution)/shard_map/ppermute | solution.py:1445
  12.4 15.8 %collective-permute-start.2 = (bf16[96,768]{1,0:T(8,128)(2,1)S(1)}, bf16[96,768]{1,0:T(8,128)(2,1)S(1)}, u32[]{:S(2)}, u32[]{:S(2)}) collective-permute-start(bf16[96,768]{1,0:T(8,128)(2,1)S(1)} %select.10.refs_8_), channel_id=1, source_target_pairs={{0,2},{1,3},{2,0},{3,1},{4,6},{5,7},{6,4},{7,5},{8,10},{9,11},{10,... | collective-permute-start | bytes 442376 | tf_op jit(solution)/shard_map/ppermute | solution.py:1445
  18.3 14.6 %collective-permute-start.5 = (bf16[96,896]{1,0:T(8,128)(2,1)S(1)}, bf16[96,896]{1,0:T(8,128)(2,1)S(1)}, u32[]{:S(2)}, u32[]{:S(2)}) collective-permute-start(bf16[96,896]{1,0:T(8,128)(2,1)S(1)} %get-tuple-element.191.refs_0_), channel_id=1, source_target_pairs={{0,4},{1,5},{2,6},{3,7},{4,0},{5,1},{6,2},{7,3},{8,12},{9,13},{10,... | collective-permute-start | bytes 516104 | tf_op jit(solution)/shard_map/ppermute | solution.py:1445
  21.5 9.0 %collective-permute-start.6 = (bf16[96,768]{1,0:T(8,128)(2,1)S(1)}, bf16[96,768]{1,0:T(8,128)(2,1)S(1)}, u32[]{:S(2)}, u32[]{:S(2)}) collective-permute-start(bf16[96,768]{1,0:T(8,128)(2,1)S(1)} %get-tuple-element.184.refs_2_), channel_id=1, source_target_pairs={{0,1},{1,0},{2,3},{3,2},{4,5},{5,4},{6,7},{7,6},{8,9},{9,8},{10,11... | collective-permute-start | bytes 442376 | tf_op jit(solution)/shard_map/ppermute | solution.py:1445
  28.2 14.2 %collective-permute-start.4 = (bf16[128,768]{1,0:T(8,128)(2,1)S(1)}, bf16[128,768]{1,0:T(8,128)(2,1)S(1)}, u32[]{:S(2)}, u32[]{:S(2)}) collective-permute-start(bf16[128,768]{1,0:T(8,128)(2,1)S(1)} %get-tuple-element.276.refs_0_), channel_id=1, source_target_pairs={{0,16},{1,17},{2,18},{3,19},{4,20},{5,21},{6,22},{7,23},{8,24},{9,... | collective-permute-start | bytes 589832 | tf_op jit(solution)/shard_map/ppermute | solution.py:1445
  28.3 17.2 %collective-permute-start.11 = (bf16[128,768]{1,0:T(8,128)(2,1)S(1)}, bf16[128,768]{1,0:T(8,128)(2,1)S(1)}, u32[]{:S(2)}, u32[]{:S(2)}) collective-permute-start(bf16[128,768]{1,0:T(8,128)(2,1)S(1)} %get-tuple-element.276.refs_0_), channel_id=1, source_target_pairs={{0,1},{1,0},{2,3},{3,2},{4,5},{5,4},{6,7},{7,6},{8,9},{9,8},{10,11... | collective-permute-start | bytes 589832 | tf_op jit(solution)/shard_map/ppermute | solution.py:1445
  30.5 8.8 %collective-permute-start.7 = (bf16[96,768]{1,0:T(8,128)(2,1)S(1)}, bf16[96,768]{1,0:T(8,128)(2,1)S(1)}, u32[]{:S(2)}, u32[]{:S(2)}) collective-permute-start(bf16[96,768]{1,0:T(8,128)(2,1)S(1)} %collective-permute-done.2.refs_10_), channel_id=1, source_target_pairs={{0,1},{1,0},{2,3},{3,2},{4,5},{5,4},{6,7},{7,6},{8,9},{9,8},{10,11... | collective-permute-start | bytes 442376 | tf_op jit(solution)/shard_map/ppermute | solution.py:1445
  32.9 9.6 %collective-permute-start.8 = (bf16[96,768]{1,0:T(8,128)(2,1)S(1)}, bf16[96,768]{1,0:T(8,128)(2,1)S(1)}, u32[]{:S(2)}, u32[]{:S(2)}) collective-permute-start(bf16[96,768]{1,0:T(8,128)(2,1)S(1)} %collective-permute-done.3.refs_12_), channel_id=1, source_target_pairs={{0,1},{1,0},{2,3},{3,2},{4,5},{5,4},{6,7},{7,6},{8,9},{9,8},{10,11... | collective-permute-start | bytes 442376 | tf_op jit(solution)/shard_map/ppermute | solution.py:1445
  32.9 12.6 %collective-permute-start.10 = (bf16[96,768]{1,0:T(8,128)(2,1)S(1)}, bf16[96,768]{1,0:T(8,128)(2,1)S(1)}, u32[]{:S(2)}, u32[]{:S(2)}) collective-permute-start(bf16[96,768]{1,0:T(8,128)(2,1)S(1)} %collective-permute-done.9.refs_14_), channel_id=1, source_target_pairs={{0,1},{1,0},{2,3},{3,2},{4,5},{5,4},{6,7},{7,6},{8,9},{9,8},{10,11... | collective-permute-start | bytes 442376 | tf_op jit(solution)/shard_map/ppermute | solution.py:1445
  39.3 8.1 %collective-permute-start.12 = (bf16[128,768]{1,0:T(8,128)(2,1)S(1)}, bf16[128,768]{1,0:T(8,128)(2,1)S(1)}, u32[]{:S(2)}, u32[]{:S(2)}) collective-permute-start(bf16[128,768]{1,0:T(8,128)(2,1)S(1)} %get-tuple-element.276.refs_0_), channel_id=1, source_target_pairs={{0,8},{1,9},{2,10},{3,11},{4,12},{5,13},{6,14},{7,15},{8,0},{9,1},... | collective-permute-start | bytes 589832 | tf_op jit(solution)/shard_map/ppermute | solution.py:1445
  52.5 16.9 %collective-permute-start.21 = (bf16[192,896]{1,0:T(8,128)(2,1)S(1)}, bf16[192,896]{1,0:T(8,128)(2,1)S(1)}, u32[]{:S(2)}, u32[]{:S(2)}) collective-permute-start(bf16[192,896]{1,0:T(8,128)(2,1)S(1)} %get-tuple-element.209.refs_0_), channel_id=1, source_target_pairs={{0,2},{1,3},{2,0},{3,1},{4,6},{5,7},{6,4},{7,5},{8,10},{9,11},{10,... | collective-permute-start | bytes 1032200 | tf_op jit(solution)/shard_map/ppermute | solution.py:1445
  52.8 16.5 %collective-permute-start.22 = (bf16[192,768]{1,0:T(8,128)(2,1)S(1)}, bf16[192,768]{1,0:T(8,128)(2,1)S(1)}, u32[]{:S(2)}, u32[]{:S(2)}) collective-permute-start(bf16[192,768]{1,0:T(8,128)(2,1)S(1)} %get-tuple-element.193.refs_2_), channel_id=1, source_target_pairs={{0,4},{1,5},{2,6},{3,7},{4,0},{5,1},{6,2},{7,3},{8,12},{9,13},{10,... | collective-permute-start | bytes 884744 | tf_op jit(solution)/shard_map/ppermute | solution.py:1445
  55.1 8.0 %collective-permute-start.17 = (bf16[192,192]{1,0:T(8,128)(2,1)S(1)}, bf16[192,192]{1,0:T(8,128)(2,1)S(1)}, u32[]{:S(2)}, u32[]{:S(2)}) collective-permute-start(bf16[192,192]{1,0:T(8,128)(2,1)S(1)} %get-tuple-element.203), channel_id=1, source_target_pairs={{0,8},{1,9},{2,10},{3,11},{4,12},{5,13},{6,14},{7,15},{8,0},{9,1},... | collective-permute-start | bytes 221192 | tf_op jit(solution)/shard_map/ppermute | solution.py:1445
  55.3 7.9 %collective-permute-start.18 = (bf16[192,192]{1,0:T(8,128)(2,1)S(1)}, bf16[192,192]{1,0:T(8,128)(2,1)S(1)}, u32[]{:S(2)}, u32[]{:S(2)}) collective-permute-start(bf16[192,192]{1,0:T(8,128)(2,1)S(1)} %get-tuple-element.204), channel_id=1, source_target_pairs={{0,16},{1,17},{2,18},{3,19},{4,20},{5,21},{6,22},{7,23},{8,24},{9,... | collective-permute-start | bytes 221192 | tf_op jit(solution)/shard_map/ppermute | solution.py:1445
  70.0 16.8 %collective-permute-start.27 = (bf16[384,896]{1,0:T(8,128)(2,1)S(1)}, bf16[384,896]{1,0:T(8,128)(2,1)S(1)}, u32[]{:S(2)}, u32[]{:S(2)}) collective-permute-start(bf16[384,896]{1,0:T(8,128)(2,1)S(1)} %get-tuple-element.217.refs_2_), channel_id=1, source_target_pairs={{0,1},{1,0},{2,3},{3,2},{4,5},{5,4},{6,7},{7,6},{8,9},{9,8},{10,11... | collective-permute-start | bytes 2064392 | tf_op jit(solution)/shard_map/ppermute | solution.py:1445
  70.7 14.6 %collective-permute-start.28 = (bf16[384,768]{1,0:T(8,128)(2,1)S(1)}, bf16[384,768]{1,0:T(8,128)(2,1)S(1)}, u32[]{:S(2)}, u32[]{:S(2)}) collective-permute-start(bf16[384,768]{1,0:T(8,128)(2,1)S(1)} %get-tuple-element.210.refs_4_), channel_id=1, source_target_pairs={{0,2},{1,3},{2,0},{3,1},{4,6},{5,7},{6,4},{7,5},{8,10},{9,11},{10,... | collective-permute-start | bytes 1769480 | tf_op jit(solution)/shard_map/ppermute | solution.py:1445
  70.7 7.3 %collective-permute-start.24 = (bf16[128,768]{1,0:T(8,128)(2,1)S(1)}, bf16[128,768]{1,0:T(8,128)(2,1)S(1)}, u32[]{:S(2)}, u32[]{:S(2)}) collective-permute-start(bf16[128,768]{1,0:T(8,128)(2,1)S(1)} %out_pass.1), channel_id=1, source_target_pairs={{0,16},{1,17},{2,18},{3,19},{4,20},{5,21},{6,22},{7,23},{8,24},{9,... | collective-permute-start | bytes 589832 | tf_op jit(solution)/shard_map/ppermute | solution.py:1445
  78.9 10.0 %collective-permute-start.25 = (bf16[128,768]{1,0:T(8,128)(2,1)S(1)}, bf16[128,768]{1,0:T(8,128)(2,1)S(1)}, u32[]{:S(2)}, u32[]{:S(2)}) collective-permute-start(bf16[128,768]{1,0:T(8,128)(2,1)S(1)} %get-tuple-element.243.refs_0_), channel_id=1, source_target_pairs={{0,16},{1,17},{2,18},{3,19},{4,20},{5,21},{6,22},{7,23},{8,24},{9,... | collective-permute-start | bytes 589832 | tf_op jit(solution)/shard_map/ppermute | solution.py:1445
  94.6 7.0 %collective-permute-start.32 = (bf16[128,768]{1,0:T(8,128)(2,1)S(1)}, bf16[128,768]{1,0:T(8,128)(2,1)S(1)}, u32[]{:S(2)}, u32[]{:S(2)}) collective-permute-start(bf16[128,768]{1,0:T(8,128)(2,1)S(1)} %mlp_pass.1), channel_id=1, source_target_pairs={{0,16},{1,17},{2,18},{3,19},{4,20},{5,21},{6,22},{7,23},{8,24},{9,... | collective-permute-start | bytes 589832 | tf_op jit(solution)/shard_map/ppermute | solution.py:1445
  108.0 7.3 %collective-permute-start.33 = (bf16[128,768]{1,0:T(8,128)(2,1)S(1)}, bf16[128,768]{1,0:T(8,128)(2,1)S(1)}, u32[]{:S(2)}, u32[]{:S(2)}) collective-permute-start(bf16[128,768]{1,0:T(8,128)(2,1)S(1)} %get-tuple-element.232.refs_0_.refs_4_), channel_id=1, source_target_pairs={{0,16},{1,17},{2,18},{3,19},{4,20},{5,21},{6,22},{7,23},{8,24},{9,... | collective-permute-start | bytes 589832 | tf_op jit(solution)/shard_map/ppermute | solution.py:1445
  120.4 7.0 %collective-permute-start.38 = (bf16[128,768]{1,0:T(8,128)(2,1)S(1)}, bf16[128,768]{1,0:T(8,128)(2,1)S(1)}, u32[]{:S(2)}, u32[]{:S(2)}) collective-permute-start(bf16[128,768]{1,0:T(8,128)(2,1)S(1)} %mlp_back_pass.1), channel_id=1, source_target_pairs={{0,16},{1,17},{2,18},{3,19},{4,20},{5,21},{6,22},{7,23},{8,24},{9,... | collective-permute-start | bytes 589832 | tf_op jit(solution)/shard_map/ppermute | solution.py:1445
  123.5 22.9 %collective-permute-start.44 = (bf16[384,896]{1,0:T(8,128)(2,1)S(1)}, bf16[384,896]{1,0:T(8,128)(2,1)S(1)}, u32[]{:S(2)}, u32[]{:S(2)}) collective-permute-start(bf16[384,896]{1,0:T(8,128)(2,1)S(1)} %get-tuple-element.251), channel_id=1, source_target_pairs={{0,2},{1,3},{2,0},{3,1},{4,6},{5,7},{6,4},{7,5},{8,10},{9,11},{10,... | collective-permute-start | bytes 2064392 | tf_op jit(solution)/shard_map/ppermute | solution.py:1445
  128.6 7.3 %collective-permute-start.39 = (bf16[128,768]{1,0:T(8,128)(2,1)S(1)}, bf16[128,768]{1,0:T(8,128)(2,1)S(1)}, u32[]{:S(2)}, u32[]{:S(2)}) collective-permute-start(bf16[128,768]{1,0:T(8,128)(2,1)S(1)} %get-tuple-element.257.refs_0_.refs_8_), channel_id=1, source_target_pairs={{0,16},{1,17},{2,18},{3,19},{4,20},{5,21},{6,22},{7,23},{8,24},{9,... | collective-permute-start | bytes 589832 | tf_op jit(solution)/shard_map/ppermute | solution.py:1445
  129.4 16.7 %collective-permute-start.43 = (bf16[384,768]{1,0:T(8,128)(2,1)S(1)}, bf16[384,768]{1,0:T(8,128)(2,1)S(1)}, u32[]{:S(2)}, u32[]{:S(2)}) collective-permute-start(bf16[384,768]{1,0:T(8,128)(2,1)S(1)} %get-tuple-element.271), channel_id=1, source_target_pairs={{0,1},{1,0},{2,3},{3,2},{4,5},{5,4},{6,7},{7,6},{8,9},{9,8},{10,11... | collective-permute-start | bytes 1769480 | tf_op jit(solution)/shard_map/ppermute | solution.py:1445
  135.9 8.4 %collective-permute-start.46 = (bf16[192,512]{1,0:T(8,128)(2,1)S(1)}, bf16[192,512]{1,0:T(8,128)(2,1)S(1)}, u32[]{:S(2)}, u32[]{:S(2)}) collective-permute-start(bf16[192,512]{1,0:T(8,128)(2,1)S(1)} %get-tuple-element.277.refs_0_.refs_12_), channel_id=1, source_target_pairs={{0,16},{1,17},{2,18},{3,19},{4,20},{5,21},{6,22},{7,23},{8,24},{9,... | collective-permute-start | bytes 589832 | tf_op jit(solution)/shard_map/ppermute | solution.py:1445
  145.2 7.7 %collective-permute-start.48 = (bf16[128,768]{1,0:T(8,128)(2,1)S(1)}, bf16[128,768]{1,0:T(8,128)(2,1)S(1)}, u32[]{:S(2)}, u32[]{:S(2)}) collective-permute-start(bf16[128,768]{1,0:T(8,128)(2,1)S(1)} %get-tuple-element.283), channel_id=1, source_target_pairs={{0,8},{1,9},{2,10},{3,11},{4,12},{5,13},{6,14},{7,15},{8,0},{9,1},... | collective-permute-start | bytes 589832 | tf_op jit(solution)/shard_map/ppermute | solution.py:1445
  146.1 7.0 %collective-permute-start.49 = (bf16[128,768]{1,0:T(8,128)(2,1)S(1)}, bf16[128,768]{1,0:T(8,128)(2,1)S(1)}, u32[]{:S(2)}, u32[]{:S(2)}) collective-permute-start(bf16[128,768]{1,0:T(8,128)(2,1)S(1)} %get-tuple-element.284), channel_id=1, source_target_pairs={{0,8},{1,9},{2,10},{3,11},{4,12},{5,13},{6,14},{7,15},{8,0},{9,1},... | collective-permute-start | bytes 589832 | tf_op jit(solution)/shard_map/ppermute | solution.py:1445
  148.5 17.4 %collective-permute-start.52 = (bf16[192,896]{1,0:T(8,128)(2,1)S(1)}, bf16[192,896]{1,0:T(8,128)(2,1)S(1)}, u32[]{:S(2)}, u32[]{:S(2)}) collective-permute-start(bf16[192,896]{1,0:T(8,128)(2,1)S(1)} %get-tuple-element.275), channel_id=1, source_target_pairs={{0,4},{1,5},{2,6},{3,7},{4,0},{5,1},{6,2},{7,3},{8,12},{9,13},{10,... | collective-permute-start | bytes 1032200 | tf_op jit(solution)/shard_map/ppermute | solution.py:1445
  150.1 13.3 %collective-permute-start.51 = (bf16[192,768]{1,0:T(8,128)(2,1)S(1)}, bf16[192,768]{1,0:T(8,128)(2,1)S(1)}, u32[]{:S(2)}, u32[]{:S(2)}) collective-permute-start(bf16[192,768]{1,0:T(8,128)(2,1)S(1)} %get-tuple-element.287), channel_id=1, source_target_pairs={{0,2},{1,3},{2,0},{3,1},{4,6},{5,7},{6,4},{7,5},{8,10},{9,11},{10,... | collective-permute-start | bytes 884744 | tf_op jit(solution)/shard_map/ppermute | solution.py:1445
  153.0 13.7 %collective-permute-start.53 = (bf16[128,768]{1,0:T(8,128)(2,1)S(1)}, bf16[128,768]{1,0:T(8,128)(2,1)S(1)}, u32[]{:S(2)}, u32[]{:S(2)}) collective-permute-start(bf16[128,768]{1,0:T(8,128)(2,1)S(1)} %get-tuple-element.293), channel_id=1, source_target_pairs={{0,8},{1,9},{2,10},{3,11},{4,12},{5,13},{6,14},{7,15},{8,0},{9,1},... | collective-permute-start | bytes 589832 | tf_op jit(solution)/shard_map/ppermute | solution.py:1445
  154.0 12.6 %collective-permute-start.54 = (bf16[128,768]{1,0:T(8,128)(2,1)S(1)}, bf16[128,768]{1,0:T(8,128)(2,1)S(1)}, u32[]{:S(2)}, u32[]{:S(2)}) collective-permute-start(bf16[128,768]{1,0:T(8,128)(2,1)S(1)} %get-tuple-element.294), channel_id=1, source_target_pairs={{0,16},{1,17},{2,18},{3,19},{4,20},{5,21},{6,22},{7,23},{8,24},{9,... | collective-permute-start | bytes 589832 | tf_op jit(solution)/shard_map/ppermute | solution.py:1445
  155.0 11.6 %collective-permute-start.55 = (bf16[128,768]{1,0:T(8,128)(2,1)S(1)}, bf16[128,768]{1,0:T(8,128)(2,1)S(1)}, u32[]{:S(2)}, u32[]{:S(2)}) collective-permute-start(bf16[128,768]{1,0:T(8,128)(2,1)S(1)} %get-tuple-element.285), channel_id=1, source_target_pairs={{0,1},{1,0},{2,3},{3,2},{4,5},{5,4},{6,7},{7,6},{8,9},{9,8},{10,11... | collective-permute-start | bytes 589832 | tf_op jit(solution)/shard_map/ppermute | solution.py:1445
  167.7 17.2 %collective-permute-start.61 = (bf16[384,384]{1,0:T(8,128)(2,1)S(1)}, bf16[384,384]{1,0:T(8,128)(2,1)S(1)}, u32[]{:S(2)}, u32[]{:S(2)}) collective-permute-start(bf16[384,384]{1,0:T(8,128)(2,1)S(1)} %get-tuple-element.309), channel_id=1, source_target_pairs={{0,1},{1,0},{2,3},{3,2},{4,5},{5,4},{6,7},{7,6},{8,9},{9,8},{10,11... | collective-permute-start | bytes 884744 | tf_op jit(solution)/shard_map/ppermute | solution.py:1445
  169.2 15.6 %collective-permute-start.62 = (bf16[384,384]{1,0:T(8,128)(2,1)S(1)}, bf16[384,384]{1,0:T(8,128)(2,1)S(1)}, u32[]{:S(2)}, u32[]{:S(2)}) collective-permute-start(bf16[384,384]{1,0:T(8,128)(2,1)S(1)} %get-tuple-element.311), channel_id=1, source_target_pairs={{0,2},{1,3},{2,0},{3,1},{4,6},{5,7},{6,4},{7,5},{8,10},{9,11},{10,... | collective-permute-start | bytes 884744 | tf_op jit(solution)/shard_map/ppermute | solution.py:1445
  169.2 14.4 %collective-permute-start.59 = (bf16[96,896]{1,0:T(8,128)(2,1)S(1)}, bf16[96,896]{1,0:T(8,128)(2,1)S(1)}, u32[]{:S(2)}, u32[]{:S(2)}) collective-permute-start(bf16[96,896]{1,0:T(8,128)(2,1)S(1)} %get-tuple-element.289), channel_id=1, source_target_pairs={{0,1},{1,0},{2,3},{3,2},{4,5},{5,4},{6,7},{7,6},{8,9},{9,8},{10,11... | collective-permute-start | bytes 516104 | tf_op jit(solution)/shard_map/ppermute | solution.py:1445
  169.8 9.1 %collective-permute-start.58 = (bf16[96,768]{1,0:T(8,128)(2,1)S(1)}, bf16[96,768]{1,0:T(8,128)(2,1)S(1)}, u32[]{:S(2)}, u32[]{:S(2)}) collective-permute-start(bf16[96,768]{1,0:T(8,128)(2,1)S(1)} %get-tuple-element.305), channel_id=1, source_target_pairs={{0,4},{1,5},{2,6},{3,7},{4,0},{5,1},{6,2},{7,3},{8,12},{9,13},{10,... | collective-permute-start | bytes 442376 | tf_op jit(solution)/shard_map/ppermute | solution.py:1445
  173.9 10.4 %collective-permute-start.60 = (f32[96,128]{1,0:T(8,128)S(1)}, f32[96,128]{1,0:T(8,128)S(1)}, u32[]{:S(2)}, u32[]{:S(2)}) collective-permute-start(f32[96,128]{1,0:T(8,128)S(1)} %sum_core.1.left_ref), channel_id=1, source_target_pairs={{0,16},{1,17},{2,18},{3,19},{4,20},{5,21},{6,22},{7,23},{8,24},{9,... | collective-permute-start | bytes 147464 | tf_op jit(solution)/shard_map/ppermute | solution.py:1445
  178.8 18.0 %collective-permute-start.56 = (bf16[144,768]{1,0:T(8,128)(2,1)S(1)}, bf16[144,768]{1,0:T(8,128)(2,1)S(1)}, u32[]{:S(2)}, u32[]{:S(2)}) collective-permute-start(bf16[144,768]{1,0:T(8,128)(2,1)S(1)} %get-tuple-element.296), channel_id=1, source_target_pairs={{0,0},{1,1},{2,16},{3,17},{4,8},{5,9},{6,24},{7,25},{8,4},{9,5},{1... | collective-permute-start | bytes 663560 | tf_op jit(solution)/shard_map/ppermute | solution.py:1445
  185.5 25.7 %collective-permute-start.71 = (bf16[96,1664]{1,0:T(8,128)(2,1)S(1)}, bf16[96,1664]{1,0:T(8,128)(2,1)S(1)}, u32[]{:S(2)}, u32[]{:S(2)}) collective-permute-start(bf16[96,1664]{1,0:T(8,128)(2,1)S(1)} %mlp_total.1.refs_0_), channel_id=1, source_target_pairs={{0,16},{1,17},{2,18},{3,19},{4,20},{5,21},{6,22},{7,23},{8,24},{9,... | collective-permute-start | bytes 958472 | tf_op jit(solution)/shard_map/ppermute | solution.py:1445
  185.6 13.3 %collective-permute-start.64 = (bf16[192,384]{1,0:T(8,128)(2,1)S(1)}, bf16[192,384]{1,0:T(8,128)(2,1)S(1)}, u32[]{:S(2)}, u32[]{:S(2)}) collective-permute-start(bf16[192,384]{1,0:T(8,128)(2,1)S(1)} %get-tuple-element.319), channel_id=1, source_target_pairs={{0,2},{1,3},{2,0},{3,1},{4,6},{5,7},{6,4},{7,5},{8,10},{9,11},{10,... | collective-permute-start | bytes 442376 | tf_op jit(solution)/shard_map/ppermute | solution.py:1445
  186.2 12.7 %collective-permute-start.65 = (bf16[192,384]{1,0:T(8,128)(2,1)S(1)}, bf16[192,384]{1,0:T(8,128)(2,1)S(1)}, u32[]{:S(2)}, u32[]{:S(2)}) collective-permute-start(bf16[192,384]{1,0:T(8,128)(2,1)S(1)} %get-tuple-element.312), channel_id=1, source_target_pairs={{0,4},{1,5},{2,6},{3,7},{4,0},{5,1},{6,2},{7,3},{8,12},{9,13},{10,... | collective-permute-start | bytes 442376 | tf_op jit(solution)/shard_map/ppermute | solution.py:1445
  187.3 10.9 %collective-permute-start.63 = (f32[96,128]{1,0:T(8,128)S(1)}, f32[96,128]{1,0:T(8,128)S(1)}, u32[]{:S(2)}, u32[]{:S(2)}) collective-permute-start(f32[96,128]{1,0:T(8,128)S(1)} %sum_x.1.left_ref), channel_id=1, source_target_pairs={{0,1},{1,0},{2,3},{3,2},{4,5},{5,4},{6,7},{7,6},{8,9},{9,8},{10,11... | collective-permute-start | bytes 147464 | tf_op jit(solution)/shard_map/ppermute | solution.py:1445
  199.5 11.1 %collective-permute-start.68 = (bf16[96,384]{1,0:T(8,128)(2,1)S(1)}, bf16[96,384]{1,0:T(8,128)(2,1)S(1)}, u32[]{:S(2)}, u32[]{:S(2)}) collective-permute-start(bf16[96,384]{1,0:T(8,128)(2,1)S(1)} %get-tuple-element.327), channel_id=1, source_target_pairs={{0,4},{1,5},{2,6},{3,7},{4,0},{5,1},{6,2},{7,3},{8,12},{9,13},{10,... | collective-permute-start | bytes 221192 | tf_op jit(solution)/shard_map/ppermute | solution.py:1445
  199.5 11.1 %collective-permute-start.69 = (bf16[96,384]{1,0:T(8,128)(2,1)S(1)}, bf16[96,384]{1,0:T(8,128)(2,1)S(1)}, u32[]{:S(2)}, u32[]{:S(2)}) collective-permute-start(bf16[96,384]{1,0:T(8,128)(2,1)S(1)} %get-tuple-element.322), channel_id=1, source_target_pairs={{0,1},{1,0},{2,3},{3,2},{4,5},{5,4},{6,7},{7,6},{8,9},{9,8},{10,11... | collective-permute-start | bytes 221192 | tf_op jit(solution)/shard_map/ppermute | solution.py:1445
  204.3 7.4 %collective-permute-start.70 = (bf16[96,1664]{1,0:T(8,128)(2,1)S(1)}, bf16[96,1664]{1,0:T(8,128)(2,1)S(1)}, u32[]{:S(2)}, u32[]{:S(2)}) collective-permute-start(bf16[96,1664]{1,0:T(8,128)(2,1)S(1)} %mlp_total.1.refs_0_), channel_id=1, source_target_pairs={{0,8},{1,9},{2,10},{3,11},{4,12},{5,13},{6,14},{7,15},{8,0},{9,1},... | collective-permute-start | bytes 958472 | tf_op jit(solution)/shard_map/ppermute | solution.py:1445
  211.3 7.5 %collective-permute-start.73 = (bf16[96,768]{1,0:T(8,128)(2,1)S(1)}, bf16[96,768]{1,0:T(8,128)(2,1)S(1)}, u32[]{:S(2)}, u32[]{:S(2)}) collective-permute-start(bf16[96,768]{1,0:T(8,128)(2,1)S(1)} %qkv_total.1.refs_0_), channel_id=1, source_target_pairs={{0,8},{1,9},{2,10},{3,11},{4,12},{5,13},{6,14},{7,15},{8,0},{9,1},... | collective-permute-start | bytes 442376 | tf_op jit(solution)/shard_map/ppermute | solution.py:1445
  (38 other events, 188.1 us)

commit v5 on v4

--- a/solution.py
+++ b/solution.py
@@ -249,7 +249,7 @@
     parts = refs[:ranks]
     qkv_ref, out_ref = refs[ranks:]
     rank = rank_ref[0]
-    blocks = ordered(parts, rank, slice(0, parts[0].shape[1]))
+    blocks = ordered(parts, rank, slice(0, 4 * quarter))
     pieces = []
     for part in range(3):
         for block in blocks:
@@ -1196,10 +1196,28 @@
         rows = slice(index * size, (index + 1) * size)
         kept_ref[rows, :] = all_ref[rows_at(2 * index + low, size), :columns]
         sent_ref[rows, :] = all_ref[rows_at(2 * index + 1 - low, size), :columns].astype(BF)
-        hi = high ^ (index // 2 * 2)
-        lo = low ^ (index % 2)
+        hi = high ^ (2 * (index % 2))
+        lo = low ^ (index // 2)
         more_kept_ref[rows, :] = all_ref[rows_at(2 * hi + lo, size), columns:]
         more_sent_ref[rows, :] = all_ref[rows_at(2 * (hi ^ 1) + lo, size), columns:].astype(BF)
+
+
+def fold(values, count):
+    size = values.shape[0] // count
+    return jnp.concatenate(
+        [values[index * size : (index + 1) * size] for index in range(count)], axis=1
+    )
+
+
+def unfold(values, count):
+    lanes = values.shape[1] // count
+    return jnp.concatenate(
+        [values[:, index * lanes : (index + 1) * lanes] for index in range(count)], axis=0
+    )
+
+
+def rounded(values):
+    return values.astype(BF).astype(F32)
 
 
 def mlp_grads_kernel(ids_ref, *refs):
@@ -1304,9 +1322,9 @@
     divide_rows(ids_ref, all_ref, refs[18:22])
 
 
-def half_kernel(ids_ref, *refs):
-    kept_ref, arrived_ref, more_kept_ref, more_arrived_ref = refs[:4]
-    own_ref, sent_ref, more_own_ref, more_sent_ref = refs[4:]
+def half_rows(ids_ref, refs, outs):
+    kept_ref, arrived_ref, more_kept_ref, more_arrived_ref = refs
+    own_ref, sent_ref, more_own_ref, more_sent_ref = outs
     size = own_ref.shape[0] // 2
     high = ids_ref[1]
     for step in range(2):
@@ -1317,25 +1335,61 @@
         sent_ref[rows, :] = (kept_ref[where, :] + arrived_ref[where, :].astype(F32)).astype(BF)
     more = more_kept_ref[...] + more_arrived_ref[...].astype(F32)
     more_own_ref[...] = more[: 2 * size]
-    more_sent_ref[...] = more[2 * size :].astype(BF)
+    more_sent_ref[: 2 * size, :] = more[2 * size :].astype(BF)
+
+
+def half_kernel(ids_ref, *refs):
+    half_rows(ids_ref, refs[:4], refs[4:])
+
+
+def half_sums_kernel(ids_ref, *refs):
+    half_rows(ids_ref, refs[:4], (refs[6], refs[7], refs[8], refs[9]))
+    sums = refs[4][...].astype(F32) + refs[5][...].astype(F32)
+    refs[9][refs[8].shape[0] :, :] = fold(sums, 3).astype(BF)
+    refs[10][...] = rounded(sums)
+
+
+def fourth_rows(refs, own_ref, sent_ref):
+    size = own_ref.shape[0]
+    start = 0
+    for kept_ref, arrived_ref in (refs[:2], refs[2:4]):
+        columns = slice(start, start + kept_ref.shape[1])
+        own_ref[:, columns] = kept_ref[:size, :] + arrived_ref[:size, :].astype(F32)
+        sent_ref[:size, columns] = (
+            kept_ref[size:, :] + arrived_ref[size : 2 * size, :].astype(F32)
+        ).astype(BF)
+        start += kept_ref.shape[1]
 
 
 def fourth_kernel(unused_ref, *refs):
-    for kept_ref, arrived_ref, own_ref, sent_ref in (refs[0:2] + refs[4:6], refs[2:4] + refs[6:8]):
-        size = own_ref.shape[0]
-        own_ref[...] = kept_ref[:size, :] + arrived_ref[:size, :].astype(F32)
-        sent_ref[...] = (kept_ref[size:, :] + arrived_ref[size:, :].astype(F32)).astype(BF)
-
-
-def total_kernel(unused_ref, kept_ref, arrived_ref, more_kept_ref, more_arrived_ref, out_ref):
-    columns = kept_ref.shape[1]
-    out_ref[:, :columns] = (kept_ref[...] + arrived_ref[...].astype(F32)).astype(BF)
-    out_ref[:, columns:] = (more_kept_ref[...] + more_arrived_ref[...].astype(F32)).astype(BF)
+    fourth_rows(refs[:4], *refs[4:])
+
+
+def fourth_sums_kernel(unused_ref, *refs):
+    arrived_ref, sums_ref = refs[3], refs[4]
+    own_ref, sent_ref, out_ref = refs[5:]
+    fourth_rows(refs[:4], own_ref, sent_ref)
+    sums = sums_ref[...] + unfold(arrived_ref[refs[2].shape[0] :, :].astype(F32), 3)
+    sent_ref[own_ref.shape[0] :, :] = fold(sums, 6).astype(BF)
+    out_ref[...] = rounded(sums)
+
+
+def total_kernel(unused_ref, kept_ref, arrived_ref, out_ref):
+    out_ref[...] = (kept_ref[...] + arrived_ref[...].astype(F32)).astype(BF)
+
+
+def total_sums_kernel(unused_ref, kept_ref, arrived_ref, sums_ref, out_ref):
+    size, columns = kept_ref.shape
+    out_ref[:, :columns] = (kept_ref[...] + arrived_ref[:size, :].astype(F32)).astype(BF)
+    out_ref[:, columns:] = (
+        sums_ref[...] + unfold(arrived_ref[size:, :].astype(F32), 6)
+    ).astype(BF)
 
 
 def norm_one_back_kernel(vectors, rank_ref, *refs):
     moved_ref, grad_ref, even_ref, arrived_ref, far_ref, side_ref, gains_ref = refs[:7]
-    learned_ref, small_ref, two_ref, up_ref, more_up_ref, back_ref, sums_ref = refs[7:]
+    learned_ref, small_ref, two_ref, up_ref, more_up_ref = refs[7:12]
+    back_ref, rounded_ref, sums_ref = refs[12:]
     count = grad_ref.shape[0]
     grad_normed = (
         even_ref[...]
@@ -1359,6 +1413,7 @@
             (7 + index) * vectors,
             jnp.where(rank_ref[0] == index, up_ref[...] + more_up_ref[...], 0.0),
         )
+    rounded_ref[...] = sums_ref[...].astype(BF)
 
 
 def back_kernel(unused_ref, moved_ref, grad_ref, learned_ref):
@@ -1367,10 +1422,14 @@
     learned_ref[...] = moved_ref[count:, :].astype(F32)
 
 
-def unpack_kernel(vectors, unused_ref, part_ref, arrived_ref, *refs):
-    sums_ref = refs[-1]
-    refs = refs[:-1]
-    sums_ref[...] = part_ref[...] + arrived_ref[...]
+def finish_sums_kernel(vectors, quarter, rank_ref, *refs):
+    parts, sums_ref = refs[:4], refs[-1]
+    finish_qkv_kernel(4, quarter, rank_ref, *parts, *refs[4:6])
+    total = None
+    for block in ordered(parts, rank_ref[0], slice(4 * quarter, parts[0].shape[1])):
+        total = block if total is None else total + block
+    sums_ref[...] = total
+    refs = refs[6:-1]
     gains_ref, shifts_ref, up_ref, down_ref, first_ref, mid_ref, mid_bias_ref = refs
     for index in range(3):
         gains_ref[index : index + 1, :] = load_rows(sums_ref, index * vectors, vectors)
@@ -1457,7 +1516,7 @@
     def ordered_run(kernel, name, scalars, arrays, outs, scratch=()):
         if last:
             arrays = [after(arrays[0], last[0])] + list(arrays[1:])
-        results = run(kernel, name, scalars, arrays, outs, scratch)
+        results = list(run(kernel, name, scalars, arrays, outs, scratch))
         last[:] = [results[-1]]
         return results
 
@@ -1493,39 +1552,39 @@
             ((blocks * size, columns), kind) for columns in (first, second) for kind in (F32, BF)
         ]
 
-    def scatter_half(parts, name):
+    def scatter_half(parts, sums, name):
         kept, sent, more_kept, more_sent = parts
-        return ordered_run(
-            half_kernel,
-            name,
-            ids,
-            [kept, flip(sent, 0, 0, 1), more_kept, flip(more_sent, 0, 1)],
-            row_parts(2, kept.shape[1], more_kept.shape[1]),
+        shapes = row_parts(2, kept.shape[1], more_kept.shape[1])
+        arrays = [kept, flip(sent, 0, 0, 1), more_kept, flip(more_sent, 0, 1)]
+        if sums is None:
+            return ordered_run(half_kernel, name, ids, arrays, shapes), None
+        shapes[3] = ((2 * size + small_rows // 3, more_kept.shape[1]), BF)
+        arrays += [sums, flip(sums, 0, 1)]
+        *parts, sums = ordered_run(
+            half_sums_kernel, name, ids, arrays, shapes + [(sums.shape, F32)]
         )
-
-    def scatter_fourth(parts, name):
+        return parts, sums
+
+    def scatter_fourth(parts, sums, name):
         kept, sent, more_kept, more_sent = parts
-        return ordered_run(
-            fourth_kernel,
-            name,
-            ids,
-            [kept, flip(sent, 0, 1), more_kept, flip(more_sent, 0, 2)],
-            row_parts(1, kept.shape[1], more_kept.shape[1]),
+        columns = kept.shape[1] + more_kept.shape[1]
+        arrays = [kept, flip(sent, 0, 1), more_kept, flip(more_sent, 0, 0, 1)]
+        if sums is None:
+            shapes = [((size, columns), F32), ((size, columns), BF)]
+            return ordered_run(fourth_kernel, name, ids, arrays, shapes), None
+        shapes = [((size, columns), F32), ((size + small_rows // 6, columns), BF)]
+        *parts, sums = ordered_run(
+            fourth_sums_kernel, name, ids, arrays + [sums], shapes + [(sums.shape, F32)]
         )
-
-    def scatter_last(parts, name):
-        kept, sent, more_kept, more_sent = parts
-        (share,) = ordered_run(
-            total_kernel,
-            name,
-            ids,
-            [kept, flip(sent, 0, 2), more_kept, flip(more_sent, 0, 0, 1)],
-            [((size, kept.shape[1] + more_kept.shape[1]), BF)],
-        )
-        return share
-
-    def add(left, right, name):
-        return ordered_run(add_kernel, name, ids, [left, right], [(left.shape, F32)])[0]
+        return parts, sums
+
+    def scatter_last(parts, sums, name):
+        kept, sent = parts
+        arrays = [kept, flip(sent, 0, 2)]
+        if sums is None:
+            return ordered_run(total_kernel, name, ids, arrays, [(kept.shape, BF)])[0]
+        shape = (size, kept.shape[1] + PAD)
+        return ordered_run(total_sums_kernel, name, ids, arrays + [sums], [(shape, BF)])[0]
 
     (pack,) = ordered_run(
         pack_kernel,
@@ -1791,7 +1850,7 @@
         pass_sum(evens[3], arrived[3], "corner_pass"),
         lambda seq, hi, lo: (seq ^ 2, hi, lo) if seq % 2 == 0 else (seq, hi, lo ^ 1),
     )
-    mlp_parts = scatter_half(mlp_parts, "mlp_half")
+    mlp_parts, unused = scatter_half(mlp_parts, None, "mlp_half")
     qkv_parts = ordered_run(
         qkv_grads_kernel,
         "qkv_grads",
@@ -1807,8 +1866,9 @@
         [evens[1], evens[2], arrived[1], arrived[2], corner],
         [((rows, width), BF), ((rows, width), BF)],
     )
+    qkv_parts[1], qkv_parts[3] = after(qkv_parts[1], far), after(qkv_parts[3], far)
     far, side = flip(far, 2), flip(side, 0, 0, 1)
-    mlp_parts = scatter_fourth(mlp_parts, "mlp_fourth")
+    mlp_parts, unused = scatter_fourth(mlp_parts, None, "mlp_fourth")
     moved_back, sums = ordered_run(
         functools.partial(norm_one_back_kernel, vectors),
         "norm_one_back",
@@ -1816,45 +1876,16 @@
         [moved, grad_after, evens[0], arrived[0], far, side, ln_gains]
         + [learned, small, rows_two]
         + biases,
-        [((rows + learned_rows, width), BF), ((small_rows, PAD), F32)],
-    )
-    qkv_parts = list(lax.optimization_barrier(tuple(qkv_parts) + (sums,))[:4])
-
-    sums = add(sums, flip(sums, 1), "sum_core")
-    mlp_share = scatter_last(mlp_parts, "mlp_total")
-    sums = add(sums, flip(sums, 2), "sum_x")
-    qkv_parts = scatter_half(qkv_parts, "qkv_half")
-    grad_input, learned = ordered_run(
-        back_kernel,
-        "back",
-        ids,
-        [from_planes(moved_back)],
-        [((rows, width), F32), ((learned_rows, width), F32)],
-    )
-    sums = add(sums, flip(sums, 0, 0, 1), "sum_y")
-    mlp_share = after(mlp_share, qkv_parts[0])
+        [((rows + learned_rows, width), BF), ((small_rows, PAD), BF)],
+        [pltpu.VMEM((small_rows, PAD), F32)],
+    )
+
+    qkv_parts, sums = scatter_half(qkv_parts, sums, "qkv_half")
+    mlp_share = scatter_last(mlp_parts, None, "mlp_total")
+    qkv_parts, sums = scatter_fourth(qkv_parts, sums, "qkv_fourth")
+    mlp_share = after(mlp_share, sums)
     mlp_far, mlp_near = flip(mlp_share, 2), flip(mlp_share, 1)
-    qkv_parts = scatter_fourth(qkv_parts, "qkv_fourth")
-    sums = add(sums, flip(sums, 0, 1), "sum_z")
-    sum_gains, sum_shifts, sum_up_bias, sum_down_bias, sum_first, sum_mid, sum_mid_bias = (
-        ordered_run(
-            functools.partial(unpack_kernel, vectors),
-            "unpack",
-            ids,
-            [sums, flip(sums, 0, 2)],
-            [
-                ((3, width), F32),
-                ((3, width), F32),
-                ((1, hidden), F32),
-                ((1, width), F32),
-                ((1, CH), F32),
-                ((3, CH, 9 * CH), F32),
-                ((3, CH), F32),
-            ],
-            [pltpu.VMEM((small_rows, PAD), F32)],
-        )
-    )
-    qkv_share = scatter_last(qkv_parts, "qkv_total")
+    qkv_share = scatter_last(qkv_parts, sums, "qkv_total")
     mlp_far = after(mlp_far, qkv_share)
     qkv_far, qkv_near = flip(qkv_share, 2), flip(qkv_share, 1)
     sum_up, sum_down, sum_conv = ordered_run(
@@ -1864,12 +1895,40 @@
         [mlp_share, mlp_near, mlp_far, flip(mlp_far, 1)],
         [((size, hidden), F32), ((ranks * unit, width), F32), ((size, 9 * CH), F32)],
     )
-    sum_qkv, sum_out = ordered_run(
-        functools.partial(finish_qkv_kernel, ranks, quarter),
+    grad_input, learned = ordered_run(
+        back_kernel,
+        "back",
+        ids,
+        [from_planes(moved_back)],
+        [((rows, width), F32), ((learned_rows, width), F32)],
+    )
+    (
+        sum_qkv,
+        sum_out,
+        sum_gains,
+        sum_shifts,
+        sum_up_bias,
+        sum_down_bias,
+        sum_first,
+        sum_mid,
+        sum_mid_bias,
+    ) = ordered_run(
+        functools.partial(finish_sums_kernel, vectors, quarter),
         "finish_qkv",
         ids,
         [qkv_share, qkv_near, qkv_far, flip(after(qkv_far, sum_down), 1)],
-        [((size, 3 * width), F32), ((size, width), F32)],
+        [
+            ((size, 3 * width), F32),
+            ((size, width), F32),
+            ((3, width), F32),
+            ((3, width), F32),
+            ((1, hidden), F32),
+            ((1, width), F32),
+            ((1, CH), F32),
+            ((3, CH, 9 * CH), F32),
+            ((3, CH), F32),
+        ],
+        [pltpu.VMEM((small_rows, PAD), F32)],
     )
     return (
         learned.reshape(1, frames_dev, CH, width),

time: 222 us -> 213 us (0.959)
  waiting for transfers between devices: 96.4 us -> 86.3 us
  starting transfers between devices: 52.1 us -> 57.2 us
  Pallas kernels: 61.6 us -> 58.2 us
    ppermute x76 -> x70, waiting for transfers between devices: 96.4 us -> 86.3 us  [permute(): return lax.ppermute(array, AXES, pairs)]
    ppermute x76 -> x70, starting transfers between devices: 52.1 us -> 57.2 us  [permute(): return lax.ppermute(array, AXES, pairs)]
    pallas_call x42 -> x37, Pallas kernels: 61.6 us -> 58.2 us  [run(): pl.pallas_call(kernel, in_specs=[pl.BlockSpec(memory_space=pltpu.SMEM)] +...]
  transfers between devices with their start and end apart: 76 -> 70, of which waited for: 35 -> 33; matrix products, arithmetic and copies ran while one was open for 2% -> 2% of each run, Pallas kernels for 22% -> 21%
where the time goes in v5:
time: 213 us; the launch traced here: 212 us
  waiting for transfers between devices  86.3 us (41%)
  Pallas kernels  58.2 us (27%)
  starting transfers between devices  57.2 us (27%)
  local copies, waits for them, and re-layouts  8.6 us (4%)
    ppermute x70, waiting for transfers between devices, permute(): return lax.ppermute(array, AXES, pairs)  86.3 us
    pallas_call x37, Pallas kernels, run(): pl.pallas_call(kernel, in_specs=[pl.BlockSpec(memory_space=pltpu.SMEM)] +...  58.2 us
    ppermute x70, starting transfers between devices, permute(): return lax.ppermute(array, AXES, pairs)  57.2 us
    unnamed x22, local copies, waits for them, and re-layouts  5.85 us
  transfers between devices with their start and end apart: 70, of which 33 were waited for; matrix products, arithmetic and copies ran while one was open for 2% of the time, Pallas kernels for 21%

profile of v5, /device:TPU:2, one launch (start us, length us, event | category | flops | bytes accessed | tf_op | source)
XLA Modules:
  0.0 212.1 jit_solution(17350180940956155750)
XLA Ops:
  3.7 3.5 %collective-permute-start = (bf16[160,768]{1,0:T(8,128)(2,1)S(1)}, bf16[160,768]{1,0:T(8,128)(2,1)S(1)}, u32[]{:S(2)}, u32[]{:S(2)}) collective-permute-start(bf16[160,768]{1,0:T(8,128)(2,1)S(1)} %pack.1), channel_id=1, source_target_pairs={{0,0},{1,1},{2,16},{3,17},{4,8},{5,9},{6,24},{7,25},{8,4},{9,5},{1... | collective-permute-start | bytes 737288 | tf_op jit(solution)/shard_map/ppermute | solution.py:1504
  10.9 1.5 collective-permute-start.1
  12.4 1.6 collective-permute-start.2
  18.7 2.8 %collective-permute-done.3.refs_12_ = bf16[96,768]{1,0:T(8,128)(2,1)S(1)} collective-permute-done((bf16[96,768]{1,0:T(8,128)(2,1)S(1)}, bf16[96,768]{1,0:T(8,128)(2,1)S(1)}, u32[]{:S(2)}, u32[]{:S(2)}) %collective-permute-start.3) | collective-permute-done | bytes 147488 | tf_op jit(solution)/shard_map/ppermute | solution.py:1504
  21.4 5.9 %collective-permute-start.6 = (bf16[96,768]{1,0:T(8,128)(2,1)S(1)}, bf16[96,768]{1,0:T(8,128)(2,1)S(1)}, u32[]{:S(2)}, u32[]{:S(2)}) collective-permute-start(bf16[96,768]{1,0:T(8,128)(2,1)S(1)} %get-tuple-element.175.refs_2_), channel_id=1, source_target_pairs={{0,1},{1,0},{2,3},{3,2},{4,5},{5,4},{6,7},{7,6},{8,9},{9,8},{10,11... | collective-permute-start | bytes 442376 | tf_op jit(solution)/shard_map/ppermute | solution.py:1504
  28.4 2.1 %collective-permute-done.6.refs_3_ = bf16[96,768]{1,0:T(8,128)(2,1)S(1)} collective-permute-done((bf16[96,768]{1,0:T(8,128)(2,1)S(1)}, bf16[96,768]{1,0:T(8,128)(2,1)S(1)}, u32[]{:S(2)}, u32[]{:S(2)}) %collective-permute-start.6) | collective-permute-done | bytes 147488 | tf_op jit(solution)/shard_map/ppermute | solution.py:1504
  30.5 2.4 %collective-permute-start.7 = (bf16[96,768]{1,0:T(8,128)(2,1)S(1)}, bf16[96,768]{1,0:T(8,128)(2,1)S(1)}, u32[]{:S(2)}, u32[]{:S(2)}) collective-permute-start(bf16[96,768]{1,0:T(8,128)(2,1)S(1)} %collective-permute-done.2.refs_10_), channel_id=1, source_target_pairs={{0,1},{1,0},{2,3},{3,2},{4,5},{5,4},{6,7},{7,6},{8,9},{9,8},{10,11... | collective-permute-start | bytes 442376 | tf_op jit(solution)/shard_map/ppermute | solution.py:1504
  32.9 2.0 collective-permute-start.10
  34.9 4.4 %collective-permute-done.7.refs_11_ = bf16[96,768]{1,0:T(8,128)(2,1)S(1)} collective-permute-done((bf16[96,768]{1,0:T(8,128)(2,1)S(1)}, bf16[96,768]{1,0:T(8,128)(2,1)S(1)}, u32[]{:S(2)}, u32[]{:S(2)}) %collective-permute-start.7) | collective-permute-done | bytes 147488 | tf_op jit(solution)/shard_map/ppermute | solution.py:1504
  39.3 3.2 %collective-permute-done.8.refs_13_ = bf16[96,768]{1,0:T(8,128)(2,1)S(1)} collective-permute-done((bf16[96,768]{1,0:T(8,128)(2,1)S(1)}, bf16[96,768]{1,0:T(8,128)(2,1)S(1)}, u32[]{:S(2)}, u32[]{:S(2)}) %collective-permute-start.8) | collective-permute-done | bytes 147488 | tf_op jit(solution)/shard_map/ppermute | solution.py:1504
  42.5 3.1 %collective-permute-done.10.refs_15_ = bf16[96,768]{1,0:T(8,128)(2,1)S(1)} collective-permute-done((bf16[96,768]{1,0:T(8,128)(2,1)S(1)}, bf16[96,768]{1,0:T(8,128)(2,1)S(1)}, u32[]{:S(2)}, u32[]{:S(2)}) %collective-permute-start.10) | collective-permute-done | bytes 147488 | tf_op jit(solution)/shard_map/ppermute | solution.py:1504
  47.4 4.5 %collective-permute-done.15.refs_6_ = bf16[128,768]{1,0:T(8,128)(2,1)S(1)} collective-permute-done((bf16[128,768]{1,0:T(8,128)(2,1)S(1)}, bf16[128,768]{1,0:T(8,128)(2,1)S(1)}, u32[]{:S(2)}, u32[]{:S(2)}) %collective-permute-start.15) | collective-permute-done | bytes 196640 | tf_op jit(solution)/shard_map/ppermute | solution.py:1504
  53.3 1.8 project.1
  55.3 1.9 collective-permute-start.18
  57.3 5.9 %attend.1 = (bf16[192,512]{1,0:T(8,128)(2,1)S(1)}, f32[8,512]{1,0:T(8,128)S(1)}) custom-call(s32[3]{0:T(128)S(1)} %pad_add_fusion.unused_ref.ids_ref.rank_ref, bf16[512,192]{1,0:T(8,128)(2,1)S(1)} %get-tuple-element.189.refs_0_.refs_3_.refs_2_, bf16[1024,384]{1,0:T(8,128)(2,1)S(1)} %get-tuple-element.190.refs_1_.refs_4_.refs_3_, ...), custom_call_target="tpu_custom_call" | custom-call | tf_op jit(solution)/shard_map/attend/pallas_call | solution.py:745
  66.4 2.9 %collective-permute-done.22.refs_3_ = bf16[192,768]{1,0:T(8,128)(2,1)S(1)} collective-permute-done((bf16[192,768]{1,0:T(8,128)(2,1)S(1)}, bf16[192,768]{1,0:T(8,128)(2,1)S(1)}, u32[]{:S(2)}, u32[]{:S(2)}) %collective-permute-start.22) | collective-permute-done | bytes 294944 | tf_op jit(solution)/shard_map/ppermute | solution.py:1504
  72.1 5.9 %collective-permute-done.24.refs_3_ = bf16[128,768]{1,0:T(8,128)(2,1)S(1)} collective-permute-done((bf16[128,768]{1,0:T(8,128)(2,1)S(1)}, bf16[128,768]{1,0:T(8,128)(2,1)S(1)}, u32[]{:S(2)}, u32[]{:S(2)}) %collective-permute-start.24) | collective-permute-done | bytes 196640 | tf_op jit(solution)/shard_map/ppermute | solution.py:1504
  80.3 5.0 %collective-permute-done.28.refs_5_ = bf16[384,768]{1,0:T(8,128)(2,1)S(1)} collective-permute-done((bf16[384,768]{1,0:T(8,128)(2,1)S(1)}, bf16[384,768]{1,0:T(8,128)(2,1)S(1)}, u32[]{:S(2)}, u32[]{:S(2)}) %collective-permute-start.28) | collective-permute-done | bytes 589856 | tf_op jit(solution)/shard_map/ppermute | solution.py:1504
  86.8 2.1 %mlp.1 = (bf16[768,768]{1,0:T(8,128)(2,1)S(1)}, bf16[768,768]{1,0:T(8,128)(2,1)S(1)}, bf16[768,128]{1,0:T(8,128)(2,1)S(1)}, f32[1,768]{1,0:T(1,128)S(1)}, bf16[2...) custom-call(s32[3]{0:T(128)S(1)} %pad_add_fusion.unused_ref.ids_ref.rank, ...), custom_call_target="tpu_custom_call" | custom-call | tf_op jit(solution)/shard_map/mlp/pallas_call | solution.py:745
  90.5 2.0 mlp_more.1
  95.3 6.2 %collective-permute-done.32.refs_3_ = bf16[128,768]{1,0:T(8,128)(2,1)S(1)} collective-permute-done((bf16[128,768]{1,0:T(8,128)(2,1)S(1)}, bf16[128,768]{1,0:T(8,128)(2,1)S(1)}, u32[]{:S(2)}, u32[]{:S(2)}) %collective-permute-start.32) | collective-permute-done | bytes 196640 | tf_op jit(solution)/shard_map/ppermute | solution.py:1504
  101.6 6.4 %tail.1 = (f32[16,768]{1,0:T(8,128)S(1)}, bf16[128,768]{1,0:T(8,128)(2,1)S(1)}, f32[128,768]{1,0:T(8,128)S(1)}, bf16[128,768]{1,0:T(8,128)(2,1)S(1)}, bf16[128,1...) custom-call(s32[3]{0:T(128)S(1)} %pad_add_fusion.unused_ref.ids_ref.rank_ref, f32[128,768]{1,0:T(8,128)S(1)} %get-tuple-element.243.refs_0_, ...), custom_call_target="tpu_custom_call" | custom-call | tf_op jit(solution)/shard_map/tail/pallas_call | solution.py:745
  109.4 1.5 mlp_back.1
  110.9 4.4 %collective-permute-done.33.refs_0_.refs_6_ = bf16[128,768]{1,0:T(8,128)(2,1)S(1)} collective-permute-done((bf16[128,768]{1,0:T(8,128)(2,1)S(1)}, bf16[128,768]{1,0:T(8,128)(2,1)S(1)}, u32[]{:S(2)}, u32[]{:S(2)}) %collective-permute-start.33) | collective-permute-done | bytes 196640 | tf_op jit(solution)/shard_map/ppermute | solution.py:1504
  116.8 1.5 mlp_back_more.1
  121.1 2.3 %mlp_grads.1 = (f32[384,768]{1,0:T(8,128)S(1)}, bf16[384,768]{1,0:T(8,128)(2,1)S(1)}, f32[384,896]{1,0:T(8,128)S(1)}, bf16[384,896]{1,0:T(8,128)(2,1)S(1)}) custom-call(s32[3]{0:T(128)S(1)} %pad_add_fusion.unused_ref.ids_ref.rank_ref, bf16[128,768]{1,0:T(8,128)(2,1)S(1)} %get-tuple-element.234.refs_0_, bf16[128,768]{1,0:T(8,128)(2,1)S(1)} %collective-permute-done.26.refs_1_, ...), custom_call_target="tpu_custom_call" | custom-call | tf_op jit(solution)/shard_map/mlp_grads/pallas_call | solution.py:745
  124.1 3.2 %collective-permute-done.38.refs_4_ = bf16[128,768]{1,0:T(8,128)(2,1)S(1)} collective-permute-done((bf16[128,768]{1,0:T(8,128)(2,1)S(1)}, bf16[128,768]{1,0:T(8,128)(2,1)S(1)}, u32[]{:S(2)}, u32[]{:S(2)}) %collective-permute-start.38) | collective-permute-done | bytes 196640 | tf_op jit(solution)/shard_map/ppermute | solution.py:1504
  130.0 4.0 %attend_back.1 = (bf16[256,192]{1,0:T(8,128)(2,1)S(1)}, f32[1024,384]{1,0:T(8,128)S(1)}) custom-call(s32[3]{0:T(128)S(1)} %pad_add_fusion.unused_ref.ids_ref.rank_ref, bf16[128,768]{1,0:T(8,128)(2,1)S(1)} %get-tuple-element.248.refs_0_.refs_8_, bf16[128,768]{1,0:T(8,128)(2,1)S(1)} %collective-permute-done.40.refs_1_.refs_9_, ...), custom_call_target="tpu_custom_call" | custom-call | tf_op jit(solution)/shard_map/attend_back/pallas_call | solution.py:745
  134.1 1.8 collective-permute-done.39.refs_0_.refs_10_
  136.6 2.8 %attend_back_next.1 = (bf16[128,192]{1,0:T(8,128)(2,1)S(1)}, f32[1024,384]{1,0:T(8,128)S(1)}) custom-call(s32[3]{0:T(128)S(1)} %pad_add_fusion.unused_ref.ids_ref.rank_ref, bf16[128,768]{1,0:T(8,128)(2,1)S(1)} %collective-permute-done.39.refs_0_.refs_10_, bf16[192,768]{1,0:T(8,128)(2,1)S(1)} %get-tuple-element.197.refs_2_.refs_1_, ...), custom_call_target="tpu_custom_call" | custom-call | tf_op jit(solution)/shard_map/attend_back_next/pallas_call | solution.py:745
  139.4 4.3 %attend_back_last.1 = (bf16[512,576]{1,0:T(8,128)(2,1)S(1)}, bf16[512,384]{1,0:T(8,128)(2,1)S(1)}, f32[128,768]{1,0:T(8,128)S(1)}, f32[128,768]{1,0:T(8,128)S(1)...) custom-call(s32[3]{0:T(128)S(1)} %pad_add_fusion.unused_ref.ids_ref., ...), custom_call_target="tpu_custom_call" | custom-call | tf_op jit(solution)/shard_map/attend_back_last/pallas_call | solution.py:745
  149.6 2.3 %qkv_grads.1 = (f32[384,384]{1,0:T(8,128)S(1)}, bf16[384,384]{1,0:T(8,128)(2,1)S(1)}, f32[384,384]{1,0:T(8,128)S(1)}, bf16[384,384]{1,0:T(8,128)(2,1)S(1)}) custom-call(s32[3]{0:T(128)S(1)} %pad_add_fusion.unused_ref.ids_ref.rank_ref, bf16[128,768]{1,0:T(8,128)(2,1)S(1)} %get-tuple-element.267.refs_0_, bf16[128,768]{1,0:T(8,128)(2,1)S(1)} %collective-permute-done.12.refs_1_, ...), custom_call_target="tpu_custom_call" | custom-call | tf_op jit(solution)/shard_map/qkv_grads/pallas_call | solution.py:745
  151.9 2.1 collective-permute-done.50.refs_4_
  156.2 1.5 collective-permute-start.57
  163.4 3.8 %collective-permute-done.55.refs_5_ = bf16[128,768]{1,0:T(8,128)(2,1)S(1)} collective-permute-done((bf16[128,768]{1,0:T(8,128)(2,1)S(1)}, bf16[128,768]{1,0:T(8,128)(2,1)S(1)}, u32[]{:S(2)}, u32[]{:S(2)}) %collective-permute-start.55) | collective-permute-done | bytes 196640 | tf_op jit(solution)/shard_map/ppermute | solution.py:1504
  168.3 3.7 %collective-permute-done.59.refs_5_ = bf16[96,128]{1,0:T(8,128)(2,1)S(1)} collective-permute-done((bf16[96,128]{1,0:T(8,128)(2,1)S(1)}, bf16[96,128]{1,0:T(8,128)(2,1)S(1)}, u32[]{:S(2)}, u32[]{:S(2)}) %collective-permute-start.59) | collective-permute-done | bytes 24608 | tf_op jit(solution)/shard_map/ppermute | solution.py:1504
  172.7 2.3 %collective-permute-start.62 = (bf16[224,384]{1,0:T(8,128)(2,1)S(1)}, bf16[224,384]{1,0:T(8,128)(2,1)S(1)}, u32[]{:S(2)}, u32[]{:S(2)}) collective-permute-start(bf16[224,384]{1,0:T(8,128)(2,1)S(1)} %get-tuple-element.302), channel_id=1, source_target_pairs={{0,1},{1,0},{2,3},{3,2},{4,5},{5,4},{6,7},{7,6},{8,9},{9,8},{10,11... | collective-permute-start | bytes 516104 | tf_op jit(solution)/shard_map/ppermute | solution.py:1504
  175.4 2.5 %collective-permute-done.60.arrived_ref = bf16[96,1664]{1,0:T(8,128)(2,1)S(1)} collective-permute-done((bf16[96,1664]{1,0:T(8,128)(2,1)S(1)}, bf16[96,1664]{1,0:T(8,128)(2,1)S(1)}, u32[]{:S(2)}, u32[]{:S(2)}) %collective-permute-start.60) | collective-permute-done | bytes 319520 | tf_op jit(solution)/shard_map/ppermute | solution.py:1504
  178.5 2.1 collective-permute-done.61.refs_1_
  182.0 2.1 collective-permute-start.63
  184.0 2.3 %collective-permute-start.64 = (bf16[96,1664]{1,0:T(8,128)(2,1)S(1)}, bf16[96,1664]{1,0:T(8,128)(2,1)S(1)}, u32[]{:S(2)}, u32[]{:S(2)}) collective-permute-start(bf16[96,1664]{1,0:T(8,128)(2,1)S(1)} %mlp_total.1.refs_0_), channel_id=1, source_target_pairs={{0,8},{1,9},{2,10},{3,11},{4,12},{5,13},{6,14},{7,15},{8,0},{9,1},... | collective-permute-start | bytes 958472 | tf_op jit(solution)/shard_map/ppermute | solution.py:1504
  186.3 5.6 %collective-permute-done.63.arrived_ref = bf16[112,768]{1,0:T(8,128)(2,1)S(1)} collective-permute-done((bf16[112,768]{1,0:T(8,128)(2,1)S(1)}, bf16[112,768]{1,0:T(8,128)(2,1)S(1)}, u32[]{:S(2)}, u32[]{:S(2)}) %collective-permute-start.63) | collective-permute-done | bytes 172064 | tf_op jit(solution)/shard_map/ppermute | solution.py:1504
  192.5 1.5 collective-permute-start.66
  194.9 1.9 collective-permute-start.56
  196.9 2.5 %collective-permute-start.67 = (bf16[96,896]{1,0:T(8,128)(2,1)S(1)}, bf16[96,896]{1,0:T(8,128)(2,1)S(1)}, u32[]{:S(2)}, u32[]{:S(2)}) collective-permute-start(bf16[96,896]{1,0:T(8,128)(2,1)S(1)} %qkv_total.1.refs_0_), channel_id=1, source_target_pairs={{0,8},{1,9},{2,10},{3,11},{4,12},{5,13},{6,14},{7,15},{8,0},{9,1},... | collective-permute-start | bytes 516104 | tf_op jit(solution)/shard_map/ppermute | solution.py:1504
  199.3 2.4 %finish_mlp.1 = (f32[96,3072]{1,0:T(8,128)}, f32[384,768]{1,0:T(8,128)}, f32[96,72]{1,0:T(8,128)S(1)}) custom-call(s32[3]{0:T(128)S(1)} %pad_add_fusion.unused_ref.ids_ref.rank_ref, bf16[96,1664]{1,0:T(8,128)(2,1)S(1)} %mlp_total.1.refs_0_, bf16[96,1664]{1,0:T(8,128)(2,1)S(1)} %collective-permute-done.64.refs_1_, ...), custom_call_target="tpu_custom_call" | custom-call | tf_op jit(solution)/shard_map/finish_mlp/pallas_call | solution.py:745
  202.4 6.0 %collective-permute-done.56.moved_ref = bf16[144,768]{1,0:T(8,128)(2,1)S(1)} collective-permute-done((bf16[144,768]{1,0:T(8,128)(2,1)S(1)}, bf16[144,768]{1,0:T(8,128)(2,1)S(1)}, u32[]{:S(2)}, u32[]{:S(2)}) %collective-permute-start.56) | collective-permute-done | bytes 221216 | tf_op jit(solution)/shard_map/ppermute | solution.py:1504
  209.7 1.8 finish_qkv.1
  (157 shorter events, 61.8 us)
Async XLA Ops:
  3.7 23.7 %collective-permute-start = (bf16[160,768]{1,0:T(8,128)(2,1)S(1)}, bf16[160,768]{1,0:T(8,128)(2,1)S(1)}, u32[]{:S(2)}, u32[]{:S(2)}) collective-permute-start(bf16[160,768]{1,0:T(8,128)(2,1)S(1)} %pack.1), channel_id=1, source_target_pairs={{0,0},{1,1},{2,16},{3,17},{4,8},{5,9},{6,24},{7,25},{8,4},{9,5},{1... | collective-permute-start | bytes 737288 | tf_op jit(solution)/shard_map/ppermute | solution.py:1504
  9.8 11.7 %collective-permute-start.3 = (bf16[96,768]{1,0:T(8,128)(2,1)S(1)}, bf16[96,768]{1,0:T(8,128)(2,1)S(1)}, u32[]{:S(2)}, u32[]{:S(2)}) collective-permute-start(bf16[96,768]{1,0:T(8,128)(2,1)S(1)} %select.10.refs_8_), channel_id=1, source_target_pairs={{0,4},{1,5},{2,6},{3,7},{4,0},{5,1},{6,2},{7,3},{8,12},{9,13},{10,... | collective-permute-start | bytes 442376 | tf_op jit(solution)/shard_map/ppermute | solution.py:1504
  10.9 17.3 %collective-permute-start.1 = (bf16[96,768]{1,0:T(8,128)(2,1)S(1)}, bf16[96,768]{1,0:T(8,128)(2,1)S(1)}, u32[]{:S(2)}, u32[]{:S(2)}) collective-permute-start(bf16[96,768]{1,0:T(8,128)(2,1)S(1)} %select.10.refs_8_), channel_id=1, source_target_pairs={{0,1},{1,0},{2,3},{3,2},{4,5},{5,4},{6,7},{7,6},{8,9},{9,8},{10,11... | collective-permute-start | bytes 442376 | tf_op jit(solution)/shard_map/ppermute | solution.py:1504
  12.4 15.8 %collective-permute-start.2 = (bf16[96,768]{1,0:T(8,128)(2,1)S(1)}, bf16[96,768]{1,0:T(8,128)(2,1)S(1)}, u32[]{:S(2)}, u32[]{:S(2)}) collective-permute-start(bf16[96,768]{1,0:T(8,128)(2,1)S(1)} %select.10.refs_8_), channel_id=1, source_target_pairs={{0,2},{1,3},{2,0},{3,1},{4,6},{5,7},{6,4},{7,5},{8,10},{9,11},{10,... | collective-permute-start | bytes 442376 | tf_op jit(solution)/shard_map/ppermute | solution.py:1504
  18.3 14.6 %collective-permute-start.5 = (bf16[96,896]{1,0:T(8,128)(2,1)S(1)}, bf16[96,896]{1,0:T(8,128)(2,1)S(1)}, u32[]{:S(2)}, u32[]{:S(2)}) collective-permute-start(bf16[96,896]{1,0:T(8,128)(2,1)S(1)} %get-tuple-element.182.refs_0_), channel_id=1, source_target_pairs={{0,4},{1,5},{2,6},{3,7},{4,0},{5,1},{6,2},{7,3},{8,12},{9,13},{10,... | collective-permute-start | bytes 516104 | tf_op jit(solution)/shard_map/ppermute | solution.py:1504
  21.4 9.0 %collective-permute-start.6 = (bf16[96,768]{1,0:T(8,128)(2,1)S(1)}, bf16[96,768]{1,0:T(8,128)(2,1)S(1)}, u32[]{:S(2)}, u32[]{:S(2)}) collective-permute-start(bf16[96,768]{1,0:T(8,128)(2,1)S(1)} %get-tuple-element.175.refs_2_), channel_id=1, source_target_pairs={{0,1},{1,0},{2,3},{3,2},{4,5},{5,4},{6,7},{7,6},{8,9},{9,8},{10,11... | collective-permute-start | bytes 442376 | tf_op jit(solution)/shard_map/ppermute | solution.py:1504
  28.2 14.2 %collective-permute-start.4 = (bf16[128,768]{1,0:T(8,128)(2,1)S(1)}, bf16[128,768]{1,0:T(8,128)(2,1)S(1)}, u32[]{:S(2)}, u32[]{:S(2)}) collective-permute-start(bf16[128,768]{1,0:T(8,128)(2,1)S(1)} %get-tuple-element.267.refs_0_), channel_id=1, source_target_pairs={{0,16},{1,17},{2,18},{3,19},{4,20},{5,21},{6,22},{7,23},{8,24},{9,... | collective-permute-start | bytes 589832 | tf_op jit(solution)/shard_map/ppermute | solution.py:1504
  28.3 17.2 %collective-permute-start.11 = (bf16[128,768]{1,0:T(8,128)(2,1)S(1)}, bf16[128,768]{1,0:T(8,128)(2,1)S(1)}, u32[]{:S(2)}, u32[]{:S(2)}) collective-permute-start(bf16[128,768]{1,0:T(8,128)(2,1)S(1)} %get-tuple-element.267.refs_0_), channel_id=1, source_target_pairs={{0,1},{1,0},{2,3},{3,2},{4,5},{5,4},{6,7},{7,6},{8,9},{9,8},{10,11... | collective-permute-start | bytes 589832 | tf_op jit(solution)/shard_map/ppermute | solution.py:1504
  30.5 8.8 %collective-permute-start.7 = (bf16[96,768]{1,0:T(8,128)(2,1)S(1)}, bf16[96,768]{1,0:T(8,128)(2,1)S(1)}, u32[]{:S(2)}, u32[]{:S(2)}) collective-permute-start(bf16[96,768]{1,0:T(8,128)(2,1)S(1)} %collective-permute-done.2.refs_10_), channel_id=1, source_target_pairs={{0,1},{1,0},{2,3},{3,2},{4,5},{5,4},{6,7},{7,6},{8,9},{9,8},{10,11... | collective-permute-start | bytes 442376 | tf_op jit(solution)/shard_map/ppermute | solution.py:1504
  32.9 9.6 %collective-permute-start.8 = (bf16[96,768]{1,0:T(8,128)(2,1)S(1)}, bf16[96,768]{1,0:T(8,128)(2,1)S(1)}, u32[]{:S(2)}, u32[]{:S(2)}) collective-permute-start(bf16[96,768]{1,0:T(8,128)(2,1)S(1)} %collective-permute-done.3.refs_12_), channel_id=1, source_target_pairs={{0,1},{1,0},{2,3},{3,2},{4,5},{5,4},{6,7},{7,6},{8,9},{9,8},{10,11... | collective-permute-start | bytes 442376 | tf_op jit(solution)/shard_map/ppermute | solution.py:1504
  32.9 12.6 %collective-permute-start.10 = (bf16[96,768]{1,0:T(8,128)(2,1)S(1)}, bf16[96,768]{1,0:T(8,128)(2,1)S(1)}, u32[]{:S(2)}, u32[]{:S(2)}) collective-permute-start(bf16[96,768]{1,0:T(8,128)(2,1)S(1)} %collective-permute-done.9.refs_14_), channel_id=1, source_target_pairs={{0,1},{1,0},{2,3},{3,2},{4,5},{5,4},{6,7},{7,6},{8,9},{9,8},{10,11... | collective-permute-start | bytes 442376 | tf_op jit(solution)/shard_map/ppermute | solution.py:1504
  39.3 8.1 %collective-permute-start.12 = (bf16[128,768]{1,0:T(8,128)(2,1)S(1)}, bf16[128,768]{1,0:T(8,128)(2,1)S(1)}, u32[]{:S(2)}, u32[]{:S(2)}) collective-permute-start(bf16[128,768]{1,0:T(8,128)(2,1)S(1)} %get-tuple-element.267.refs_0_), channel_id=1, source_target_pairs={{0,8},{1,9},{2,10},{3,11},{4,12},{5,13},{6,14},{7,15},{8,0},{9,1},... | collective-permute-start | bytes 589832 | tf_op jit(solution)/shard_map/ppermute | solution.py:1504
  46.1 5.7 %collective-permute-start.15 = (bf16[128,768]{1,0:T(8,128)(2,1)S(1)}, bf16[128,768]{1,0:T(8,128)(2,1)S(1)}, u32[]{:S(2)}, u32[]{:S(2)}) collective-permute-start(bf16[128,768]{1,0:T(8,128)(2,1)S(1)} %pick.1), channel_id=1, source_target_pairs={{0,1},{1,0},{2,3},{3,2},{4,5},{5,4},{6,7},{7,6},{8,24},{9,25},{10,... | collective-permute-start | bytes 589832 | tf_op jit(solution)/shard_map/ppermute | solution.py:1504
  52.5 16.9 %collective-permute-start.21 = (bf16[192,896]{1,0:T(8,128)(2,1)S(1)}, bf16[192,896]{1,0:T(8,128)(2,1)S(1)}, u32[]{:S(2)}, u32[]{:S(2)}) collective-permute-start(bf16[192,896]{1,0:T(8,128)(2,1)S(1)} %get-tuple-element.200.refs_0_), channel_id=1, source_target_pairs={{0,2},{1,3},{2,0},{3,1},{4,6},{5,7},{6,4},{7,5},{8,10},{9,11},{10,... | collective-permute-start | bytes 1032200 | tf_op jit(solution)/shard_map/ppermute | solution.py:1504
  52.8 16.5 %collective-permute-start.22 = (bf16[192,768]{1,0:T(8,128)(2,1)S(1)}, bf16[192,768]{1,0:T(8,128)(2,1)S(1)}, u32[]{:S(2)}, u32[]{:S(2)}) collective-permute-start(bf16[192,768]{1,0:T(8,128)(2,1)S(1)} %get-tuple-element.184.refs_2_), channel_id=1, source_target_pairs={{0,4},{1,5},{2,6},{3,7},{4,0},{5,1},{6,2},{7,3},{8,12},{9,13},{10,... | collective-permute-start | bytes 884744 | tf_op jit(solution)/shard_map/ppermute | solution.py:1504
  55.1 8.1 %collective-permute-start.17 = (bf16[192,192]{1,0:T(8,128)(2,1)S(1)}, bf16[192,192]{1,0:T(8,128)(2,1)S(1)}, u32[]{:S(2)}, u32[]{:S(2)}) collective-permute-start(bf16[192,192]{1,0:T(8,128)(2,1)S(1)} %get-tuple-element.194), channel_id=1, source_target_pairs={{0,8},{1,9},{2,10},{3,11},{4,12},{5,13},{6,14},{7,15},{8,0},{9,1},... | collective-permute-start | bytes 221192 | tf_op jit(solution)/shard_map/ppermute | solution.py:1504
  55.3 7.9 %collective-permute-start.18 = (bf16[192,192]{1,0:T(8,128)(2,1)S(1)}, bf16[192,192]{1,0:T(8,128)(2,1)S(1)}, u32[]{:S(2)}, u32[]{:S(2)}) collective-permute-start(bf16[192,192]{1,0:T(8,128)(2,1)S(1)} %get-tuple-element.195), channel_id=1, source_target_pairs={{0,16},{1,17},{2,18},{3,19},{4,20},{5,21},{6,22},{7,23},{8,24},{9,... | collective-permute-start | bytes 221192 | tf_op jit(solution)/shard_map/ppermute | solution.py:1504
  57.2 6.0 %collective-permute-start.19 = (bf16[192,192]{1,0:T(8,128)(2,1)S(1)}, bf16[192,192]{1,0:T(8,128)(2,1)S(1)}, u32[]{:S(2)}, u32[]{:S(2)}) collective-permute-start(bf16[192,192]{1,0:T(8,128)(2,1)S(1)} %get-tuple-element.188), channel_id=1, source_target_pairs={{0,24},{1,25},{2,26},{3,27},{4,28},{5,29},{6,30},{7,31},{8,16},{9,... | collective-permute-start | bytes 221192 | tf_op jit(solution)/shard_map/ppermute | solution.py:1504
  69.9 16.8 %collective-permute-start.27 = (bf16[384,896]{1,0:T(8,128)(2,1)S(1)}, bf16[384,896]{1,0:T(8,128)(2,1)S(1)}, u32[]{:S(2)}, u32[]{:S(2)}) collective-permute-start(bf16[384,896]{1,0:T(8,128)(2,1)S(1)} %get-tuple-element.208.refs_2_), channel_id=1, source_target_pairs={{0,1},{1,0},{2,3},{3,2},{4,5},{5,4},{6,7},{7,6},{8,9},{9,8},{10,11... | collective-permute-start | bytes 2064392 | tf_op jit(solution)/shard_map/ppermute | solution.py:1504
  70.7 14.6 %collective-permute-start.28 = (bf16[384,768]{1,0:T(8,128)(2,1)S(1)}, bf16[384,768]{1,0:T(8,128)(2,1)S(1)}, u32[]{:S(2)}, u32[]{:S(2)}) collective-permute-start(bf16[384,768]{1,0:T(8,128)(2,1)S(1)} %get-tuple-element.201.refs_4_), channel_id=1, source_target_pairs={{0,2},{1,3},{2,0},{3,1},{4,6},{5,7},{6,4},{7,5},{8,10},{9,11},{10,... | collective-permute-start | bytes 1769480 | tf_op jit(solution)/shard_map/ppermute | solution.py:1504
  70.7 7.3 %collective-permute-start.24 = (bf16[128,768]{1,0:T(8,128)(2,1)S(1)}, bf16[128,768]{1,0:T(8,128)(2,1)S(1)}, u32[]{:S(2)}, u32[]{:S(2)}) collective-permute-start(bf16[128,768]{1,0:T(8,128)(2,1)S(1)} %out_pass.1), channel_id=1, source_target_pairs={{0,16},{1,17},{2,18},{3,19},{4,20},{5,21},{6,22},{7,23},{8,24},{9,... | collective-permute-start | bytes 589832 | tf_op jit(solution)/shard_map/ppermute | solution.py:1504
  78.9 10.0 %collective-permute-start.25 = (bf16[128,768]{1,0:T(8,128)(2,1)S(1)}, bf16[128,768]{1,0:T(8,128)(2,1)S(1)}, u32[]{:S(2)}, u32[]{:S(2)}) collective-permute-start(bf16[128,768]{1,0:T(8,128)(2,1)S(1)} %get-tuple-element.234.refs_0_), channel_id=1, source_target_pairs={{0,16},{1,17},{2,18},{3,19},{4,20},{5,21},{6,22},{7,23},{8,24},{9,... | collective-permute-start | bytes 589832 | tf_op jit(solution)/shard_map/ppermute | solution.py:1504
  94.5 7.0 %collective-permute-start.32 = (bf16[128,768]{1,0:T(8,128)(2,1)S(1)}, bf16[128,768]{1,0:T(8,128)(2,1)S(1)}, u32[]{:S(2)}, u32[]{:S(2)}) collective-permute-start(bf16[128,768]{1,0:T(8,128)(2,1)S(1)} %mlp_pass.1), channel_id=1, source_target_pairs={{0,16},{1,17},{2,18},{3,19},{4,20},{5,21},{6,22},{7,23},{8,24},{9,... | collective-permute-start | bytes 589832 | tf_op jit(solution)/shard_map/ppermute | solution.py:1504
  108.0 7.3 %collective-permute-start.33 = (bf16[128,768]{1,0:T(8,128)(2,1)S(1)}, bf16[128,768]{1,0:T(8,128)(2,1)S(1)}, u32[]{:S(2)}, u32[]{:S(2)}) collective-permute-start(bf16[128,768]{1,0:T(8,128)(2,1)S(1)} %get-tuple-element.223.refs_0_.refs_4_), channel_id=1, source_target_pairs={{0,16},{1,17},{2,18},{3,19},{4,20},{5,21},{6,22},{7,23},{8,24},{9,... | collective-permute-start | bytes 589832 | tf_op jit(solution)/shard_map/ppermute | solution.py:1504
  118.5 5.7 %collective-permute-start.37 = (bf16[128,768]{1,0:T(8,128)(2,1)S(1)}, bf16[128,768]{1,0:T(8,128)(2,1)S(1)}, u32[]{:S(2)}, u32[]{:S(2)}) collective-permute-start(bf16[128,768]{1,0:T(8,128)(2,1)S(1)} %get-tuple-element.245), channel_id=1, source_target_pairs={{0,8},{1,9},{2,10},{3,11},{4,12},{5,13},{6,14},{7,15},{8,0},{9,1},... | collective-permute-start | bytes 589832 | tf_op jit(solution)/shard_map/ppermute | solution.py:1504
  120.4 7.0 %collective-permute-start.38 = (bf16[128,768]{1,0:T(8,128)(2,1)S(1)}, bf16[128,768]{1,0:T(8,128)(2,1)S(1)}, u32[]{:S(2)}, u32[]{:S(2)}) collective-permute-start(bf16[128,768]{1,0:T(8,128)(2,1)S(1)} %mlp_back_pass.1), channel_id=1, source_target_pairs={{0,16},{1,17},{2,18},{3,19},{4,20},{5,21},{6,22},{7,23},{8,24},{9,... | collective-permute-start | bytes 589832 | tf_op jit(solution)/shard_map/ppermute | solution.py:1504
  123.5 22.4 %collective-permute-start.44 = (bf16[384,896]{1,0:T(8,128)(2,1)S(1)}, bf16[384,896]{1,0:T(8,128)(2,1)S(1)}, u32[]{:S(2)}, u32[]{:S(2)}) collective-permute-start(bf16[384,896]{1,0:T(8,128)(2,1)S(1)} %get-tuple-element.242), channel_id=1, source_target_pairs={{0,2},{1,3},{2,0},{3,1},{4,6},{5,7},{6,4},{7,5},{8,10},{9,11},{10,... | collective-permute-start | bytes 2064392 | tf_op jit(solution)/shard_map/ppermute | solution.py:1504
  128.6 7.3 %collective-permute-start.39 = (bf16[128,768]{1,0:T(8,128)(2,1)S(1)}, bf16[128,768]{1,0:T(8,128)(2,1)S(1)}, u32[]{:S(2)}, u32[]{:S(2)}) collective-permute-start(bf16[128,768]{1,0:T(8,128)(2,1)S(1)} %get-tuple-element.248.refs_0_.refs_8_), channel_id=1, source_target_pairs={{0,16},{1,17},{2,18},{3,19},{4,20},{5,21},{6,22},{7,23},{8,24},{9,... | collective-permute-start | bytes 589832 | tf_op jit(solution)/shard_map/ppermute | solution.py:1504
  129.4 16.5 %collective-permute-start.43 = (bf16[384,768]{1,0:T(8,128)(2,1)S(1)}, bf16[384,768]{1,0:T(8,128)(2,1)S(1)}, u32[]{:S(2)}, u32[]{:S(2)}) collective-permute-start(bf16[384,768]{1,0:T(8,128)(2,1)S(1)} %get-tuple-element.262), channel_id=1, source_target_pairs={{0,1},{1,0},{2,3},{3,2},{4,5},{5,4},{6,7},{7,6},{8,9},{9,8},{10,11... | collective-permute-start | bytes 1769480 | tf_op jit(solution)/shard_map/ppermute | solution.py:1504
  135.9 8.4 %collective-permute-start.46 = (bf16[192,512]{1,0:T(8,128)(2,1)S(1)}, bf16[192,512]{1,0:T(8,128)(2,1)S(1)}, u32[]{:S(2)}, u32[]{:S(2)}) collective-permute-start(bf16[192,512]{1,0:T(8,128)(2,1)S(1)} %get-tuple-element.268.refs_0_.refs_12_), channel_id=1, source_target_pairs={{0,16},{1,17},{2,18},{3,19},{4,20},{5,21},{6,22},{7,23},{8,24},{9,... | collective-permute-start | bytes 589832 | tf_op jit(solution)/shard_map/ppermute | solution.py:1504
  146.6 12.4 %collective-permute-start.52 = (bf16[192,896]{1,0:T(8,128)(2,1)S(1)}, bf16[192,896]{1,0:T(8,128)(2,1)S(1)}, u32[]{:S(2)}, u32[]{:S(2)}) collective-permute-start(bf16[192,896]{1,0:T(8,128)(2,1)S(1)} %get-tuple-element.266), channel_id=1, source_target_pairs={{0,1},{1,0},{2,3},{3,2},{4,5},{5,4},{6,7},{7,6},{8,9},{9,8},{10,11... | collective-permute-start | bytes 1032200 | tf_op jit(solution)/shard_map/ppermute | solution.py:1504
  147.2 10.5 %collective-permute-start.51 = (bf16[192,768]{1,0:T(8,128)(2,1)S(1)}, bf16[192,768]{1,0:T(8,128)(2,1)S(1)}, u32[]{:S(2)}, u32[]{:S(2)}) collective-permute-start(bf16[192,768]{1,0:T(8,128)(2,1)S(1)} %get-tuple-element.278), channel_id=1, source_target_pairs={{0,2},{1,3},{2,0},{3,1},{4,6},{5,7},{6,4},{7,5},{8,10},{9,11},{10,... | collective-permute-start | bytes 884744 | tf_op jit(solution)/shard_map/ppermute | solution.py:1504
  148.4 5.7 %collective-permute-start.50 = (bf16[128,768]{1,0:T(8,128)(2,1)S(1)}, bf16[128,768]{1,0:T(8,128)(2,1)S(1)}, u32[]{:S(2)}, u32[]{:S(2)}) collective-permute-start(bf16[128,768]{1,0:T(8,128)(2,1)S(1)} %corner_pass.1), channel_id=1, source_target_pairs={{0,16},{1,17},{2,18},{3,19},{4,20},{5,21},{6,22},{7,23},{8,9},{9,8... | collective-permute-start | bytes 589832 | tf_op jit(solution)/shard_map/ppermute | solution.py:1504
  149.5 11.1 %collective-permute-start.53 = (bf16[128,768]{1,0:T(8,128)(2,1)S(1)}, bf16[128,768]{1,0:T(8,128)(2,1)S(1)}, u32[]{:S(2)}, u32[]{:S(2)}) collective-permute-start(bf16[128,768]{1,0:T(8,128)(2,1)S(1)} %get-tuple-element.284), channel_id=1, source_target_pairs={{0,8},{1,9},{2,10},{3,11},{4,12},{5,13},{6,14},{7,15},{8,0},{9,1},... | collective-permute-start | bytes 589832 | tf_op jit(solution)/shard_map/ppermute | solution.py:1504
  155.0 17.0 %collective-permute-start.58 = (bf16[384,384]{1,0:T(8,128)(2,1)S(1)}, bf16[384,384]{1,0:T(8,128)(2,1)S(1)}, u32[]{:S(2)}, u32[]{:S(2)}) collective-permute-start(bf16[384,384]{1,0:T(8,128)(2,1)S(1)} %get-tuple-element.295), channel_id=1, source_target_pairs={{0,2},{1,3},{2,0},{3,1},{4,6},{5,7},{6,4},{7,5},{8,10},{9,11},{10,... | collective-permute-start | bytes 884744 | tf_op jit(solution)/shard_map/ppermute | solution.py:1504
  156.2 15.8 %collective-permute-start.57 = (bf16[384,384]{1,0:T(8,128)(2,1)S(1)}, bf16[384,384]{1,0:T(8,128)(2,1)S(1)}, u32[]{:S(2)}, u32[]{:S(2)}) collective-permute-start(bf16[384,384]{1,0:T(8,128)(2,1)S(1)} %get-tuple-element.293), channel_id=1, source_target_pairs={{0,1},{1,0},{2,3},{3,2},{4,5},{5,4},{6,7},{7,6},{8,9},{9,8},{10,11... | collective-permute-start | bytes 884744 | tf_op jit(solution)/shard_map/ppermute | solution.py:1504
  157.7 5.7 %collective-permute-start.54 = (bf16[128,768]{1,0:T(8,128)(2,1)S(1)}, bf16[128,768]{1,0:T(8,128)(2,1)S(1)}, u32[]{:S(2)}, u32[]{:S(2)}) collective-permute-start(bf16[128,768]{1,0:T(8,128)(2,1)S(1)} %get-tuple-element.285), channel_id=1, source_target_pairs={{0,16},{1,17},{2,18},{3,19},{4,20},{5,21},{6,22},{7,23},{8,24},{9,... | collective-permute-start | bytes 589832 | tf_op jit(solution)/shard_map/ppermute | solution.py:1504
  159.0 8.1 %collective-permute-start.55 = (bf16[128,768]{1,0:T(8,128)(2,1)S(1)}, bf16[128,768]{1,0:T(8,128)(2,1)S(1)}, u32[]{:S(2)}, u32[]{:S(2)}) collective-permute-start(bf16[128,768]{1,0:T(8,128)(2,1)S(1)} %get-tuple-element.276), channel_id=1, source_target_pairs={{0,1},{1,0},{2,3},{3,2},{4,5},{5,4},{6,7},{7,6},{8,9},{9,8},{10,11... | collective-permute-start | bytes 589832 | tf_op jit(solution)/shard_map/ppermute | solution.py:1504
  160.6 17.2 %collective-permute-start.60 = (bf16[96,1664]{1,0:T(8,128)(2,1)S(1)}, bf16[96,1664]{1,0:T(8,128)(2,1)S(1)}, u32[]{:S(2)}, u32[]{:S(2)}) collective-permute-start(bf16[96,1664]{1,0:T(8,128)(2,1)S(1)} %get-tuple-element.280), channel_id=1, source_target_pairs={{0,4},{1,5},{2,6},{3,7},{4,0},{5,1},{6,2},{7,3},{8,12},{9,13},{10,... | collective-permute-start | bytes 958472 | tf_op jit(solution)/shard_map/ppermute | solution.py:1504
  172.7 7.9 %collective-permute-start.62 = (bf16[224,384]{1,0:T(8,128)(2,1)S(1)}, bf16[224,384]{1,0:T(8,128)(2,1)S(1)}, u32[]{:S(2)}, u32[]{:S(2)}) collective-permute-start(bf16[224,384]{1,0:T(8,128)(2,1)S(1)} %get-tuple-element.302), channel_id=1, source_target_pairs={{0,1},{1,0},{2,3},{3,2},{4,5},{5,4},{6,7},{7,6},{8,9},{9,8},{10,11... | collective-permute-start | bytes 516104 | tf_op jit(solution)/shard_map/ppermute | solution.py:1504
  181.2 11.3 %collective-permute-start.65 = (bf16[96,1664]{1,0:T(8,128)(2,1)S(1)}, bf16[96,1664]{1,0:T(8,128)(2,1)S(1)}, u32[]{:S(2)}, u32[]{:S(2)}) collective-permute-start(bf16[96,1664]{1,0:T(8,128)(2,1)S(1)} %mlp_total.1.refs_0_), channel_id=1, source_target_pairs={{0,16},{1,17},{2,18},{3,19},{4,20},{5,21},{6,22},{7,23},{8,24},{9,... | collective-permute-start | bytes 958472 | tf_op jit(solution)/shard_map/ppermute | solution.py:1504
  182.0 10.0 %collective-permute-start.63 = (bf16[112,768]{1,0:T(8,128)(2,1)S(1)}, bf16[112,768]{1,0:T(8,128)(2,1)S(1)}, u32[]{:S(2)}, u32[]{:S(2)}) collective-permute-start(bf16[112,768]{1,0:T(8,128)(2,1)S(1)} %get-tuple-element.307), channel_id=1, source_target_pairs={{0,4},{1,5},{2,6},{3,7},{4,0},{5,1},{6,2},{7,3},{8,12},{9,13},{10,... | collective-permute-start | bytes 516104 | tf_op jit(solution)/shard_map/ppermute | solution.py:1504
  184.0 15.3 %collective-permute-start.64 = (bf16[96,1664]{1,0:T(8,128)(2,1)S(1)}, bf16[96,1664]{1,0:T(8,128)(2,1)S(1)}, u32[]{:S(2)}, u32[]{:S(2)}) collective-permute-start(bf16[96,1664]{1,0:T(8,128)(2,1)S(1)} %mlp_total.1.refs_0_), channel_id=1, source_target_pairs={{0,8},{1,9},{2,10},{3,11},{4,12},{5,13},{6,14},{7,15},{8,0},{9,1},... | collective-permute-start | bytes 958472 | tf_op jit(solution)/shard_map/ppermute | solution.py:1504
  192.5 6.8 %collective-permute-start.66 = (bf16[96,1664]{1,0:T(8,128)(2,1)S(1)}, bf16[96,1664]{1,0:T(8,128)(2,1)S(1)}, u32[]{:S(2)}, u32[]{:S(2)}) collective-permute-start(bf16[96,1664]{1,0:T(8,128)(2,1)S(1)} %collective-permute-done.65.refs_2_), channel_id=1, source_target_pairs={{0,8},{1,9},{2,10},{3,11},{4,12},{5,13},{6,14},{7,15},{8,0},{9,1},... | collective-permute-start | bytes 958472 | tf_op jit(solution)/shard_map/ppermute | solution.py:1504
  194.1 7.6 %collective-permute-start.68 = (bf16[96,896]{1,0:T(8,128)(2,1)S(1)}, bf16[96,896]{1,0:T(8,128)(2,1)S(1)}, u32[]{:S(2)}, u32[]{:S(2)}) collective-permute-start(bf16[96,896]{1,0:T(8,128)(2,1)S(1)} %qkv_total.1.refs_0_), channel_id=1, source_target_pairs={{0,16},{1,17},{2,18},{3,19},{4,20},{5,21},{6,22},{7,23},{8,24},{9,... | collective-permute-start | bytes 516104 | tf_op jit(solution)/shard_map/ppermute | solution.py:1504
  194.9 13.4 %collective-permute-start.56 = (bf16[144,768]{1,0:T(8,128)(2,1)S(1)}, bf16[144,768]{1,0:T(8,128)(2,1)S(1)}, u32[]{:S(2)}, u32[]{:S(2)}) collective-permute-start(bf16[144,768]{1,0:T(8,128)(2,1)S(1)} %get-tuple-element.287), channel_id=1, source_target_pairs={{0,0},{1,1},{2,16},{3,17},{4,8},{5,9},{6,24},{7,25},{8,4},{9,5},{1... | collective-permute-start | bytes 663560 | tf_op jit(solution)/shard_map/ppermute | solution.py:1504
  196.9 12.8 %collective-permute-start.67 = (bf16[96,896]{1,0:T(8,128)(2,1)S(1)}, bf16[96,896]{1,0:T(8,128)(2,1)S(1)}, u32[]{:S(2)}, u32[]{:S(2)}) collective-permute-start(bf16[96,896]{1,0:T(8,128)(2,1)S(1)} %qkv_total.1.refs_0_), channel_id=1, source_target_pairs={{0,8},{1,9},{2,10},{3,11},{4,12},{5,13},{6,14},{7,15},{8,0},{9,1},... | collective-permute-start | bytes 516104 | tf_op jit(solution)/shard_map/ppermute | solution.py:1504
  201.7 8.0 %collective-permute-start.69 = (bf16[96,896]{1,0:T(8,128)(2,1)S(1)}, bf16[96,896]{1,0:T(8,128)(2,1)S(1)}, u32[]{:S(2)}, u32[]{:S(2)}) collective-permute-start(bf16[96,896]{1,0:T(8,128)(2,1)S(1)} %collective-permute-done.68.refs_2_), channel_id=1, source_target_pairs={{0,8},{1,9},{2,10},{3,11},{4,12},{5,13},{6,14},{7,15},{8,0},{9,1},... | collective-permute-start | bytes 516104 | tf_op jit(solution)/shard_map/ppermute | solution.py:1504
  (32 other events, 156.9 us)

commit v6 on v5

--- a/solution.py
+++ b/solution.py
@@ -784,17 +784,14 @@
     return result, column_sum(grad * normed), column_sum(grad)
 
 
-def pack_kernel(unused_ref, tokens_ref, grads_ref, clip_ref, pack_ref):
-    count, width = tokens_ref.shape
-    more = grads_ref.shape[0]
-    pack_ref[:count, :] = tokens_ref[...]
-    pack_ref[count : count + more, :] = grads_ref[...]
+def pack_kernel(unused_ref, grads_ref, clip_ref, pack_ref):
+    more, width = grads_ref.shape
+    rest = pack_ref.shape[0] - more
+    pack_ref[:more, :] = grads_ref[...]
     clips = clip_ref[...].astype(F32)
     clips = jnp.concatenate([clips, jnp.zeros((1, PAD - clips.shape[1]), F32)], axis=1)
-    pack_ref[count + more :, :] = jnp.zeros((pack_ref.shape[0] - count - more, width), BF)
-    pack_ref[count + more :, :PAD] = jnp.broadcast_to(
-        clips, (pack_ref.shape[0] - count - more, PAD)
-    ).astype(BF)
+    pack_ref[more:, :] = jnp.zeros((rest, width), BF)
+    pack_ref[more:, :PAD] = jnp.broadcast_to(clips, (rest, PAD)).astype(BF)
 
 
 def select_kernel(ids_ref, qkv_ref, out_ref, own_ref):
@@ -835,14 +832,15 @@
     )
 
 
-def norm_one_kernel(ids_ref, moved_ref, gains_ref, shifts_ref, low_ref, qclip_ref, kclip_ref):
+def norm_one_kernel(ids_ref, *refs):
+    moved_ref, extra_ref, gains_ref, shifts_ref, low_ref, qclip_ref, kclip_ref = refs
     count = low_ref.shape[0]
     frames = count // (GRID * GRID)
     patches = GRID * GRID
     normed, unused = norm_stats(moved_ref[:count, :].astype(F32))
     low_ref[...] = (normed * gains_ref[0:1, :] + shifts_ref[0:1, :]).astype(BF)
-    start = count + frames * CH
-    clips = moved_ref[start : start + 16, :PAD].astype(F32)[0:1]
+    start = frames * CH
+    clips = extra_ref[start : start + 16, :PAD].astype(F32)[0:1]
     lane = lax.broadcasted_iota(jnp.int32, (1, PAD), 1)
     rank, low = ids_ref[0], ids_ref[2]
     for side in range(2):
@@ -1132,7 +1130,7 @@
         wide = moved if wide is None else wide + moved
     cotangent = jnp.concatenate(
         [
-            moved_ref[count : count + frames * CH, :].astype(F32),
+            moved_ref[: frames * CH, :].astype(F32),
             jnp.zeros((PAD - frames * CH, value.shape[1]), F32),
         ],
         axis=0,
@@ -1586,18 +1584,19 @@
         shape = (size, kept.shape[1] + PAD)
         return ordered_run(total_sums_kernel, name, ids, arrays + [sums], [(shape, BF)])[0]
 
+    (own_pack,) = ordered_run(
+        select_kernel, "select", ids, [w_qkv, w_out], [((size, width), BF)]
+    )
+
+    moved = to_planes(inputs.reshape(rows, width))
     (pack,) = ordered_run(
         pack_kernel,
         "pack",
         ids,
-        [inputs.reshape(rows, width), cotangent.reshape(learned_rows, width), clip_id],
-        [((rows + learned_rows + 16, width), BF)],
-    )
-    moved = to_planes(pack)
-
-    (own_pack,) = ordered_run(
-        select_kernel, "select", ids, [w_qkv, w_out], [((size, width), BF)]
-    )
+        [cotangent.reshape(learned_rows, width), clip_id],
+        [((learned_rows + 16, width), BF)],
+    )
+    extra = to_planes(pack)
     pack_two = flip(own_pack, 0, 2)
     pack_one = flip(own_pack, 0, 1)
     pack_side = flip(own_pack, 0, 0, 1)
@@ -1628,7 +1627,7 @@
         norm_one_kernel,
         "norm_one",
         ids,
-        [moved, ln_gains, ln_biases],
+        [moved, extra, ln_gains, ln_biases],
         [((rows, width), BF), ((1, own_count), F32), ((2 * own_count, 1), F32)],
     )
     low_norm = after(low_norm, pack_side, pack_one, pack_two)
@@ -1753,7 +1752,7 @@
             first_bias_pad,
             mid_pad,
             mid_bias_pad,
-            moved,
+            extra,
         ],
         [
             ((learned_rows, width), F32),

time: 213 us -> 211 us (level)
  waiting for transfers between devices: 86.3 us -> 72.7 us
  starting transfers between devices: 57.2 us -> 68.7 us
    ppermute x70 -> x71, waiting for transfers between devices: 86.3 us -> 72.7 us  [permute(): return lax.ppermute(array, AXES, pairs)]
    ppermute x70 -> x71, starting transfers between devices: 57.2 us -> 68.7 us  [permute(): return lax.ppermute(array, AXES, pairs)]
    unnamed x22 -> x20, local copies, waits for them, and re-layouts: 5.85 us -> 5.91 us
  transfers between devices with their start and end apart: 70 -> 71, of which waited for: 33 -> 28; matrix products, arithmetic and copies ran while one was open for 2% -> 2% of each run, Pallas kernels for 21% -> 22%
where the time goes in v6:
time: 211 us; the launch traced here: 210 us
  waiting for transfers between devices  72.7 us (34%)
  starting transfers between devices  68.7 us (33%)
  Pallas kernels  58.2 us (28%)
  local copies, waits for them, and re-layouts  8.67 us (4%)
    ppermute x71, waiting for transfers between devices, permute(): return lax.ppermute(array, AXES, pairs)  72.7 us
    ppermute x71, starting transfers between devices, permute(): return lax.ppermute(array, AXES, pairs)  68.7 us
    pallas_call x37, Pallas kernels, run(): pl.pallas_call(kernel, in_specs=[pl.BlockSpec(memory_space=pltpu.SMEM)] +...  58.2 us
    unnamed x20, local copies, waits for them, and re-layouts  5.91 us
  transfers between devices with their start and end apart: 71, of which 28 were waited for; matrix products, arithmetic and copies ran while one was open for 2% of the time, Pallas kernels for 22%

profile of v6, /device:TPU:2, one launch (start us, length us, event | category | flops | bytes accessed | tf_op | source)
XLA Modules:
  0.0 210.1 jit_solution(6988387572400907183)
XLA Ops:
  0.7 3.6 %collective-permute-start = (bf16[128,768]{1,0:T(8,128)(2,1)}, bf16[128,768]{1,0:T(8,128)(2,1)S(1)}, u32[]{:S(2)}, u32[]{:S(2)}) collective-permute-start(bf16[128,768]{1,0:T(8,128)(2,1)} %bitcast.15), channel_id=1, source_target_pairs={{0,0},{1,1},{2,16},{3,17},{4,8},{5,9},{6,24},{7,25},{8,4},{9,5},{1... | collective-permute-start | bytes 589832 | tf_op jit(solution)/shard_map/ppermute | solution.py:1502
  8.1 1.6 collective-permute-start.3
  13.1 2.5 %collective-permute-start.1 = (bf16[32,768]{1,0:T(8,128)(2,1)S(1)}, bf16[32,768]{1,0:T(8,128)(2,1)S(1)}, u32[]{:S(2)}, u32[]{:S(2)}) collective-permute-start(bf16[32,768]{1,0:T(8,128)(2,1)S(1)} %pack.1), channel_id=1, source_target_pairs={{0,0},{1,1},{2,16},{3,17},{4,8},{5,9},{6,24},{7,25},{8,4},{9,5},{1... | collective-permute-start | bytes 147464 | tf_op jit(solution)/shard_map/ppermute | solution.py:1502
  22.8 1.8 collective-permute-start.10
  29.0 3.5 %collective-permute-done.6.refs_1_ = bf16[96,896]{1,0:T(8,128)(2,1)S(1)} collective-permute-done((bf16[96,896]{1,0:T(8,128)(2,1)S(1)}, bf16[96,896]{1,0:T(8,128)(2,1)S(1)}, u32[]{:S(2)}, u32[]{:S(2)}) %collective-permute-start.6) | collective-permute-done | bytes 172064 | tf_op jit(solution)/shard_map/ppermute | solution.py:1502
  34.4 2.8 %collective-permute-done.9.refs_13_ = bf16[96,768]{1,0:T(8,128)(2,1)S(1)} collective-permute-done((bf16[96,768]{1,0:T(8,128)(2,1)S(1)}, bf16[96,768]{1,0:T(8,128)(2,1)S(1)}, u32[]{:S(2)}, u32[]{:S(2)}) %collective-permute-start.9) | collective-permute-done | bytes 147488 | tf_op jit(solution)/shard_map/ppermute | solution.py:1502
  37.9 2.6 %collective-permute-done.8.refs_11_ = bf16[96,768]{1,0:T(8,128)(2,1)S(1)} collective-permute-done((bf16[96,768]{1,0:T(8,128)(2,1)S(1)}, bf16[96,768]{1,0:T(8,128)(2,1)S(1)}, u32[]{:S(2)}, u32[]{:S(2)}) %collective-permute-start.8) | collective-permute-done | bytes 147488 | tf_op jit(solution)/shard_map/ppermute | solution.py:1502
  40.5 2.1 collective-permute-done.11.refs_15_
  44.6 4.2 %collective-permute-done.16.refs_6_ = bf16[128,768]{1,0:T(8,128)(2,1)S(1)} collective-permute-done((bf16[128,768]{1,0:T(8,128)(2,1)S(1)}, bf16[128,768]{1,0:T(8,128)(2,1)S(1)}, u32[]{:S(2)}, u32[]{:S(2)}) %collective-permute-start.16) | collective-permute-done | bytes 196640 | tf_op jit(solution)/shard_map/ppermute | solution.py:1502
  49.9 1.7 collective-permute-start.23
  51.6 1.8 project.1
  55.3 5.9 %attend.1 = (bf16[192,512]{1,0:T(8,128)(2,1)S(1)}, f32[8,512]{1,0:T(8,128)S(1)}) custom-call(s32[3]{0:T(128)S(1)} %pad_add_fusion.ids_ref.unused_ref.rank_ref, bf16[512,192]{1,0:T(8,128)(2,1)S(1)} %get-tuple-element.189.refs_0_.refs_3_.refs_2_, bf16[1024,384]{1,0:T(8,128)(2,1)S(1)} %get-tuple-element.190.refs_1_.refs_4_.refs_3_, ...), custom_call_target="tpu_custom_call" | custom-call | tf_op jit(solution)/shard_map/attend/pallas_call | solution.py:745
  64.5 1.8 collective-permute-done.22.refs_1_
  70.4 5.9 %collective-permute-done.25.refs_3_ = bf16[128,768]{1,0:T(8,128)(2,1)S(1)} collective-permute-done((bf16[128,768]{1,0:T(8,128)(2,1)S(1)}, bf16[128,768]{1,0:T(8,128)(2,1)S(1)}, u32[]{:S(2)}, u32[]{:S(2)}) %collective-permute-start.25) | collective-permute-done | bytes 196640 | tf_op jit(solution)/shard_map/ppermute | solution.py:1502
  78.7 4.4 %collective-permute-done.29.refs_5_ = bf16[384,768]{1,0:T(8,128)(2,1)S(1)} collective-permute-done((bf16[384,768]{1,0:T(8,128)(2,1)S(1)}, bf16[384,768]{1,0:T(8,128)(2,1)S(1)}, u32[]{:S(2)}, u32[]{:S(2)}) %collective-permute-start.29) | collective-permute-done | bytes 589856 | tf_op jit(solution)/shard_map/ppermute | solution.py:1502
  84.1 2.1 %mlp.1 = (bf16[768,768]{1,0:T(8,128)(2,1)S(1)}, bf16[768,768]{1,0:T(8,128)(2,1)S(1)}, bf16[768,128]{1,0:T(8,128)(2,1)S(1)}, f32[1,768]{1,0:T(1,128)S(1)}, bf16[2...) custom-call(s32[3]{0:T(128)S(1)} %pad_add_fusion.ids_ref.unused_ref.rank, ...), custom_call_target="tpu_custom_call" | custom-call | tf_op jit(solution)/shard_map/mlp/pallas_call | solution.py:745
  87.7 2.0 mlp_more.1
  91.8 1.9 collective-permute-start.33
  93.7 5.2 %collective-permute-done.33.refs_3_ = bf16[128,768]{1,0:T(8,128)(2,1)S(1)} collective-permute-done((bf16[128,768]{1,0:T(8,128)(2,1)S(1)}, bf16[128,768]{1,0:T(8,128)(2,1)S(1)}, u32[]{:S(2)}, u32[]{:S(2)}) %collective-permute-start.33) | collective-permute-done | bytes 196640 | tf_op jit(solution)/shard_map/ppermute | solution.py:1502
  98.9 6.4 %tail.1 = (f32[16,768]{1,0:T(8,128)S(1)}, bf16[128,768]{1,0:T(8,128)(2,1)S(1)}, f32[128,768]{1,0:T(8,128)S(1)}, bf16[128,768]{1,0:T(8,128)(2,1)S(1)}, bf16[128,1...) custom-call(s32[3]{0:T(128)S(1)} %pad_add_fusion.ids_ref.unused_ref.rank_ref, f32[128,768]{1,0:T(8,128)S(1)} %get-tuple-element.243.refs_0_, ...), custom_call_target="tpu_custom_call" | custom-call | tf_op jit(solution)/shard_map/tail/pallas_call | solution.py:745
  105.3 1.8 collective-permute-start.34
  108.6 4.0 %collective-permute-done.34.refs_0_.refs_6_ = bf16[128,768]{1,0:T(8,128)(2,1)S(1)} collective-permute-done((bf16[128,768]{1,0:T(8,128)(2,1)S(1)}, bf16[128,768]{1,0:T(8,128)(2,1)S(1)}, u32[]{:S(2)}, u32[]{:S(2)}) %collective-permute-start.34) | collective-permute-done | bytes 196640 | tf_op jit(solution)/shard_map/ppermute | solution.py:1502
  117.7 1.8 collective-permute-start.39
  119.5 2.3 %mlp_grads.1 = (f32[384,768]{1,0:T(8,128)S(1)}, bf16[384,768]{1,0:T(8,128)(2,1)S(1)}, f32[384,896]{1,0:T(8,128)S(1)}, bf16[384,896]{1,0:T(8,128)(2,1)S(1)}) custom-call(s32[3]{0:T(128)S(1)} %pad_add_fusion.ids_ref.unused_ref.rank_ref, bf16[128,768]{1,0:T(8,128)(2,1)S(1)} %get-tuple-element.234.refs_0_, bf16[128,768]{1,0:T(8,128)(2,1)S(1)} %collective-permute-done.27.refs_1_, ...), custom_call_target="tpu_custom_call" | custom-call | tf_op jit(solution)/shard_map/mlp_grads/pallas_call | solution.py:745
  122.0 2.7 %collective-permute-done.39.refs_4_ = bf16[128,768]{1,0:T(8,128)(2,1)S(1)} collective-permute-done((bf16[128,768]{1,0:T(8,128)(2,1)S(1)}, bf16[128,768]{1,0:T(8,128)(2,1)S(1)}, u32[]{:S(2)}, u32[]{:S(2)}) %collective-permute-start.39) | collective-permute-done | bytes 196640 | tf_op jit(solution)/shard_map/ppermute | solution.py:1502
  125.9 1.8 collective-permute-start.40
  128.0 4.0 %attend_back.1 = (bf16[256,192]{1,0:T(8,128)(2,1)S(1)}, f32[1024,384]{1,0:T(8,128)S(1)}) custom-call(s32[3]{0:T(128)S(1)} %pad_add_fusion.ids_ref.unused_ref.rank_ref, bf16[128,768]{1,0:T(8,128)(2,1)S(1)} %get-tuple-element.248.refs_0_.refs_8_, bf16[128,768]{1,0:T(8,128)(2,1)S(1)} %collective-permute-done.41.refs_1_.refs_9_, ...), custom_call_target="tpu_custom_call" | custom-call | tf_op jit(solution)/shard_map/attend_back/pallas_call | solution.py:745
  133.3 1.7 collective-permute-start.47
  135.0 2.8 %attend_back_next.1 = (bf16[128,192]{1,0:T(8,128)(2,1)S(1)}, f32[1024,384]{1,0:T(8,128)S(1)}) custom-call(s32[3]{0:T(128)S(1)} %pad_add_fusion.ids_ref.unused_ref.rank_ref, bf16[128,768]{1,0:T(8,128)(2,1)S(1)} %collective-permute-done.40.refs_0_.refs_10_, bf16[192,768]{1,0:T(8,128)(2,1)S(1)} %get-tuple-element.197.refs_2_.refs_1_, ...), custom_call_target="tpu_custom_call" | custom-call | tf_op jit(solution)/shard_map/attend_back_next/pallas_call | solution.py:745
  137.8 4.3 %attend_back_last.1 = (bf16[512,576]{1,0:T(8,128)(2,1)S(1)}, bf16[512,384]{1,0:T(8,128)(2,1)S(1)}, f32[128,768]{1,0:T(8,128)S(1)}, f32[128,768]{1,0:T(8,128)S(1)...) custom-call(s32[3]{0:T(128)S(1)} %pad_add_fusion.ids_ref.unused_ref., ...), custom_call_target="tpu_custom_call" | custom-call | tf_op jit(solution)/shard_map/attend_back_last/pallas_call | solution.py:745
  147.5 2.3 %qkv_grads.1 = (f32[384,384]{1,0:T(8,128)S(1)}, bf16[384,384]{1,0:T(8,128)(2,1)S(1)}, f32[384,384]{1,0:T(8,128)S(1)}, bf16[384,384]{1,0:T(8,128)(2,1)S(1)}) custom-call(s32[3]{0:T(128)S(1)} %pad_add_fusion.ids_ref.unused_ref.rank_ref, bf16[128,768]{1,0:T(8,128)(2,1)S(1)} %get-tuple-element.267.refs_0_, bf16[128,768]{1,0:T(8,128)(2,1)S(1)} %collective-permute-done.13.refs_1_, ...), custom_call_target="tpu_custom_call" | custom-call | tf_op jit(solution)/shard_map/qkv_grads/pallas_call | solution.py:745
  149.9 2.7 %collective-permute-done.51.refs_4_ = bf16[128,768]{1,0:T(8,128)(2,1)S(1)} collective-permute-done((bf16[128,768]{1,0:T(8,128)(2,1)S(1)}, bf16[128,768]{1,0:T(8,128)(2,1)S(1)}, u32[]{:S(2)}, u32[]{:S(2)}) %collective-permute-start.51) | collective-permute-done | bytes 196640 | tf_op jit(solution)/shard_map/ppermute | solution.py:1502
  154.3 1.7 collective-permute-start.58
  159.6 2.1 %collective-permute-done.55.refs_4_ = bf16[128,768]{1,0:T(8,128)(2,1)S(1)} collective-permute-done((bf16[128,768]{1,0:T(8,128)(2,1)S(1)}, bf16[128,768]{1,0:T(8,128)(2,1)S(1)}, u32[]{:S(2)}, u32[]{:S(2)}) %collective-permute-start.55) | collective-permute-done | bytes 196640 | tf_op jit(solution)/shard_map/ppermute | solution.py:1502
  161.7 3.4 %collective-permute-done.56.refs_5_ = bf16[128,768]{1,0:T(8,128)(2,1)S(1)} collective-permute-done((bf16[128,768]{1,0:T(8,128)(2,1)S(1)}, bf16[128,768]{1,0:T(8,128)(2,1)S(1)}, u32[]{:S(2)}, u32[]{:S(2)}) %collective-permute-start.56) | collective-permute-done | bytes 196640 | tf_op jit(solution)/shard_map/ppermute | solution.py:1502
  167.0 3.0 %collective-permute-done.60.refs_5_ = bf16[96,128]{1,0:T(8,128)(2,1)S(1)} collective-permute-done((bf16[96,128]{1,0:T(8,128)(2,1)S(1)}, bf16[96,128]{1,0:T(8,128)(2,1)S(1)}, u32[]{:S(2)}, u32[]{:S(2)}) %collective-permute-start.60) | collective-permute-done | bytes 24608 | tf_op jit(solution)/shard_map/ppermute | solution.py:1502
  170.7 2.5 %collective-permute-start.63 = (bf16[224,384]{1,0:T(8,128)(2,1)S(1)}, bf16[224,384]{1,0:T(8,128)(2,1)S(1)}, u32[]{:S(2)}, u32[]{:S(2)}) collective-permute-start(bf16[224,384]{1,0:T(8,128)(2,1)S(1)} %get-tuple-element.302), channel_id=1, source_target_pairs={{0,1},{1,0},{2,3},{3,2},{4,5},{5,4},{6,7},{7,6},{8,9},{9,8},{10,11... | collective-permute-start | bytes 516104 | tf_op jit(solution)/shard_map/ppermute | solution.py:1502
  173.6 2.0 collective-permute-done.61.arrived_ref
  176.2 2.2 %collective-permute-done.62.refs_1_ = bf16[192,384]{1,0:T(8,128)(2,1)S(1)} collective-permute-done((bf16[192,384]{1,0:T(8,128)(2,1)S(1)}, bf16[192,384]{1,0:T(8,128)(2,1)S(1)}, u32[]{:S(2)}, u32[]{:S(2)}) %collective-permute-start.62) | collective-permute-done | bytes 147488 | tf_op jit(solution)/shard_map/ppermute | solution.py:1502
  180.0 1.5 collective-permute-start.64
  181.5 3.1 %collective-permute-start.65 = (bf16[96,1664]{1,0:T(8,128)(2,1)S(1)}, bf16[96,1664]{1,0:T(8,128)(2,1)S(1)}, u32[]{:S(2)}, u32[]{:S(2)}) collective-permute-start(bf16[96,1664]{1,0:T(8,128)(2,1)S(1)} %mlp_total.1.refs_0_), channel_id=1, source_target_pairs={{0,8},{1,9},{2,10},{3,11},{4,12},{5,13},{6,14},{7,15},{8,0},{9,1},... | collective-permute-start | bytes 958472 | tf_op jit(solution)/shard_map/ppermute | solution.py:1502
  184.6 3.1 %collective-permute-done.64.arrived_ref = bf16[112,768]{1,0:T(8,128)(2,1)S(1)} collective-permute-done((bf16[112,768]{1,0:T(8,128)(2,1)S(1)}, bf16[112,768]{1,0:T(8,128)(2,1)S(1)}, u32[]{:S(2)}, u32[]{:S(2)}) %collective-permute-start.64) | collective-permute-done | bytes 172064 | tf_op jit(solution)/shard_map/ppermute | solution.py:1502
  188.3 3.7 %collective-permute-start.67 = (bf16[96,1664]{1,0:T(8,128)(2,1)S(1)}, bf16[96,1664]{1,0:T(8,128)(2,1)S(1)}, u32[]{:S(2)}, u32[]{:S(2)}) collective-permute-start(bf16[96,1664]{1,0:T(8,128)(2,1)S(1)} %collective-permute-done.66.refs_2_), channel_id=1, source_target_pairs={{0,8},{1,9},{2,10},{3,11},{4,12},{5,13},{6,14},{7,15},{8,0},{9,1},... | collective-permute-start | bytes 958472 | tf_op jit(solution)/shard_map/ppermute | solution.py:1502
  193.2 1.9 collective-permute-start.57
  195.1 2.2 %collective-permute-start.68 = (bf16[96,896]{1,0:T(8,128)(2,1)S(1)}, bf16[96,896]{1,0:T(8,128)(2,1)S(1)}, u32[]{:S(2)}, u32[]{:S(2)}) collective-permute-start(bf16[96,896]{1,0:T(8,128)(2,1)S(1)} %qkv_total.1.refs_0_), channel_id=1, source_target_pairs={{0,8},{1,9},{2,10},{3,11},{4,12},{5,13},{6,14},{7,15},{8,0},{9,1},... | collective-permute-start | bytes 516104 | tf_op jit(solution)/shard_map/ppermute | solution.py:1502
  197.4 2.4 %finish_mlp.1 = (f32[96,3072]{1,0:T(8,128)}, f32[384,768]{1,0:T(8,128)}, f32[96,72]{1,0:T(8,128)S(1)}) custom-call(s32[3]{0:T(128)S(1)} %pad_add_fusion.ids_ref.unused_ref.rank_ref, bf16[96,1664]{1,0:T(8,128)(2,1)S(1)} %mlp_total.1.refs_0_, bf16[96,1664]{1,0:T(8,128)(2,1)S(1)} %collective-permute-done.65.refs_1_, ...), custom_call_target="tpu_custom_call" | custom-call | tf_op jit(solution)/shard_map/finish_mlp/pallas_call | solution.py:745
  200.4 5.9 %collective-permute-done.57.moved_ref = bf16[144,768]{1,0:T(8,128)(2,1)S(1)} collective-permute-done((bf16[144,768]{1,0:T(8,128)(2,1)S(1)}, bf16[144,768]{1,0:T(8,128)(2,1)S(1)}, u32[]{:S(2)}, u32[]{:S(2)}) %collective-permute-start.57) | collective-permute-done | bytes 221216 | tf_op jit(solution)/shard_map/ppermute | solution.py:1502
  207.6 1.8 finish_qkv.1
  (157 shorter events, 70.2 us)
Async XLA Ops:
  0.7 22.1 %collective-permute-start = (bf16[128,768]{1,0:T(8,128)(2,1)}, bf16[128,768]{1,0:T(8,128)(2,1)S(1)}, u32[]{:S(2)}, u32[]{:S(2)}) collective-permute-start(bf16[128,768]{1,0:T(8,128)(2,1)} %bitcast.15), channel_id=1, source_target_pairs={{0,0},{1,1},{2,16},{3,17},{4,8},{5,9},{6,24},{7,25},{8,4},{9,5},{1... | collective-permute-start | bytes 589832 | tf_op jit(solution)/shard_map/ppermute | solution.py:1502
  6.9 14.9 %collective-permute-start.4 = (bf16[96,768]{1,0:T(8,128)(2,1)S(1)}, bf16[96,768]{1,0:T(8,128)(2,1)S(1)}, u32[]{:S(2)}, u32[]{:S(2)}) collective-permute-start(bf16[96,768]{1,0:T(8,128)(2,1)S(1)} %select.10.refs_8_), channel_id=1, source_target_pairs={{0,4},{1,5},{2,6},{3,7},{4,0},{5,1},{6,2},{7,3},{8,12},{9,13},{10,... | collective-permute-start | bytes 442376 | tf_op jit(solution)/shard_map/ppermute | solution.py:1502
  8.1 17.3 %collective-permute-start.3 = (bf16[96,768]{1,0:T(8,128)(2,1)S(1)}, bf16[96,768]{1,0:T(8,128)(2,1)S(1)}, u32[]{:S(2)}, u32[]{:S(2)}) collective-permute-start(bf16[96,768]{1,0:T(8,128)(2,1)S(1)} %select.10.refs_8_), channel_id=1, source_target_pairs={{0,2},{1,3},{2,0},{3,1},{4,6},{5,7},{6,4},{7,5},{8,10},{9,11},{10,... | collective-permute-start | bytes 442376 | tf_op jit(solution)/shard_map/ppermute | solution.py:1502
  9.6 15.8 %collective-permute-start.2 = (bf16[96,768]{1,0:T(8,128)(2,1)S(1)}, bf16[96,768]{1,0:T(8,128)(2,1)S(1)}, u32[]{:S(2)}, u32[]{:S(2)}) collective-permute-start(bf16[96,768]{1,0:T(8,128)(2,1)S(1)} %select.10.refs_8_), channel_id=1, source_target_pairs={{0,1},{1,0},{2,3},{3,2},{4,5},{5,4},{6,7},{7,6},{8,9},{9,8},{10,11... | collective-permute-start | bytes 442376 | tf_op jit(solution)/shard_map/ppermute | solution.py:1502
  13.1 8.1 %collective-permute-start.1 = (bf16[32,768]{1,0:T(8,128)(2,1)S(1)}, bf16[32,768]{1,0:T(8,128)(2,1)S(1)}, u32[]{:S(2)}, u32[]{:S(2)}) collective-permute-start(bf16[32,768]{1,0:T(8,128)(2,1)S(1)} %pack.1), channel_id=1, source_target_pairs={{0,0},{1,1},{2,16},{3,17},{4,8},{5,9},{6,24},{7,25},{8,4},{9,5},{1... | collective-permute-start | bytes 147464 | tf_op jit(solution)/shard_map/ppermute | solution.py:1502
  21.2 11.2 %collective-permute-start.6 = (bf16[96,896]{1,0:T(8,128)(2,1)S(1)}, bf16[96,896]{1,0:T(8,128)(2,1)S(1)}, u32[]{:S(2)}, u32[]{:S(2)}) collective-permute-start(bf16[96,896]{1,0:T(8,128)(2,1)S(1)} %get-tuple-element.182.refs_0_), channel_id=1, source_target_pairs={{0,4},{1,5},{2,6},{3,7},{4,0},{5,1},{6,2},{7,3},{8,12},{9,13},{10,... | collective-permute-start | bytes 516104 | tf_op jit(solution)/shard_map/ppermute | solution.py:1502
  21.9 6.6 %collective-permute-start.7 = (bf16[96,768]{1,0:T(8,128)(2,1)S(1)}, bf16[96,768]{1,0:T(8,128)(2,1)S(1)}, u32[]{:S(2)}, u32[]{:S(2)}) collective-permute-start(bf16[96,768]{1,0:T(8,128)(2,1)S(1)} %get-tuple-element.175.refs_2_), channel_id=1, source_target_pairs={{0,1},{1,0},{2,3},{3,2},{4,5},{5,4},{6,7},{7,6},{8,9},{9,8},{10,11... | collective-permute-start | bytes 442376 | tf_op jit(solution)/shard_map/ppermute | solution.py:1502
  22.8 10.3 %collective-permute-start.10 = (bf16[96,768]{1,0:T(8,128)(2,1)S(1)}, bf16[96,768]{1,0:T(8,128)(2,1)S(1)}, u32[]{:S(2)}, u32[]{:S(2)}) collective-permute-start(bf16[96,768]{1,0:T(8,128)(2,1)S(1)} %collective-permute-done.4.refs_12_), channel_id=1, source_target_pairs={{0,2},{1,3},{2,0},{3,1},{4,6},{5,7},{6,4},{7,5},{8,10},{9,11},{10,... | collective-permute-start | bytes 442376 | tf_op jit(solution)/shard_map/ppermute | solution.py:1502
  25.4 11.9 %collective-permute-start.5 = (bf16[128,768]{1,0:T(8,128)(2,1)S(1)}, bf16[128,768]{1,0:T(8,128)(2,1)S(1)}, u32[]{:S(2)}, u32[]{:S(2)}) collective-permute-start(bf16[128,768]{1,0:T(8,128)(2,1)S(1)} %get-tuple-element.267.refs_0_), channel_id=1, source_target_pairs={{0,16},{1,17},{2,18},{3,19},{4,20},{5,21},{6,22},{7,23},{8,24},{9,... | collective-permute-start | bytes 589832 | tf_op jit(solution)/shard_map/ppermute | solution.py:1502
  26.9 10.9 %collective-permute-start.12 = (bf16[128,768]{1,0:T(8,128)(2,1)S(1)}, bf16[128,768]{1,0:T(8,128)(2,1)S(1)}, u32[]{:S(2)}, u32[]{:S(2)}) collective-permute-start(bf16[128,768]{1,0:T(8,128)(2,1)S(1)} %get-tuple-element.267.refs_0_), channel_id=1, source_target_pairs={{0,1},{1,0},{2,3},{3,2},{4,5},{5,4},{6,7},{7,6},{8,9},{9,8},{10,11... | collective-permute-start | bytes 589832 | tf_op jit(solution)/shard_map/ppermute | solution.py:1502
  28.5 8.8 %collective-permute-start.9 = (bf16[96,768]{1,0:T(8,128)(2,1)S(1)}, bf16[96,768]{1,0:T(8,128)(2,1)S(1)}, u32[]{:S(2)}, u32[]{:S(2)}) collective-permute-start(bf16[96,768]{1,0:T(8,128)(2,1)S(1)} %collective-permute-done.4.refs_12_), channel_id=1, source_target_pairs={{0,1},{1,0},{2,3},{3,2},{4,5},{5,4},{6,7},{7,6},{8,9},{9,8},{10,11... | collective-permute-start | bytes 442376 | tf_op jit(solution)/shard_map/ppermute | solution.py:1502
  32.4 8.0 %collective-permute-start.8 = (bf16[96,768]{1,0:T(8,128)(2,1)S(1)}, bf16[96,768]{1,0:T(8,128)(2,1)S(1)}, u32[]{:S(2)}, u32[]{:S(2)}) collective-permute-start(bf16[96,768]{1,0:T(8,128)(2,1)S(1)} %collective-permute-done.3.refs_10_), channel_id=1, source_target_pairs={{0,1},{1,0},{2,3},{3,2},{4,5},{5,4},{6,7},{7,6},{8,9},{9,8},{10,11... | collective-permute-start | bytes 442376 | tf_op jit(solution)/shard_map/ppermute | solution.py:1502
  33.0 9.5 %collective-permute-start.11 = (bf16[96,768]{1,0:T(8,128)(2,1)S(1)}, bf16[96,768]{1,0:T(8,128)(2,1)S(1)}, u32[]{:S(2)}, u32[]{:S(2)}) collective-permute-start(bf16[96,768]{1,0:T(8,128)(2,1)S(1)} %collective-permute-done.10.refs_14_), channel_id=1, source_target_pairs={{0,1},{1,0},{2,3},{3,2},{4,5},{5,4},{6,7},{7,6},{8,9},{9,8},{10,11... | collective-permute-start | bytes 442376 | tf_op jit(solution)/shard_map/ppermute | solution.py:1502
  37.3 7.3 %collective-permute-start.13 = (bf16[128,768]{1,0:T(8,128)(2,1)S(1)}, bf16[128,768]{1,0:T(8,128)(2,1)S(1)}, u32[]{:S(2)}, u32[]{:S(2)}) collective-permute-start(bf16[128,768]{1,0:T(8,128)(2,1)S(1)} %get-tuple-element.267.refs_0_), channel_id=1, source_target_pairs={{0,8},{1,9},{2,10},{3,11},{4,12},{5,13},{6,14},{7,15},{8,0},{9,1},... | collective-permute-start | bytes 589832 | tf_op jit(solution)/shard_map/ppermute | solution.py:1502
  37.3 7.3 %collective-permute-start.14 = (bf16[128,768]{1,0:T(8,128)(2,1)S(1)}, bf16[128,768]{1,0:T(8,128)(2,1)S(1)}, u32[]{:S(2)}, u32[]{:S(2)}) collective-permute-start(bf16[128,768]{1,0:T(8,128)(2,1)S(1)} %collective-permute-done.5.far_ref.refs_2_), channel_id=1, source_target_pairs={{0,8},{1,9},{2,10},{3,11},{4,12},{5,13},{6,14},{7,15},{8,0},{9,1},... | collective-permute-start | bytes 589832 | tf_op jit(solution)/shard_map/ppermute | solution.py:1502
  37.8 6.8 %collective-permute-start.15 = (bf16[128,768]{1,0:T(8,128)(2,1)S(1)}, bf16[128,768]{1,0:T(8,128)(2,1)S(1)}, u32[]{:S(2)}, u32[]{:S(2)}) collective-permute-start(bf16[128,768]{1,0:T(8,128)(2,1)S(1)} %collective-permute-done.12.side_ref.refs_4_), channel_id=1, source_target_pairs={{0,8},{1,9},{2,10},{3,11},{4,12},{5,13},{6,14},{7,15},{8,0},{9,1},... | collective-permute-start | bytes 589832 | tf_op jit(solution)/shard_map/ppermute | solution.py:1502
  49.5 16.9 %collective-permute-start.22 = (bf16[192,896]{1,0:T(8,128)(2,1)S(1)}, bf16[192,896]{1,0:T(8,128)(2,1)S(1)}, u32[]{:S(2)}, u32[]{:S(2)}) collective-permute-start(bf16[192,896]{1,0:T(8,128)(2,1)S(1)} %get-tuple-element.200.refs_0_), channel_id=1, source_target_pairs={{0,2},{1,3},{2,0},{3,1},{4,6},{5,7},{6,4},{7,5},{8,10},{9,11},{10,... | collective-permute-start | bytes 1032200 | tf_op jit(solution)/shard_map/ppermute | solution.py:1502
  49.9 14.6 %collective-permute-start.23 = (bf16[192,768]{1,0:T(8,128)(2,1)S(1)}, bf16[192,768]{1,0:T(8,128)(2,1)S(1)}, u32[]{:S(2)}, u32[]{:S(2)}) collective-permute-start(bf16[192,768]{1,0:T(8,128)(2,1)S(1)} %get-tuple-element.184.refs_2_), channel_id=1, source_target_pairs={{0,4},{1,5},{2,6},{3,7},{4,0},{5,1},{6,2},{7,3},{8,12},{9,13},{10,... | collective-permute-start | bytes 884744 | tf_op jit(solution)/shard_map/ppermute | solution.py:1502
  53.4 7.9 %collective-permute-start.18 = (bf16[192,192]{1,0:T(8,128)(2,1)S(1)}, bf16[192,192]{1,0:T(8,128)(2,1)S(1)}, u32[]{:S(2)}, u32[]{:S(2)}) collective-permute-start(bf16[192,192]{1,0:T(8,128)(2,1)S(1)} %get-tuple-element.194), channel_id=1, source_target_pairs={{0,8},{1,9},{2,10},{3,11},{4,12},{5,13},{6,14},{7,15},{8,0},{9,1},... | collective-permute-start | bytes 221192 | tf_op jit(solution)/shard_map/ppermute | solution.py:1502
  53.5 7.8 %collective-permute-start.19 = (bf16[192,192]{1,0:T(8,128)(2,1)S(1)}, bf16[192,192]{1,0:T(8,128)(2,1)S(1)}, u32[]{:S(2)}, u32[]{:S(2)}) collective-permute-start(bf16[192,192]{1,0:T(8,128)(2,1)S(1)} %get-tuple-element.195), channel_id=1, source_target_pairs={{0,16},{1,17},{2,18},{3,19},{4,20},{5,21},{6,22},{7,23},{8,24},{9,... | collective-permute-start | bytes 221192 | tf_op jit(solution)/shard_map/ppermute | solution.py:1502
  54.7 6.6 %collective-permute-start.20 = (bf16[192,192]{1,0:T(8,128)(2,1)S(1)}, bf16[192,192]{1,0:T(8,128)(2,1)S(1)}, u32[]{:S(2)}, u32[]{:S(2)}) collective-permute-start(bf16[192,192]{1,0:T(8,128)(2,1)S(1)} %get-tuple-element.188), channel_id=1, source_target_pairs={{0,24},{1,25},{2,26},{3,27},{4,28},{5,29},{6,30},{7,31},{8,16},{9,... | collective-permute-start | bytes 221192 | tf_op jit(solution)/shard_map/ppermute | solution.py:1502
  66.9 17.1 %collective-permute-start.28 = (bf16[384,896]{1,0:T(8,128)(2,1)S(1)}, bf16[384,896]{1,0:T(8,128)(2,1)S(1)}, u32[]{:S(2)}, u32[]{:S(2)}) collective-permute-start(bf16[384,896]{1,0:T(8,128)(2,1)S(1)} %get-tuple-element.208.refs_2_), channel_id=1, source_target_pairs={{0,1},{1,0},{2,3},{3,2},{4,5},{5,4},{6,7},{7,6},{8,9},{9,8},{10,11... | collective-permute-start | bytes 2064392 | tf_op jit(solution)/shard_map/ppermute | solution.py:1502
  68.4 14.7 %collective-permute-start.29 = (bf16[384,768]{1,0:T(8,128)(2,1)S(1)}, bf16[384,768]{1,0:T(8,128)(2,1)S(1)}, u32[]{:S(2)}, u32[]{:S(2)}) collective-permute-start(bf16[384,768]{1,0:T(8,128)(2,1)S(1)} %get-tuple-element.201.refs_4_), channel_id=1, source_target_pairs={{0,2},{1,3},{2,0},{3,1},{4,6},{5,7},{6,4},{7,5},{8,10},{9,11},{10,... | collective-permute-start | bytes 1769480 | tf_op jit(solution)/shard_map/ppermute | solution.py:1502
  69.0 7.3 %collective-permute-start.25 = (bf16[128,768]{1,0:T(8,128)(2,1)S(1)}, bf16[128,768]{1,0:T(8,128)(2,1)S(1)}, u32[]{:S(2)}, u32[]{:S(2)}) collective-permute-start(bf16[128,768]{1,0:T(8,128)(2,1)S(1)} %out_pass.1), channel_id=1, source_target_pairs={{0,16},{1,17},{2,18},{3,19},{4,20},{5,21},{6,22},{7,23},{8,24},{9,... | collective-permute-start | bytes 589832 | tf_op jit(solution)/shard_map/ppermute | solution.py:1502
  77.2 9.0 %collective-permute-start.26 = (bf16[128,768]{1,0:T(8,128)(2,1)S(1)}, bf16[128,768]{1,0:T(8,128)(2,1)S(1)}, u32[]{:S(2)}, u32[]{:S(2)}) collective-permute-start(bf16[128,768]{1,0:T(8,128)(2,1)S(1)} %get-tuple-element.234.refs_0_), channel_id=1, source_target_pairs={{0,16},{1,17},{2,18},{3,19},{4,20},{5,21},{6,22},{7,23},{8,24},{9,... | collective-permute-start | bytes 589832 | tf_op jit(solution)/shard_map/ppermute | solution.py:1502
  91.8 7.1 %collective-permute-start.33 = (bf16[128,768]{1,0:T(8,128)(2,1)S(1)}, bf16[128,768]{1,0:T(8,128)(2,1)S(1)}, u32[]{:S(2)}, u32[]{:S(2)}) collective-permute-start(bf16[128,768]{1,0:T(8,128)(2,1)S(1)} %mlp_pass.1), channel_id=1, source_target_pairs={{0,16},{1,17},{2,18},{3,19},{4,20},{5,21},{6,22},{7,23},{8,24},{9,... | collective-permute-start | bytes 589832 | tf_op jit(solution)/shard_map/ppermute | solution.py:1502
  105.3 7.3 %collective-permute-start.34 = (bf16[128,768]{1,0:T(8,128)(2,1)S(1)}, bf16[128,768]{1,0:T(8,128)(2,1)S(1)}, u32[]{:S(2)}, u32[]{:S(2)}) collective-permute-start(bf16[128,768]{1,0:T(8,128)(2,1)S(1)} %get-tuple-element.223.refs_0_.refs_4_), channel_id=1, source_target_pairs={{0,16},{1,17},{2,18},{3,19},{4,20},{5,21},{6,22},{7,23},{8,24},{9,... | collective-permute-start | bytes 589832 | tf_op jit(solution)/shard_map/ppermute | solution.py:1502
  117.7 7.0 %collective-permute-start.39 = (bf16[128,768]{1,0:T(8,128)(2,1)S(1)}, bf16[128,768]{1,0:T(8,128)(2,1)S(1)}, u32[]{:S(2)}, u32[]{:S(2)}) collective-permute-start(bf16[128,768]{1,0:T(8,128)(2,1)S(1)} %mlp_back_pass.1), channel_id=1, source_target_pairs={{0,16},{1,17},{2,18},{3,19},{4,20},{5,21},{6,22},{7,23},{8,24},{9,... | collective-permute-start | bytes 589832 | tf_op jit(solution)/shard_map/ppermute | solution.py:1502
  121.8 22.4 %collective-permute-start.45 = (bf16[384,896]{1,0:T(8,128)(2,1)S(1)}, bf16[384,896]{1,0:T(8,128)(2,1)S(1)}, u32[]{:S(2)}, u32[]{:S(2)}) collective-permute-start(bf16[384,896]{1,0:T(8,128)(2,1)S(1)} %get-tuple-element.242), channel_id=1, source_target_pairs={{0,2},{1,3},{2,0},{3,1},{4,6},{5,7},{6,4},{7,5},{8,10},{9,11},{10,... | collective-permute-start | bytes 2064392 | tf_op jit(solution)/shard_map/ppermute | solution.py:1502
  125.9 7.3 %collective-permute-start.40 = (bf16[128,768]{1,0:T(8,128)(2,1)S(1)}, bf16[128,768]{1,0:T(8,128)(2,1)S(1)}, u32[]{:S(2)}, u32[]{:S(2)}) collective-permute-start(bf16[128,768]{1,0:T(8,128)(2,1)S(1)} %get-tuple-element.248.refs_0_.refs_8_), channel_id=1, source_target_pairs={{0,16},{1,17},{2,18},{3,19},{4,20},{5,21},{6,22},{7,23},{8,24},{9,... | collective-permute-start | bytes 589832 | tf_op jit(solution)/shard_map/ppermute | solution.py:1502
  127.8 16.5 %collective-permute-start.44 = (bf16[384,768]{1,0:T(8,128)(2,1)S(1)}, bf16[384,768]{1,0:T(8,128)(2,1)S(1)}, u32[]{:S(2)}, u32[]{:S(2)}) collective-permute-start(bf16[384,768]{1,0:T(8,128)(2,1)S(1)} %get-tuple-element.262), channel_id=1, source_target_pairs={{0,1},{1,0},{2,3},{3,2},{4,5},{5,4},{6,7},{7,6},{8,9},{9,8},{10,11... | collective-permute-start | bytes 1769480 | tf_op jit(solution)/shard_map/ppermute | solution.py:1502
  133.3 9.4 %collective-permute-start.47 = (bf16[192,512]{1,0:T(8,128)(2,1)S(1)}, bf16[192,512]{1,0:T(8,128)(2,1)S(1)}, u32[]{:S(2)}, u32[]{:S(2)}) collective-permute-start(bf16[192,512]{1,0:T(8,128)(2,1)S(1)} %get-tuple-element.268.refs_0_.refs_12_), channel_id=1, source_target_pairs={{0,16},{1,17},{2,18},{3,19},{4,20},{5,21},{6,22},{7,23},{8,24},{9,... | collective-permute-start | bytes 589832 | tf_op jit(solution)/shard_map/ppermute | solution.py:1502
  145.0 11.3 %collective-permute-start.53 = (bf16[192,896]{1,0:T(8,128)(2,1)S(1)}, bf16[192,896]{1,0:T(8,128)(2,1)S(1)}, u32[]{:S(2)}, u32[]{:S(2)}) collective-permute-start(bf16[192,896]{1,0:T(8,128)(2,1)S(1)} %get-tuple-element.266), channel_id=1, source_target_pairs={{0,1},{1,0},{2,3},{3,2},{4,5},{5,4},{6,7},{7,6},{8,9},{9,8},{10,11... | collective-permute-start | bytes 1032200 | tf_op jit(solution)/shard_map/ppermute | solution.py:1502
  145.4 10.7 %collective-permute-start.52 = (bf16[192,768]{1,0:T(8,128)(2,1)S(1)}, bf16[192,768]{1,0:T(8,128)(2,1)S(1)}, u32[]{:S(2)}, u32[]{:S(2)}) collective-permute-start(bf16[192,768]{1,0:T(8,128)(2,1)S(1)} %get-tuple-element.278), channel_id=1, source_target_pairs={{0,2},{1,3},{2,0},{3,1},{4,6},{5,7},{6,4},{7,5},{8,10},{9,11},{10,... | collective-permute-start | bytes 884744 | tf_op jit(solution)/shard_map/ppermute | solution.py:1502
  147.5 10.9 %collective-permute-start.54 = (bf16[128,768]{1,0:T(8,128)(2,1)S(1)}, bf16[128,768]{1,0:T(8,128)(2,1)S(1)}, u32[]{:S(2)}, u32[]{:S(2)}) collective-permute-start(bf16[128,768]{1,0:T(8,128)(2,1)S(1)} %get-tuple-element.284), channel_id=1, source_target_pairs={{0,8},{1,9},{2,10},{3,11},{4,12},{5,13},{6,14},{7,15},{8,0},{9,1},... | collective-permute-start | bytes 589832 | tf_op jit(solution)/shard_map/ppermute | solution.py:1502
  153.5 16.5 %collective-permute-start.59 = (bf16[384,384]{1,0:T(8,128)(2,1)S(1)}, bf16[384,384]{1,0:T(8,128)(2,1)S(1)}, u32[]{:S(2)}, u32[]{:S(2)}) collective-permute-start(bf16[384,384]{1,0:T(8,128)(2,1)S(1)} %get-tuple-element.295), channel_id=1, source_target_pairs={{0,2},{1,3},{2,0},{3,1},{4,6},{5,7},{6,4},{7,5},{8,10},{9,11},{10,... | collective-permute-start | bytes 884744 | tf_op jit(solution)/shard_map/ppermute | solution.py:1502
  154.3 15.7 %collective-permute-start.58 = (bf16[384,384]{1,0:T(8,128)(2,1)S(1)}, bf16[384,384]{1,0:T(8,128)(2,1)S(1)}, u32[]{:S(2)}, u32[]{:S(2)}) collective-permute-start(bf16[384,384]{1,0:T(8,128)(2,1)S(1)} %get-tuple-element.293), channel_id=1, source_target_pairs={{0,1},{1,0},{2,3},{3,2},{4,5},{5,4},{6,7},{7,6},{8,9},{9,8},{10,11... | collective-permute-start | bytes 884744 | tf_op jit(solution)/shard_map/ppermute | solution.py:1502
  156.4 8.8 %collective-permute-start.56 = (bf16[128,768]{1,0:T(8,128)(2,1)S(1)}, bf16[128,768]{1,0:T(8,128)(2,1)S(1)}, u32[]{:S(2)}, u32[]{:S(2)}) collective-permute-start(bf16[128,768]{1,0:T(8,128)(2,1)S(1)} %get-tuple-element.276), channel_id=1, source_target_pairs={{0,1},{1,0},{2,3},{3,2},{4,5},{5,4},{6,7},{7,6},{8,9},{9,8},{10,11... | collective-permute-start | bytes 589832 | tf_op jit(solution)/shard_map/ppermute | solution.py:1502
  158.4 17.2 %collective-permute-start.61 = (bf16[96,1664]{1,0:T(8,128)(2,1)S(1)}, bf16[96,1664]{1,0:T(8,128)(2,1)S(1)}, u32[]{:S(2)}, u32[]{:S(2)}) collective-permute-start(bf16[96,1664]{1,0:T(8,128)(2,1)S(1)} %get-tuple-element.280), channel_id=1, source_target_pairs={{0,4},{1,5},{2,6},{3,7},{4,0},{5,1},{6,2},{7,3},{8,12},{9,13},{10,... | collective-permute-start | bytes 958472 | tf_op jit(solution)/shard_map/ppermute | solution.py:1502
  170.7 7.7 %collective-permute-start.63 = (bf16[224,384]{1,0:T(8,128)(2,1)S(1)}, bf16[224,384]{1,0:T(8,128)(2,1)S(1)}, u32[]{:S(2)}, u32[]{:S(2)}) collective-permute-start(bf16[224,384]{1,0:T(8,128)(2,1)S(1)} %get-tuple-element.302), channel_id=1, source_target_pairs={{0,1},{1,0},{2,3},{3,2},{4,5},{5,4},{6,7},{7,6},{8,9},{9,8},{10,11... | collective-permute-start | bytes 516104 | tf_op jit(solution)/shard_map/ppermute | solution.py:1502
  179.0 9.3 %collective-permute-start.66 = (bf16[96,1664]{1,0:T(8,128)(2,1)S(1)}, bf16[96,1664]{1,0:T(8,128)(2,1)S(1)}, u32[]{:S(2)}, u32[]{:S(2)}) collective-permute-start(bf16[96,1664]{1,0:T(8,128)(2,1)S(1)} %mlp_total.1.refs_0_), channel_id=1, source_target_pairs={{0,16},{1,17},{2,18},{3,19},{4,20},{5,21},{6,22},{7,23},{8,24},{9,... | collective-permute-start | bytes 958472 | tf_op jit(solution)/shard_map/ppermute | solution.py:1502
  180.0 7.7 %collective-permute-start.64 = (bf16[112,768]{1,0:T(8,128)(2,1)S(1)}, bf16[112,768]{1,0:T(8,128)(2,1)S(1)}, u32[]{:S(2)}, u32[]{:S(2)}) collective-permute-start(bf16[112,768]{1,0:T(8,128)(2,1)S(1)} %get-tuple-element.307), channel_id=1, source_target_pairs={{0,4},{1,5},{2,6},{3,7},{4,0},{5,1},{6,2},{7,3},{8,12},{9,13},{10,... | collective-permute-start | bytes 516104 | tf_op jit(solution)/shard_map/ppermute | solution.py:1502
  181.5 15.8 %collective-permute-start.65 = (bf16[96,1664]{1,0:T(8,128)(2,1)S(1)}, bf16[96,1664]{1,0:T(8,128)(2,1)S(1)}, u32[]{:S(2)}, u32[]{:S(2)}) collective-permute-start(bf16[96,1664]{1,0:T(8,128)(2,1)S(1)} %mlp_total.1.refs_0_), channel_id=1, source_target_pairs={{0,8},{1,9},{2,10},{3,11},{4,12},{5,13},{6,14},{7,15},{8,0},{9,1},... | collective-permute-start | bytes 958472 | tf_op jit(solution)/shard_map/ppermute | solution.py:1502
  188.3 9.0 %collective-permute-start.67 = (bf16[96,1664]{1,0:T(8,128)(2,1)S(1)}, bf16[96,1664]{1,0:T(8,128)(2,1)S(1)}, u32[]{:S(2)}, u32[]{:S(2)}) collective-permute-start(bf16[96,1664]{1,0:T(8,128)(2,1)S(1)} %collective-permute-done.66.refs_2_), channel_id=1, source_target_pairs={{0,8},{1,9},{2,10},{3,11},{4,12},{5,13},{6,14},{7,15},{8,0},{9,1},... | collective-permute-start | bytes 958472 | tf_op jit(solution)/shard_map/ppermute | solution.py:1502
  192.0 7.7 %collective-permute-start.69 = (bf16[96,896]{1,0:T(8,128)(2,1)S(1)}, bf16[96,896]{1,0:T(8,128)(2,1)S(1)}, u32[]{:S(2)}, u32[]{:S(2)}) collective-permute-start(bf16[96,896]{1,0:T(8,128)(2,1)S(1)} %qkv_total.1.refs_0_), channel_id=1, source_target_pairs={{0,16},{1,17},{2,18},{3,19},{4,20},{5,21},{6,22},{7,23},{8,24},{9,... | collective-permute-start | bytes 516104 | tf_op jit(solution)/shard_map/ppermute | solution.py:1502
  193.2 13.1 %collective-permute-start.57 = (bf16[144,768]{1,0:T(8,128)(2,1)S(1)}, bf16[144,768]{1,0:T(8,128)(2,1)S(1)}, u32[]{:S(2)}, u32[]{:S(2)}) collective-permute-start(bf16[144,768]{1,0:T(8,128)(2,1)S(1)} %get-tuple-element.287), channel_id=1, source_target_pairs={{0,0},{1,1},{2,16},{3,17},{4,8},{5,9},{6,24},{7,25},{8,4},{9,5},{1... | collective-permute-start | bytes 663560 | tf_op jit(solution)/shard_map/ppermute | solution.py:1502
  195.1 12.5 %collective-permute-start.68 = (bf16[96,896]{1,0:T(8,128)(2,1)S(1)}, bf16[96,896]{1,0:T(8,128)(2,1)S(1)}, u32[]{:S(2)}, u32[]{:S(2)}) collective-permute-start(bf16[96,896]{1,0:T(8,128)(2,1)S(1)} %qkv_total.1.refs_0_), channel_id=1, source_target_pairs={{0,8},{1,9},{2,10},{3,11},{4,12},{5,13},{6,14},{7,15},{8,0},{9,1},... | collective-permute-start | bytes 516104 | tf_op jit(solution)/shard_map/ppermute | solution.py:1502
  199.7 7.9 %collective-permute-start.70 = (bf16[96,896]{1,0:T(8,128)(2,1)S(1)}, bf16[96,896]{1,0:T(8,128)(2,1)S(1)}, u32[]{:S(2)}, u32[]{:S(2)}) collective-permute-start(bf16[96,896]{1,0:T(8,128)(2,1)S(1)} %collective-permute-done.69.refs_2_), channel_id=1, source_target_pairs={{0,8},{1,9},{2,10},{3,11},{4,12},{5,13},{6,14},{7,15},{8,0},{9,1},... | collective-permute-start | bytes 516104 | tf_op jit(solution)/shard_map/ppermute | solution.py:1502
  (32 other events, 152.3 us)

commit v7 on v6

--- a/solution.py
+++ b/solution.py
@@ -1885,7 +1885,6 @@
     mlp_share = after(mlp_share, sums)
     mlp_far, mlp_near = flip(mlp_share, 2), flip(mlp_share, 1)
     qkv_share = scatter_last(qkv_parts, sums, "qkv_total")
-    mlp_far = after(mlp_far, qkv_share)
     qkv_far, qkv_near = flip(qkv_share, 2), flip(qkv_share, 1)
     sum_up, sum_down, sum_conv = ordered_run(
         functools.partial(finish_mlp_kernel, ranks, hidden_quarter, width, unit),

time: 211 us -> 210 us (level)
  no operation moved by 1% of the time
where the time goes in v7:
time: 210 us; the launch traced here: 209 us
  waiting for transfers between devices  72 us (34%)
  starting transfers between devices  68.7 us (33%)
  Pallas kernels  58.2 us (28%)
  local copies, waits for them, and re-layouts  8.67 us (4%)
    ppermute x71, waiting for transfers between devices, permute(): return lax.ppermute(array, AXES, pairs)  72 us
    ppermute x71, starting transfers between devices, permute(): return lax.ppermute(array, AXES, pairs)  68.7 us
    pallas_call x37, Pallas kernels, run(): pl.pallas_call(kernel, in_specs=[pl.BlockSpec(memory_space=pltpu.SMEM)] +...  58.2 us
    unnamed x20, local copies, waits for them, and re-layouts  5.91 us
  transfers between devices with their start and end apart: 71, of which 28 were waited for; matrix products, arithmetic and copies ran while one was open for 2% of the time, Pallas kernels for 22%

profile of v7, /device:TPU:2, one launch (start us, length us, event | category | flops | bytes accessed | tf_op | source)
XLA Modules:
  0.0 209.4 jit_solution(2470605771382709099)
XLA Ops:
  0.7 3.6 %collective-permute-start = (bf16[128,768]{1,0:T(8,128)(2,1)}, bf16[128,768]{1,0:T(8,128)(2,1)S(1)}, u32[]{:S(2)}, u32[]{:S(2)}) collective-permute-start(bf16[128,768]{1,0:T(8,128)(2,1)} %bitcast.15), channel_id=1, source_target_pairs={{0,0},{1,1},{2,16},{3,17},{4,8},{5,9},{6,24},{7,25},{8,4},{9,5},{1... | collective-permute-start | bytes 589832 | tf_op jit(solution)/shard_map/ppermute | solution.py:1502
  8.1 1.6 collective-permute-start.3
  13.1 2.5 %collective-permute-start.1 = (bf16[32,768]{1,0:T(8,128)(2,1)S(1)}, bf16[32,768]{1,0:T(8,128)(2,1)S(1)}, u32[]{:S(2)}, u32[]{:S(2)}) collective-permute-start(bf16[32,768]{1,0:T(8,128)(2,1)S(1)} %pack.1), channel_id=1, source_target_pairs={{0,0},{1,1},{2,16},{3,17},{4,8},{5,9},{6,24},{7,25},{8,4},{9,5},{1... | collective-permute-start | bytes 147464 | tf_op jit(solution)/shard_map/ppermute | solution.py:1502
  22.8 1.8 collective-permute-start.10
  29.0 3.5 %collective-permute-done.6.refs_1_ = bf16[96,896]{1,0:T(8,128)(2,1)S(1)} collective-permute-done((bf16[96,896]{1,0:T(8,128)(2,1)S(1)}, bf16[96,896]{1,0:T(8,128)(2,1)S(1)}, u32[]{:S(2)}, u32[]{:S(2)}) %collective-permute-start.6) | collective-permute-done | bytes 172064 | tf_op jit(solution)/shard_map/ppermute | solution.py:1502
  34.4 2.8 %collective-permute-done.9.refs_13_ = bf16[96,768]{1,0:T(8,128)(2,1)S(1)} collective-permute-done((bf16[96,768]{1,0:T(8,128)(2,1)S(1)}, bf16[96,768]{1,0:T(8,128)(2,1)S(1)}, u32[]{:S(2)}, u32[]{:S(2)}) %collective-permute-start.9) | collective-permute-done | bytes 147488 | tf_op jit(solution)/shard_map/ppermute | solution.py:1502
  37.9 2.6 %collective-permute-done.8.refs_11_ = bf16[96,768]{1,0:T(8,128)(2,1)S(1)} collective-permute-done((bf16[96,768]{1,0:T(8,128)(2,1)S(1)}, bf16[96,768]{1,0:T(8,128)(2,1)S(1)}, u32[]{:S(2)}, u32[]{:S(2)}) %collective-permute-start.8) | collective-permute-done | bytes 147488 | tf_op jit(solution)/shard_map/ppermute | solution.py:1502
  40.5 2.1 collective-permute-done.11.refs_15_
  44.6 4.2 %collective-permute-done.16.refs_6_ = bf16[128,768]{1,0:T(8,128)(2,1)S(1)} collective-permute-done((bf16[128,768]{1,0:T(8,128)(2,1)S(1)}, bf16[128,768]{1,0:T(8,128)(2,1)S(1)}, u32[]{:S(2)}, u32[]{:S(2)}) %collective-permute-start.16) | collective-permute-done | bytes 196640 | tf_op jit(solution)/shard_map/ppermute | solution.py:1502
  49.9 1.7 collective-permute-start.23
  51.6 1.8 project.1
  55.3 5.9 %attend.1 = (bf16[192,512]{1,0:T(8,128)(2,1)S(1)}, f32[8,512]{1,0:T(8,128)S(1)}) custom-call(s32[3]{0:T(128)S(1)} %pad_add_fusion.ids_ref.unused_ref.rank_ref, bf16[512,192]{1,0:T(8,128)(2,1)S(1)} %get-tuple-element.188.refs_0_.refs_3_.refs_2_, bf16[1024,384]{1,0:T(8,128)(2,1)S(1)} %get-tuple-element.189.refs_1_.refs_4_.refs_3_, ...), custom_call_target="tpu_custom_call" | custom-call | tf_op jit(solution)/shard_map/attend/pallas_call | solution.py:745
  64.5 1.8 collective-permute-done.22.refs_1_
  70.4 5.9 %collective-permute-done.25.refs_3_ = bf16[128,768]{1,0:T(8,128)(2,1)S(1)} collective-permute-done((bf16[128,768]{1,0:T(8,128)(2,1)S(1)}, bf16[128,768]{1,0:T(8,128)(2,1)S(1)}, u32[]{:S(2)}, u32[]{:S(2)}) %collective-permute-start.25) | collective-permute-done | bytes 196640 | tf_op jit(solution)/shard_map/ppermute | solution.py:1502
  78.7 4.4 %collective-permute-done.29.refs_5_ = bf16[384,768]{1,0:T(8,128)(2,1)S(1)} collective-permute-done((bf16[384,768]{1,0:T(8,128)(2,1)S(1)}, bf16[384,768]{1,0:T(8,128)(2,1)S(1)}, u32[]{:S(2)}, u32[]{:S(2)}) %collective-permute-start.29) | collective-permute-done | bytes 589856 | tf_op jit(solution)/shard_map/ppermute | solution.py:1502
  84.1 2.1 %mlp.1 = (bf16[768,768]{1,0:T(8,128)(2,1)S(1)}, bf16[768,768]{1,0:T(8,128)(2,1)S(1)}, bf16[768,128]{1,0:T(8,128)(2,1)S(1)}, f32[1,768]{1,0:T(1,128)S(1)}, bf16[2...) custom-call(s32[3]{0:T(128)S(1)} %pad_add_fusion.ids_ref.unused_ref.rank, ...), custom_call_target="tpu_custom_call" | custom-call | tf_op jit(solution)/shard_map/mlp/pallas_call | solution.py:745
  87.7 2.0 mlp_more.1
  91.8 1.9 collective-permute-start.33
  93.7 5.2 %collective-permute-done.33.refs_3_ = bf16[128,768]{1,0:T(8,128)(2,1)S(1)} collective-permute-done((bf16[128,768]{1,0:T(8,128)(2,1)S(1)}, bf16[128,768]{1,0:T(8,128)(2,1)S(1)}, u32[]{:S(2)}, u32[]{:S(2)}) %collective-permute-start.33) | collective-permute-done | bytes 196640 | tf_op jit(solution)/shard_map/ppermute | solution.py:1502
  98.9 6.4 %tail.1 = (f32[16,768]{1,0:T(8,128)S(1)}, bf16[128,768]{1,0:T(8,128)(2,1)S(1)}, f32[128,768]{1,0:T(8,128)S(1)}, bf16[128,768]{1,0:T(8,128)(2,1)S(1)}, bf16[128,1...) custom-call(s32[3]{0:T(128)S(1)} %pad_add_fusion.ids_ref.unused_ref.rank_ref, f32[128,768]{1,0:T(8,128)S(1)} %get-tuple-element.242.refs_0_, ...), custom_call_target="tpu_custom_call" | custom-call | tf_op jit(solution)/shard_map/tail/pallas_call | solution.py:745
  105.3 1.8 collective-permute-start.34
  108.6 4.0 %collective-permute-done.34.refs_0_.refs_6_ = bf16[128,768]{1,0:T(8,128)(2,1)S(1)} collective-permute-done((bf16[128,768]{1,0:T(8,128)(2,1)S(1)}, bf16[128,768]{1,0:T(8,128)(2,1)S(1)}, u32[]{:S(2)}, u32[]{:S(2)}) %collective-permute-start.34) | collective-permute-done | bytes 196640 | tf_op jit(solution)/shard_map/ppermute | solution.py:1502
  117.7 1.8 collective-permute-start.39
  119.5 2.3 %mlp_grads.1 = (f32[384,768]{1,0:T(8,128)S(1)}, bf16[384,768]{1,0:T(8,128)(2,1)S(1)}, f32[384,896]{1,0:T(8,128)S(1)}, bf16[384,896]{1,0:T(8,128)(2,1)S(1)}) custom-call(s32[3]{0:T(128)S(1)} %pad_add_fusion.ids_ref.unused_ref.rank_ref, bf16[128,768]{1,0:T(8,128)(2,1)S(1)} %get-tuple-element.233.refs_0_, bf16[128,768]{1,0:T(8,128)(2,1)S(1)} %collective-permute-done.27.refs_1_, ...), custom_call_target="tpu_custom_call" | custom-call | tf_op jit(solution)/shard_map/mlp_grads/pallas_call | solution.py:745
  122.0 2.7 %collective-permute-done.39.refs_4_ = bf16[128,768]{1,0:T(8,128)(2,1)S(1)} collective-permute-done((bf16[128,768]{1,0:T(8,128)(2,1)S(1)}, bf16[128,768]{1,0:T(8,128)(2,1)S(1)}, u32[]{:S(2)}, u32[]{:S(2)}) %collective-permute-start.39) | collective-permute-done | bytes 196640 | tf_op jit(solution)/shard_map/ppermute | solution.py:1502
  125.9 1.8 collective-permute-start.40
  128.0 4.0 %attend_back.1 = (bf16[256,192]{1,0:T(8,128)(2,1)S(1)}, f32[1024,384]{1,0:T(8,128)S(1)}) custom-call(s32[3]{0:T(128)S(1)} %pad_add_fusion.ids_ref.unused_ref.rank_ref, bf16[128,768]{1,0:T(8,128)(2,1)S(1)} %get-tuple-element.247.refs_0_.refs_8_, bf16[128,768]{1,0:T(8,128)(2,1)S(1)} %collective-permute-done.41.refs_1_.refs_9_, ...), custom_call_target="tpu_custom_call" | custom-call | tf_op jit(solution)/shard_map/attend_back/pallas_call | solution.py:745
  133.3 1.7 collective-permute-start.47
  135.0 2.8 %attend_back_next.1 = (bf16[128,192]{1,0:T(8,128)(2,1)S(1)}, f32[1024,384]{1,0:T(8,128)S(1)}) custom-call(s32[3]{0:T(128)S(1)} %pad_add_fusion.ids_ref.unused_ref.rank_ref, bf16[128,768]{1,0:T(8,128)(2,1)S(1)} %collective-permute-done.40.refs_0_.refs_10_, bf16[192,768]{1,0:T(8,128)(2,1)S(1)} %get-tuple-element.196.refs_2_.refs_1_, ...), custom_call_target="tpu_custom_call" | custom-call | tf_op jit(solution)/shard_map/attend_back_next/pallas_call | solution.py:745
  137.8 4.3 %attend_back_last.1 = (bf16[512,576]{1,0:T(8,128)(2,1)S(1)}, bf16[512,384]{1,0:T(8,128)(2,1)S(1)}, f32[128,768]{1,0:T(8,128)S(1)}, f32[128,768]{1,0:T(8,128)S(1)...) custom-call(s32[3]{0:T(128)S(1)} %pad_add_fusion.ids_ref.unused_ref., ...), custom_call_target="tpu_custom_call" | custom-call | tf_op jit(solution)/shard_map/attend_back_last/pallas_call | solution.py:745
  147.5 2.3 %qkv_grads.1 = (f32[384,384]{1,0:T(8,128)S(1)}, bf16[384,384]{1,0:T(8,128)(2,1)S(1)}, f32[384,384]{1,0:T(8,128)S(1)}, bf16[384,384]{1,0:T(8,128)(2,1)S(1)}) custom-call(s32[3]{0:T(128)S(1)} %pad_add_fusion.ids_ref.unused_ref.rank_ref, bf16[128,768]{1,0:T(8,128)(2,1)S(1)} %get-tuple-element.266.refs_0_, bf16[128,768]{1,0:T(8,128)(2,1)S(1)} %collective-permute-done.13.refs_1_, ...), custom_call_target="tpu_custom_call" | custom-call | tf_op jit(solution)/shard_map/qkv_grads/pallas_call | solution.py:745
  149.9 2.7 %collective-permute-done.51.refs_4_ = bf16[128,768]{1,0:T(8,128)(2,1)S(1)} collective-permute-done((bf16[128,768]{1,0:T(8,128)(2,1)S(1)}, bf16[128,768]{1,0:T(8,128)(2,1)S(1)}, u32[]{:S(2)}, u32[]{:S(2)}) %collective-permute-start.51) | collective-permute-done | bytes 196640 | tf_op jit(solution)/shard_map/ppermute | solution.py:1502
  154.3 1.7 collective-permute-start.58
  159.6 2.1 %collective-permute-done.55.refs_4_ = bf16[128,768]{1,0:T(8,128)(2,1)S(1)} collective-permute-done((bf16[128,768]{1,0:T(8,128)(2,1)S(1)}, bf16[128,768]{1,0:T(8,128)(2,1)S(1)}, u32[]{:S(2)}, u32[]{:S(2)}) %collective-permute-start.55) | collective-permute-done | bytes 196640 | tf_op jit(solution)/shard_map/ppermute | solution.py:1502
  161.7 3.4 %collective-permute-done.56.refs_5_ = bf16[128,768]{1,0:T(8,128)(2,1)S(1)} collective-permute-done((bf16[128,768]{1,0:T(8,128)(2,1)S(1)}, bf16[128,768]{1,0:T(8,128)(2,1)S(1)}, u32[]{:S(2)}, u32[]{:S(2)}) %collective-permute-start.56) | collective-permute-done | bytes 196640 | tf_op jit(solution)/shard_map/ppermute | solution.py:1502
  167.0 3.0 %collective-permute-done.60.refs_5_ = bf16[96,128]{1,0:T(8,128)(2,1)S(1)} collective-permute-done((bf16[96,128]{1,0:T(8,128)(2,1)S(1)}, bf16[96,128]{1,0:T(8,128)(2,1)S(1)}, u32[]{:S(2)}, u32[]{:S(2)}) %collective-permute-start.60) | collective-permute-done | bytes 24608 | tf_op jit(solution)/shard_map/ppermute | solution.py:1502
  170.7 2.5 %collective-permute-start.63 = (bf16[224,384]{1,0:T(8,128)(2,1)S(1)}, bf16[224,384]{1,0:T(8,128)(2,1)S(1)}, u32[]{:S(2)}, u32[]{:S(2)}) collective-permute-start(bf16[224,384]{1,0:T(8,128)(2,1)S(1)} %get-tuple-element.301), channel_id=1, source_target_pairs={{0,1},{1,0},{2,3},{3,2},{4,5},{5,4},{6,7},{7,6},{8,9},{9,8},{10,11... | collective-permute-start | bytes 516104 | tf_op jit(solution)/shard_map/ppermute | solution.py:1502
  173.6 2.0 collective-permute-done.61.arrived_ref
  176.2 2.2 %collective-permute-done.62.refs_1_ = bf16[192,384]{1,0:T(8,128)(2,1)S(1)} collective-permute-done((bf16[192,384]{1,0:T(8,128)(2,1)S(1)}, bf16[192,384]{1,0:T(8,128)(2,1)S(1)}, u32[]{:S(2)}, u32[]{:S(2)}) %collective-permute-start.62) | collective-permute-done | bytes 147488 | tf_op jit(solution)/shard_map/ppermute | solution.py:1502
  181.5 3.1 %collective-permute-start.65 = (bf16[96,1664]{1,0:T(8,128)(2,1)S(1)}, bf16[96,1664]{1,0:T(8,128)(2,1)S(1)}, u32[]{:S(2)}, u32[]{:S(2)}) collective-permute-start(bf16[96,1664]{1,0:T(8,128)(2,1)S(1)} %mlp_total.1.refs_0_), channel_id=1, source_target_pairs={{0,8},{1,9},{2,10},{3,11},{4,12},{5,13},{6,14},{7,15},{8,0},{9,1},... | collective-permute-start | bytes 958472 | tf_op jit(solution)/shard_map/ppermute | solution.py:1502
  184.6 1.7 collective-permute-done.66.refs_2_
  186.3 3.0 %collective-permute-start.67 = (bf16[96,1664]{1,0:T(8,128)(2,1)S(1)}, bf16[96,1664]{1,0:T(8,128)(2,1)S(1)}, u32[]{:S(2)}, u32[]{:S(2)}) collective-permute-start(bf16[96,1664]{1,0:T(8,128)(2,1)S(1)} %collective-permute-done.66.refs_2_), channel_id=1, source_target_pairs={{0,8},{1,9},{2,10},{3,11},{4,12},{5,13},{6,14},{7,15},{8,0},{9,1},... | collective-permute-start | bytes 958472 | tf_op jit(solution)/shard_map/ppermute | solution.py:1502
  189.9 2.3 %collective-permute-start.69 = (bf16[96,896]{1,0:T(8,128)(2,1)S(1)}, bf16[96,896]{1,0:T(8,128)(2,1)S(1)}, u32[]{:S(2)}, u32[]{:S(2)}) collective-permute-start(bf16[96,896]{1,0:T(8,128)(2,1)S(1)} %qkv_total.1.refs_0_), channel_id=1, source_target_pairs={{0,16},{1,17},{2,18},{3,19},{4,20},{5,21},{6,22},{7,23},{8,24},{9,... | collective-permute-start | bytes 516104 | tf_op jit(solution)/shard_map/ppermute | solution.py:1502
  192.2 1.9 collective-permute-start.57
  194.1 1.8 collective-permute-start.68
  196.0 2.4 %finish_mlp.1 = (f32[96,3072]{1,0:T(8,128)}, f32[384,768]{1,0:T(8,128)}, f32[96,72]{1,0:T(8,128)S(1)}) custom-call(s32[3]{0:T(128)S(1)} %pad_add_fusion.ids_ref.unused_ref.rank_ref, bf16[96,1664]{1,0:T(8,128)(2,1)S(1)} %mlp_total.1.refs_0_, bf16[96,1664]{1,0:T(8,128)(2,1)S(1)} %collective-permute-done.65.refs_1_, ...), custom_call_target="tpu_custom_call" | custom-call | tf_op jit(solution)/shard_map/finish_mlp/pallas_call | solution.py:745
  199.1 6.6 %collective-permute-done.57.moved_ref = bf16[144,768]{1,0:T(8,128)(2,1)S(1)} collective-permute-done((bf16[144,768]{1,0:T(8,128)(2,1)S(1)}, bf16[144,768]{1,0:T(8,128)(2,1)S(1)}, u32[]{:S(2)}, u32[]{:S(2)}) %collective-permute-start.57) | collective-permute-done | bytes 221216 | tf_op jit(solution)/shard_map/ppermute | solution.py:1502
  207.0 1.8 finish_qkv.1
  (157 shorter events, 70.5 us)
Async XLA Ops:
  0.7 22.1 %collective-permute-start = (bf16[128,768]{1,0:T(8,128)(2,1)}, bf16[128,768]{1,0:T(8,128)(2,1)S(1)}, u32[]{:S(2)}, u32[]{:S(2)}) collective-permute-start(bf16[128,768]{1,0:T(8,128)(2,1)} %bitcast.15), channel_id=1, source_target_pairs={{0,0},{1,1},{2,16},{3,17},{4,8},{5,9},{6,24},{7,25},{8,4},{9,5},{1... | collective-permute-start | bytes 589832 | tf_op jit(solution)/shard_map/ppermute | solution.py:1502
  6.9 14.9 %collective-permute-start.4 = (bf16[96,768]{1,0:T(8,128)(2,1)S(1)}, bf16[96,768]{1,0:T(8,128)(2,1)S(1)}, u32[]{:S(2)}, u32[]{:S(2)}) collective-permute-start(bf16[96,768]{1,0:T(8,128)(2,1)S(1)} %select.10.refs_8_), channel_id=1, source_target_pairs={{0,4},{1,5},{2,6},{3,7},{4,0},{5,1},{6,2},{7,3},{8,12},{9,13},{10,... | collective-permute-start | bytes 442376 | tf_op jit(solution)/shard_map/ppermute | solution.py:1502
  8.1 17.3 %collective-permute-start.3 = (bf16[96,768]{1,0:T(8,128)(2,1)S(1)}, bf16[96,768]{1,0:T(8,128)(2,1)S(1)}, u32[]{:S(2)}, u32[]{:S(2)}) collective-permute-start(bf16[96,768]{1,0:T(8,128)(2,1)S(1)} %select.10.refs_8_), channel_id=1, source_target_pairs={{0,2},{1,3},{2,0},{3,1},{4,6},{5,7},{6,4},{7,5},{8,10},{9,11},{10,... | collective-permute-start | bytes 442376 | tf_op jit(solution)/shard_map/ppermute | solution.py:1502
  9.6 15.8 %collective-permute-start.2 = (bf16[96,768]{1,0:T(8,128)(2,1)S(1)}, bf16[96,768]{1,0:T(8,128)(2,1)S(1)}, u32[]{:S(2)}, u32[]{:S(2)}) collective-permute-start(bf16[96,768]{1,0:T(8,128)(2,1)S(1)} %select.10.refs_8_), channel_id=1, source_target_pairs={{0,1},{1,0},{2,3},{3,2},{4,5},{5,4},{6,7},{7,6},{8,9},{9,8},{10,11... | collective-permute-start | bytes 442376 | tf_op jit(solution)/shard_map/ppermute | solution.py:1502
  13.1 8.1 %collective-permute-start.1 = (bf16[32,768]{1,0:T(8,128)(2,1)S(1)}, bf16[32,768]{1,0:T(8,128)(2,1)S(1)}, u32[]{:S(2)}, u32[]{:S(2)}) collective-permute-start(bf16[32,768]{1,0:T(8,128)(2,1)S(1)} %pack.1), channel_id=1, source_target_pairs={{0,0},{1,1},{2,16},{3,17},{4,8},{5,9},{6,24},{7,25},{8,4},{9,5},{1... | collective-permute-start | bytes 147464 | tf_op jit(solution)/shard_map/ppermute | solution.py:1502
  21.2 11.2 %collective-permute-start.6 = (bf16[96,896]{1,0:T(8,128)(2,1)S(1)}, bf16[96,896]{1,0:T(8,128)(2,1)S(1)}, u32[]{:S(2)}, u32[]{:S(2)}) collective-permute-start(bf16[96,896]{1,0:T(8,128)(2,1)S(1)} %get-tuple-element.181.refs_0_), channel_id=1, source_target_pairs={{0,4},{1,5},{2,6},{3,7},{4,0},{5,1},{6,2},{7,3},{8,12},{9,13},{10,... | collective-permute-start | bytes 516104 | tf_op jit(solution)/shard_map/ppermute | solution.py:1502
  21.9 6.6 %collective-permute-start.7 = (bf16[96,768]{1,0:T(8,128)(2,1)S(1)}, bf16[96,768]{1,0:T(8,128)(2,1)S(1)}, u32[]{:S(2)}, u32[]{:S(2)}) collective-permute-start(bf16[96,768]{1,0:T(8,128)(2,1)S(1)} %get-tuple-element.174.refs_2_), channel_id=1, source_target_pairs={{0,1},{1,0},{2,3},{3,2},{4,5},{5,4},{6,7},{7,6},{8,9},{9,8},{10,11... | collective-permute-start | bytes 442376 | tf_op jit(solution)/shard_map/ppermute | solution.py:1502
  22.8 10.3 %collective-permute-start.10 = (bf16[96,768]{1,0:T(8,128)(2,1)S(1)}, bf16[96,768]{1,0:T(8,128)(2,1)S(1)}, u32[]{:S(2)}, u32[]{:S(2)}) collective-permute-start(bf16[96,768]{1,0:T(8,128)(2,1)S(1)} %collective-permute-done.4.refs_12_), channel_id=1, source_target_pairs={{0,2},{1,3},{2,0},{3,1},{4,6},{5,7},{6,4},{7,5},{8,10},{9,11},{10,... | collective-permute-start | bytes 442376 | tf_op jit(solution)/shard_map/ppermute | solution.py:1502
  25.4 11.9 %collective-permute-start.5 = (bf16[128,768]{1,0:T(8,128)(2,1)S(1)}, bf16[128,768]{1,0:T(8,128)(2,1)S(1)}, u32[]{:S(2)}, u32[]{:S(2)}) collective-permute-start(bf16[128,768]{1,0:T(8,128)(2,1)S(1)} %get-tuple-element.266.refs_0_), channel_id=1, source_target_pairs={{0,16},{1,17},{2,18},{3,19},{4,20},{5,21},{6,22},{7,23},{8,24},{9,... | collective-permute-start | bytes 589832 | tf_op jit(solution)/shard_map/ppermute | solution.py:1502
  26.9 10.9 %collective-permute-start.12 = (bf16[128,768]{1,0:T(8,128)(2,1)S(1)}, bf16[128,768]{1,0:T(8,128)(2,1)S(1)}, u32[]{:S(2)}, u32[]{:S(2)}) collective-permute-start(bf16[128,768]{1,0:T(8,128)(2,1)S(1)} %get-tuple-element.266.refs_0_), channel_id=1, source_target_pairs={{0,1},{1,0},{2,3},{3,2},{4,5},{5,4},{6,7},{7,6},{8,9},{9,8},{10,11... | collective-permute-start | bytes 589832 | tf_op jit(solution)/shard_map/ppermute | solution.py:1502
  28.5 8.8 %collective-permute-start.9 = (bf16[96,768]{1,0:T(8,128)(2,1)S(1)}, bf16[96,768]{1,0:T(8,128)(2,1)S(1)}, u32[]{:S(2)}, u32[]{:S(2)}) collective-permute-start(bf16[96,768]{1,0:T(8,128)(2,1)S(1)} %collective-permute-done.4.refs_12_), channel_id=1, source_target_pairs={{0,1},{1,0},{2,3},{3,2},{4,5},{5,4},{6,7},{7,6},{8,9},{9,8},{10,11... | collective-permute-start | bytes 442376 | tf_op jit(solution)/shard_map/ppermute | solution.py:1502
  32.4 8.0 %collective-permute-start.8 = (bf16[96,768]{1,0:T(8,128)(2,1)S(1)}, bf16[96,768]{1,0:T(8,128)(2,1)S(1)}, u32[]{:S(2)}, u32[]{:S(2)}) collective-permute-start(bf16[96,768]{1,0:T(8,128)(2,1)S(1)} %collective-permute-done.3.refs_10_), channel_id=1, source_target_pairs={{0,1},{1,0},{2,3},{3,2},{4,5},{5,4},{6,7},{7,6},{8,9},{9,8},{10,11... | collective-permute-start | bytes 442376 | tf_op jit(solution)/shard_map/ppermute | solution.py:1502
  33.0 9.5 %collective-permute-start.11 = (bf16[96,768]{1,0:T(8,128)(2,1)S(1)}, bf16[96,768]{1,0:T(8,128)(2,1)S(1)}, u32[]{:S(2)}, u32[]{:S(2)}) collective-permute-start(bf16[96,768]{1,0:T(8,128)(2,1)S(1)} %collective-permute-done.10.refs_14_), channel_id=1, source_target_pairs={{0,1},{1,0},{2,3},{3,2},{4,5},{5,4},{6,7},{7,6},{8,9},{9,8},{10,11... | collective-permute-start | bytes 442376 | tf_op jit(solution)/shard_map/ppermute | solution.py:1502
  37.3 7.3 %collective-permute-start.13 = (bf16[128,768]{1,0:T(8,128)(2,1)S(1)}, bf16[128,768]{1,0:T(8,128)(2,1)S(1)}, u32[]{:S(2)}, u32[]{:S(2)}) collective-permute-start(bf16[128,768]{1,0:T(8,128)(2,1)S(1)} %get-tuple-element.266.refs_0_), channel_id=1, source_target_pairs={{0,8},{1,9},{2,10},{3,11},{4,12},{5,13},{6,14},{7,15},{8,0},{9,1},... | collective-permute-start | bytes 589832 | tf_op jit(solution)/shard_map/ppermute | solution.py:1502
  37.3 7.3 %collective-permute-start.14 = (bf16[128,768]{1,0:T(8,128)(2,1)S(1)}, bf16[128,768]{1,0:T(8,128)(2,1)S(1)}, u32[]{:S(2)}, u32[]{:S(2)}) collective-permute-start(bf16[128,768]{1,0:T(8,128)(2,1)S(1)} %collective-permute-done.5.far_ref.refs_2_), channel_id=1, source_target_pairs={{0,8},{1,9},{2,10},{3,11},{4,12},{5,13},{6,14},{7,15},{8,0},{9,1},... | collective-permute-start | bytes 589832 | tf_op jit(solution)/shard_map/ppermute | solution.py:1502
  37.8 6.8 %collective-permute-start.15 = (bf16[128,768]{1,0:T(8,128)(2,1)S(1)}, bf16[128,768]{1,0:T(8,128)(2,1)S(1)}, u32[]{:S(2)}, u32[]{:S(2)}) collective-permute-start(bf16[128,768]{1,0:T(8,128)(2,1)S(1)} %collective-permute-done.12.side_ref.refs_4_), channel_id=1, source_target_pairs={{0,8},{1,9},{2,10},{3,11},{4,12},{5,13},{6,14},{7,15},{8,0},{9,1},... | collective-permute-start | bytes 589832 | tf_op jit(solution)/shard_map/ppermute | solution.py:1502
  49.5 16.9 %collective-permute-start.22 = (bf16[192,896]{1,0:T(8,128)(2,1)S(1)}, bf16[192,896]{1,0:T(8,128)(2,1)S(1)}, u32[]{:S(2)}, u32[]{:S(2)}) collective-permute-start(bf16[192,896]{1,0:T(8,128)(2,1)S(1)} %get-tuple-element.199.refs_0_), channel_id=1, source_target_pairs={{0,2},{1,3},{2,0},{3,1},{4,6},{5,7},{6,4},{7,5},{8,10},{9,11},{10,... | collective-permute-start | bytes 1032200 | tf_op jit(solution)/shard_map/ppermute | solution.py:1502
  49.9 14.6 %collective-permute-start.23 = (bf16[192,768]{1,0:T(8,128)(2,1)S(1)}, bf16[192,768]{1,0:T(8,128)(2,1)S(1)}, u32[]{:S(2)}, u32[]{:S(2)}) collective-permute-start(bf16[192,768]{1,0:T(8,128)(2,1)S(1)} %get-tuple-element.183.refs_2_), channel_id=1, source_target_pairs={{0,4},{1,5},{2,6},{3,7},{4,0},{5,1},{6,2},{7,3},{8,12},{9,13},{10,... | collective-permute-start | bytes 884744 | tf_op jit(solution)/shard_map/ppermute | solution.py:1502
  53.4 7.9 %collective-permute-start.18 = (bf16[192,192]{1,0:T(8,128)(2,1)S(1)}, bf16[192,192]{1,0:T(8,128)(2,1)S(1)}, u32[]{:S(2)}, u32[]{:S(2)}) collective-permute-start(bf16[192,192]{1,0:T(8,128)(2,1)S(1)} %get-tuple-element.193), channel_id=1, source_target_pairs={{0,8},{1,9},{2,10},{3,11},{4,12},{5,13},{6,14},{7,15},{8,0},{9,1},... | collective-permute-start | bytes 221192 | tf_op jit(solution)/shard_map/ppermute | solution.py:1502
  53.5 7.8 %collective-permute-start.19 = (bf16[192,192]{1,0:T(8,128)(2,1)S(1)}, bf16[192,192]{1,0:T(8,128)(2,1)S(1)}, u32[]{:S(2)}, u32[]{:S(2)}) collective-permute-start(bf16[192,192]{1,0:T(8,128)(2,1)S(1)} %get-tuple-element.194), channel_id=1, source_target_pairs={{0,16},{1,17},{2,18},{3,19},{4,20},{5,21},{6,22},{7,23},{8,24},{9,... | collective-permute-start | bytes 221192 | tf_op jit(solution)/shard_map/ppermute | solution.py:1502
  54.7 6.6 %collective-permute-start.20 = (bf16[192,192]{1,0:T(8,128)(2,1)S(1)}, bf16[192,192]{1,0:T(8,128)(2,1)S(1)}, u32[]{:S(2)}, u32[]{:S(2)}) collective-permute-start(bf16[192,192]{1,0:T(8,128)(2,1)S(1)} %get-tuple-element.187), channel_id=1, source_target_pairs={{0,24},{1,25},{2,26},{3,27},{4,28},{5,29},{6,30},{7,31},{8,16},{9,... | collective-permute-start | bytes 221192 | tf_op jit(solution)/shard_map/ppermute | solution.py:1502
  66.9 17.1 %collective-permute-start.28 = (bf16[384,896]{1,0:T(8,128)(2,1)S(1)}, bf16[384,896]{1,0:T(8,128)(2,1)S(1)}, u32[]{:S(2)}, u32[]{:S(2)}) collective-permute-start(bf16[384,896]{1,0:T(8,128)(2,1)S(1)} %get-tuple-element.207.refs_2_), channel_id=1, source_target_pairs={{0,1},{1,0},{2,3},{3,2},{4,5},{5,4},{6,7},{7,6},{8,9},{9,8},{10,11... | collective-permute-start | bytes 2064392 | tf_op jit(solution)/shard_map/ppermute | solution.py:1502
  68.4 14.7 %collective-permute-start.29 = (bf16[384,768]{1,0:T(8,128)(2,1)S(1)}, bf16[384,768]{1,0:T(8,128)(2,1)S(1)}, u32[]{:S(2)}, u32[]{:S(2)}) collective-permute-start(bf16[384,768]{1,0:T(8,128)(2,1)S(1)} %get-tuple-element.200.refs_4_), channel_id=1, source_target_pairs={{0,2},{1,3},{2,0},{3,1},{4,6},{5,7},{6,4},{7,5},{8,10},{9,11},{10,... | collective-permute-start | bytes 1769480 | tf_op jit(solution)/shard_map/ppermute | solution.py:1502
  69.0 7.3 %collective-permute-start.25 = (bf16[128,768]{1,0:T(8,128)(2,1)S(1)}, bf16[128,768]{1,0:T(8,128)(2,1)S(1)}, u32[]{:S(2)}, u32[]{:S(2)}) collective-permute-start(bf16[128,768]{1,0:T(8,128)(2,1)S(1)} %out_pass.1), channel_id=1, source_target_pairs={{0,16},{1,17},{2,18},{3,19},{4,20},{5,21},{6,22},{7,23},{8,24},{9,... | collective-permute-start | bytes 589832 | tf_op jit(solution)/shard_map/ppermute | solution.py:1502
  77.2 9.0 %collective-permute-start.26 = (bf16[128,768]{1,0:T(8,128)(2,1)S(1)}, bf16[128,768]{1,0:T(8,128)(2,1)S(1)}, u32[]{:S(2)}, u32[]{:S(2)}) collective-permute-start(bf16[128,768]{1,0:T(8,128)(2,1)S(1)} %get-tuple-element.233.refs_0_), channel_id=1, source_target_pairs={{0,16},{1,17},{2,18},{3,19},{4,20},{5,21},{6,22},{7,23},{8,24},{9,... | collective-permute-start | bytes 589832 | tf_op jit(solution)/shard_map/ppermute | solution.py:1502
  91.8 7.1 %collective-permute-start.33 = (bf16[128,768]{1,0:T(8,128)(2,1)S(1)}, bf16[128,768]{1,0:T(8,128)(2,1)S(1)}, u32[]{:S(2)}, u32[]{:S(2)}) collective-permute-start(bf16[128,768]{1,0:T(8,128)(2,1)S(1)} %mlp_pass.1), channel_id=1, source_target_pairs={{0,16},{1,17},{2,18},{3,19},{4,20},{5,21},{6,22},{7,23},{8,24},{9,... | collective-permute-start | bytes 589832 | tf_op jit(solution)/shard_map/ppermute | solution.py:1502
  105.3 7.3 %collective-permute-start.34 = (bf16[128,768]{1,0:T(8,128)(2,1)S(1)}, bf16[128,768]{1,0:T(8,128)(2,1)S(1)}, u32[]{:S(2)}, u32[]{:S(2)}) collective-permute-start(bf16[128,768]{1,0:T(8,128)(2,1)S(1)} %get-tuple-element.222.refs_0_.refs_4_), channel_id=1, source_target_pairs={{0,16},{1,17},{2,18},{3,19},{4,20},{5,21},{6,22},{7,23},{8,24},{9,... | collective-permute-start | bytes 589832 | tf_op jit(solution)/shard_map/ppermute | solution.py:1502
  117.7 7.0 %collective-permute-start.39 = (bf16[128,768]{1,0:T(8,128)(2,1)S(1)}, bf16[128,768]{1,0:T(8,128)(2,1)S(1)}, u32[]{:S(2)}, u32[]{:S(2)}) collective-permute-start(bf16[128,768]{1,0:T(8,128)(2,1)S(1)} %mlp_back_pass.1), channel_id=1, source_target_pairs={{0,16},{1,17},{2,18},{3,19},{4,20},{5,21},{6,22},{7,23},{8,24},{9,... | collective-permute-start | bytes 589832 | tf_op jit(solution)/shard_map/ppermute | solution.py:1502
  121.8 22.4 %collective-permute-start.45 = (bf16[384,896]{1,0:T(8,128)(2,1)S(1)}, bf16[384,896]{1,0:T(8,128)(2,1)S(1)}, u32[]{:S(2)}, u32[]{:S(2)}) collective-permute-start(bf16[384,896]{1,0:T(8,128)(2,1)S(1)} %get-tuple-element.241), channel_id=1, source_target_pairs={{0,2},{1,3},{2,0},{3,1},{4,6},{5,7},{6,4},{7,5},{8,10},{9,11},{10,... | collective-permute-start | bytes 2064392 | tf_op jit(solution)/shard_map/ppermute | solution.py:1502
  125.9 7.3 %collective-permute-start.40 = (bf16[128,768]{1,0:T(8,128)(2,1)S(1)}, bf16[128,768]{1,0:T(8,128)(2,1)S(1)}, u32[]{:S(2)}, u32[]{:S(2)}) collective-permute-start(bf16[128,768]{1,0:T(8,128)(2,1)S(1)} %get-tuple-element.247.refs_0_.refs_8_), channel_id=1, source_target_pairs={{0,16},{1,17},{2,18},{3,19},{4,20},{5,21},{6,22},{7,23},{8,24},{9,... | collective-permute-start | bytes 589832 | tf_op jit(solution)/shard_map/ppermute | solution.py:1502
  127.8 16.5 %collective-permute-start.44 = (bf16[384,768]{1,0:T(8,128)(2,1)S(1)}, bf16[384,768]{1,0:T(8,128)(2,1)S(1)}, u32[]{:S(2)}, u32[]{:S(2)}) collective-permute-start(bf16[384,768]{1,0:T(8,128)(2,1)S(1)} %get-tuple-element.261), channel_id=1, source_target_pairs={{0,1},{1,0},{2,3},{3,2},{4,5},{5,4},{6,7},{7,6},{8,9},{9,8},{10,11... | collective-permute-start | bytes 1769480 | tf_op jit(solution)/shard_map/ppermute | solution.py:1502
  133.3 9.4 %collective-permute-start.47 = (bf16[192,512]{1,0:T(8,128)(2,1)S(1)}, bf16[192,512]{1,0:T(8,128)(2,1)S(1)}, u32[]{:S(2)}, u32[]{:S(2)}) collective-permute-start(bf16[192,512]{1,0:T(8,128)(2,1)S(1)} %get-tuple-element.267.refs_0_.refs_12_), channel_id=1, source_target_pairs={{0,16},{1,17},{2,18},{3,19},{4,20},{5,21},{6,22},{7,23},{8,24},{9,... | collective-permute-start | bytes 589832 | tf_op jit(solution)/shard_map/ppermute | solution.py:1502
  145.0 11.3 %collective-permute-start.53 = (bf16[192,896]{1,0:T(8,128)(2,1)S(1)}, bf16[192,896]{1,0:T(8,128)(2,1)S(1)}, u32[]{:S(2)}, u32[]{:S(2)}) collective-permute-start(bf16[192,896]{1,0:T(8,128)(2,1)S(1)} %get-tuple-element.265), channel_id=1, source_target_pairs={{0,1},{1,0},{2,3},{3,2},{4,5},{5,4},{6,7},{7,6},{8,9},{9,8},{10,11... | collective-permute-start | bytes 1032200 | tf_op jit(solution)/shard_map/ppermute | solution.py:1502
  145.4 10.7 %collective-permute-start.52 = (bf16[192,768]{1,0:T(8,128)(2,1)S(1)}, bf16[192,768]{1,0:T(8,128)(2,1)S(1)}, u32[]{:S(2)}, u32[]{:S(2)}) collective-permute-start(bf16[192,768]{1,0:T(8,128)(2,1)S(1)} %get-tuple-element.277), channel_id=1, source_target_pairs={{0,2},{1,3},{2,0},{3,1},{4,6},{5,7},{6,4},{7,5},{8,10},{9,11},{10,... | collective-permute-start | bytes 884744 | tf_op jit(solution)/shard_map/ppermute | solution.py:1502
  147.5 10.9 %collective-permute-start.54 = (bf16[128,768]{1,0:T(8,128)(2,1)S(1)}, bf16[128,768]{1,0:T(8,128)(2,1)S(1)}, u32[]{:S(2)}, u32[]{:S(2)}) collective-permute-start(bf16[128,768]{1,0:T(8,128)(2,1)S(1)} %get-tuple-element.283), channel_id=1, source_target_pairs={{0,8},{1,9},{2,10},{3,11},{4,12},{5,13},{6,14},{7,15},{8,0},{9,1},... | collective-permute-start | bytes 589832 | tf_op jit(solution)/shard_map/ppermute | solution.py:1502
  153.5 16.5 %collective-permute-start.59 = (bf16[384,384]{1,0:T(8,128)(2,1)S(1)}, bf16[384,384]{1,0:T(8,128)(2,1)S(1)}, u32[]{:S(2)}, u32[]{:S(2)}) collective-permute-start(bf16[384,384]{1,0:T(8,128)(2,1)S(1)} %get-tuple-element.294), channel_id=1, source_target_pairs={{0,2},{1,3},{2,0},{3,1},{4,6},{5,7},{6,4},{7,5},{8,10},{9,11},{10,... | collective-permute-start | bytes 884744 | tf_op jit(solution)/shard_map/ppermute | solution.py:1502
  154.3 15.7 %collective-permute-start.58 = (bf16[384,384]{1,0:T(8,128)(2,1)S(1)}, bf16[384,384]{1,0:T(8,128)(2,1)S(1)}, u32[]{:S(2)}, u32[]{:S(2)}) collective-permute-start(bf16[384,384]{1,0:T(8,128)(2,1)S(1)} %get-tuple-element.292), channel_id=1, source_target_pairs={{0,1},{1,0},{2,3},{3,2},{4,5},{5,4},{6,7},{7,6},{8,9},{9,8},{10,11... | collective-permute-start | bytes 884744 | tf_op jit(solution)/shard_map/ppermute | solution.py:1502
  156.4 8.8 %collective-permute-start.56 = (bf16[128,768]{1,0:T(8,128)(2,1)S(1)}, bf16[128,768]{1,0:T(8,128)(2,1)S(1)}, u32[]{:S(2)}, u32[]{:S(2)}) collective-permute-start(bf16[128,768]{1,0:T(8,128)(2,1)S(1)} %get-tuple-element.275), channel_id=1, source_target_pairs={{0,1},{1,0},{2,3},{3,2},{4,5},{5,4},{6,7},{7,6},{8,9},{9,8},{10,11... | collective-permute-start | bytes 589832 | tf_op jit(solution)/shard_map/ppermute | solution.py:1502
  158.4 17.2 %collective-permute-start.61 = (bf16[96,1664]{1,0:T(8,128)(2,1)S(1)}, bf16[96,1664]{1,0:T(8,128)(2,1)S(1)}, u32[]{:S(2)}, u32[]{:S(2)}) collective-permute-start(bf16[96,1664]{1,0:T(8,128)(2,1)S(1)} %get-tuple-element.279), channel_id=1, source_target_pairs={{0,4},{1,5},{2,6},{3,7},{4,0},{5,1},{6,2},{7,3},{8,12},{9,13},{10,... | collective-permute-start | bytes 958472 | tf_op jit(solution)/shard_map/ppermute | solution.py:1502
  170.7 7.7 %collective-permute-start.63 = (bf16[224,384]{1,0:T(8,128)(2,1)S(1)}, bf16[224,384]{1,0:T(8,128)(2,1)S(1)}, u32[]{:S(2)}, u32[]{:S(2)}) collective-permute-start(bf16[224,384]{1,0:T(8,128)(2,1)S(1)} %get-tuple-element.301), channel_id=1, source_target_pairs={{0,1},{1,0},{2,3},{3,2},{4,5},{5,4},{6,7},{7,6},{8,9},{9,8},{10,11... | collective-permute-start | bytes 516104 | tf_op jit(solution)/shard_map/ppermute | solution.py:1502
  179.0 7.3 %collective-permute-start.66 = (bf16[96,1664]{1,0:T(8,128)(2,1)S(1)}, bf16[96,1664]{1,0:T(8,128)(2,1)S(1)}, u32[]{:S(2)}, u32[]{:S(2)}) collective-permute-start(bf16[96,1664]{1,0:T(8,128)(2,1)S(1)} %mlp_total.1.refs_0_), channel_id=1, source_target_pairs={{0,16},{1,17},{2,18},{3,19},{4,20},{5,21},{6,22},{7,23},{8,24},{9,... | collective-permute-start | bytes 958472 | tf_op jit(solution)/shard_map/ppermute | solution.py:1502
  180.0 9.3 %collective-permute-start.64 = (bf16[112,768]{1,0:T(8,128)(2,1)S(1)}, bf16[112,768]{1,0:T(8,128)(2,1)S(1)}, u32[]{:S(2)}, u32[]{:S(2)}) collective-permute-start(bf16[112,768]{1,0:T(8,128)(2,1)S(1)} %get-tuple-element.306), channel_id=1, source_target_pairs={{0,4},{1,5},{2,6},{3,7},{4,0},{5,1},{6,2},{7,3},{8,12},{9,13},{10,... | collective-permute-start | bytes 516104 | tf_op jit(solution)/shard_map/ppermute | solution.py:1502
  181.5 14.4 %collective-permute-start.65 = (bf16[96,1664]{1,0:T(8,128)(2,1)S(1)}, bf16[96,1664]{1,0:T(8,128)(2,1)S(1)}, u32[]{:S(2)}, u32[]{:S(2)}) collective-permute-start(bf16[96,1664]{1,0:T(8,128)(2,1)S(1)} %mlp_total.1.refs_0_), channel_id=1, source_target_pairs={{0,8},{1,9},{2,10},{3,11},{4,12},{5,13},{6,14},{7,15},{8,0},{9,1},... | collective-permute-start | bytes 958472 | tf_op jit(solution)/shard_map/ppermute | solution.py:1502
  186.3 9.6 %collective-permute-start.67 = (bf16[96,1664]{1,0:T(8,128)(2,1)S(1)}, bf16[96,1664]{1,0:T(8,128)(2,1)S(1)}, u32[]{:S(2)}, u32[]{:S(2)}) collective-permute-start(bf16[96,1664]{1,0:T(8,128)(2,1)S(1)} %collective-permute-done.66.refs_2_), channel_id=1, source_target_pairs={{0,8},{1,9},{2,10},{3,11},{4,12},{5,13},{6,14},{7,15},{8,0},{9,1},... | collective-permute-start | bytes 958472 | tf_op jit(solution)/shard_map/ppermute | solution.py:1502
  189.9 8.4 %collective-permute-start.69 = (bf16[96,896]{1,0:T(8,128)(2,1)S(1)}, bf16[96,896]{1,0:T(8,128)(2,1)S(1)}, u32[]{:S(2)}, u32[]{:S(2)}) collective-permute-start(bf16[96,896]{1,0:T(8,128)(2,1)S(1)} %qkv_total.1.refs_0_), channel_id=1, source_target_pairs={{0,16},{1,17},{2,18},{3,19},{4,20},{5,21},{6,22},{7,23},{8,24},{9,... | collective-permute-start | bytes 516104 | tf_op jit(solution)/shard_map/ppermute | solution.py:1502
  192.2 13.5 %collective-permute-start.57 = (bf16[144,768]{1,0:T(8,128)(2,1)S(1)}, bf16[144,768]{1,0:T(8,128)(2,1)S(1)}, u32[]{:S(2)}, u32[]{:S(2)}) collective-permute-start(bf16[144,768]{1,0:T(8,128)(2,1)S(1)} %get-tuple-element.286), channel_id=1, source_target_pairs={{0,0},{1,1},{2,16},{3,17},{4,8},{5,9},{6,24},{7,25},{8,4},{9,5},{1... | collective-permute-start | bytes 663560 | tf_op jit(solution)/shard_map/ppermute | solution.py:1502
  194.1 12.9 %collective-permute-start.68 = (bf16[96,896]{1,0:T(8,128)(2,1)S(1)}, bf16[96,896]{1,0:T(8,128)(2,1)S(1)}, u32[]{:S(2)}, u32[]{:S(2)}) collective-permute-start(bf16[96,896]{1,0:T(8,128)(2,1)S(1)} %qkv_total.1.refs_0_), channel_id=1, source_target_pairs={{0,8},{1,9},{2,10},{3,11},{4,12},{5,13},{6,14},{7,15},{8,0},{9,1},... | collective-permute-start | bytes 516104 | tf_op jit(solution)/shard_map/ppermute | solution.py:1502
  198.3 8.7 %collective-permute-start.70 = (bf16[96,896]{1,0:T(8,128)(2,1)S(1)}, bf16[96,896]{1,0:T(8,128)(2,1)S(1)}, u32[]{:S(2)}, u32[]{:S(2)}) collective-permute-start(bf16[96,896]{1,0:T(8,128)(2,1)S(1)} %collective-permute-done.69.refs_2_), channel_id=1, source_target_pairs={{0,8},{1,9},{2,10},{3,11},{4,12},{5,13},{6,14},{7,15},{8,0},{9,1},... | collective-permute-start | bytes 516104 | tf_op jit(solution)/shard_map/ppermute | solution.py:1502
  (32 other events, 152.3 us)
